TPU v7x, 32 devices: a whole 2x2x4 slice. The times are simulated.
32 devices in a mesh: spec: 4 (over y, x), wave: 8 (over z, core).
Axes of the slice: x: 2, y: 2, z: 4, core: 2. Of those that a mesh axis runs over, the one named last changes fastest.
Arguments:
- pixels: float32 [8, 8, 400, 500], P(None, 'spec', 'wave')
- ivar: float32 [8, 8, 400, 500], P(None, 'spec', 'wave'), may hold values from 0.25 to 4
- mask: int32 [8, 8, 400, 500], P(None, 'spec', 'wave'), may hold values 0 or 1
- psf_left: float32 [8, 8, 400, 500], P(None, 'spec', 'wave'), may hold values from 0.1 to 0.45
- psf_right: float32 [8, 8, 400, 500], P(None, 'spec', 'wave'), may hold values from 0.1 to 0.45
- sky_index: int32 [8, 40], P('spec'), may hold values from 0 to 499, as said below
Outputs:
- cleaned: float32 [8, 8, 400, 500], P(None, 'spec', 'wave')
- sky_model: float32 [8, 400], P(None, 'wave')
Inputs may be any that keep to these rules, and one draw needn't show every extreme that they name: `sky_index`: each row names 40 different fibres.
All inputs are finite; a program needn't handle non-finite values. No bound on the sum of `mask` on one device may be relied on, other than what follows from the above.
Results may differ from a plain program's by a relative error of at most 0.0002.
Values sent between devices are 32-bit elements; how exact they have to be, the bound alone decides.
No kernel may reach another device: no remote copies, remote signals or barrier semaphores. Data moves between devices by JAX's collectives and lax.ppermute only.
A program may use at most 128 MiB of HBM per device.

v0:
```python
import jax
import jax.numpy as jnp
from jax import lax
from jax.sharding import PartitionSpec as P

F = 500


REG = 0.05
RIDGE = 1.0


def extended_2(cells, sides, width):
    for axis, dim in sides:
        count = lax.axis_size(axis)
        ends = count - 1
        head = lax.slice_in_dim(cells, 0, width, axis=dim)
        tail = lax.slice_in_dim(cells, cells.shape[dim] - width, cells.shape[dim], axis=dim)
        cells = jnp.concatenate(
            [
                lax.ppermute(tail, axis, [(i, (i + 1) % count) for i in range(ends)]),
                cells,
                lax.ppermute(head, axis, [((i + 1) % count, i) for i in range(ends)]),
            ],
            axis=dim,
        )
    return cells


def shift_up(values):
    return jnp.concatenate([values[1:], jnp.zeros_like(values[:1])], axis=0)


def shift_down(values):
    return jnp.concatenate([jnp.zeros_like(values[:1]), values[:-1]], axis=0)


def band_terms(pixel_rows, weight, left, right):
    diag_main = weight + shift_up(weight * left * left) + shift_down(weight * right * right) + REG
    first_off = weight * right + shift_up(weight * left)
    second_off = shift_up(weight * left * right)
    rhs_rows = (
        weight * pixel_rows
        + shift_up(weight * left * pixel_rows)
        + shift_down(weight * right * pixel_rows)
    )
    return (diag_main, first_off, second_off, rhs_rows)


def band_factor(diag_main, first_off, second_off):
    length = diag_main.shape[0]
    unit_fill = jnp.ones_like(diag_main[0])
    zero_fill = jnp.zeros_like(diag_main[0])
    pivots, lowers, farther = ([], [], [])
    pivot_last, pivot_before, lower_last = (unit_fill, unit_fill, zero_fill)
    for step_row in range(length):
        prev_one = first_off[step_row - 1] if step_row >= 1 else zero_fill
        prev_two = second_off[step_row - 2] if step_row >= 2 else zero_fill
        far_term = prev_two / pivot_before
        lower_term = (prev_one - far_term * lower_last) / pivot_last
        pivot_now = jnp.sqrt(diag_main[step_row] - lower_term * lower_term - far_term * far_term)
        pivots.append(pivot_now)
        lowers.append(lower_term)
        farther.append(far_term)
        pivot_before, pivot_last = (pivot_last, pivot_now)
        lower_last = lower_term
    return (pivots, lowers, farther)


def band_substitute(factors, rhs_rows):
    pivots, lowers, farther = factors
    length = len(pivots)
    zero_fill = jnp.zeros_like(rhs_rows[0])
    forward = []
    forward_last, forward_before = (zero_fill, zero_fill)
    for step_row in range(length):
        forward_now = (
            rhs_rows[step_row]
            - lowers[step_row] * forward_last
            - farther[step_row] * forward_before
        ) / pivots[step_row]
        forward.append(forward_now)
        forward_before, forward_last = (forward_last, forward_now)
    solved = [None] * length
    next_one, next_two = (zero_fill, zero_fill)
    for step_row in reversed(range(length)):
        result_now = forward[step_row]
        if step_row + 1 < length:
            result_now = result_now - lowers[step_row + 1] * next_one
        if step_row + 2 < length:
            result_now = result_now - farther[step_row + 2] * next_two
        result_now = result_now / pivots[step_row]
        solved[step_row] = result_now
        next_two, next_one = (next_one, result_now)
    return jnp.stack(solved)


def band_solve(pixel_rows, weight, left, right):
    diag_main, first_off, second_off, rhs_rows = band_terms(pixel_rows, weight, left, right)
    factors = band_factor(diag_main, first_off, second_off)
    return (band_substitute(factors, rhs_rows), diag_main)


def local(pixels, ivar, mask, psf_left, psf_right, sky_index):
    weight = ivar * (1.0 - mask.astype(jnp.float32))
    stacked = jnp.stack([pixels, weight, psf_left, psf_right])
    rows_here = pixels.shape[2]
    extended = extended_2(stacked, (("wave", 3),), 4)
    full_rows = jnp.moveaxis(extended, 3, 1)
    solved_all, diag_main = band_solve(full_rows[0], full_rows[1], full_rows[2], full_rows[3])
    solved = solved_all[4 : 4 + rows_here]
    diag_kept = diag_main[4 : 4 + rows_here]
    flux = jnp.moveaxis(solved, 0, 2)
    precision = jnp.moveaxis(diag_kept, 0, 2)
    is_sky = jnp.sum(
        (sky_index[:, :, None] == jnp.arange(F)[None, None, :]).astype(jnp.float32), axis=1
    )
    numer = jnp.einsum("eswf,sf->ew", precision * flux, is_sky, precision=lax.Precision.HIGHEST)
    denom = jnp.einsum("eswf,sf->ew", precision, is_sky, precision=lax.Precision.HIGHEST)
    numer, denom = lax.psum((numer, denom), "spec")
    sky_model = numer / denom
    total_rows = rows_here * lax.axis_size("wave")
    offsets = lax.axis_index("wave") * rows_here + jnp.arange(rows_here)
    position = 2.0 * offsets.astype(jnp.float32) / (total_rows - 1) - 1.0
    square = sky_model * sky_model
    moments = jnp.stack(
        [
            jnp.sum(square, axis=1),
            jnp.sum(square * position, axis=1),
            jnp.sum(square * position * position, axis=1),
        ],
        axis=1,
    )
    first_sum = jnp.einsum("eswf,ew->esf", flux, sky_model, precision=lax.Precision.HIGHEST)
    second_sum = jnp.einsum(
        "eswf,ew->esf", flux, sky_model * position, precision=lax.Precision.HIGHEST
    )
    fibre_sums = jnp.stack([first_sum, second_sum])
    moments, fibre_sums = lax.psum((moments, fibre_sums), "wave")
    upper_left = (moments[:, 0] + RIDGE)[:, None, None]
    lower_right = (moments[:, 2] + RIDGE)[:, None, None]
    cross = moments[:, 1][:, None, None]
    determinant = upper_left * lower_right - cross * cross
    slope_a = (lower_right * fibre_sums[0] - cross * fibre_sums[1]) / determinant
    slope_b = (upper_left * fibre_sums[1] - cross * fibre_sums[0]) / determinant
    fitted = (
        slope_a[:, :, None, :] + slope_b[:, :, None, :] * position[None, None, :, None]
    ) * sky_model[:, None, :, None]
    cleaned = flux - fitted
    return (cleaned, sky_model)


def solution(mesh):
    in_specs = (
        P(None, "spec", "wave", None),
        P(None, "spec", "wave", None),
        P(None, "spec", "wave", None),
        P(None, "spec", "wave", None),
        P(None, "spec", "wave", None),
        P("spec", None),
    )
    out_specs = (P(None, "spec", "wave", None), P(None, "wave"))
    return jax.shard_map(local, mesh=mesh, in_specs=in_specs, out_specs=out_specs, check_vma=False)
```

profile of v0, /device:TPU:0, one launch (start us, length us, event | category | flops | bytes accessed | tf_op | source)
XLA Modules:
  0.0 106.2 jit_solution(12239304600849943687)
XLA Ops:
  0.7 3.0 %copy_bitcast_fusion.3 = (f32[1,8,2,50,500]{4,1,3,2,0:T(8,128)S(1)}, f32[1,8,2,50,500]{4,1,3,2,0:T(8,128)S(1)}) fusion(f32[8,2,50,500]{3,1,2,0:T(2,128)} %param.10, f32[8,2,50,500]{3,1,2,0:T(2,128)} %param.9), kind=kLoop, calls=%fused_computation.25 | loop fusion | bytes 6400000 | tf_op jit(solution)/shard_map/stack | solution.py:106
  4.0 1.6 %fusion.9 = (f32[1,8,2,50,500]{4,1,3,2,0:T(8,128)S(1)}, f32[1,8,2,50,500]{4,1,3,2,0:T(8,128)S(1)}) fusion(f32[8,2,50,500]{3,1,2,0:T(2,128)S(1)} %copy-done.10, s32[8,2,50,500]{3,1,2,0:T(2,128)S(1)} %copy-done.11, f32[8,2,50,500]{3,1,2,0:T(2,128)S(1)} %copy-done.12), kind=kLoop, calls=%fused_computation.28 | loop fusion | flops 1200000 | bytes 8000000 | tf_op jit(solution)/shard_map/stack | solution.py:106
  5.6 1.1 %copy-done.8 = f32[1,8,2,50,500]{4,1,3,2,0:T(8,128)} copy-done((f32[1,8,2,50,500]{4,1,3,2,0:T(8,128)}, f32[1,8,2,50,500]{4,1,3,2,0:T(8,128)S(1)}, u32[]{:S(2)}) %copy-start.8) | copy-done | bytes 1600024
  6.8 1.1 %pad_maximum_fusion.3 = (f32[4,8,2,4,500]{4,1,3,2,0:T(8,128)}, f32[4,8,2,4,500]{4,1,3,2,0:T(8,128)}) fusion(f32[1,8,2,50,500]{4,1,3,2,0:T(8,128)S(1)} %get-tuple-element.425, f32[1,8,2,50,500]{4,1,3,2,0:T(8,128)S(1)} %get-tuple-element.426, f32[1,8,2,50,500]{4,1,3,2,0:T(8,128)S(1)} %get-tuple-element.427, f32[1,8,2,50,500]{4,1,3,2,0:T(8,128)S(1)} %get-tuple-element.428), kind=kLoop, calls=%fused_computation.37 | loop fusion | flops 768000 | bytes 7424000 | tf_op jit(solution)/shard_map/slice | solution.py:18
  7.9 3.1 %collective-permute-start = (f32[4,8,2,4,500]{4,1,3,2,0:T(8,128)}, f32[4,8,2,4,500]{4,1,3,2,0:T(8,128)}, u32[]{:S(2)}, u32[]{:S(2)}) collective-permute-start(f32[4,8,2,4,500]{4,1,3,2,0:T(8,128)} %get-tuple-element.410), channel_id=1, source_target_pairs={{0,1},{1,2},{2,3},{3,4},{4,5},{5,6},{6,7},{8,9},{9,10},{10,11},{11... | collective-permute-start | bytes 1536008 | tf_op jit(solution)/shard_map/ppermute | solution.py:21
  11.0 1.3 %collective-permute-start.1 = (f32[4,8,2,4,500]{4,1,3,2,0:T(8,128)}, f32[4,8,2,4,500]{4,1,3,2,0:T(8,128)}, u32[]{:S(2)}, u32[]{:S(2)}) collective-permute-start(f32[4,8,2,4,500]{4,1,3,2,0:T(8,128)} %get-tuple-element.411), channel_id=1, source_target_pairs={{1,0},{2,1},{3,2},{4,3},{5,4},{6,5},{7,6},{9,8},{10,9},{11,10},{12... | collective-permute-start | bytes 1536008 | tf_op jit(solution)/shard_map/ppermute | solution.py:23
  12.5 4.1 %collective-permute-done.1 = f32[4,8,2,4,500]{4,1,3,2,0:T(8,128)} collective-permute-done((f32[4,8,2,4,500]{4,1,3,2,0:T(8,128)}, f32[4,8,2,4,500]{4,1,3,2,0:T(8,128)}, u32[]{:S(2)}, u32[]{:S(2)}) %collective-permute-start.1) | collective-permute-done | bytes 512032 | tf_op jit(solution)/shard_map/ppermute | solution.py:23
  16.6 2.9 %maximum_bitcast_fusion = f32[4,58,8,2,500]{4,2,1,3,0:T(8,128)S(1)} fusion(f32[4,8,2,4,500]{4,1,3,2,0:T(8,128)} %collective-permute-done.1, f32[1,8,2,50,500]{4,1,3,2,0:T(8,128)S(1)} %get-tuple-element.425, f32[1,8,2,50,500]{4,1,3,2,0:T(8,128)S(1)} %get-tuple-element.426, f32[1,8,2,50,500]{4,1,3,2,0:T(8,128)} %copy-done.8, f32[1,8,2,50,500]{4,1,3,2,0:T(8,128)} %copy-done.9, ...), kind=kLoop, calls=%fused_computation | loop fusion | flops 9280000 | bytes 14848000 | tf_op jit(solution)/shard_map/transpose | solution.py:109
  24.2 1.2 %pad_add_fusion.2 = (f32[58,8,2,500]{3,1,2,0:T(8,128)S(1)}, f32[58,8,2,500]{3,1,2,0:T(8,128)S(1)}) fusion(f32[57,8,2,500]{3,1,2,0:T(8,128)S(1)} %get-tuple-element.418, f32[57,8,2,500]{3,1,2,0:T(8,128)S(1)} %get-tuple-element.415, f32[1,58,8,2,500]{4,2,1,3,0:T(8,128)S(1)} %get-tuple-element.407, f32[1,58,8,2,500]{4,2,1,3,0:T(8,128)S(1)} %get-tuple-element.406, ...), kind=kLoop, calls=%fused_computation.9 | loop fusion | flops 1856000 | bytes 12896000 | tf_op jit(solution)/shard_map/add | solution.py:43
  26.5 1.0 fusion.277
  27.5 1.0 subtract_divide_fusion.186
  30.7 1.1 %subtract_divide_fusion.107 = (f32[1,8,2,500]{3,1,2,0:T(8,128)S(1)}, f32[1,8,2,500]{3,1,2,0:T(8,128)S(1)}, f32[1,8,2,500]{3,1,2,0:T(8,128)S(1)}, f32[1,8,2,500]{...) fusion(f32[1,8,2,500]{3,1,2,0:T(8,128)S(1)} %get-tuple-element.160, ...), kind=kLoop, calls=%fused_computation.887 | loop fusion | flops 272000 | bytes 704000 | tf_op jit(solution)/shard_map/div | solution.py:77
  31.8 1.0 subtract_divide_fusion.105
  33.9 1.1 %subtract_divide_fusion.101 = (f32[1,8,2,500]{3,1,2,0:T(8,128)S(1)}, f32[1,8,2,500]{3,1,2,0:T(8,128)S(1)}, f32[1,8,2,500]{3,1,2,0:T(8,128)S(1)}, f32[1,8,2,500]{...) fusion(f32[1,8,2,500]{3,1,2,0:T(8,128)S(1)} %get-tuple-element.142, ...), kind=kLoop, calls=%fused_computation.881 | loop fusion | flops 272000 | bytes 704000 | tf_op jit(solution)/shard_map/div | solution.py:77
  36.1 1.1 %subtract_divide_fusion.97 = (f32[1,8,2,500]{3,1,2,0:T(8,128)S(1)}, f32[1,8,2,500]{3,1,2,0:T(8,128)S(1)}, f32[1,8,2,500]{3,1,2,0:T(8,128)S(1)}, f32[1,8,2,500]{3...) fusion(f32[1,8,2,500]{3,1,2,0:T(8,128)S(1)} %get-tuple-element.130, ...), kind=kLoop, calls=%fused_computation.877 | loop fusion | flops 272000 | bytes 704000 | tf_op jit(solution)/shard_map/div | solution.py:77
  38.3 1.1 %subtract_divide_fusion.93 = (f32[1,8,2,500]{3,1,2,0:T(8,128)S(1)}, f32[1,8,2,500]{3,1,2,0:T(8,128)S(1)}, f32[1,8,2,500]{3,1,2,0:T(8,128)S(1)}, f32[1,8,2,500]{3...) fusion(f32[1,8,2,500]{3,1,2,0:T(8,128)S(1)} %get-tuple-element.118, ...), kind=kLoop, calls=%fused_computation.873 | loop fusion | flops 272000 | bytes 704000 | tf_op jit(solution)/shard_map/div | solution.py:77
  42.5 1.0 subtract_divide_fusion.24
  50.1 3.3 %fusion.3 = f32[1,8,50,1]{2,0,3,1:T(1,128)S(1)} fusion(f32[8,2,50,500]{3,0,2,1:T(8,128)S(1)} %bitcast_multiply_fusion.5, f32[2,500,1,1]{1,0,2,3:T(2,128)S(1)} %bitcast.2827), kind=kOutput, calls=%fused_computation.16 | convolution fusion | flops 4800000 | bytes 1605600 | tf_op jit(solution)/shard_map/eswf,sf->ew/dot_general | solution.py:118
  53.3 3.3 %fusion.1 = f32[1,8,50,1]{2,0,3,1:T(1,128)S(1)} fusion(f32[8,2,50,500]{3,0,2,1:T(8,128)S(1)} %slice_bitcast_fusion.1, f32[2,500,1,1]{1,0,2,3:T(2,128)S(1)} %bitcast.2828), kind=kOutput, calls=%fused_computation.14 | convolution fusion | flops 4800000 | bytes 1605600 | tf_op jit(solution)/shard_map/eswf,sf->ew/dot_general | solution.py:119
  56.7 10.1 %all-reduce.6 = (f32[8,50]{1,0:T(8,128)S(1)}, f32[8,50]{1,0:T(8,128)S(1)}) all-reduce(f32[8,50]{1,0:T(8,128)S(1)} %bitcast.2829, f32[8,50]{1,0:T(8,128)S(1)} %bitcast.2830), channel_id=1, replica_groups=mesh['spec'=4,'wave'=8] {'spec'}, use_global_device_ids=true, to_apply=%region_1.0 | all-reduce | flops 800 | bytes 6400 | tf_op jit(solution)/shard_map/psum | solution.py:120
  66.9 2.0 %fusion.7 = f32[8,1,2,500]{3,1,2,0:T(1,128)S(1)} fusion(f32[8,50,1,1]{1,2,3,0:T(1,128)S(1)} %bitcast.2826, f32[8,2,50,500]{3,0,2,1:T(8,128)S(1)} %bitcast.2819), kind=kOutput, calls=%fused_computation.20 | convolution fusion | flops 4800000 | bytes 1633600 | tf_op jit(solution)/shard_map/eswf,ew->esf/dot_general | solution.py:134
  69.0 2.0 %fusion.5 = f32[8,1,2,500]{3,1,2,0:T(1,128)S(1)} fusion(f32[8,50,1,1]{1,2,3,0:T(1,128)S(1)} %bitcast.2831, f32[8,2,50,500]{3,0,2,1:T(8,128)S(1)} %bitcast.2820), kind=kOutput, calls=%fused_computation.18 | convolution fusion | flops 4800000 | bytes 1633600 | tf_op jit(solution)/shard_map/eswf,ew->esf/dot_general | solution.py:135
  71.1 32.2 %all-reduce.5 = (f32[2,8,2,500]{3,1,2,0:T(8,128)S(1)}, f32[8,3]{0,1:T(4,128)S(1)}) all-reduce(f32[2,8,2,500]{3,1,2,0:T(8,128)S(1)} %pad_maximum_fusion.4, f32[8,3]{0,1:T(4,128)S(1)} %pad_maximum_fusion.5), channel_id=1, replica_groups=mesh['spec'=4,'wave'=8] {'wave'}, use_global_device_ids=true, to_apply=%region_7.0 | all-reduce | flops 16024 | bytes 128192 | tf_op jit(solution)/shard_map/psum | solution.py:139
  103.8 2.4 %copy.467 = f32[8,2,50,500]{3,1,2,0:T(2,128)} copy(f32[8,2,50,500]{3,0,2,1:T(8,128)S(1)} %multiply_subtract_fusion) | data formatting | bytes 3200000
  (128 shorter events, 21.1 us)
Async XLA Ops:
  0.6 3.1 %copy-start.12 = (f32[8,2,50,500]{3,1,2,0:T(2,128)S(1)}, f32[8,2,50,500]{3,1,2,0:T(2,128)}, u32[]{:S(2)}) copy-start(f32[8,2,50,500]{3,1,2,0:T(2,128)} %param.6) | copy-start | bytes 4800004
  0.6 3.1 %copy-start.10 = (f32[8,2,50,500]{3,1,2,0:T(2,128)S(1)}, f32[8,2,50,500]{3,1,2,0:T(2,128)}, u32[]{:S(2)}) copy-start(f32[8,2,50,500]{3,1,2,0:T(2,128)} %param.7) | copy-start | bytes 4800004
  0.7 3.4 %copy-start.11 = (s32[8,2,50,500]{3,1,2,0:T(2,128)S(1)}, s32[8,2,50,500]{3,1,2,0:T(2,128)}, u32[]{:S(2)}) copy-start(s32[8,2,50,500]{3,1,2,0:T(2,128)} %param.8) | copy-start | bytes 4800004
  5.6 1.2 %copy-start.8 = (f32[1,8,2,50,500]{4,1,3,2,0:T(8,128)}, f32[1,8,2,50,500]{4,1,3,2,0:T(8,128)S(1)}, u32[]{:S(2)}) copy-start(f32[1,8,2,50,500]{4,1,3,2,0:T(8,128)S(1)} %get-tuple-element.427) | copy-start | bytes 4800004
  5.6 2.3 %copy-start.9 = (f32[1,8,2,50,500]{4,1,3,2,0:T(8,128)}, f32[1,8,2,50,500]{4,1,3,2,0:T(8,128)S(1)}, u32[]{:S(2)}) copy-start(f32[1,8,2,50,500]{4,1,3,2,0:T(8,128)S(1)} %get-tuple-element.428) | copy-start | bytes 4800004
  6.8 5.6 %copy-start.14 = (s32[2,40]{1,0:T(2,128)S(1)}, s32[2,40]{1,0:T(2,128)}, u32[]{:S(2)}) copy-start(s32[2,40]{1,0:T(2,128)} %param.11) | copy-start | bytes 964
  7.9 4.6 %collective-permute-start = (f32[4,8,2,4,500]{4,1,3,2,0:T(8,128)}, f32[4,8,2,4,500]{4,1,3,2,0:T(8,128)}, u32[]{:S(2)}, u32[]{:S(2)}) collective-permute-start(f32[4,8,2,4,500]{4,1,3,2,0:T(8,128)} %get-tuple-element.410), channel_id=1, source_target_pairs={{0,1},{1,2},{2,3},{3,4},{4,5},{5,6},{6,7},{8,9},{9,10},{10,11},{11... | collective-permute-start | bytes 1536008 | tf_op jit(solution)/shard_map/ppermute | solution.py:21
  11.0 5.5 %collective-permute-start.1 = (f32[4,8,2,4,500]{4,1,3,2,0:T(8,128)}, f32[4,8,2,4,500]{4,1,3,2,0:T(8,128)}, u32[]{:S(2)}, u32[]{:S(2)}) collective-permute-start(f32[4,8,2,4,500]{4,1,3,2,0:T(8,128)} %get-tuple-element.411), channel_id=1, source_target_pairs={{1,0},{2,1},{3,2},{4,3},{5,4},{6,5},{7,6},{9,8},{10,9},{11,10},{12... | collective-permute-start | bytes 1536008 | tf_op jit(solution)/shard_map/ppermute | solution.py:23
  21.5 7.5 %copy-start.2 = (f32[58,8,2,500]{3,1,2,0:T(8,128)}, f32[58,8,2,500]{3,1,2,0:T(8,128)S(1)}, u32[]{:S(2)}) copy-start(f32[58,8,2,500]{3,1,2,0:T(8,128)S(1)} %get-tuple-element.402) | copy-start | bytes 5568004
  23.3 4.2 %copy-start.6 = (f32[58,8,2,500]{3,1,2,0:T(8,128)}, f32[58,8,2,500]{3,1,2,0:T(8,128)S(1)}, u32[]{:S(2)}) copy-start(f32[58,8,2,500]{3,1,2,0:T(8,128)S(1)} %get-tuple-element.404) | copy-start | bytes 5568004
  25.4 2.1 %copy-start.4 = (f32[58,8,2,500]{3,1,2,0:T(8,128)}, f32[58,8,2,500]{3,1,2,0:T(8,128)S(1)}, u32[]{:S(2)}) copy-start(f32[58,8,2,500]{3,1,2,0:T(8,128)S(1)} %get-tuple-element.413) | copy-start | bytes 5568004
  25.9 1.6 %copy-start = (f32[58,8,2,500]{3,1,0,2:T(8,128)}, f32[58,8,2,500]{3,1,0,2:T(8,128)S(1)}, u32[]{:S(2)}) copy-start(f32[58,8,2,500]{3,1,0,2:T(8,128)S(1)} %fusion) | copy-start | bytes 5568004
  30.7 9.8 %copy-start.7 = (f32[58,8,2,500]{3,1,2,0:T(8,128)S(1)}, f32[58,8,2,500]{3,1,2,0:T(8,128)}, u32[]{:S(2)}) copy-start(f32[58,8,2,500]{3,1,2,0:T(8,128)} %copy-done.6) | copy-start | bytes 5568004
  33.9 6.6 %copy-start.3 = (f32[58,8,2,500]{3,1,2,0:T(8,128)S(1)}, f32[58,8,2,500]{3,1,2,0:T(8,128)}, u32[]{:S(2)}) copy-start(f32[58,8,2,500]{3,1,2,0:T(8,128)} %copy-done.2) | copy-start | bytes 5568004
  36.1 4.4 %copy-start.1 = (f32[58,8,2,500]{3,1,0,2:T(8,128)S(1)}, f32[58,8,2,500]{3,1,0,2:T(8,128)}, u32[]{:S(2)}) copy-start(f32[58,8,2,500]{3,1,0,2:T(8,128)} %copy-done) | copy-start | bytes 5568004
  38.2 2.4 %copy-start.5 = (f32[58,8,2,500]{3,1,2,0:T(8,128)S(1)}, f32[58,8,2,500]{3,1,2,0:T(8,128)}, u32[]{:S(2)}) copy-start(f32[58,8,2,500]{3,1,2,0:T(8,128)} %copy-done.4) | copy-start | bytes 5568004
  66.9 36.4 %copy-start.13 = (f32[8,50]{1,0:T(8,128)}, f32[8,50]{1,0:T(8,128)S(1)}, u32[]{:S(2)}) copy-start(f32[8,50]{1,0:T(8,128)S(1)} %get-tuple-element.11) | copy-start | bytes 4804
where the time goes:
time: 107 us; the launch traced here: 106 us
  blocking collectives  42.2 us (39%)
  other arithmetic  34.4 us (32%)
  matrix products  10.7 us (10%)
  local copies, waits for them, and re-layouts  8.75 us (8%)
  starting transfers between devices  4.43 us (4%)
  waiting for transfers between devices  4.12 us (4%)
  between operations  1.58 us (1%)
    psum x1, blocking collectives, local(): moments, fibre_sums = lax.psum((moments, fibre_sums), 'wave')  32.2 us
    div x12, other arithmetic, band_substitute(): (rhs_rows[step_row] - lowers[step_row] * forward_last - farther[step_row]...  10.9 us
    psum x1, blocking collectives, local(): numer, denom = lax.psum((numer, denom), 'spec')  10.1 us
    div x16, other arithmetic, band_substitute(): result_now = result_now / pivots[step_row]  10 us
    unnamed x80, local copies, waits for them, and re-layouts  4.58 us
    ppermute x1, waiting for transfers between devices, extended_2(): lax.ppermute(head, axis, [((i + 1) % count, i) for i in range(ends)])  4.12 us
    dot_general x1, matrix products, local(): jnp.einsum('eswf,sf->ew', precision, is_sky, precision=lax.Precision.HIGH...  3.31 us
    dot_general x1, matrix products, local(): jnp.einsum('eswf,sf->ew', precision * flux, is_sky, precision=lax.Precisi...  3.29 us
  transfers between devices with their start and end apart: 2, of which 1 were waited for; matrix products, arithmetic and copies ran while one was open for 0% of the time, Pallas kernels for 0%

commit v1 on v0

v1 whole, which is shorter than its diff:
```python
import functools

import jax
import jax.numpy as jnp
from jax import lax
from jax.experimental import pallas as pl
from jax.experimental.pallas import tpu as pltpu
from jax.sharding import PartitionSpec as P

REG = 0.05
RIDGE = 1.0
HALO = 4
PARTS = 6
LANES = 128

F32 = jnp.float32
VM = pl.BlockSpec(memory_space=pltpu.VMEM)
SM = pl.BlockSpec(memory_space=pltpu.SMEM)
HB = pl.BlockSpec(memory_space=pl.ANY)


def in_vmem(shape, dtype=F32):
    return jax.ShapeDtypeStruct(shape, dtype)


def recip(values):
    return 1.0 / values


def weight_of(ivar, mask):
    return jnp.where(mask == 0, ivar, 0.0)


def edge_message(p, w, l, r):
    wl = [a * b for a, b in zip(w, l)]
    wr = [a * b for a, b in zip(w, r)]
    d0 = w[0] + wl[1] * l[1] + REG
    d1 = w[1] + wr[0] * r[0] + wl[2] * l[2] + REG
    d2 = w[2] + wr[1] * r[1] + wl[3] * l[3] + REG
    d3 = w[3] + wr[2] * r[2]
    d4 = wr[3] * r[3]
    raw = d4
    a01 = wr[0] + wl[1]
    a12 = wr[1] + wl[2]
    a23 = wr[2] + wl[3]
    a34 = wr[3]
    a02 = wl[1] * r[1]
    a13 = wl[2] * r[2]
    a24 = wl[3] * r[3]
    b0 = w[0] * p[0] + wl[1] * p[1]
    b1 = w[1] * p[1] + wr[0] * p[0] + wl[2] * p[2]
    b2 = w[2] * p[2] + wr[1] * p[1] + wl[3] * p[3]
    b3 = w[3] * p[3] + wr[2] * p[2]
    b4 = wr[3] * p[3]
    inv = recip(d0)
    near, far = a01 * inv, a02 * inv
    d1, a12, d2 = d1 - near * a01, a12 - near * a02, d2 - far * a02
    b1, b2 = b1 - near * b0, b2 - far * b0
    inv = recip(d1)
    near, far = a12 * inv, a13 * inv
    d2, a23, d3 = d2 - near * a12, a23 - near * a13, d3 - far * a13
    b2, b3 = b2 - near * b1, b3 - far * b1
    inv = recip(d2)
    near, far = a23 * inv, a24 * inv
    d3, a34, d4 = d3 - near * a23, a34 - near * a24, d4 - far * a24
    b3, b4 = b3 - near * b2, b4 - far * b2
    return (d3, a34, d4, b3, b4, raw)


def edge_kernel(pix, iva, msk, lef, rig, near_out, far_out, bufs, mbuf, out_buf, sems, out_sems):
    exposures, rows = pix.shape[0], pix.shape[1]
    odd = lax.rem(lax.axis_index("wave"), 2)
    copies = []
    for end, start in enumerate((0, rows - HALO)):
        for slot, ref in enumerate((pix, iva, lef, rig)):
            copies.append(
                pltpu.make_async_copy(
                    ref.at[:, start : start + HALO], bufs.at[end, slot], sems.at[end, slot]
                )
            )
        copies.append(
            pltpu.make_async_copy(msk.at[:, start : start + HALO], mbuf.at[end], sems.at[end, 4])
        )
    for copy in copies:
        copy.start()
    for end in range(2):
        for copy in copies[5 * end : 5 * end + 5]:
            copy.wait()
        order = range(HALO - 1, -1, -1) if end == 0 else range(HALO)
        for e in range(exposures):
            p = [bufs[end, 0, e, k] for k in order]
            w = [weight_of(bufs[end, 1, e, k], mbuf[end, e, k]) for k in order]
            l = [bufs[end, 2, e, k] for k in order]
            r = [bufs[end, 3, e, k] for k in order]
            if end == 0:
                l, r = r, l
            for slot, part in enumerate(edge_message(p, w, l, r)):
                out_buf[end, slot, e] = part

    def send(end, out, base):
        return [
            pltpu.make_async_copy(out_buf.at[end, :, e], out.at[:, :, e], out_sems.at[base + e])
            for e in range(exposures)
        ]

    for parity in range(2):

        @pl.when(odd == parity)
        def _():
            sends = send(1 - parity, near_out, 0) + send(parity, far_out, exposures)
            for copy in sends:
                copy.start()
            for copy in sends:
                copy.wait()


def edge_call(arrays):
    exposures, rows, specs, fibres = arrays[0].shape
    out = jax.ShapeDtypeStruct((PARTS, specs, exposures, fibres), F32)
    return pl.pallas_call(
        edge_kernel,
        out_shape=(out, out),
        in_specs=[HB] * 5,
        out_specs=(HB, HB),
        scratch_shapes=[
            pltpu.VMEM((2, 4, exposures, HALO, specs, fibres), F32),
            pltpu.VMEM((2, exposures, HALO, specs, fibres), jnp.int32),
            pltpu.VMEM((2, PARTS, exposures, specs, fibres), F32),
            pltpu.SemaphoreType.DMA((2, 5)),
            pltpu.SemaphoreType.DMA((2 * exposures,)),
        ],
        cost_estimate=pl.CostEstimate(flops=10**6, bytes_accessed=10**6, transcendentals=0),
        name="edges",
    )(*arrays)


def band_kernel(pix, iva, msk, lef, rig, sky_index, diag, off_one, off_two, rhs, sky_mask, bufs, mbuf, sems):
    exposures, rows, specs, fibres = pix.shape
    copies = []
    for e in range(exposures):
        for slot, ref in enumerate((pix, iva, lef, rig)):
            copies.append(
                pltpu.make_async_copy(ref.at[e], bufs.at[slot, :, :, e], sems.at[slot, e])
            )
        copies.append(pltpu.make_async_copy(msk.at[e], mbuf.at[:, :, e], sems.at[4, e]))
    for copy in copies:
        copy.start()
    lane = lax.broadcasted_iota(jnp.int32, (exposures, fibres), 1)
    for s in range(specs):
        found = lane == sky_index[s, 0]
        for k in range(1, sky_index.shape[1]):
            found = found | (lane == sky_index[s, k])
        sky_mask[s] = jnp.where(found, 1.0, 0.0)
    for copy in copies:
        copy.wait()

    for s in range(specs):

        def terms(k):
            p, l, r = bufs[0, k, s], bufs[2, k, s], bufs[3, k, s]
            w = weight_of(bufs[1, k, s], mbuf[k, s])
            wl, wr, wp = w * l, w * r, w * p
            return (w, wp, wl, wr, wl * l, wr * r, wl * p, wr * p, wl * r)

        def body(k, carry):
            w1, wp1, wr1, wrr2, wrp2, wrr1, wrp1 = carry
            w, wp, wl, wr, wll, wrr, wlp, wrp, wlr = terms(k)
            diag[k, s] = w1 + wll + (wrr2 + REG)
            off_one[k, s] = wr1 + wl
            off_two[k, s] = wlr
            rhs[k, s] = wp1 + wlp + wrp2
            return (w, wp, wr, wrr1, wrp1, wrr, wrp)

        last = body(1, body(0, (0.0,) * 7))
        last = lax.fori_loop(2, rows, body, last, unroll=4)
        w1, wp1, wr1, wrr2, wrp2, wrr1, wrp1 = last
        diag[rows, s] = w1 + (wrr2 + REG)
        off_one[rows, s] = wr1
        rhs[rows, s] = wp1 + wrp2
        diag[rows + 1, s] = wrr1 + REG
        rhs[rows + 1, s] = wrp1


def band_call(arrays, sky_index):
    exposures, rows, specs, fibres = arrays[0].shape
    grown = in_vmem((rows + 2, specs, exposures, fibres))
    return pl.pallas_call(
        band_kernel,
        out_shape=(grown, grown, grown, grown, in_vmem((specs, exposures, fibres))),
        in_specs=[HB] * 5 + [SM],
        out_specs=(VM,) * 5,
        scratch_shapes=[
            pltpu.VMEM((4, rows, specs, exposures, fibres), F32),
            pltpu.VMEM((rows, specs, exposures, fibres), jnp.int32),
            pltpu.SemaphoreType.DMA((5, exposures)),
        ],
        compiler_params=pltpu.CompilerParams(vmem_limit_bytes=40 * 2**20),
        cost_estimate=pl.CostEstimate(flops=10**7, bytes_accessed=10**7, transcendentals=0),
        name="bands",
    )(*arrays, sky_index)


def solve_kernel(near, far, diag, off_one, off_two, rhs, sky_mask, flux, sums, lower, lower_far, half):
    count, specs, exposures, fibres = diag.shape
    rows = count - 2
    odd = lax.rem(lax.axis_index("wave"), 2)
    is_odd = odd == 1

    def left(part, s):
        return jnp.where(is_odd, near[part, s], far[part, s])

    def right(part, s):
        return jnp.where(is_odd, far[part, s], near[part, s])

    lane = lax.broadcasted_iota(jnp.int32, (exposures, LANES), 1)
    numer = jnp.zeros((exposures, LANES), F32)
    denom = jnp.zeros((exposures, LANES), F32)

    zero = jnp.zeros((exposures, fibres), F32)
    spans = range(specs)

    def step(k, state, d, a, b, far_a):
        inv1, inv2, mult1, y1, y2 = state
        f = far_a * inv2
        upper = a - far_a * mult1
        g = upper * inv1
        pivot = d - f * far_a - g * upper
        y = b - f * y2 - g * y1
        return f, g, y, (recip(pivot), inv1, g, y, y1)

    def put(k, s, f, g, y, state):
        lower_far[k, s] = f
        lower[k, s] = g
        half[k, s] = y * state[0]

    states = []
    for s in spans:
        state = (zero,) * 5
        f, g, y, state = step(0, state, diag[0, s] + left(0, s), zero, rhs[0, s] + left(3, s), zero)
        put(0, s, f, g, y, state)
        f, g, y, state = step(
            1,
            state,
            diag[1, s] + left(2, s),
            off_one[0, s] + left(1, s),
            rhs[1, s] + left(4, s),
            zero,
        )
        put(1, s, f, g, y, state)
        states.append(state)

    def forward(k, states):
        results = []
        for s in spans:
            f, g, y, state = step(
                k, states[s], diag[k, s], off_one[k - 1, s], rhs[k, s], off_two[k - 2, s]
            )
            put(k, s, f, g, y, state)
            results.append(state)
        return tuple(results)

    states = lax.fori_loop(2, rows, forward, tuple(states), unroll=4)

    after = [None] * specs
    for s in spans:
        f, g, y, state = step(
            rows,
            states[s],
            diag[rows, s] + right(2, s),
            off_one[rows - 1, s],
            rhs[rows, s] + right(4, s),
            off_two[rows - 2, s],
        )
        f1, g1, y1, state1 = step(
            rows + 1,
            state,
            diag[rows + 1, s] + right(0, s),
            off_one[rows, s] + right(1, s),
            rhs[rows + 1, s] + right(3, s),
            off_two[rows - 1, s],
        )
        last = y1 * state1[0]
        here = y * state[0] - g1 * last
        flux[rows - 1, s] = here
        after[s] = (here, last, g, f1, f)

    def total(parts):
        return jnp.sum(parts, axis=1, keepdims=True)

    masks = [sky_mask[s] for s in spans]

    def spread(k, numer, denom, precs, values):
        weighted = sum(masks[s] * precs[s] for s in spans)
        valued = sum(masks[s] * precs[s] * values[s] for s in spans)
        return (
            jnp.where(lane == k, total(valued), numer),
            jnp.where(lane == k, total(weighted), denom),
        )

    precs = [diag[rows, s] + right(5, s) for s in spans]
    numer, denom = spread(rows - 1, numer, denom, precs, [after[s][0] for s in spans])

    def backward(step_row, carry):
        k = rows - 1 - step_row
        numer, denom, after = carry
        results = []
        for s in spans:
            x1, x2, g1, f2, f1 = after[s]
            value = half[k, s] - g1 * x1 - f2 * x2
            flux[k - 1, s] = value
            results.append((value, x1, lower[k, s], f1, lower_far[k, s]))
        precs = [diag[k, s] for s in spans]
        numer, denom = spread(k - 1, numer, denom, precs, [r[0] for r in results])
        return (numer, denom, tuple(results))

    numer, denom, after = lax.fori_loop(0, rows - 2, backward, (numer, denom, tuple(after)), unroll=4)
    values = []
    for s in spans:
        x1, x2, g1, f2, f1 = after[s]
        value = half[1, s] - g1 * x1 - f2 * x2
        flux[0, s] = value
        values.append(value)
    precs = [diag[1, s] + left(5, s) for s in spans]
    numer, denom = spread(0, numer, denom, precs, values)
    sums[0] = numer
    sums[1] = denom


def solve_call(near, far, bands):
    count, specs, exposures, fibres = bands[0].shape
    rows = count - 2
    scratch = pltpu.VMEM((count, specs, exposures, fibres), F32)
    return pl.pallas_call(
        solve_kernel,
        out_shape=(in_vmem((rows, specs, exposures, fibres)), in_vmem((2, exposures, LANES))),
        in_specs=[VM] * 7,
        out_specs=(VM, VM),
        scratch_shapes=[scratch] * 3,
        compiler_params=pltpu.CompilerParams(vmem_limit_bytes=40 * 2**20),
        cost_estimate=pl.CostEstimate(flops=10**7, bytes_accessed=10**7, transcendentals=0),
        name="solve",
    )(near, far, *bands)


def position_of(index, total_rows):
    return 2.0 * index.astype(F32) / (total_rows - 1) - 1.0


def regress_kernel(total_rows, flux, other, sums, regress, sky_out):
    rows, specs, exposures, fibres = flux.shape
    device = lax.axis_index("wave")
    lane = lax.broadcasted_iota(jnp.int32, (exposures, LANES), 1)
    valid = lane < rows
    first = [[jnp.zeros((exposures, fibres), F32) for _ in range(specs)] for _ in range(2)]
    moments = [jnp.zeros((exposures, 1), F32) for _ in range(3)]
    for which, (ref, base) in enumerate(((flux, device * rows), (other, (device - 1) * rows))):
        sky = jnp.where(valid, sums[2 * which] / jnp.where(valid, sums[2 * which + 1], 1.0), 0.0)
        position = position_of(base + lane, total_rows)
        tilted = sky * position
        moments[0] += jnp.sum(sky * sky, axis=1, keepdims=True)
        moments[1] += jnp.sum(sky * tilted, axis=1, keepdims=True)
        moments[2] += jnp.sum(tilted * tilted, axis=1, keepdims=True)
        if which == 0:
            sky_out[...] = sky
        for k in range(rows):
            plain_k = jnp.broadcast_to(sky[:, k : k + 1], (exposures, fibres))
            tilted_k = jnp.broadcast_to(tilted[:, k : k + 1], (exposures, fibres))
            for s in range(specs):
                values = ref[k, s]
                first[0][s] += values * plain_k
                first[1][s] += values * tilted_k
    for r in range(2):
        for s in range(specs):
            regress[r * specs + s] = first[r][s]
    wide = lax.broadcasted_iota(jnp.int32, (exposures, fibres), 1)
    regress[2 * specs] = jnp.where(wide == 0, moments[0], jnp.where(wide == 1, moments[1], moments[2]))


def regress_call(total_rows, flux, other, sums):
    rows, specs, exposures, fibres = flux.shape
    return pl.pallas_call(
        functools.partial(regress_kernel, total_rows),
        out_shape=(
            in_vmem((2 * specs + 1, exposures, fibres)),
            in_vmem((exposures, LANES)),
        ),
        in_specs=[VM] * 3,
        out_specs=(VM, VM),
        compiler_params=pltpu.CompilerParams(vmem_limit_bytes=40 * 2**20),
        cost_estimate=pl.CostEstimate(flops=10**6, bytes_accessed=10**6, transcendentals=0),
        name="regress",
    )(flux, other, sums)


def clean_kernel(total_rows, flux, sky_ref, mine, sent, out, buf, sems):
    rows, specs, exposures, fibres = flux.shape
    device = lax.axis_index("wave")
    is_odd = lax.rem(device, 2) == 1

    def got(slot):
        return jnp.where(is_odd, mine[slot], sent[slot])

    moments = got(2 * specs)
    upper_left = moments[:, 0:1] + RIDGE
    cross = moments[:, 1:2]
    lower_right = moments[:, 2:3] + RIDGE
    inverse = 1.0 / (upper_left * lower_right - cross * cross)
    slope_a, slope_b = [], []
    for s in range(specs):
        r1, r2 = got(s), got(specs + s)
        slope_a.append((lower_right * r1 - cross * r2) * inverse)
        slope_b.append((upper_left * r2 - cross * r1) * inverse)
    lane = lax.broadcasted_iota(jnp.int32, (exposures, LANES), 1)
    sky = sky_ref[...]
    tilted = sky * position_of(device * rows + lane, total_rows)
    chunks = sems.shape[0]
    size = -(-rows // chunks)
    copies = []
    for c in range(chunks):
        low, high = c * size, min(rows, (c + 1) * size)
        for k in range(low, high):
            plain_k = jnp.broadcast_to(sky[:, k : k + 1], (exposures, fibres))
            tilted_k = jnp.broadcast_to(tilted[:, k : k + 1], (exposures, fibres))
            for s in range(specs):
                buf[k, s] = flux[k, s] - (slope_a[s] * plain_k + slope_b[s] * tilted_k)
        for e in range(exposures):
            copy = pltpu.make_async_copy(
                buf.at[low:high, :, e], out.at[e, low:high], sems.at[c, e]
            )
            copy.start()
            copies.append(copy)
    for copy in copies:
        copy.wait()


def clean_call(total_rows, flux, sky, mine, sent):
    rows, specs, exposures, fibres = flux.shape
    return pl.pallas_call(
        functools.partial(clean_kernel, total_rows),
        out_shape=jax.ShapeDtypeStruct((exposures, rows, specs, fibres), F32),
        in_specs=[VM] * 4,
        out_specs=HB,
        scratch_shapes=[
            pltpu.VMEM((rows, specs, exposures, fibres), F32),
            pltpu.SemaphoreType.DMA((2, exposures)),
        ],
        compiler_params=pltpu.CompilerParams(vmem_limit_bytes=40 * 2**20),
        cost_estimate=pl.CostEstimate(flops=10**6, bytes_accessed=10**6, transcendentals=0),
        name="clean",
    )(flux, sky, mine, sent)


def powers(low, high):
    steps = []
    while low < high:
        steps.append(low)
        low *= 2
    return steps


def local(pixels, ivar, mask, psf_left, psf_right, sky_index):
    arrays = [jnp.transpose(x, (0, 2, 1, 3)) for x in (pixels, ivar, mask, psf_left, psf_right)]
    rows = pixels.shape[2]
    wave, spec = lax.axis_size("wave"), lax.axis_size("spec")
    total_rows = rows * wave
    near, far = edge_call(arrays)
    far = lax.ppermute(
        far, "wave", [pair for i in range(1, wave - 1, 2) for pair in ((i, i + 1), (i + 1, i))]
    )
    near = lax.ppermute(near, "wave", [(i, i ^ 1) for i in range(wave)])
    bands = band_call(arrays, sky_index)
    flux, sums = solve_call(near, far, bands)
    to_odd = [(i, i + 1) for i in range(0, wave, 2)]
    sums = jnp.concatenate([sums, lax.ppermute(sums, "wave", to_odd)])
    other = lax.ppermute(flux, "wave", to_odd)
    for k in powers(1, spec):
        sums = sums + lax.ppermute(sums, "spec", [(i, i ^ k) for i in range(spec)])
    regress, sky = regress_call(total_rows, flux, other, sums)
    for k in powers(2, wave):
        regress = regress + lax.ppermute(regress, "wave", [(i, i ^ k) for i in range(1, wave, 2)])
    sent = lax.ppermute(regress, "wave", [(i + 1, i) for i in range(0, wave, 2)])
    cleaned = clean_call(total_rows, flux, sky, regress, sent)
    return (jnp.transpose(cleaned, (0, 2, 1, 3)), sky[:, :rows])


def solution(mesh):
    block = P(None, "spec", "wave", None)
    return jax.shard_map(
        local,
        mesh=mesh,
        in_specs=(block,) * 5 + (P("spec", None),),
        out_specs=(block, P(None, "wave")),
        check_vma=False,
    )
```

time: 107 us -> 53.7 us (0.50)
  blocking collectives: 42.2 us -> 0 us
  other arithmetic: 34.4 us -> 0.04 us
  Pallas kernels: 0 us -> 17.1 us
  waiting for transfers between devices: 4.12 us -> 14.9 us
  matrix products: 10.7 us -> 0 us
  starting transfers between devices: 4.43 us -> 14.1 us
  local copies, waits for them, and re-layouts: 8.75 us -> 6.44 us
    psum x2 -> x0, blocking collectives: 42.2 us -> none  [the longest x1 32.2 us: local(): moments, fibre_sums = lax.psum((moments, fibre_sums), 'wave')]
    div x33 -> x0, other arithmetic: 22.4 us -> none  [the longest x12 10.9 us: band_substitute(): (rhs_rows[step_row] - lowers[step_row] * forward_last - farther[step_row]...]
    pallas_call x0 -> x5, Pallas kernels: none -> 17.1 us  [the longest x1 9.07 us: band_call(): pl.pallas_call(band_kernel, out_shape=(grown, grown, grown, grown, in_vme...]
    ppermute x2 -> x9, waiting for transfers between devices: 4.12 us -> 14.9 us  [the longest x1 8.7 us: local(): lax.ppermute(regress, 'wave', [(i + 1, i) for i in range(0, wave, 2)])]
    dot_general x4 -> x0, matrix products: 10.7 us -> none  [the longest x1 3.31 us: local(): jnp.einsum('eswf,sf->ew', precision, is_sky, precision=lax.Precision.HIGH...]
    ppermute x2 -> x9, starting transfers between devices: 4.43 us -> 14.1 us  [the longest x1 5.95 us: local(): other = lax.ppermute(flux, 'wave', to_odd)]
    another operation x2 -> x0, local copies, waits for them, and re-layouts: 3.05 us -> none  [the longest x1 3.05 us: local(): stacked = jnp.stack([pixels, weight, psf_left, psf_right])]
    transpose x1 -> x0, other arithmetic: 2.94 us -> none  [local(): full_rows = jnp.moveaxis(extended, 3, 1)]
  transfers between devices with their start and end apart: 2 -> 9, of which waited for: 1 -> 4; matrix products, arithmetic and copies ran while one was open for 0% -> 0% of each run, Pallas kernels for 0% -> 17%
where the time goes in v1:
time: 53.7 us; the launch traced here: 53.3 us
  Pallas kernels  17.1 us (32%)
  waiting for transfers between devices  14.9 us (28%)
  starting transfers between devices  14.1 us (26%)
  local copies, waits for them, and re-layouts  6.44 us (12%)
  between operations  0.82 us (2%)
    pallas_call x1, Pallas kernels, band_call(): pl.pallas_call(band_kernel, out_shape=(grown, grown, grown, grown, in_vme...  9.07 us
    ppermute x1, waiting for transfers between devices, local(): lax.ppermute(regress, 'wave', [(i + 1, i) for i in range(0, wave, 2)])  8.7 us
    unnamed x17, local copies, waits for them, and re-layouts  6.43 us
    ppermute x1, starting transfers between devices, local(): other = lax.ppermute(flux, 'wave', to_odd)  5.95 us
    ppermute x2, waiting for transfers between devices, local(): sums = sums + lax.ppermute(sums, 'spec', [(i, i ^ k) for i in range(spec)])  4.47 us
    ppermute x2, starting transfers between devices, local(): sums = sums + lax.ppermute(sums, 'spec', [(i, i ^ k) for i in range(spec)])  3.02 us
    pallas_call x1, Pallas kernels, solve_call(): pl.pallas_call(solve_kernel, out_shape=(in_vmem((rows, specs, exposures,...  2.77 us
    pallas_call x1, Pallas kernels, edge_call(): pl.pallas_call(edge_kernel, out_shape=(out, out), in_specs=[HB] * 5, out_...  2.58 us
  transfers between devices with their start and end apart: 9, of which 4 were waited for; matrix products, arithmetic and copies ran while one was open for 0% of the time, Pallas kernels for 17%

profile of v1, /device:TPU:0, one launch (start us, length us, event | category | flops | bytes accessed | tf_op | source)
XLA Modules:
  0.0 53.3 jit_solution(7616821108868915692)
XLA Ops:
  0.7 2.6 %edges.1 = (f32[6,2,8,500]{3,2,1,0:T(8,128)}, f32[6,2,8,500]{3,2,1,0:T(8,128)}) custom-call(f32[8,50,2,500]{3,2,1,0:T(2,128)} %bitcast.7, f32[8,50,2,500]{3,2,1,0:T(2,128)} %bitcast.9, s32[8,50,2,500]{3,2,1,0:T(2,128)} %bitcast.11, f32[8,50,2,500]{3,2,1,0:T(2,128)} %bitcast.13, f32[8,50,2,500]{3,2,1,0:T(2,128)} %bitcast.15), custom_call_target="tpu_custom_call" | custom-call | flops 1000000 | bytes 1000000 | tf_op jit(solution)/shard_map/edges/pallas_call | solution.py:120
  3.2 0.5 collective-permute-start
  3.8 0.7 %collective-permute-start.1 = (f32[6,2,8,500]{3,2,1,0:T(8,128)}, f32[6,2,8,500]{3,2,1,0:T(8,128)S(1)}, u32[]{:S(2)}, u32[]{:S(2)}) collective-permute-start(f32[6,2,8,500]{3,2,1,0:T(8,128)} %get-tuple-element.14), channel_id=1, source_target_pairs={{1,2},{2,1},{3,4},{4,3},{5,6},{6,5},{9,10},{10,9},{11,12},{12,11},... | collective-permute-start | bytes 576008 | tf_op jit(solution)/shard_map/ppermute | solution.py:467
  4.5 0.0 copy-start.2
  4.5 1.4 %copy-done.2 = s32[8,2,50,500]{3,1,2,0:T(2,128)S(1)} copy-done((s32[8,2,50,500]{3,1,2,0:T(2,128)S(1)}, s32[8,2,50,500]{3,1,2,0:T(2,128)}, u32[]{:S(2)}) %copy-start.2) | copy-done | bytes 1600024
  5.9 1.4 %copy-done.3 = f32[8,2,50,500]{3,1,2,0:T(2,128)S(1)} copy-done((f32[8,2,50,500]{3,1,2,0:T(2,128)S(1)}, f32[8,2,50,500]{3,1,2,0:T(2,128)}, u32[]{:S(2)}) %copy-start.3) | copy-done | bytes 1600024
  7.3 1.4 %copy-done.4 = f32[8,2,50,500]{3,1,2,0:T(2,128)S(1)} copy-done((f32[8,2,50,500]{3,1,2,0:T(2,128)S(1)}, f32[8,2,50,500]{3,1,2,0:T(2,128)}, u32[]{:S(2)}) %copy-start.4) | copy-done | bytes 1600024
  8.8 9.1 %bands.1 = (f32[52,2,8,500]{3,2,1,0:T(8,128)S(1)}, f32[52,2,8,500]{3,2,1,0:T(8,128)S(1)}, f32[52,2,8,500]{3,2,1,0:T(8,128)S(1)}, f32[52,2,8,500]{3,2,1,0:T(8,128)}, f32[2,8,500]{2,1,0:T(8,128)S(1)}) custom-call(f32[8,50,2,500]{3,2,1,0:T(2,128)S(1)} %bitcast.8, f32[8,50,2,500]{3,2,1,0:T(2,128)S(1)} %bitcast.10, s32[8,50,2,500]{3,2,1,0:T(2,128)S(1)} %bitcast.12, ...), custom_call_target="tpu_custom_call" | custom-call | flops 10000000 | bytes 10000000 | tf_op jit(solution)/shard_map/bands/pallas_call | solution.py:187
  17.9 1.4 %copy-done.5 = f32[52,2,8,500]{3,2,1,0:T(8,128)S(1)} copy-done((f32[52,2,8,500]{3,2,1,0:T(8,128)S(1)}, f32[52,2,8,500]{3,2,1,0:T(8,128)}, u32[]{:S(2)}) %copy-start.5) | copy-done | bytes 1664024
  19.3 2.8 %solve.1 = (f32[50,2,8,500]{3,2,1,0:T(8,128)S(1)}, f32[2,8,128]{2,1,0:T(8,128)S(1)}) custom-call(f32[6,2,8,500]{3,2,1,0:T(8,128)S(1)} %collective-permute-done.near, f32[6,2,8,500]{3,2,1,0:T(8,128)S(1)} %collective-permute-done.1.far, f32[52,2,8,500]{3,2,1,0:T(8,128)S(1)} %get-tuple-element.15.diag, f32[52,2,8,500]{3,2,1,0:T(8,128)S(1)} %get-tuple-element.16.off_one, ...), custom_call_target="tpu_custom_call" | custom-call | flops 10000000 | bytes 10000000 | tf_op jit(solution)/shard_map/solve/pallas_call | solution.py:333
  22.1 5.9 %collective-permute-start.2 = (f32[50,2,8,500]{3,2,1,0:T(8,128)S(1)}, f32[50,2,8,500]{3,2,1,0:T(8,128)S(1)}, u32[]{:S(2)}, u32[]{:S(2)}) collective-permute-start(f32[50,2,8,500]{3,2,1,0:T(8,128)S(1)} %get-tuple-element.20.flux), channel_id=1, source_target_pairs={{0,1},{2,3},{4,5},{6,7},{8,9},{10,11},{12,13},{14,15},{16,17},{18,... | collective-permute-start | bytes 4800008 | tf_op jit(solution)/shard_map/ppermute | solution.py:475
  28.0 1.3 %collective-permute-start.3 = (f32[2,8,128]{2,1,0:T(8,128)S(1)}, f32[2,8,128]{2,1,0:T(8,128)S(1)}, u32[]{:S(2)}, u32[]{:S(2)}) collective-permute-start(f32[2,8,128]{2,1,0:T(8,128)S(1)} %get-tuple-element.21), channel_id=1, source_target_pairs={{0,1},{2,3},{4,5},{6,7},{8,9},{10,11},{12,13},{14,15},{16,17},{18,... | collective-permute-start | bytes 24584 | tf_op jit(solution)/shard_map/ppermute | solution.py:474
  29.4 1.7 %collective-permute-done.3 = f32[2,8,128]{2,1,0:T(8,128)S(1)} collective-permute-done((f32[2,8,128]{2,1,0:T(8,128)S(1)}, f32[2,8,128]{2,1,0:T(8,128)S(1)}, u32[]{:S(2)}, u32[]{:S(2)}) %collective-permute-start.3) | collective-permute-done | bytes 8224 | tf_op jit(solution)/shard_map/ppermute | solution.py:474
  31.1 1.5 %collective-permute-start.4 = (f32[4,8,128]{2,1,0:T(8,128)S(1)}, f32[4,8,128]{2,1,0:T(8,128)S(1)}, u32[]{:S(2)}, u32[]{:S(2)}) collective-permute-start(f32[4,8,128]{2,1,0:T(8,128)S(1)} %constant_dynamic-update-slice_fusion), channel_id=1, source_target_pairs={{0,8},{8,0},{16,24},{24,16},{1,9},{9,1},{17,25},{25,17},{2,10},{10... | collective-permute-start | bytes 49160 | tf_op jit(solution)/shard_map/ppermute | solution.py:477
  32.6 2.2 %collective-permute-done.4 = f32[4,8,128]{2,1,0:T(8,128)S(1)} collective-permute-done((f32[4,8,128]{2,1,0:T(8,128)S(1)}, f32[4,8,128]{2,1,0:T(8,128)S(1)}, u32[]{:S(2)}, u32[]{:S(2)}) %collective-permute-start.4) | collective-permute-done | bytes 16416 | tf_op jit(solution)/shard_map/ppermute | solution.py:477
  34.8 1.5 %collective-permute-start.5 = (f32[4,8,128]{2,1,0:T(8,128)S(1)}, f32[4,8,128]{2,1,0:T(8,128)S(1)}, u32[]{:S(2)}, u32[]{:S(2)}) collective-permute-start(f32[4,8,128]{2,1,0:T(8,128)S(1)} %add.12), channel_id=1, source_target_pairs={{0,16},{8,24},{16,0},{24,8},{1,17},{9,25},{17,1},{25,9},{2,18},{10... | collective-permute-start | bytes 49160 | tf_op jit(solution)/shard_map/ppermute | solution.py:477
  36.3 2.2 %collective-permute-done.5 = f32[4,8,128]{2,1,0:T(8,128)S(1)} collective-permute-done((f32[4,8,128]{2,1,0:T(8,128)S(1)}, f32[4,8,128]{2,1,0:T(8,128)S(1)}, u32[]{:S(2)}, u32[]{:S(2)}) %collective-permute-start.5) | collective-permute-done | bytes 16416 | tf_op jit(solution)/shard_map/ppermute | solution.py:477
  38.6 1.0 %regress.1 = (f32[5,8,500]{2,1,0:T(8,128)S(1)}, f32[8,128]{1,0:T(8,128)}) custom-call(f32[50,2,8,500]{3,2,1,0:T(8,128)S(1)} %get-tuple-element.20.flux, f32[50,2,8,500]{3,2,1,0:T(8,128)S(1)} %collective-permute-done.2.other, f32[4,8,128]{2,1,0:T(8,128)S(1)} %add.13.sums), custom_call_target="tpu_custom_call" | custom-call | flops 1000000 | bytes 1000000 | tf_op jit(solution)/shard_map/regress/pallas_call | solution.py:381
  39.6 0.7 %collective-permute-start.6 = (f32[5,8,500]{2,1,0:T(8,128)S(1)}, f32[5,8,500]{2,1,0:T(8,128)S(1)}, u32[]{:S(2)}, u32[]{:S(2)}) collective-permute-start(f32[5,8,500]{2,1,0:T(8,128)S(1)} %get-tuple-element.23), channel_id=1, source_target_pairs={{1,3},{3,1},{5,7},{7,5},{9,11},{11,9},{13,15},{15,13},{17,19},{19,... | collective-permute-start | bytes 240008 | tf_op jit(solution)/shard_map/ppermute | solution.py:480
  40.3 0.7 %collective-permute-start.7 = (f32[5,8,500]{2,1,0:T(8,128)S(1)}, f32[5,8,500]{2,1,0:T(8,128)S(1)}, u32[]{:S(2)}, u32[]{:S(2)}) collective-permute-start(f32[5,8,500]{2,1,0:T(8,128)S(1)} %add.14), channel_id=1, source_target_pairs={{1,5},{3,7},{5,1},{7,3},{9,13},{11,15},{13,9},{15,11},{17,21},{19,... | collective-permute-start | bytes 240008 | tf_op jit(solution)/shard_map/ppermute | solution.py:480
  41.0 1.3 %collective-permute-start.8 = (f32[5,8,500]{2,1,0:T(8,128)S(1)}, f32[5,8,500]{2,1,0:T(8,128)S(1)}, u32[]{:S(2)}, u32[]{:S(2)}) collective-permute-start(f32[5,8,500]{2,1,0:T(8,128)S(1)} %add.15.mine), channel_id=1, source_target_pairs={{1,0},{3,2},{5,4},{7,6},{9,8},{11,10},{13,12},{15,14},{17,16},{19,... | collective-permute-start | bytes 240008 | tf_op jit(solution)/shard_map/ppermute | solution.py:481
  42.3 8.7 %collective-permute-done.8.sent = f32[5,8,500]{2,1,0:T(8,128)S(1)} collective-permute-done((f32[5,8,500]{2,1,0:T(8,128)S(1)}, f32[5,8,500]{2,1,0:T(8,128)S(1)}, u32[]{:S(2)}, u32[]{:S(2)}) %collective-permute-start.8) | collective-permute-done | bytes 80032 | tf_op jit(solution)/shard_map/ppermute | solution.py:481
  51.0 0.7 %copy-done.6 = f32[8,128]{1,0:T(8,128)S(1)} copy-done((f32[8,128]{1,0:T(8,128)S(1)}, f32[8,128]{1,0:T(8,128)}, u32[]{:S(2)}) %copy-start.6) | copy-done | bytes 4120
  51.6 1.7 %clean.1 = f32[8,50,2,500]{3,2,1,0:T(2,128)} custom-call(f32[50,2,8,500]{3,2,1,0:T(8,128)S(1)} %get-tuple-element.20.flux, f32[8,128]{1,0:T(8,128)S(1)} %copy-done.6, f32[5,8,500]{2,1,0:T(8,128)S(1)} %add.15.mine, f32[5,8,500]{2,1,0:T(8,128)S(1)} %collective-permute-done.8.sent), custom_call_target="tpu_custom_call" | custom-call | flops 1000000 | bytes 1000000 | tf_op jit(solution)/shard_map/clean/pallas_call | solution.py:438
  (21 shorter events, 0.1 us)
Async XLA Ops:
  0.6 3.8 %copy-start = (f32[8,2,50,500]{3,1,2,0:T(2,128)S(1)}, f32[8,2,50,500]{3,1,2,0:T(2,128)}, u32[]{:S(2)}) copy-start(f32[8,2,50,500]{3,1,2,0:T(2,128)} %param.6) | copy-start | bytes 4800004
  0.6 3.8 %copy-start.1 = (f32[8,2,50,500]{3,1,2,0:T(2,128)S(1)}, f32[8,2,50,500]{3,1,2,0:T(2,128)}, u32[]{:S(2)}) copy-start(f32[8,2,50,500]{3,1,2,0:T(2,128)} %param.7) | copy-start | bytes 4800004
  0.6 3.8 %copy-start.7 = (s32[2,40]{1,0:T(2,128)S(1)}, s32[2,40]{1,0:T(2,128)}, u32[]{:S(2)}) copy-start(s32[2,40]{1,0:T(2,128)} %sky_index.1) | copy-start | bytes 964
  3.2 14.6 %collective-permute-start = (f32[6,2,8,500]{3,2,1,0:T(8,128)}, f32[6,2,8,500]{3,2,1,0:T(8,128)S(1)}, u32[]{:S(2)}, u32[]{:S(2)}) collective-permute-start(f32[6,2,8,500]{3,2,1,0:T(8,128)} %get-tuple-element.13), channel_id=1, source_target_pairs={{0,1},{1,0},{2,3},{3,2},{4,5},{5,4},{6,7},{7,6},{8,9},{9,8},{10,11... | collective-permute-start | bytes 576008 | tf_op jit(solution)/shard_map/ppermute | solution.py:470
  3.8 14.1 %collective-permute-start.1 = (f32[6,2,8,500]{3,2,1,0:T(8,128)}, f32[6,2,8,500]{3,2,1,0:T(8,128)S(1)}, u32[]{:S(2)}, u32[]{:S(2)}) collective-permute-start(f32[6,2,8,500]{3,2,1,0:T(8,128)} %get-tuple-element.14), channel_id=1, source_target_pairs={{1,2},{2,1},{3,4},{4,3},{5,6},{6,5},{9,10},{10,9},{11,12},{12,11},... | collective-permute-start | bytes 576008 | tf_op jit(solution)/shard_map/ppermute | solution.py:467
  4.5 1.4 %copy-start.2 = (s32[8,2,50,500]{3,1,2,0:T(2,128)S(1)}, s32[8,2,50,500]{3,1,2,0:T(2,128)}, u32[]{:S(2)}) copy-start(s32[8,2,50,500]{3,1,2,0:T(2,128)} %param.8) | copy-start | bytes 4800004
  5.9 1.4 %copy-start.3 = (f32[8,2,50,500]{3,1,2,0:T(2,128)S(1)}, f32[8,2,50,500]{3,1,2,0:T(2,128)}, u32[]{:S(2)}) copy-start(f32[8,2,50,500]{3,1,2,0:T(2,128)} %param.9) | copy-start | bytes 4800004
  7.3 1.4 %copy-start.4 = (f32[8,2,50,500]{3,1,2,0:T(2,128)S(1)}, f32[8,2,50,500]{3,1,2,0:T(2,128)}, u32[]{:S(2)}) copy-start(f32[8,2,50,500]{3,1,2,0:T(2,128)} %param.10) | copy-start | bytes 4800004
  17.9 1.5 %copy-start.5 = (f32[52,2,8,500]{3,2,1,0:T(8,128)S(1)}, f32[52,2,8,500]{3,2,1,0:T(8,128)}, u32[]{:S(2)}) copy-start(f32[52,2,8,500]{3,2,1,0:T(8,128)} %get-tuple-element.18.rhs) | copy-start | bytes 4992004
  22.1 16.5 %collective-permute-start.2 = (f32[50,2,8,500]{3,2,1,0:T(8,128)S(1)}, f32[50,2,8,500]{3,2,1,0:T(8,128)S(1)}, u32[]{:S(2)}, u32[]{:S(2)}) collective-permute-start(f32[50,2,8,500]{3,2,1,0:T(8,128)S(1)} %get-tuple-element.20.flux), channel_id=1, source_target_pairs={{0,1},{2,3},{4,5},{6,7},{8,9},{10,11},{12,13},{14,15},{16,17},{18,... | collective-permute-start | bytes 4800008 | tf_op jit(solution)/shard_map/ppermute | solution.py:475
  28.0 3.0 %collective-permute-start.3 = (f32[2,8,128]{2,1,0:T(8,128)S(1)}, f32[2,8,128]{2,1,0:T(8,128)S(1)}, u32[]{:S(2)}, u32[]{:S(2)}) collective-permute-start(f32[2,8,128]{2,1,0:T(8,128)S(1)} %get-tuple-element.21), channel_id=1, source_target_pairs={{0,1},{2,3},{4,5},{6,7},{8,9},{10,11},{12,13},{14,15},{16,17},{18,... | collective-permute-start | bytes 24584 | tf_op jit(solution)/shard_map/ppermute | solution.py:474
  31.1 3.8 %collective-permute-start.4 = (f32[4,8,128]{2,1,0:T(8,128)S(1)}, f32[4,8,128]{2,1,0:T(8,128)S(1)}, u32[]{:S(2)}, u32[]{:S(2)}) collective-permute-start(f32[4,8,128]{2,1,0:T(8,128)S(1)} %constant_dynamic-update-slice_fusion), channel_id=1, source_target_pairs={{0,8},{8,0},{16,24},{24,16},{1,9},{9,1},{17,25},{25,17},{2,10},{10... | collective-permute-start | bytes 49160 | tf_op jit(solution)/shard_map/ppermute | solution.py:477
  34.8 3.7 %collective-permute-start.5 = (f32[4,8,128]{2,1,0:T(8,128)S(1)}, f32[4,8,128]{2,1,0:T(8,128)S(1)}, u32[]{:S(2)}, u32[]{:S(2)}) collective-permute-start(f32[4,8,128]{2,1,0:T(8,128)S(1)} %add.12), channel_id=1, source_target_pairs={{0,16},{8,24},{16,0},{24,8},{1,17},{9,25},{17,1},{25,9},{2,18},{10... | collective-permute-start | bytes 49160 | tf_op jit(solution)/shard_map/ppermute | solution.py:477
  39.6 0.7 %collective-permute-start.6 = (f32[5,8,500]{2,1,0:T(8,128)S(1)}, f32[5,8,500]{2,1,0:T(8,128)S(1)}, u32[]{:S(2)}, u32[]{:S(2)}) collective-permute-start(f32[5,8,500]{2,1,0:T(8,128)S(1)} %get-tuple-element.23), channel_id=1, source_target_pairs={{1,3},{3,1},{5,7},{7,5},{9,11},{11,9},{13,15},{15,13},{17,19},{19,... | collective-permute-start | bytes 240008 | tf_op jit(solution)/shard_map/ppermute | solution.py:480
  40.3 0.7 %collective-permute-start.7 = (f32[5,8,500]{2,1,0:T(8,128)S(1)}, f32[5,8,500]{2,1,0:T(8,128)S(1)}, u32[]{:S(2)}, u32[]{:S(2)}) collective-permute-start(f32[5,8,500]{2,1,0:T(8,128)S(1)} %add.14), channel_id=1, source_target_pairs={{1,5},{3,7},{5,1},{7,3},{9,13},{11,15},{13,9},{15,11},{17,21},{19,... | collective-permute-start | bytes 240008 | tf_op jit(solution)/shard_map/ppermute | solution.py:480
  41.0 10.0 %collective-permute-start.8 = (f32[5,8,500]{2,1,0:T(8,128)S(1)}, f32[5,8,500]{2,1,0:T(8,128)S(1)}, u32[]{:S(2)}, u32[]{:S(2)}) collective-permute-start(f32[5,8,500]{2,1,0:T(8,128)S(1)} %add.15.mine), channel_id=1, source_target_pairs={{1,0},{3,2},{5,4},{7,6},{9,8},{11,10},{13,12},{15,14},{17,16},{19,... | collective-permute-start | bytes 240008 | tf_op jit(solution)/shard_map/ppermute | solution.py:481
  51.0 0.7 %copy-start.6 = (f32[8,128]{1,0:T(8,128)S(1)}, f32[8,128]{1,0:T(8,128)}, u32[]{:S(2)}) copy-start(f32[8,128]{1,0:T(8,128)} %get-tuple-element.22.sky_ref) | copy-start | bytes 12292

commit v2 on v1

--- a/solution.py
+++ b/solution.py
@@ -67,136 +67,91 @@
     return (d3, a34, d4, b3, b4, raw)
 
 
-def edge_kernel(pix, iva, msk, lef, rig, near_out, far_out, bufs, mbuf, out_buf, sems, out_sems):
-    exposures, rows = pix.shape[0], pix.shape[1]
-    odd = lax.rem(lax.axis_index("wave"), 2)
-    copies = []
-    for end, start in enumerate((0, rows - HALO)):
-        for slot, ref in enumerate((pix, iva, lef, rig)):
-            copies.append(
+def prepare_kernel(
+    chunks, pix, iva, msk, lef, rig, sky_index, near_out, far_out, diag, off_one, off_two, rhs, sky_mask, bufs, mbuf, sems
+):
+    exposures, rows, specs, fibres = pix.shape
+    odd = lax.rem(lax.axis_index("wave"), 2) == 1
+    bounds = [rows * c // chunks for c in range(chunks + 1)]
+    for c in range(chunks):
+        low, high = bounds[c], bounds[c + 1]
+        for e in range(exposures):
+            for slot, ref in enumerate((pix, iva, lef, rig)):
                 pltpu.make_async_copy(
-                    ref.at[:, start : start + HALO], bufs.at[end, slot], sems.at[end, slot]
-                )
-            )
-        copies.append(
-            pltpu.make_async_copy(msk.at[:, start : start + HALO], mbuf.at[end], sems.at[end, 4])
-        )
-    for copy in copies:
-        copy.start()
-    for end in range(2):
-        for copy in copies[5 * end : 5 * end + 5]:
-            copy.wait()
-        order = range(HALO - 1, -1, -1) if end == 0 else range(HALO)
-        for e in range(exposures):
-            p = [bufs[end, 0, e, k] for k in order]
-            w = [weight_of(bufs[end, 1, e, k], mbuf[end, e, k]) for k in order]
-            l = [bufs[end, 2, e, k] for k in order]
-            r = [bufs[end, 3, e, k] for k in order]
-            if end == 0:
-                l, r = r, l
-            for slot, part in enumerate(edge_message(p, w, l, r)):
-                out_buf[end, slot, e] = part
-
-    def send(end, out, base):
-        return [
-            pltpu.make_async_copy(out_buf.at[end, :, e], out.at[:, :, e], out_sems.at[base + e])
-            for e in range(exposures)
-        ]
-
-    for parity in range(2):
-
-        @pl.when(odd == parity)
-        def _():
-            sends = send(1 - parity, near_out, 0) + send(parity, far_out, exposures)
-            for copy in sends:
-                copy.start()
-            for copy in sends:
-                copy.wait()
-
-
-def edge_call(arrays):
-    exposures, rows, specs, fibres = arrays[0].shape
-    out = jax.ShapeDtypeStruct((PARTS, specs, exposures, fibres), F32)
-    return pl.pallas_call(
-        edge_kernel,
-        out_shape=(out, out),
-        in_specs=[HB] * 5,
-        out_specs=(HB, HB),
-        scratch_shapes=[
-            pltpu.VMEM((2, 4, exposures, HALO, specs, fibres), F32),
-            pltpu.VMEM((2, exposures, HALO, specs, fibres), jnp.int32),
-            pltpu.VMEM((2, PARTS, exposures, specs, fibres), F32),
-            pltpu.SemaphoreType.DMA((2, 5)),
-            pltpu.SemaphoreType.DMA((2 * exposures,)),
-        ],
-        cost_estimate=pl.CostEstimate(flops=10**6, bytes_accessed=10**6, transcendentals=0),
-        name="edges",
-    )(*arrays)
-
-
-def band_kernel(pix, iva, msk, lef, rig, sky_index, diag, off_one, off_two, rhs, sky_mask, bufs, mbuf, sems):
-    exposures, rows, specs, fibres = pix.shape
-    copies = []
-    for e in range(exposures):
-        for slot, ref in enumerate((pix, iva, lef, rig)):
-            copies.append(
-                pltpu.make_async_copy(ref.at[e], bufs.at[slot, :, :, e], sems.at[slot, e])
-            )
-        copies.append(pltpu.make_async_copy(msk.at[e], mbuf.at[:, :, e], sems.at[4, e]))
-    for copy in copies:
-        copy.start()
+                    ref.at[e, low:high], bufs.at[slot, low:high, :, e], sems.at[0, c]
+                ).start()
+            pltpu.make_async_copy(
+                msk.at[e, low:high], mbuf.at[low:high, :, e], sems.at[1, c]
+            ).start()
     lane = lax.broadcasted_iota(jnp.int32, (exposures, fibres), 1)
     for s in range(specs):
         found = lane == sky_index[s, 0]
         for k in range(1, sky_index.shape[1]):
             found = found | (lane == sky_index[s, k])
         sky_mask[s] = jnp.where(found, 1.0, 0.0)
-    for copy in copies:
-        copy.wait()
-
+
+    def load(k, s):
+        return bufs[0, k, s], weight_of(bufs[1, k, s], mbuf[k, s]), bufs[2, k, s], bufs[3, k, s]
+
+    def row(k, s, carry):
+        w1, wp1, wr1, wrr2, wrp2, wrr1, wrp1 = carry
+        p, w, l, r = load(k, s)
+        wl, wr, wp = w * l, w * r, w * p
+        diag[k, s] = w1 + wl * l + (wrr2 + REG)
+        off_one[k, s] = wr1 + wl
+        off_two[k, s] = wl * r
+        rhs[k, s] = wp1 + wl * p + wrp2
+        return (w, wp, wr, wrr1, wrp1, wr * r, wr * p)
+
+    def message(end, s):
+        order = range(HALO - 1, -1, -1) if end == 0 else range(rows - HALO, rows)
+        p, w, l, r = zip(*[load(k, s) for k in order])
+        return edge_message(p, w, r, l) if end == 0 else edge_message(p, w, l, r)
+
+    carries = [(0.0,) * 7 for _ in range(specs)]
+    for c in range(chunks):
+        low, high = bounds[c], bounds[c + 1]
+        part, mpart = bufs.at[:, low:high], mbuf.at[low:high]
+        pltpu.make_async_copy(part, part, sems.at[0, c]).wait()
+        pltpu.make_async_copy(mpart, mpart, sems.at[1, c]).wait()
+        for s in range(specs):
+            for k in range(low, high):
+                carries[s] = row(k, s, carries[s])
+            if c == 0:
+                for slot, value in enumerate(message(0, s)):
+                    near_out[slot, s] = value
     for s in range(specs):
-
-        def terms(k):
-            p, l, r = bufs[0, k, s], bufs[2, k, s], bufs[3, k, s]
-            w = weight_of(bufs[1, k, s], mbuf[k, s])
-            wl, wr, wp = w * l, w * r, w * p
-            return (w, wp, wl, wr, wl * l, wr * r, wl * p, wr * p, wl * r)
-
-        def body(k, carry):
-            w1, wp1, wr1, wrr2, wrp2, wrr1, wrp1 = carry
-            w, wp, wl, wr, wll, wrr, wlp, wrp, wlr = terms(k)
-            diag[k, s] = w1 + wll + (wrr2 + REG)
-            off_one[k, s] = wr1 + wl
-            off_two[k, s] = wlr
-            rhs[k, s] = wp1 + wlp + wrp2
-            return (w, wp, wr, wrr1, wrp1, wrr, wrp)
-
-        last = body(1, body(0, (0.0,) * 7))
-        last = lax.fori_loop(2, rows, body, last, unroll=4)
-        w1, wp1, wr1, wrr2, wrp2, wrr1, wrp1 = last
+        w1, wp1, wr1, wrr2, wrp2, wrr1, wrp1 = carries[s]
         diag[rows, s] = w1 + (wrr2 + REG)
         off_one[rows, s] = wr1
         rhs[rows, s] = wp1 + wrp2
         diag[rows + 1, s] = wrr1 + REG
         rhs[rows + 1, s] = wrp1
-
-
-def band_call(arrays, sky_index):
+        for slot, value in enumerate(message(1, s)):
+            top = near_out[slot, s]
+            near_out[slot, s] = jnp.where(odd, top, value)
+            far_out[slot, s] = jnp.where(odd, value, top)
+
+
+def prepare_call(arrays, sky_index):
     exposures, rows, specs, fibres = arrays[0].shape
+    chunks = 5
+    message = in_vmem((PARTS, specs, exposures, fibres))
     grown = in_vmem((rows + 2, specs, exposures, fibres))
+    arrays = [pltpu.with_memory_space_constraint(x, pltpu.HBM) for x in arrays]
     return pl.pallas_call(
-        band_kernel,
-        out_shape=(grown, grown, grown, grown, in_vmem((specs, exposures, fibres))),
-        in_specs=[HB] * 5 + [SM],
-        out_specs=(VM,) * 5,
+        functools.partial(prepare_kernel, chunks),
+        out_shape=(message, message, grown, grown, grown, grown, in_vmem((specs, exposures, fibres))),
+        in_specs=[pl.BlockSpec(memory_space=pltpu.HBM)] * 5 + [SM],
+        out_specs=(VM,) * 7,
         scratch_shapes=[
             pltpu.VMEM((4, rows, specs, exposures, fibres), F32),
             pltpu.VMEM((rows, specs, exposures, fibres), jnp.int32),
-            pltpu.SemaphoreType.DMA((5, exposures)),
+            pltpu.SemaphoreType.DMA((2, chunks)),
         ],
-        compiler_params=pltpu.CompilerParams(vmem_limit_bytes=40 * 2**20),
+        compiler_params=pltpu.CompilerParams(vmem_limit_bytes=24 * 2**20),
         cost_estimate=pl.CostEstimate(flops=10**7, bytes_accessed=10**7, transcendentals=0),
-        name="bands",
+        name="prepare",
     )(*arrays, sky_index)
 
 
@@ -336,7 +291,7 @@
         in_specs=[VM] * 7,
         out_specs=(VM, VM),
         scratch_shapes=[scratch] * 3,
-        compiler_params=pltpu.CompilerParams(vmem_limit_bytes=40 * 2**20),
+        compiler_params=pltpu.CompilerParams(vmem_limit_bytes=24 * 2**20),
         cost_estimate=pl.CostEstimate(flops=10**7, bytes_accessed=10**7, transcendentals=0),
         name="solve",
     )(near, far, *bands)
@@ -386,7 +341,7 @@
         ),
         in_specs=[VM] * 3,
         out_specs=(VM, VM),
-        compiler_params=pltpu.CompilerParams(vmem_limit_bytes=40 * 2**20),
+        compiler_params=pltpu.CompilerParams(vmem_limit_bytes=24 * 2**20),
         cost_estimate=pl.CostEstimate(flops=10**6, bytes_accessed=10**6, transcendentals=0),
         name="regress",
     )(flux, other, sums)
@@ -444,7 +399,7 @@
             pltpu.VMEM((rows, specs, exposures, fibres), F32),
             pltpu.SemaphoreType.DMA((2, exposures)),
         ],
-        compiler_params=pltpu.CompilerParams(vmem_limit_bytes=40 * 2**20),
+        compiler_params=pltpu.CompilerParams(vmem_limit_bytes=24 * 2**20),
         cost_estimate=pl.CostEstimate(flops=10**6, bytes_accessed=10**6, transcendentals=0),
         name="clean",
     )(flux, sky, mine, sent)
@@ -463,16 +418,17 @@
     rows = pixels.shape[2]
     wave, spec = lax.axis_size("wave"), lax.axis_size("spec")
     total_rows = rows * wave
-    near, far = edge_call(arrays)
+    near, far, *bands = prepare_call(arrays, sky_index)
     far = lax.ppermute(
         far, "wave", [pair for i in range(1, wave - 1, 2) for pair in ((i, i + 1), (i + 1, i))]
     )
     near = lax.ppermute(near, "wave", [(i, i ^ 1) for i in range(wave)])
-    bands = band_call(arrays, sky_index)
     flux, sums = solve_call(near, far, bands)
     to_odd = [(i, i + 1) for i in range(0, wave, 2)]
-    sums = jnp.concatenate([sums, lax.ppermute(sums, "wave", to_odd)])
+    got = lax.ppermute(sums, "wave", to_odd)
+    flux, got = lax.optimization_barrier((flux, got))
     other = lax.ppermute(flux, "wave", to_odd)
+    sums = jnp.concatenate([sums, got])
     for k in powers(1, spec):
         sums = sums + lax.ppermute(sums, "spec", [(i, i ^ k) for i in range(spec)])
     regress, sky = regress_call(total_rows, flux, other, sums)

time: 53.7 us -> 44 us (0.82)
  Pallas kernels: 17.1 us -> 9.78 us
  local copies, waits for them, and re-layouts: 6.44 us -> 1.36 us
  starting transfers between devices: 14.1 us -> 19 us
  waiting for transfers between devices: 14.9 us -> 12.7 us
    ppermute x1, starting transfers between devices: 1.29 us -> 8.78 us  [local(): got = lax.ppermute(sums, 'wave', to_odd)]
    pallas_call x2 -> x1, Pallas kernels: 11.7 us -> 4.37 us  [prepare_call(): pl.pallas_call(functools.partial(prepare_kernel, chunks), out_shape=(mess...]
    unnamed x17 -> x5, local copies, waits for them, and re-layouts: 6.43 us -> 1.36 us
    ppermute x1, starting transfers between devices: 5.95 us -> 2.34 us  [local(): other = lax.ppermute(flux, 'wave', to_odd)]
    ppermute x2, starting transfers between devices: 3.02 us -> 4.13 us  [local(): sums = sums + lax.ppermute(sums, 'spec', [(i, i ^ k) for i in range(spec)])]
    ppermute x2, waiting for transfers between devices: 4.47 us -> 3.44 us  [local(): sums = sums + lax.ppermute(sums, 'spec', [(i, i ^ k) for i in range(spec)])]
    ppermute x1, waiting for transfers between devices: 1.71 us -> 0.81 us  [local(): got = lax.ppermute(sums, 'wave', to_odd)]
    ppermute x1, waiting for transfers between devices: 8.7 us -> 8.08 us  [local(): lax.ppermute(regress, 'wave', [(i + 1, i) for i in range(0, wave, 2)])]
  transfers between devices with their start and end apart: 9 -> 9, of which waited for: 4 -> 5; matrix products, arithmetic and copies ran while one was open for 0% -> 0% of each run, Pallas kernels for 17% -> 0%
where the time goes in v2:
time: 44 us; the launch traced here: 43.7 us
  starting transfers between devices  19 us (43%)
  waiting for transfers between devices  12.7 us (29%)
  Pallas kernels  9.78 us (22%)
  local copies, waits for them, and re-layouts  1.36 us (3%)
  between operations  0.75 us (2%)
    ppermute x1, starting transfers between devices, local(): got = lax.ppermute(sums, 'wave', to_odd)  8.78 us
    ppermute x1, waiting for transfers between devices, local(): lax.ppermute(regress, 'wave', [(i + 1, i) for i in range(0, wave, 2)])  8.08 us
    pallas_call x1, Pallas kernels, prepare_call(): pl.pallas_call(functools.partial(prepare_kernel, chunks), out_shape=(mess...  4.37 us
    ppermute x2, starting transfers between devices, local(): sums = sums + lax.ppermute(sums, 'spec', [(i, i ^ k) for i in range(spec)])  4.13 us
    ppermute x2, waiting for transfers between devices, local(): sums = sums + lax.ppermute(sums, 'spec', [(i, i ^ k) for i in range(spec)])  3.44 us
    pallas_call x1, Pallas kernels, solve_call(): pl.pallas_call(solve_kernel, out_shape=(in_vmem((rows, specs, exposures,...  2.73 us
    ppermute x1, starting transfers between devices, local(): other = lax.ppermute(flux, 'wave', to_odd)  2.34 us
    pallas_call x1, Pallas kernels, clean_call(): pl.pallas_call(functools.partial(clean_kernel, total_rows), out_shape=jax...  1.7 us
  transfers between devices with their start and end apart: 9, of which 5 were waited for; matrix products, arithmetic and copies ran while one was open for 0% of the time, Pallas kernels for 0%

profile of v2, /device:TPU:0, one launch (start us, length us, event | category | flops | bytes accessed | tf_op | source)
XLA Modules:
  0.0 43.7 jit_solution(2338411023704243095)
XLA Ops:
  0.6 0.7 %copy-done.1 = s32[2,40]{1,0:T(2,128)S(1)} copy-done((s32[2,40]{1,0:T(2,128)S(1)}, s32[2,40]{1,0:T(2,128)}, u32[]{:S(2)}) %copy-start.1) | copy-done | bytes 344
  1.3 4.4 %prepare.1 = (f32[6,2,8,500]{3,2,1,0:T(8,128)S(1)}, f32[6,2,8,500]{3,2,1,0:T(8,128)S(1)}, f32[52,2,8,500]{3,2,1,0:T(8,128)S(1)}, f32[52,2,8,500]{3,2,1,0:T(8,128...) custom-call(f32[8,50,2,500]{3,2,1,0:T(2,128)} %bitcast.9, ...), custom_call_target="tpu_custom_call" | custom-call | flops 10000000 | bytes 10000000 | tf_op jit(solution)/shard_map/prepare/pallas_call | solution.py:142
  5.7 0.5 %collective-permute-start = (f32[6,2,8,500]{3,2,1,0:T(8,128)S(1)}, f32[6,2,8,500]{3,2,1,0:T(8,128)S(1)}, u32[]{:S(2)}, u32[]{:S(2)}) collective-permute-start(f32[6,2,8,500]{3,2,1,0:T(8,128)S(1)} %get-tuple-element.15), channel_id=1, source_target_pairs={{0,1},{1,0},{2,3},{3,2},{4,5},{5,4},{6,7},{7,6},{8,9},{9,8},{10,11... | collective-permute-start | bytes 576008 | tf_op jit(solution)/shard_map/ppermute | solution.py:425
  6.2 0.7 %collective-permute-start.1 = (f32[6,2,8,500]{3,2,1,0:T(8,128)S(1)}, f32[6,2,8,500]{3,2,1,0:T(8,128)S(1)}, u32[]{:S(2)}, u32[]{:S(2)}) collective-permute-start(f32[6,2,8,500]{3,2,1,0:T(8,128)S(1)} %get-tuple-element.16), channel_id=1, source_target_pairs={{1,2},{2,1},{3,4},{4,3},{5,6},{6,5},{9,10},{10,9},{11,12},{12,11},... | collective-permute-start | bytes 576008 | tf_op jit(solution)/shard_map/ppermute | solution.py:422
  6.9 0.4 collective-permute-done.near
  7.3 0.0 collective-permute-done.1.far
  7.3 2.7 %solve.1 = (f32[50,2,8,500]{3,2,1,0:T(8,128)S(1)}, f32[2,8,128]{2,1,0:T(8,128)S(1)}) custom-call(f32[6,2,8,500]{3,2,1,0:T(8,128)S(1)} %collective-permute-done.near, f32[6,2,8,500]{3,2,1,0:T(8,128)S(1)} %collective-permute-done.1.far, f32[52,2,8,500]{3,2,1,0:T(8,128)S(1)} %get-tuple-element.17.diag, f32[52,2,8,500]{3,2,1,0:T(8,128)S(1)} %get-tuple-element.18.off_one, ...), custom_call_target="tpu_custom_call" | custom-call | flops 10000000 | bytes 10000000 | tf_op jit(solution)/shard_map/solve/pallas_call | solution.py:288
  10.0 8.8 %collective-permute-start.2 = (f32[2,8,128]{2,1,0:T(8,128)S(1)}, f32[2,8,128]{2,1,0:T(8,128)S(1)}, u32[]{:S(2)}, u32[]{:S(2)}) collective-permute-start(f32[2,8,128]{2,1,0:T(8,128)S(1)} %get-tuple-element.23), channel_id=1, source_target_pairs={{0,1},{2,3},{4,5},{6,7},{8,9},{10,11},{12,13},{14,15},{16,17},{18,... | collective-permute-start | bytes 24584 | tf_op jit(solution)/shard_map/ppermute | solution.py:428
  18.8 0.8 %collective-permute-done.2 = f32[2,8,128]{2,1,0:T(8,128)S(1)} collective-permute-done((f32[2,8,128]{2,1,0:T(8,128)S(1)}, f32[2,8,128]{2,1,0:T(8,128)S(1)}, u32[]{:S(2)}, u32[]{:S(2)}) %collective-permute-start.2) | collective-permute-done | bytes 8224 | tf_op jit(solution)/shard_map/ppermute | solution.py:428
  19.6 2.3 %collective-permute-start.3 = (f32[50,2,8,500]{3,2,1,0:T(8,128)S(1)}, f32[50,2,8,500]{3,2,1,0:T(8,128)S(1)}, u32[]{:S(2)}, u32[]{:S(2)}) collective-permute-start(f32[50,2,8,500]{3,2,1,0:T(8,128)S(1)} %get-tuple-element.24.flux), channel_id=1, source_target_pairs={{0,1},{2,3},{4,5},{6,7},{8,9},{10,11},{12,13},{14,15},{16,17},{18,... | collective-permute-start | bytes 4800008 | tf_op jit(solution)/shard_map/ppermute | solution.py:430
  22.0 2.1 %collective-permute-start.4 = (f32[4,8,128]{2,1,0:T(8,128)S(1)}, f32[4,8,128]{2,1,0:T(8,128)S(1)}, u32[]{:S(2)}, u32[]{:S(2)}) collective-permute-start(f32[4,8,128]{2,1,0:T(8,128)S(1)} %constant_dynamic-update-slice_fusion), channel_id=1, source_target_pairs={{0,8},{8,0},{16,24},{24,16},{1,9},{9,1},{17,25},{25,17},{2,10},{10... | collective-permute-start | bytes 49160 | tf_op jit(solution)/shard_map/ppermute | solution.py:433
  24.1 1.7 %collective-permute-done.4 = f32[4,8,128]{2,1,0:T(8,128)S(1)} collective-permute-done((f32[4,8,128]{2,1,0:T(8,128)S(1)}, f32[4,8,128]{2,1,0:T(8,128)S(1)}, u32[]{:S(2)}, u32[]{:S(2)}) %collective-permute-start.4) | collective-permute-done | bytes 16416 | tf_op jit(solution)/shard_map/ppermute | solution.py:433
  25.8 2.0 %collective-permute-start.5 = (f32[4,8,128]{2,1,0:T(8,128)S(1)}, f32[4,8,128]{2,1,0:T(8,128)S(1)}, u32[]{:S(2)}, u32[]{:S(2)}) collective-permute-start(f32[4,8,128]{2,1,0:T(8,128)S(1)} %add.12), channel_id=1, source_target_pairs={{0,16},{8,24},{16,0},{24,8},{1,17},{9,25},{17,1},{25,9},{2,18},{10... | collective-permute-start | bytes 49160 | tf_op jit(solution)/shard_map/ppermute | solution.py:433
  27.8 1.7 %collective-permute-done.5 = f32[4,8,128]{2,1,0:T(8,128)S(1)} collective-permute-done((f32[4,8,128]{2,1,0:T(8,128)S(1)}, f32[4,8,128]{2,1,0:T(8,128)S(1)}, u32[]{:S(2)}, u32[]{:S(2)}) %collective-permute-start.5) | collective-permute-done | bytes 16416 | tf_op jit(solution)/shard_map/ppermute | solution.py:433
  29.6 0.0 collective-permute-done.3.other
  29.6 1.0 %regress.1 = (f32[5,8,500]{2,1,0:T(8,128)S(1)}, f32[8,128]{1,0:T(8,128)}) custom-call(f32[50,2,8,500]{3,2,1,0:T(8,128)S(1)} %get-tuple-element.24.flux, f32[50,2,8,500]{3,2,1,0:T(8,128)S(1)} %collective-permute-done.3.other, f32[4,8,128]{2,1,0:T(8,128)S(1)} %add.13.sums), custom_call_target="tpu_custom_call" | custom-call | flops 1000000 | bytes 1000000 | tf_op jit(solution)/shard_map/regress/pallas_call | solution.py:336
  30.5 0.7 %collective-permute-start.6 = (f32[5,8,500]{2,1,0:T(8,128)S(1)}, f32[5,8,500]{2,1,0:T(8,128)S(1)}, u32[]{:S(2)}, u32[]{:S(2)}) collective-permute-start(f32[5,8,500]{2,1,0:T(8,128)S(1)} %get-tuple-element.27), channel_id=1, source_target_pairs={{1,3},{3,1},{5,7},{7,5},{9,11},{11,9},{13,15},{15,13},{17,19},{19,... | collective-permute-start | bytes 240008 | tf_op jit(solution)/shard_map/ppermute | solution.py:436
  31.2 0.0 collective-permute-done.6
  31.2 0.7 %collective-permute-start.7 = (f32[5,8,500]{2,1,0:T(8,128)S(1)}, f32[5,8,500]{2,1,0:T(8,128)S(1)}, u32[]{:S(2)}, u32[]{:S(2)}) collective-permute-start(f32[5,8,500]{2,1,0:T(8,128)S(1)} %add.14), channel_id=1, source_target_pairs={{1,5},{3,7},{5,1},{7,3},{9,13},{11,15},{13,9},{15,11},{17,21},{19,... | collective-permute-start | bytes 240008 | tf_op jit(solution)/shard_map/ppermute | solution.py:436
  31.9 0.0 collective-permute-done.7
  31.9 1.3 %collective-permute-start.8 = (f32[5,8,500]{2,1,0:T(8,128)S(1)}, f32[5,8,500]{2,1,0:T(8,128)S(1)}, u32[]{:S(2)}, u32[]{:S(2)}) collective-permute-start(f32[5,8,500]{2,1,0:T(8,128)S(1)} %add.15.mine), channel_id=1, source_target_pairs={{1,0},{3,2},{5,4},{7,6},{9,8},{11,10},{13,12},{15,14},{17,16},{19,... | collective-permute-start | bytes 240008 | tf_op jit(solution)/shard_map/ppermute | solution.py:437
  33.2 8.1 %collective-permute-done.8.sent = f32[5,8,500]{2,1,0:T(8,128)S(1)} collective-permute-done((f32[5,8,500]{2,1,0:T(8,128)S(1)}, f32[5,8,500]{2,1,0:T(8,128)S(1)}, u32[]{:S(2)}, u32[]{:S(2)}) %collective-permute-start.8) | collective-permute-done | bytes 80032 | tf_op jit(solution)/shard_map/ppermute | solution.py:437
  41.3 0.7 %copy-done = f32[8,128]{1,0:T(8,128)S(1)} copy-done((f32[8,128]{1,0:T(8,128)S(1)}, f32[8,128]{1,0:T(8,128)}, u32[]{:S(2)}) %copy-start) | copy-done | bytes 4120
  42.0 1.7 %clean.1 = f32[8,50,2,500]{3,2,1,0:T(2,128)} custom-call(f32[50,2,8,500]{3,2,1,0:T(8,128)S(1)} %get-tuple-element.24.flux, f32[8,128]{1,0:T(8,128)S(1)} %copy-done, f32[5,8,500]{2,1,0:T(8,128)S(1)} %add.15.mine, f32[5,8,500]{2,1,0:T(8,128)S(1)} %collective-permute-done.8.sent), custom_call_target="tpu_custom_call" | custom-call | flops 1000000 | bytes 1000000 | tf_op jit(solution)/shard_map/clean/pallas_call | solution.py:393
  (8 shorter events, 0.0 us)
Async XLA Ops:
  0.6 0.7 %copy-start.1 = (s32[2,40]{1,0:T(2,128)S(1)}, s32[2,40]{1,0:T(2,128)}, u32[]{:S(2)}) copy-start(s32[2,40]{1,0:T(2,128)} %sky_index.1) | copy-start | bytes 964
  5.7 1.6 %collective-permute-start = (f32[6,2,8,500]{3,2,1,0:T(8,128)S(1)}, f32[6,2,8,500]{3,2,1,0:T(8,128)S(1)}, u32[]{:S(2)}, u32[]{:S(2)}) collective-permute-start(f32[6,2,8,500]{3,2,1,0:T(8,128)S(1)} %get-tuple-element.15), channel_id=1, source_target_pairs={{0,1},{1,0},{2,3},{3,2},{4,5},{5,4},{6,7},{7,6},{8,9},{9,8},{10,11... | collective-permute-start | bytes 576008 | tf_op jit(solution)/shard_map/ppermute | solution.py:425
  6.2 1.1 %collective-permute-start.1 = (f32[6,2,8,500]{3,2,1,0:T(8,128)S(1)}, f32[6,2,8,500]{3,2,1,0:T(8,128)S(1)}, u32[]{:S(2)}, u32[]{:S(2)}) collective-permute-start(f32[6,2,8,500]{3,2,1,0:T(8,128)S(1)} %get-tuple-element.16), channel_id=1, source_target_pairs={{1,2},{2,1},{3,4},{4,3},{5,6},{6,5},{9,10},{10,9},{11,12},{12,11},... | collective-permute-start | bytes 576008 | tf_op jit(solution)/shard_map/ppermute | solution.py:422
  10.0 9.6 %collective-permute-start.2 = (f32[2,8,128]{2,1,0:T(8,128)S(1)}, f32[2,8,128]{2,1,0:T(8,128)S(1)}, u32[]{:S(2)}, u32[]{:S(2)}) collective-permute-start(f32[2,8,128]{2,1,0:T(8,128)S(1)} %get-tuple-element.23), channel_id=1, source_target_pairs={{0,1},{2,3},{4,5},{6,7},{8,9},{10,11},{12,13},{14,15},{16,17},{18,... | collective-permute-start | bytes 24584 | tf_op jit(solution)/shard_map/ppermute | solution.py:428
  19.6 9.9 %collective-permute-start.3 = (f32[50,2,8,500]{3,2,1,0:T(8,128)S(1)}, f32[50,2,8,500]{3,2,1,0:T(8,128)S(1)}, u32[]{:S(2)}, u32[]{:S(2)}) collective-permute-start(f32[50,2,8,500]{3,2,1,0:T(8,128)S(1)} %get-tuple-element.24.flux), channel_id=1, source_target_pairs={{0,1},{2,3},{4,5},{6,7},{8,9},{10,11},{12,13},{14,15},{16,17},{18,... | collective-permute-start | bytes 4800008 | tf_op jit(solution)/shard_map/ppermute | solution.py:430
  22.0 3.8 %collective-permute-start.4 = (f32[4,8,128]{2,1,0:T(8,128)S(1)}, f32[4,8,128]{2,1,0:T(8,128)S(1)}, u32[]{:S(2)}, u32[]{:S(2)}) collective-permute-start(f32[4,8,128]{2,1,0:T(8,128)S(1)} %constant_dynamic-update-slice_fusion), channel_id=1, source_target_pairs={{0,8},{8,0},{16,24},{24,16},{1,9},{9,1},{17,25},{25,17},{2,10},{10... | collective-permute-start | bytes 49160 | tf_op jit(solution)/shard_map/ppermute | solution.py:433
  25.8 3.8 %collective-permute-start.5 = (f32[4,8,128]{2,1,0:T(8,128)S(1)}, f32[4,8,128]{2,1,0:T(8,128)S(1)}, u32[]{:S(2)}, u32[]{:S(2)}) collective-permute-start(f32[4,8,128]{2,1,0:T(8,128)S(1)} %add.12), channel_id=1, source_target_pairs={{0,16},{8,24},{16,0},{24,8},{1,17},{9,25},{17,1},{25,9},{2,18},{10... | collective-permute-start | bytes 49160 | tf_op jit(solution)/shard_map/ppermute | solution.py:433
  30.5 0.7 %collective-permute-start.6 = (f32[5,8,500]{2,1,0:T(8,128)S(1)}, f32[5,8,500]{2,1,0:T(8,128)S(1)}, u32[]{:S(2)}, u32[]{:S(2)}) collective-permute-start(f32[5,8,500]{2,1,0:T(8,128)S(1)} %get-tuple-element.27), channel_id=1, source_target_pairs={{1,3},{3,1},{5,7},{7,5},{9,11},{11,9},{13,15},{15,13},{17,19},{19,... | collective-permute-start | bytes 240008 | tf_op jit(solution)/shard_map/ppermute | solution.py:436
  31.2 0.7 %collective-permute-start.7 = (f32[5,8,500]{2,1,0:T(8,128)S(1)}, f32[5,8,500]{2,1,0:T(8,128)S(1)}, u32[]{:S(2)}, u32[]{:S(2)}) collective-permute-start(f32[5,8,500]{2,1,0:T(8,128)S(1)} %add.14), channel_id=1, source_target_pairs={{1,5},{3,7},{5,1},{7,3},{9,13},{11,15},{13,9},{15,11},{17,21},{19,... | collective-permute-start | bytes 240008 | tf_op jit(solution)/shard_map/ppermute | solution.py:436
  31.9 9.4 %collective-permute-start.8 = (f32[5,8,500]{2,1,0:T(8,128)S(1)}, f32[5,8,500]{2,1,0:T(8,128)S(1)}, u32[]{:S(2)}, u32[]{:S(2)}) collective-permute-start(f32[5,8,500]{2,1,0:T(8,128)S(1)} %add.15.mine), channel_id=1, source_target_pairs={{1,0},{3,2},{5,4},{7,6},{9,8},{11,10},{13,12},{15,14},{17,16},{19,... | collective-permute-start | bytes 240008 | tf_op jit(solution)/shard_map/ppermute | solution.py:437
  41.3 0.7 %copy-start = (f32[8,128]{1,0:T(8,128)S(1)}, f32[8,128]{1,0:T(8,128)}, u32[]{:S(2)}) copy-start(f32[8,128]{1,0:T(8,128)} %get-tuple-element.26.sky_ref) | copy-start | bytes 12292

commit v3 on v2

--- a/solution.py
+++ b/solution.py
@@ -16,7 +16,7 @@
 F32 = jnp.float32
 VM = pl.BlockSpec(memory_space=pltpu.VMEM)
 SM = pl.BlockSpec(memory_space=pltpu.SMEM)
-HB = pl.BlockSpec(memory_space=pl.ANY)
+HB = pl.BlockSpec(memory_space=pltpu.HBM)
 
 
 def in_vmem(shape, dtype=F32):
@@ -67,11 +67,60 @@
     return (d3, a34, d4, b3, b4, raw)
 
 
+def edge_kernel(pix, iva, msk, lef, rig, near_out, far_out, bufs, mbuf, sems):
+    exposures, rows, specs, fibres = pix.shape
+    odd = lax.rem(lax.axis_index("wave"), 2) == 1
+    for end, start in enumerate((0, rows - HALO)):
+        for e in range(exposures):
+            for slot, ref in enumerate((pix, iva, lef, rig)):
+                pltpu.make_async_copy(
+                    ref.at[e, start : start + HALO], bufs.at[end, slot, :, :, e], sems.at[0, end]
+                ).start()
+            pltpu.make_async_copy(
+                msk.at[e, start : start + HALO], mbuf.at[end, :, :, e], sems.at[1, end]
+            ).start()
+    for end in range(2):
+        pltpu.make_async_copy(bufs.at[end], bufs.at[end], sems.at[0, end]).wait()
+        pltpu.make_async_copy(mbuf.at[end], mbuf.at[end], sems.at[1, end]).wait()
+        order = range(HALO - 1, -1, -1) if end == 0 else range(HALO)
+        for s in range(specs):
+            p = [bufs[end, 0, k, s] for k in order]
+            w = [weight_of(bufs[end, 1, k, s], mbuf[end, k, s]) for k in order]
+            l = [bufs[end, 2, k, s] for k in order]
+            r = [bufs[end, 3, k, s] for k in order]
+            if end == 0:
+                for slot, value in enumerate(edge_message(p, w, r, l)):
+                    near_out[slot, s] = value
+                continue
+            for slot, value in enumerate(edge_message(p, w, l, r)):
+                top = near_out[slot, s]
+                near_out[slot, s] = jnp.where(odd, top, value)
+                far_out[slot, s] = jnp.where(odd, value, top)
+
+
+def edge_call(arrays):
+    exposures, rows, specs, fibres = arrays[0].shape
+    message = in_vmem((PARTS, specs, exposures, fibres))
+    return pl.pallas_call(
+        edge_kernel,
+        out_shape=(message, message),
+        in_specs=[HB] * 5,
+        out_specs=(VM, VM),
+        scratch_shapes=[
+            pltpu.VMEM((2, 4, HALO, specs, exposures, fibres), F32),
+            pltpu.VMEM((2, HALO, specs, exposures, fibres), jnp.int32),
+            pltpu.SemaphoreType.DMA((2, 2)),
+        ],
+        compiler_params=pltpu.CompilerParams(vmem_limit_bytes=8 * 2**20),
+        cost_estimate=pl.CostEstimate(flops=10**6, bytes_accessed=10**6, transcendentals=0),
+        name="edges",
+    )(*arrays)
+
+
 def prepare_kernel(
-    chunks, pix, iva, msk, lef, rig, sky_index, near_out, far_out, diag, off_one, off_two, rhs, sky_mask, bufs, mbuf, sems
+    chunks, pix, iva, msk, lef, rig, sky_index, diag, off_one, off_two, rhs, sky_mask, bufs, mbuf, sems
 ):
     exposures, rows, specs, fibres = pix.shape
-    odd = lax.rem(lax.axis_index("wave"), 2) == 1
     bounds = [rows * c // chunks for c in range(chunks + 1)]
     for c in range(chunks):
         low, high = bounds[c], bounds[c + 1]
@@ -90,23 +139,15 @@
             found = found | (lane == sky_index[s, k])
         sky_mask[s] = jnp.where(found, 1.0, 0.0)
 
-    def load(k, s):
-        return bufs[0, k, s], weight_of(bufs[1, k, s], mbuf[k, s]), bufs[2, k, s], bufs[3, k, s]
-
     def row(k, s, carry):
         w1, wp1, wr1, wrr2, wrp2, wrr1, wrp1 = carry
-        p, w, l, r = load(k, s)
+        p, w, l, r = bufs[0, k, s], weight_of(bufs[1, k, s], mbuf[k, s]), bufs[2, k, s], bufs[3, k, s]
         wl, wr, wp = w * l, w * r, w * p
         diag[k, s] = w1 + wl * l + (wrr2 + REG)
         off_one[k, s] = wr1 + wl
         off_two[k, s] = wl * r
         rhs[k, s] = wp1 + wl * p + wrp2
         return (w, wp, wr, wrr1, wrp1, wr * r, wr * p)
-
-    def message(end, s):
-        order = range(HALO - 1, -1, -1) if end == 0 else range(rows - HALO, rows)
-        p, w, l, r = zip(*[load(k, s) for k in order])
-        return edge_message(p, w, r, l) if end == 0 else edge_message(p, w, l, r)
 
     carries = [(0.0,) * 7 for _ in range(specs)]
     for c in range(chunks):
@@ -117,9 +158,6 @@
         for s in range(specs):
             for k in range(low, high):
                 carries[s] = row(k, s, carries[s])
-            if c == 0:
-                for slot, value in enumerate(message(0, s)):
-                    near_out[slot, s] = value
     for s in range(specs):
         w1, wp1, wr1, wrr2, wrp2, wrr1, wrp1 = carries[s]
         diag[rows, s] = w1 + (wrr2 + REG)
@@ -127,23 +165,17 @@
         rhs[rows, s] = wp1 + wrp2
         diag[rows + 1, s] = wrr1 + REG
         rhs[rows + 1, s] = wrp1
-        for slot, value in enumerate(message(1, s)):
-            top = near_out[slot, s]
-            near_out[slot, s] = jnp.where(odd, top, value)
-            far_out[slot, s] = jnp.where(odd, value, top)
 
 
 def prepare_call(arrays, sky_index):
     exposures, rows, specs, fibres = arrays[0].shape
     chunks = 5
-    message = in_vmem((PARTS, specs, exposures, fibres))
     grown = in_vmem((rows + 2, specs, exposures, fibres))
-    arrays = [pltpu.with_memory_space_constraint(x, pltpu.HBM) for x in arrays]
     return pl.pallas_call(
         functools.partial(prepare_kernel, chunks),
-        out_shape=(message, message, grown, grown, grown, grown, in_vmem((specs, exposures, fibres))),
-        in_specs=[pl.BlockSpec(memory_space=pltpu.HBM)] * 5 + [SM],
-        out_specs=(VM,) * 7,
+        out_shape=(grown, grown, grown, grown, in_vmem((specs, exposures, fibres))),
+        in_specs=[HB] * 5 + [SM],
+        out_specs=(VM,) * 5,
         scratch_shapes=[
             pltpu.VMEM((4, rows, specs, exposures, fibres), F32),
             pltpu.VMEM((rows, specs, exposures, fibres), jnp.int32),
@@ -155,17 +187,21 @@
     )(*arrays, sky_index)
 
 
-def solve_kernel(near, far, diag, off_one, off_two, rhs, sky_mask, flux, sums, lower, lower_far, half):
+def solve_kernel(wave, near, far, diag, off_one, off_two, rhs, sky_mask, flux, sums, lower, lower_far, half):
     count, specs, exposures, fibres = diag.shape
     rows = count - 2
-    odd = lax.rem(lax.axis_index("wave"), 2)
-    is_odd = odd == 1
+    device = lax.axis_index("wave")
+    is_odd = lax.rem(device, 2) == 1
+    at_end = (device == 0) | (device == wave - 1)
+
+    def from_far(part, s):
+        return jnp.where(at_end, 0.0, far[part, s])
 
     def left(part, s):
-        return jnp.where(is_odd, near[part, s], far[part, s])
+        return jnp.where(is_odd, near[part, s], from_far(part, s))
 
     def right(part, s):
-        return jnp.where(is_odd, far[part, s], near[part, s])
+        return jnp.where(is_odd, from_far(part, s), near[part, s])
 
     lane = lax.broadcasted_iota(jnp.int32, (exposures, LANES), 1)
     numer = jnp.zeros((exposures, LANES), F32)
@@ -281,12 +317,12 @@
     sums[1] = denom
 
 
-def solve_call(near, far, bands):
+def solve_call(wave, near, far, bands):
     count, specs, exposures, fibres = bands[0].shape
     rows = count - 2
     scratch = pltpu.VMEM((count, specs, exposures, fibres), F32)
     return pl.pallas_call(
-        solve_kernel,
+        functools.partial(solve_kernel, wave),
         out_shape=(in_vmem((rows, specs, exposures, fibres)), in_vmem((2, exposures, LANES))),
         in_specs=[VM] * 7,
         out_specs=(VM, VM),
@@ -301,14 +337,15 @@
     return 2.0 * index.astype(F32) / (total_rows - 1) - 1.0
 
 
-def regress_kernel(total_rows, flux, other, sums, regress, sky_out):
+def regress_kernel(total_rows, flux, other, sums, regress, sky_out, sky_copy):
     rows, specs, exposures, fibres = flux.shape
     device = lax.axis_index("wave")
+    partner = device + 1 - 2 * lax.rem(device, 2)
     lane = lax.broadcasted_iota(jnp.int32, (exposures, LANES), 1)
     valid = lane < rows
     first = [[jnp.zeros((exposures, fibres), F32) for _ in range(specs)] for _ in range(2)]
     moments = [jnp.zeros((exposures, 1), F32) for _ in range(3)]
-    for which, (ref, base) in enumerate(((flux, device * rows), (other, (device - 1) * rows))):
+    for which, (ref, base) in enumerate(((flux, device * rows), (other, partner * rows))):
         sky = jnp.where(valid, sums[2 * which] / jnp.where(valid, sums[2 * which + 1], 1.0), 0.0)
         position = position_of(base + lane, total_rows)
         tilted = sky * position
@@ -317,6 +354,7 @@
         moments[2] += jnp.sum(tilted * tilted, axis=1, keepdims=True)
         if which == 0:
             sky_out[...] = sky
+            sky_copy[...] = sky
         for k in range(rows):
             plain_k = jnp.broadcast_to(sky[:, k : k + 1], (exposures, fibres))
             tilted_k = jnp.broadcast_to(tilted[:, k : k + 1], (exposures, fibres))
@@ -338,9 +376,10 @@
         out_shape=(
             in_vmem((2 * specs + 1, exposures, fibres)),
             in_vmem((exposures, LANES)),
+            in_vmem((exposures, LANES)),
         ),
         in_specs=[VM] * 3,
-        out_specs=(VM, VM),
+        out_specs=(VM, VM, VM),
         compiler_params=pltpu.CompilerParams(vmem_limit_bytes=24 * 2**20),
         cost_estimate=pl.CostEstimate(flops=10**6, bytes_accessed=10**6, transcendentals=0),
         name="regress",
@@ -369,23 +408,21 @@
     sky = sky_ref[...]
     tilted = sky * position_of(device * rows + lane, total_rows)
     chunks = sems.shape[0]
-    size = -(-rows // chunks)
-    copies = []
+    bounds = [rows * c // chunks for c in range(chunks + 1)]
     for c in range(chunks):
-        low, high = c * size, min(rows, (c + 1) * size)
+        low, high = bounds[c], bounds[c + 1]
         for k in range(low, high):
             plain_k = jnp.broadcast_to(sky[:, k : k + 1], (exposures, fibres))
             tilted_k = jnp.broadcast_to(tilted[:, k : k + 1], (exposures, fibres))
             for s in range(specs):
                 buf[k, s] = flux[k, s] - (slope_a[s] * plain_k + slope_b[s] * tilted_k)
         for e in range(exposures):
-            copy = pltpu.make_async_copy(
-                buf.at[low:high, :, e], out.at[e, low:high], sems.at[c, e]
-            )
-            copy.start()
-            copies.append(copy)
-    for copy in copies:
-        copy.wait()
+            pltpu.make_async_copy(
+                buf.at[low:high, :, e], out.at[e, low:high], sems.at[c]
+            ).start()
+    for c in range(chunks):
+        part = buf.at[bounds[c] : bounds[c + 1]]
+        pltpu.make_async_copy(part, part, sems.at[c]).wait()
 
 
 def clean_call(total_rows, flux, sky, mine, sent):
@@ -397,7 +434,7 @@
         out_specs=HB,
         scratch_shapes=[
             pltpu.VMEM((rows, specs, exposures, fibres), F32),
-            pltpu.SemaphoreType.DMA((2, exposures)),
+            pltpu.SemaphoreType.DMA((4,)),
         ],
         compiler_params=pltpu.CompilerParams(vmem_limit_bytes=24 * 2**20),
         cost_estimate=pl.CostEstimate(flops=10**6, bytes_accessed=10**6, transcendentals=0),
@@ -413,30 +450,42 @@
     return steps
 
 
+def swap(values, partner):
+    spec, wave = lax.axis_size("spec"), lax.axis_size("wave")
+    pairs = []
+    for s in range(spec):
+        for i in range(wave):
+            t, j = partner(s, i)
+            if not 0 <= j < wave:
+                t, j = s ^ 1, i
+            if t < spec:
+                pairs.append((s * wave + i, t * wave + j))
+    return lax.ppermute(values, ("spec", "wave"), pairs)
+
+
 def local(pixels, ivar, mask, psf_left, psf_right, sky_index):
     arrays = [jnp.transpose(x, (0, 2, 1, 3)) for x in (pixels, ivar, mask, psf_left, psf_right)]
     rows = pixels.shape[2]
     wave, spec = lax.axis_size("wave"), lax.axis_size("spec")
     total_rows = rows * wave
-    near, far, *bands = prepare_call(arrays, sky_index)
-    far = lax.ppermute(
-        far, "wave", [pair for i in range(1, wave - 1, 2) for pair in ((i, i + 1), (i + 1, i))]
-    )
-    near = lax.ppermute(near, "wave", [(i, i ^ 1) for i in range(wave)])
-    flux, sums = solve_call(near, far, bands)
-    to_odd = [(i, i + 1) for i in range(0, wave, 2)]
-    got = lax.ppermute(sums, "wave", to_odd)
+    hbm = [pltpu.with_memory_space_constraint(x, pltpu.HBM) for x in arrays]
+    near, far = edge_call(hbm)
+    far = swap(far, lambda s, i: (s, i + 1 if i % 2 else i - 1))
+    near = swap(near, lambda s, i: (s, i ^ 1))
+    bands = prepare_call(hbm, sky_index)
+    flux, sums = solve_call(wave, near, far, bands)
+    got = swap(sums, lambda s, i: (s, i ^ 1))
     flux, got = lax.optimization_barrier((flux, got))
-    other = lax.ppermute(flux, "wave", to_odd)
+    other = swap(flux, lambda s, i: (s, i ^ 1))
     sums = jnp.concatenate([sums, got])
     for k in powers(1, spec):
-        sums = sums + lax.ppermute(sums, "spec", [(i, i ^ k) for i in range(spec)])
-    regress, sky = regress_call(total_rows, flux, other, sums)
+        sums = sums + swap(sums, lambda s, i: (s ^ k, i))
+    regress, sky, sky_out = regress_call(total_rows, flux, other, sums)
     for k in powers(2, wave):
-        regress = regress + lax.ppermute(regress, "wave", [(i, i ^ k) for i in range(1, wave, 2)])
-    sent = lax.ppermute(regress, "wave", [(i + 1, i) for i in range(0, wave, 2)])
+        regress = regress + swap(regress, lambda s, i: (s, i ^ k if i % 2 else -1))
+    sent = swap(regress, lambda s, i: (s, i ^ 1))
     cleaned = clean_call(total_rows, flux, sky, regress, sent)
-    return (jnp.transpose(cleaned, (0, 2, 1, 3)), sky[:, :rows])
+    return (jnp.transpose(cleaned, (0, 2, 1, 3)), sky_out[:, :rows])
 
 
 def solution(mesh):

time: 44 us -> 34.1 us (0.78)
  starting transfers between devices: 19 us -> 9.63 us
  local copies, waits for them, and re-layouts: 1.36 us -> 0.01 us
  Pallas kernels: 9.78 us -> 10.9 us
    ppermute x9, starting transfers between devices: 19 us -> 9.63 us  [swap(): return lax.ppermute(values, ('spec', 'wave'), pairs)]
    unnamed x5 -> x3, local copies, waits for them, and re-layouts: 1.36 us -> 0.01 us
    pallas_call x2 -> x3, Pallas kernels: 7.1 us -> 8.45 us  [the longest x1 4.25 us: prepare_call(): pl.pallas_call(functools.partial(prepare_kernel, chunks), out_shape=(grow...]
  transfers between devices with their start and end apart: 9 -> 9, of which waited for: 5 -> 6; matrix products, arithmetic and copies ran while one was open for 0% -> 0% of each run, Pallas kernels for 0% -> 13%
where the time goes in v3:
time: 34.1 us; the launch traced here: 33.8 us
  waiting for transfers between devices  12.6 us (37%)
  Pallas kernels  10.9 us (32%)
  starting transfers between devices  9.63 us (28%)
  between operations  0.7 us (2%)
    ppermute x9, waiting for transfers between devices, swap(): return lax.ppermute(values, ('spec', 'wave'), pairs)  12.6 us
    ppermute x9, starting transfers between devices, swap(): return lax.ppermute(values, ('spec', 'wave'), pairs)  9.63 us
    pallas_call x1, Pallas kernels, prepare_call(): pl.pallas_call(functools.partial(prepare_kernel, chunks), out_shape=(grow...  4.25 us
    pallas_call x1, Pallas kernels, solve_call(): pl.pallas_call(functools.partial(solve_kernel, wave), out_shape=(in_vmem(...  2.73 us
    pallas_call x1, Pallas kernels, edge_call(): pl.pallas_call(edge_kernel, out_shape=(message, message), in_specs=[HB] *...  1.48 us
    pallas_call x1, Pallas kernels, clean_call(): pl.pallas_call(functools.partial(clean_kernel, total_rows), out_shape=jax...  1.44 us
    pallas_call x1, Pallas kernels, regress_call(): pl.pallas_call(functools.partial(regress_kernel, total_rows), out_shape=(...  0.98 us
  transfers between devices with their start and end apart: 9, of which 6 were waited for; matrix products, arithmetic and copies ran while one was open for 0% of the time, Pallas kernels for 13%

profile of v3, /device:TPU:0, one launch (start us, length us, event | category | flops | bytes accessed | tf_op | source)
XLA Modules:
  0.0 33.8 jit_solution(16673357180096049333)
XLA Ops:
  0.6 0.0 copy-start
  0.6 1.5 %edges.1 = (f32[6,2,8,500]{3,2,1,0:T(8,128)S(1)}, f32[6,2,8,500]{3,2,1,0:T(8,128)S(1)}) custom-call(f32[8,50,2,500]{3,2,1,0:T(2,128)} %bitcast.7, f32[8,50,2,500]{3,2,1,0:T(2,128)} %bitcast.9, s32[8,50,2,500]{3,2,1,0:T(2,128)} %bitcast.11, f32[8,50,2,500]{3,2,1,0:T(2,128)} %bitcast.13, f32[8,50,2,500]{3,2,1,0:T(2,128)} %bitcast.15), custom_call_target="tpu_custom_call" | custom-call | flops 1000000 | bytes 1000000 | tf_op jit(solution)/shard_map/edges/pallas_call | solution.py:104
  2.1 0.5 %collective-permute-start = (f32[6,2,8,500]{3,2,1,0:T(8,128)S(1)}, f32[6,2,8,500]{3,2,1,0:T(8,128)S(1)}, u32[]{:S(2)}, u32[]{:S(2)}) collective-permute-start(f32[6,2,8,500]{3,2,1,0:T(8,128)S(1)} %get-tuple-element.16), channel_id=1, source_target_pairs={{0,1},{1,0},{2,3},{3,2},{4,5},{5,4},{6,7},{7,6},{8,9},{9,8},{10,11... | collective-permute-start | bytes 576008 | tf_op jit(solution)/shard_map/ppermute | solution.py:463
  2.6 2.6 %collective-permute-start.1 = (f32[6,2,8,500]{3,2,1,0:T(8,128)S(1)}, f32[6,2,8,500]{3,2,1,0:T(8,128)S(1)}, u32[]{:S(2)}, u32[]{:S(2)}) collective-permute-start(f32[6,2,8,500]{3,2,1,0:T(8,128)S(1)} %get-tuple-element.17), channel_id=1, source_target_pairs={{0,8},{1,2},{2,1},{3,4},{4,3},{5,6},{6,5},{7,15},{8,0},{9,10},{10,... | collective-permute-start | bytes 576008 | tf_op jit(solution)/shard_map/ppermute | solution.py:463
  5.2 4.2 %prepare.1 = (f32[52,2,8,500]{3,2,1,0:T(8,128)S(1)}, f32[52,2,8,500]{3,2,1,0:T(8,128)S(1)}, f32[52,2,8,500]{3,2,1,0:T(8,128)S(1)}, f32[52,2,8,500]{3,2,1,0:T(8,128)S(1)}, f32[2,8,500]{2,1,0:T(8,128)S(1)}) custom-call(f32[8,50,2,500]{3,2,1,0:T(2,128)} %bitcast.8, f32[8,50,2,500]{3,2,1,0:T(2,128)} %bitcast.10, s32[8,50,2,500]{3,2,1,0:T(2,128)} %bitcast.12, ...), custom_call_target="tpu_custom_call" | custom-call | flops 10000000 | bytes 10000000 | tf_op jit(solution)/shard_map/prepare/pallas_call | solution.py:174
  9.5 0.0 collective-permute-done.near
  9.5 0.0 collective-permute-done.1.far
  9.5 2.7 %solve.1 = (f32[50,2,8,500]{3,2,1,0:T(8,128)S(1)}, f32[2,8,128]{2,1,0:T(8,128)S(1)}) custom-call(f32[6,2,8,500]{3,2,1,0:T(8,128)S(1)} %collective-permute-done.near, f32[6,2,8,500]{3,2,1,0:T(8,128)S(1)} %collective-permute-done.1.far, f32[52,2,8,500]{3,2,1,0:T(8,128)S(1)} %get-tuple-element.18.diag, f32[52,2,8,500]{3,2,1,0:T(8,128)S(1)} %get-tuple-element.19.off_one, ...), custom_call_target="tpu_custom_call" | custom-call | flops 10000000 | bytes 10000000 | tf_op jit(solution)/shard_map/solve/pallas_call | solution.py:324
  12.2 0.2 collective-permute-start.2
  12.4 1.0 %collective-permute-done.2 = f32[2,8,128]{2,1,0:T(8,128)S(1)} collective-permute-done((f32[2,8,128]{2,1,0:T(8,128)S(1)}, f32[2,8,128]{2,1,0:T(8,128)S(1)}, u32[]{:S(2)}, u32[]{:S(2)}) %collective-permute-start.2) | collective-permute-done | bytes 8224 | tf_op jit(solution)/shard_map/ppermute | solution.py:463
  13.4 0.2 collective-permute-start.3
  13.6 1.5 %collective-permute-start.4 = (f32[4,8,128]{2,1,0:T(8,128)S(1)}, f32[4,8,128]{2,1,0:T(8,128)S(1)}, u32[]{:S(2)}, u32[]{:S(2)}) collective-permute-start(f32[4,8,128]{2,1,0:T(8,128)S(1)} %constant_dynamic-update-slice_fusion), channel_id=1, source_target_pairs={{0,8},{1,9},{2,10},{3,11},{4,12},{5,13},{6,14},{7,15},{8,0},{9,1},... | collective-permute-start | bytes 49160 | tf_op jit(solution)/shard_map/ppermute | solution.py:463
  15.1 2.2 %collective-permute-done.4 = f32[4,8,128]{2,1,0:T(8,128)S(1)} collective-permute-done((f32[4,8,128]{2,1,0:T(8,128)S(1)}, f32[4,8,128]{2,1,0:T(8,128)S(1)}, u32[]{:S(2)}, u32[]{:S(2)}) %collective-permute-start.4) | collective-permute-done | bytes 16416 | tf_op jit(solution)/shard_map/ppermute | solution.py:463
  17.3 1.5 %collective-permute-start.5 = (f32[4,8,128]{2,1,0:T(8,128)S(1)}, f32[4,8,128]{2,1,0:T(8,128)S(1)}, u32[]{:S(2)}, u32[]{:S(2)}) collective-permute-start(f32[4,8,128]{2,1,0:T(8,128)S(1)} %add.12), channel_id=1, source_target_pairs={{0,16},{1,17},{2,18},{3,19},{4,20},{5,21},{6,22},{7,23},{8,24},{9,... | collective-permute-start | bytes 49160 | tf_op jit(solution)/shard_map/ppermute | solution.py:463
  18.9 2.2 %collective-permute-done.5 = f32[4,8,128]{2,1,0:T(8,128)S(1)} collective-permute-done((f32[4,8,128]{2,1,0:T(8,128)S(1)}, f32[4,8,128]{2,1,0:T(8,128)S(1)}, u32[]{:S(2)}, u32[]{:S(2)}) %collective-permute-start.5) | collective-permute-done | bytes 16416 | tf_op jit(solution)/shard_map/ppermute | solution.py:463
  21.1 0.0 collective-permute-done.3.other
  21.1 1.0 %regress.1 = (f32[5,8,500]{2,1,0:T(8,128)S(1)}, f32[8,128]{1,0:T(8,128)S(1)}, f32[8,128]{1,0:T(8,128)}) custom-call(f32[50,2,8,500]{3,2,1,0:T(8,128)S(1)} %get-tuple-element.25.flux, f32[50,2,8,500]{3,2,1,0:T(8,128)S(1)} %collective-permute-done.3.other, f32[4,8,128]{2,1,0:T(8,128)S(1)} %add.13.sums), custom_call_target="tpu_custom_call" | custom-call | flops 1000000 | bytes 1000000 | tf_op jit(solution)/shard_map/regress/pallas_call | solution.py:374
  22.1 1.5 %collective-permute-start.6 = (f32[5,8,500]{2,1,0:T(8,128)S(1)}, f32[5,8,500]{2,1,0:T(8,128)S(1)}, u32[]{:S(2)}, u32[]{:S(2)}) collective-permute-start(f32[5,8,500]{2,1,0:T(8,128)S(1)} %get-tuple-element.28), channel_id=1, source_target_pairs={{0,8},{1,3},{2,10},{3,1},{4,12},{5,7},{6,14},{7,5},{8,0},{9,11},{1... | collective-permute-start | bytes 240008 | tf_op jit(solution)/shard_map/ppermute | solution.py:463
  23.6 2.9 %collective-permute-done.6 = f32[5,8,500]{2,1,0:T(8,128)S(1)} collective-permute-done((f32[5,8,500]{2,1,0:T(8,128)S(1)}, f32[5,8,500]{2,1,0:T(8,128)S(1)}, u32[]{:S(2)}, u32[]{:S(2)}) %collective-permute-start.6) | collective-permute-done | bytes 80032 | tf_op jit(solution)/shard_map/ppermute | solution.py:463
  26.5 1.6 %collective-permute-start.7 = (f32[5,8,500]{2,1,0:T(8,128)S(1)}, f32[5,8,500]{2,1,0:T(8,128)S(1)}, u32[]{:S(2)}, u32[]{:S(2)}) collective-permute-start(f32[5,8,500]{2,1,0:T(8,128)S(1)} %add.14), channel_id=1, source_target_pairs={{0,8},{1,5},{2,10},{3,7},{4,12},{5,1},{6,14},{7,3},{8,0},{9,13},{1... | collective-permute-start | bytes 240008 | tf_op jit(solution)/shard_map/ppermute | solution.py:463
  28.1 2.9 %collective-permute-done.7 = f32[5,8,500]{2,1,0:T(8,128)S(1)} collective-permute-done((f32[5,8,500]{2,1,0:T(8,128)S(1)}, f32[5,8,500]{2,1,0:T(8,128)S(1)}, u32[]{:S(2)}, u32[]{:S(2)}) %collective-permute-start.7) | collective-permute-done | bytes 80032 | tf_op jit(solution)/shard_map/ppermute | solution.py:463
  31.1 0.1 collective-permute-start.8
  31.1 1.3 %collective-permute-done.8.sent = f32[5,8,500]{2,1,0:T(8,128)S(1)} collective-permute-done((f32[5,8,500]{2,1,0:T(8,128)S(1)}, f32[5,8,500]{2,1,0:T(8,128)S(1)}, u32[]{:S(2)}, u32[]{:S(2)}) %collective-permute-start.8) | collective-permute-done | bytes 80032 | tf_op jit(solution)/shard_map/ppermute | solution.py:463
  32.4 1.4 %clean.1 = f32[8,50,2,500]{3,2,1,0:T(2,128)} custom-call(f32[50,2,8,500]{3,2,1,0:T(8,128)S(1)} %get-tuple-element.25.flux, f32[8,128]{1,0:T(8,128)S(1)} %get-tuple-element.27.sky_ref, f32[5,8,500]{2,1,0:T(8,128)S(1)} %add.15.mine, f32[5,8,500]{2,1,0:T(8,128)S(1)} %collective-permute-done.8.sent), custom_call_target="tpu_custom_call" | custom-call | flops 1000000 | bytes 1000000 | tf_op jit(solution)/shard_map/clean/pallas_call | solution.py:430
  (7 shorter events, 0.0 us)
Async XLA Ops:
  0.6 4.6 %copy-start = (s32[2,40]{1,0:T(2,128)S(1)}, s32[2,40]{1,0:T(2,128)}, u32[]{:S(2)}) copy-start(s32[2,40]{1,0:T(2,128)} %sky_index.1) | copy-start | bytes 964
  2.1 7.3 %collective-permute-start = (f32[6,2,8,500]{3,2,1,0:T(8,128)S(1)}, f32[6,2,8,500]{3,2,1,0:T(8,128)S(1)}, u32[]{:S(2)}, u32[]{:S(2)}) collective-permute-start(f32[6,2,8,500]{3,2,1,0:T(8,128)S(1)} %get-tuple-element.16), channel_id=1, source_target_pairs={{0,1},{1,0},{2,3},{3,2},{4,5},{5,4},{6,7},{7,6},{8,9},{9,8},{10,11... | collective-permute-start | bytes 576008 | tf_op jit(solution)/shard_map/ppermute | solution.py:463
  2.6 6.8 %collective-permute-start.1 = (f32[6,2,8,500]{3,2,1,0:T(8,128)S(1)}, f32[6,2,8,500]{3,2,1,0:T(8,128)S(1)}, u32[]{:S(2)}, u32[]{:S(2)}) collective-permute-start(f32[6,2,8,500]{3,2,1,0:T(8,128)S(1)} %get-tuple-element.17), channel_id=1, source_target_pairs={{0,8},{1,2},{2,1},{3,4},{4,3},{5,6},{6,5},{7,15},{8,0},{9,10},{10,... | collective-permute-start | bytes 576008 | tf_op jit(solution)/shard_map/ppermute | solution.py:463
  12.2 1.2 %collective-permute-start.2 = (f32[2,8,128]{2,1,0:T(8,128)S(1)}, f32[2,8,128]{2,1,0:T(8,128)S(1)}, u32[]{:S(2)}, u32[]{:S(2)}) collective-permute-start(f32[2,8,128]{2,1,0:T(8,128)S(1)} %get-tuple-element.24), channel_id=1, source_target_pairs={{0,1},{1,0},{2,3},{3,2},{4,5},{5,4},{6,7},{7,6},{8,9},{9,8},{10,11... | collective-permute-start | bytes 24584 | tf_op jit(solution)/shard_map/ppermute | solution.py:463
  13.4 7.7 %collective-permute-start.3 = (f32[50,2,8,500]{3,2,1,0:T(8,128)S(1)}, f32[50,2,8,500]{3,2,1,0:T(8,128)S(1)}, u32[]{:S(2)}, u32[]{:S(2)}) collective-permute-start(f32[50,2,8,500]{3,2,1,0:T(8,128)S(1)} %get-tuple-element.25.flux), channel_id=1, source_target_pairs={{0,1},{1,0},{2,3},{3,2},{4,5},{5,4},{6,7},{7,6},{8,9},{9,8},{10,11... | collective-permute-start | bytes 4800008 | tf_op jit(solution)/shard_map/ppermute | solution.py:463
  13.6 3.7 %collective-permute-start.4 = (f32[4,8,128]{2,1,0:T(8,128)S(1)}, f32[4,8,128]{2,1,0:T(8,128)S(1)}, u32[]{:S(2)}, u32[]{:S(2)}) collective-permute-start(f32[4,8,128]{2,1,0:T(8,128)S(1)} %constant_dynamic-update-slice_fusion), channel_id=1, source_target_pairs={{0,8},{1,9},{2,10},{3,11},{4,12},{5,13},{6,14},{7,15},{8,0},{9,1},... | collective-permute-start | bytes 49160 | tf_op jit(solution)/shard_map/ppermute | solution.py:463
  17.3 3.7 %collective-permute-start.5 = (f32[4,8,128]{2,1,0:T(8,128)S(1)}, f32[4,8,128]{2,1,0:T(8,128)S(1)}, u32[]{:S(2)}, u32[]{:S(2)}) collective-permute-start(f32[4,8,128]{2,1,0:T(8,128)S(1)} %add.12), channel_id=1, source_target_pairs={{0,16},{1,17},{2,18},{3,19},{4,20},{5,21},{6,22},{7,23},{8,24},{9,... | collective-permute-start | bytes 49160 | tf_op jit(solution)/shard_map/ppermute | solution.py:463
  22.1 4.4 %collective-permute-start.6 = (f32[5,8,500]{2,1,0:T(8,128)S(1)}, f32[5,8,500]{2,1,0:T(8,128)S(1)}, u32[]{:S(2)}, u32[]{:S(2)}) collective-permute-start(f32[5,8,500]{2,1,0:T(8,128)S(1)} %get-tuple-element.28), channel_id=1, source_target_pairs={{0,8},{1,3},{2,10},{3,1},{4,12},{5,7},{6,14},{7,5},{8,0},{9,11},{1... | collective-permute-start | bytes 240008 | tf_op jit(solution)/shard_map/ppermute | solution.py:463
  26.5 4.5 %collective-permute-start.7 = (f32[5,8,500]{2,1,0:T(8,128)S(1)}, f32[5,8,500]{2,1,0:T(8,128)S(1)}, u32[]{:S(2)}, u32[]{:S(2)}) collective-permute-start(f32[5,8,500]{2,1,0:T(8,128)S(1)} %add.14), channel_id=1, source_target_pairs={{0,8},{1,5},{2,10},{3,7},{4,12},{5,1},{6,14},{7,3},{8,0},{9,13},{1... | collective-permute-start | bytes 240008 | tf_op jit(solution)/shard_map/ppermute | solution.py:463
  31.1 1.3 %collective-permute-start.8 = (f32[5,8,500]{2,1,0:T(8,128)S(1)}, f32[5,8,500]{2,1,0:T(8,128)S(1)}, u32[]{:S(2)}, u32[]{:S(2)}) collective-permute-start(f32[5,8,500]{2,1,0:T(8,128)S(1)} %add.15.mine), channel_id=1, source_target_pairs={{0,1},{1,0},{2,3},{3,2},{4,5},{5,4},{6,7},{7,6},{8,9},{9,8},{10,11... | collective-permute-start | bytes 240008 | tf_op jit(solution)/shard_map/ppermute | solution.py:463

commit v4 on v3

--- a/solution.py
+++ b/solution.py
@@ -11,6 +11,7 @@
 RIDGE = 1.0
 HALO = 4
 PARTS = 6
+PREFETCH = 3
 LANES = 128
 
 F32 = jnp.float32
@@ -118,7 +119,7 @@
 
 
 def prepare_kernel(
-    chunks, pix, iva, msk, lef, rig, sky_index, diag, off_one, off_two, rhs, sky_mask, bufs, mbuf, sems
+    chunks, pix, iva, msk, lef, rig, sky_index, diag, off_one, off_two, rhs, shares, sky_mask, denom, bufs, mbuf, sems
 ):
     exposures, rows, specs, fibres = pix.shape
     bounds = [rows * c // chunks for c in range(chunks + 1)]
@@ -139,17 +140,28 @@
             found = found | (lane == sky_index[s, k])
         sky_mask[s] = jnp.where(found, 1.0, 0.0)
 
-    def row(k, s, carry):
+    spot = lax.broadcasted_iota(jnp.int32, (exposures, LANES), 1)
+
+    def share(k, s, value, total):
+        part = sky_mask[s] * value
+        shares[k, s] = part
+        return jnp.where(spot == k, total + jnp.sum(part, axis=1, keepdims=True), total)
+
+    def row(k, s, carry, total):
         w1, wp1, wr1, wrr2, wrp2, wrr1, wrp1 = carry
         p, w, l, r = bufs[0, k, s], weight_of(bufs[1, k, s], mbuf[k, s]), bufs[2, k, s], bufs[3, k, s]
         wl, wr, wp = w * l, w * r, w * p
-        diag[k, s] = w1 + wl * l + (wrr2 + REG)
+        here = w1 + wl * l + (wrr2 + REG)
+        diag[k, s] = here
+        if k > 0:
+            total = share(k - 1, s, here, total)
         off_one[k, s] = wr1 + wl
         off_two[k, s] = wl * r
         rhs[k, s] = wp1 + wl * p + wrp2
-        return (w, wp, wr, wrr1, wrp1, wr * r, wr * p)
+        return (w, wp, wr, wrr1, wrp1, wr * r, wr * p), total
 
     carries = [(0.0,) * 7 for _ in range(specs)]
+    total = jnp.zeros((exposures, LANES), F32)
     for c in range(chunks):
         low, high = bounds[c], bounds[c + 1]
         part, mpart = bufs.at[:, low:high], mbuf.at[low:high]
@@ -157,14 +169,17 @@
         pltpu.make_async_copy(mpart, mpart, sems.at[1, c]).wait()
         for s in range(specs):
             for k in range(low, high):
-                carries[s] = row(k, s, carries[s])
+                carries[s], total = row(k, s, carries[s], total)
     for s in range(specs):
         w1, wp1, wr1, wrr2, wrp2, wrr1, wrp1 = carries[s]
-        diag[rows, s] = w1 + (wrr2 + REG)
+        here = w1 + (wrr2 + REG)
+        diag[rows, s] = here
+        total = share(rows - 1, s, here, total)
         off_one[rows, s] = wr1
         rhs[rows, s] = wp1 + wrp2
         diag[rows + 1, s] = wrr1 + REG
         rhs[rows + 1, s] = wrp1
+    denom[...] = total
 
 
 def prepare_call(arrays, sky_index):
@@ -173,9 +188,17 @@
     grown = in_vmem((rows + 2, specs, exposures, fibres))
     return pl.pallas_call(
         functools.partial(prepare_kernel, chunks),
-        out_shape=(grown, grown, grown, grown, in_vmem((specs, exposures, fibres))),
-        in_specs=[HB] * 5 + [SM],
-        out_specs=(VM,) * 5,
+        out_shape=(
+            grown,
+            grown,
+            grown,
+            grown,
+            in_vmem((rows, specs, exposures, fibres)),
+            in_vmem((specs, exposures, fibres)),
+            in_vmem((exposures, LANES)),
+        ),
+        in_specs=[pl.BlockSpec(memory_space=pl.ANY)] * 5 + [SM],
+        out_specs=(VM,) * 7,
         scratch_shapes=[
             pltpu.VMEM((4, rows, specs, exposures, fibres), F32),
             pltpu.VMEM((rows, specs, exposures, fibres), jnp.int32),
@@ -187,7 +210,9 @@
     )(*arrays, sky_index)
 
 
-def solve_kernel(wave, near, far, diag, off_one, off_two, rhs, sky_mask, flux, sums, lower, lower_far, half):
+def solve_kernel(
+    wave, near, far, diag, off_one, off_two, rhs, shares, sky_mask, denom, flux, sums, lower, lower_far, half
+):
     count, specs, exposures, fibres = diag.shape
     rows = count - 2
     device = lax.axis_index("wave")
@@ -205,7 +230,6 @@
 
     lane = lax.broadcasted_iota(jnp.int32, (exposures, LANES), 1)
     numer = jnp.zeros((exposures, LANES), F32)
-    denom = jnp.zeros((exposures, LANES), F32)
 
     zero = jnp.zeros((exposures, fibres), F32)
     spans = range(specs)
@@ -278,43 +302,37 @@
     def total(parts):
         return jnp.sum(parts, axis=1, keepdims=True)
 
-    masks = [sky_mask[s] for s in spans]
-
-    def spread(k, numer, denom, precs, values):
-        weighted = sum(masks[s] * precs[s] for s in spans)
-        valued = sum(masks[s] * precs[s] * values[s] for s in spans)
-        return (
-            jnp.where(lane == k, total(valued), numer),
-            jnp.where(lane == k, total(weighted), denom),
-        )
-
-    precs = [diag[rows, s] + right(5, s) for s in spans]
-    numer, denom = spread(rows - 1, numer, denom, precs, [after[s][0] for s in spans])
+    def spread(k, numer, parts, values):
+        return jnp.where(lane == k, total(sum(parts[s] * values[s] for s in spans)), numer)
+
+    extra = [sky_mask[s] * right(5, s) for s in spans]
+    parts = [shares[rows - 1, s] + extra[s] for s in spans]
+    numer = spread(rows - 1, numer, parts, [after[s][0] for s in spans])
+    weights = denom[...] + jnp.where(lane == rows - 1, total(sum(extra)), 0.0)
 
     def backward(step_row, carry):
         k = rows - 1 - step_row
-        numer, denom, after = carry
+        numer, after = carry
         results = []
         for s in spans:
             x1, x2, g1, f2, f1 = after[s]
             value = half[k, s] - g1 * x1 - f2 * x2
             flux[k - 1, s] = value
             results.append((value, x1, lower[k, s], f1, lower_far[k, s]))
-        precs = [diag[k, s] for s in spans]
-        numer, denom = spread(k - 1, numer, denom, precs, [r[0] for r in results])
-        return (numer, denom, tuple(results))
-
-    numer, denom, after = lax.fori_loop(0, rows - 2, backward, (numer, denom, tuple(after)), unroll=4)
+        parts = [shares[k - 1, s] for s in spans]
+        return (spread(k - 1, numer, parts, [r[0] for r in results]), tuple(results))
+
+    numer, after = lax.fori_loop(0, rows - 2, backward, (numer, tuple(after)), unroll=4)
     values = []
     for s in spans:
         x1, x2, g1, f2, f1 = after[s]
         value = half[1, s] - g1 * x1 - f2 * x2
         flux[0, s] = value
         values.append(value)
-    precs = [diag[1, s] + left(5, s) for s in spans]
-    numer, denom = spread(0, numer, denom, precs, values)
-    sums[0] = numer
-    sums[1] = denom
+    extra = [sky_mask[s] * left(5, s) for s in spans]
+    parts = [shares[0, s] + extra[s] for s in spans]
+    sums[0] = spread(0, numer, parts, values)
+    sums[1] = weights + jnp.where(lane == 0, total(sum(extra)), 0.0)
 
 
 def solve_call(wave, near, far, bands):
@@ -324,7 +342,7 @@
     return pl.pallas_call(
         functools.partial(solve_kernel, wave),
         out_shape=(in_vmem((rows, specs, exposures, fibres)), in_vmem((2, exposures, LANES))),
-        in_specs=[VM] * 7,
+        in_specs=[VM] * 9,
         out_specs=(VM, VM),
         scratch_shapes=[scratch] * 3,
         compiler_params=pltpu.CompilerParams(vmem_limit_bytes=24 * 2**20),
@@ -334,47 +352,58 @@
 
 
 def position_of(index, total_rows):
-    return 2.0 * index.astype(F32) / (total_rows - 1) - 1.0
+    return 2.0 * jnp.asarray(index).astype(F32) / (total_rows - 1) - 1.0
 
 
 def regress_kernel(total_rows, flux, other, sums, regress, sky_out, sky_copy):
     rows, specs, exposures, fibres = flux.shape
+    lanes = regress.shape[2]
     device = lax.axis_index("wave")
     partner = device + 1 - 2 * lax.rem(device, 2)
     lane = lax.broadcasted_iota(jnp.int32, (exposures, LANES), 1)
     valid = lane < rows
-    first = [[jnp.zeros((exposures, fibres), F32) for _ in range(specs)] for _ in range(2)]
-    moments = [jnp.zeros((exposures, 1), F32) for _ in range(3)]
-    for which, (ref, base) in enumerate(((flux, device * rows), (other, partner * rows))):
+    step = 2.0 / (total_rows - 1)
+    plain = [0.0] * specs
+    tilted = [0.0] * specs
+    moments = [0.0] * 3
+    for which, (ref, owner) in enumerate(((flux, device), (other, partner))):
         sky = jnp.where(valid, sums[2 * which] / jnp.where(valid, sums[2 * which + 1], 1.0), 0.0)
-        position = position_of(base + lane, total_rows)
-        tilted = sky * position
+        position = position_of(owner * rows + lane, total_rows)
+        slanted = sky * position
         moments[0] += jnp.sum(sky * sky, axis=1, keepdims=True)
-        moments[1] += jnp.sum(sky * tilted, axis=1, keepdims=True)
-        moments[2] += jnp.sum(tilted * tilted, axis=1, keepdims=True)
+        moments[1] += jnp.sum(sky * slanted, axis=1, keepdims=True)
+        moments[2] += jnp.sum(slanted * slanted, axis=1, keepdims=True)
         if which == 0:
             sky_out[...] = sky
             sky_copy[...] = sky
+        end = position_of(owner * rows + rows, total_rows)
+        running = [None] * specs
+        summed = [None] * specs
         for k in range(rows):
-            plain_k = jnp.broadcast_to(sky[:, k : k + 1], (exposures, fibres))
-            tilted_k = jnp.broadcast_to(tilted[:, k : k + 1], (exposures, fibres))
+            sky_k = jnp.broadcast_to(sky[:, k : k + 1], (exposures, fibres))
             for s in range(specs):
-                values = ref[k, s]
-                first[0][s] += values * plain_k
-                first[1][s] += values * tilted_k
-    for r in range(2):
+                term = ref[k, s] * sky_k
+                running[s] = term if k == 0 else running[s] + term
+                summed[s] = running[s] if k == 0 else summed[s] + running[s]
         for s in range(specs):
-            regress[r * specs + s] = first[r][s]
-    wide = lax.broadcasted_iota(jnp.int32, (exposures, fibres), 1)
-    regress[2 * specs] = jnp.where(wide == 0, moments[0], jnp.where(wide == 1, moments[1], moments[2]))
+            plain[s] += running[s]
+            tilted[s] += end * running[s] - step * summed[s]
+    wide = lax.broadcasted_iota(jnp.int32, (exposures, lanes - fibres), 1)
+    held = jnp.where(wide == 0, moments[0], jnp.where(wide == 1, moments[1], moments[2]))
+    for s in range(specs):
+        regress[s, :, :fibres] = plain[s]
+        regress[specs + s, :, :fibres] = tilted[s]
+        for r in (s, specs + s):
+            regress[r, :, fibres:] = held
 
 
 def regress_call(total_rows, flux, other, sums):
     rows, specs, exposures, fibres = flux.shape
+    lanes = -(-(fibres + 3) // LANES) * LANES
     return pl.pallas_call(
         functools.partial(regress_kernel, total_rows),
         out_shape=(
-            in_vmem((2 * specs + 1, exposures, fibres)),
+            in_vmem((2 * specs, exposures, lanes)),
             in_vmem((exposures, LANES)),
             in_vmem((exposures, LANES)),
         ),
@@ -386,36 +415,37 @@
     )(flux, other, sums)
 
 
-def clean_kernel(total_rows, flux, sky_ref, mine, sent, out, buf, sems):
+def clean_kernel(total_rows, flux, sky_ref, *refs):
+    *terms, out, buf, sems = refs
     rows, specs, exposures, fibres = flux.shape
     device = lax.axis_index("wave")
-    is_odd = lax.rem(device, 2) == 1
 
     def got(slot):
-        return jnp.where(is_odd, mine[slot], sent[slot])
-
-    moments = got(2 * specs)
-    upper_left = moments[:, 0:1] + RIDGE
-    cross = moments[:, 1:2]
-    lower_right = moments[:, 2:3] + RIDGE
+        return sum(term[slot] for term in terms)
+
+    sums = [got(slot) for slot in range(2 * specs)]
+    moments = [sums[0][:, fibres + m : fibres + m + 1] for m in range(3)]
+    upper_left, cross, lower_right = moments[0] + RIDGE, moments[1], moments[2] + RIDGE
     inverse = 1.0 / (upper_left * lower_right - cross * cross)
-    slope_a, slope_b = [], []
+    start = position_of(device * rows, total_rows)
+    step = 2.0 / (total_rows - 1)
+    level, change = [], []
     for s in range(specs):
-        r1, r2 = got(s), got(specs + s)
-        slope_a.append((lower_right * r1 - cross * r2) * inverse)
-        slope_b.append((upper_left * r2 - cross * r1) * inverse)
-    lane = lax.broadcasted_iota(jnp.int32, (exposures, LANES), 1)
+        r1, r2 = sums[s][:, :fibres], sums[specs + s][:, :fibres]
+        slope_a = (lower_right * r1 - cross * r2) * inverse
+        slope_b = (upper_left * r2 - cross * r1) * inverse
+        level.append(slope_a + slope_b * start)
+        change.append(slope_b * step)
     sky = sky_ref[...]
-    tilted = sky * position_of(device * rows + lane, total_rows)
     chunks = sems.shape[0]
     bounds = [rows * c // chunks for c in range(chunks + 1)]
     for c in range(chunks):
         low, high = bounds[c], bounds[c + 1]
         for k in range(low, high):
-            plain_k = jnp.broadcast_to(sky[:, k : k + 1], (exposures, fibres))
-            tilted_k = jnp.broadcast_to(tilted[:, k : k + 1], (exposures, fibres))
+            sky_k = jnp.broadcast_to(sky[:, k : k + 1], (exposures, fibres))
             for s in range(specs):
-                buf[k, s] = flux[k, s] - (slope_a[s] * plain_k + slope_b[s] * tilted_k)
+                buf[k, s] = flux[k, s] - level[s] * sky_k
+                level[s] = level[s] + change[s]
         for e in range(exposures):
             pltpu.make_async_copy(
                 buf.at[low:high, :, e], out.at[e, low:high], sems.at[c]
@@ -425,21 +455,21 @@
         pltpu.make_async_copy(part, part, sems.at[c]).wait()
 
 
-def clean_call(total_rows, flux, sky, mine, sent):
+def clean_call(total_rows, flux, sky, terms):
     rows, specs, exposures, fibres = flux.shape
     return pl.pallas_call(
         functools.partial(clean_kernel, total_rows),
         out_shape=jax.ShapeDtypeStruct((exposures, rows, specs, fibres), F32),
-        in_specs=[VM] * 4,
+        in_specs=[VM] * (2 + len(terms)),
         out_specs=HB,
         scratch_shapes=[
             pltpu.VMEM((rows, specs, exposures, fibres), F32),
-            pltpu.SemaphoreType.DMA((4,)),
+            pltpu.SemaphoreType.DMA((5,)),
         ],
         compiler_params=pltpu.CompilerParams(vmem_limit_bytes=24 * 2**20),
         cost_estimate=pl.CostEstimate(flops=10**6, bytes_accessed=10**6, transcendentals=0),
         name="clean",
-    )(flux, sky, mine, sent)
+    )(flux, sky, *terms)
 
 
 def powers(low, high):
@@ -469,22 +499,40 @@
     wave, spec = lax.axis_size("wave"), lax.axis_size("spec")
     total_rows = rows * wave
     hbm = [pltpu.with_memory_space_constraint(x, pltpu.HBM) for x in arrays]
+    odd = lax.rem(lax.axis_index("wave"), 2) == 1
+
+    def other_core(s, i):
+        return (s, i ^ 1)
+
     near, far = edge_call(hbm)
     far = swap(far, lambda s, i: (s, i + 1 if i % 2 else i - 1))
-    near = swap(near, lambda s, i: (s, i ^ 1))
-    bands = prepare_call(hbm, sky_index)
+    near = swap(near, other_core)
+    bands = prepare_call(arrays[:PREFETCH] + hbm[PREFETCH:], sky_index)
     flux, sums = solve_call(wave, near, far, bands)
-    got = swap(sums, lambda s, i: (s, i ^ 1))
+    got = swap(sums, other_core)
     flux, got = lax.optimization_barrier((flux, got))
-    other = swap(flux, lambda s, i: (s, i ^ 1))
+    other = swap(flux, other_core)
     sums = jnp.concatenate([sums, got])
-    for k in powers(1, spec):
-        sums = sums + swap(sums, lambda s, i: (s ^ k, i))
+    if spec == 4:
+        first = swap(sums, lambda s, i: (s ^ (1 if i % 2 else 2), i))
+        third = swap(sums, lambda s, i: (s ^ 3, i))
+        second = swap(first, other_core)
+        second = jnp.concatenate([second[2:], second[:2]])
+        sums = (sums + jnp.where(odd, first, second)) + (jnp.where(odd, second, first) + third)
+    else:
+        for k in powers(1, spec):
+            sums = sums + swap(sums, lambda s, i: (s ^ k, i))
     regress, sky, sky_out = regress_call(total_rows, flux, other, sums)
-    for k in powers(2, wave):
-        regress = regress + swap(regress, lambda s, i: (s, i ^ k if i % 2 else -1))
-    sent = swap(regress, lambda s, i: (s, i ^ 1))
-    cleaned = clean_call(total_rows, flux, sky, regress, sent)
+    if wave == 8:
+        first = swap(regress, lambda s, i: (s, i ^ (4 if i % 2 else 2)))
+        third = swap(regress, lambda s, i: (s, i ^ 6 if i % 2 else -1))
+        fetched = first + jnp.where(odd, third, 0.0)
+        terms = [regress, fetched, swap(fetched, other_core)]
+    else:
+        for k in powers(2, wave):
+            regress = regress + swap(regress, lambda s, i: (s, i ^ k if i % 2 else -1))
+        terms = [jnp.where(odd, regress, swap(regress, other_core))]
+    cleaned = clean_call(total_rows, flux, sky, terms)
     return (jnp.transpose(cleaned, (0, 2, 1, 3)), sky_out[:, :rows])
 
 

time: 34.1 us -> 34.2 us (level)
  waiting for transfers between devices: 12.6 us -> 9.06 us
  starting transfers between devices: 9.63 us -> 11.6 us
  Pallas kernels: 10.9 us -> 12.6 us
    ppermute x9 -> x10, waiting for transfers between devices: 12.6 us -> 9.06 us  [swap(): return lax.ppermute(values, ('spec', 'wave'), pairs)]
    ppermute x9 -> x10, starting transfers between devices: 9.63 us -> 11.6 us  [swap(): return lax.ppermute(values, ('spec', 'wave'), pairs)]
    pallas_call x1, Pallas kernels: 4.25 us -> 6.06 us  [prepare_call(): pl.pallas_call(functools.partial(prepare_kernel, chunks), out_shape=(grow...]
  transfers between devices with their start and end apart: 9 -> 10, of which waited for: 6 -> 6; matrix products, arithmetic and copies ran while one was open for 0% -> 0% of each run, Pallas kernels for 13% -> 18%
where the time goes in v4:
time: 34.2 us; the launch traced here: 34 us
  Pallas kernels  12.6 us (37%)
  starting transfers between devices  11.6 us (34%)
  waiting for transfers between devices  9.06 us (26%)
  between operations  0.72 us (2%)
    ppermute x10, starting transfers between devices, swap(): return lax.ppermute(values, ('spec', 'wave'), pairs)  11.6 us
    ppermute x10, waiting for transfers between devices, swap(): return lax.ppermute(values, ('spec', 'wave'), pairs)  9.06 us
    pallas_call x1, Pallas kernels, prepare_call(): pl.pallas_call(functools.partial(prepare_kernel, chunks), out_shape=(grow...  6.06 us
    pallas_call x1, Pallas kernels, solve_call(): pl.pallas_call(functools.partial(solve_kernel, wave), out_shape=(in_vmem(...  2.58 us
    pallas_call x1, Pallas kernels, edge_call(): pl.pallas_call(edge_kernel, out_shape=(message, message), in_specs=[HB] *...  1.69 us
    pallas_call x1, Pallas kernels, clean_call(): pl.pallas_call(functools.partial(clean_kernel, total_rows), out_shape=jax...  1.36 us
    pallas_call x1, Pallas kernels, regress_call(): pl.pallas_call(functools.partial(regress_kernel, total_rows), out_shape=(...  0.9 us
  transfers between devices with their start and end apart: 10, of which 6 were waited for; matrix products, arithmetic and copies ran while one was open for 0% of the time, Pallas kernels for 18%

profile of v4, /device:TPU:0, one launch (start us, length us, event | category | flops | bytes accessed | tf_op | source)
XLA Modules:
  0.0 34.0 jit_solution(14353891217108516553)
XLA Ops:
  0.7 1.7 %edges.1 = (f32[6,2,8,500]{3,2,1,0:T(8,128)S(1)}, f32[6,2,8,500]{3,2,1,0:T(8,128)S(1)}) custom-call(f32[8,50,2,500]{3,2,1,0:T(2,128)} %bitcast.7, f32[8,50,2,500]{3,2,1,0:T(2,128)} %bitcast.9, s32[8,50,2,500]{3,2,1,0:T(2,128)} %bitcast.11, f32[8,50,2,500]{3,2,1,0:T(2,128)} %bitcast.13, f32[8,50,2,500]{3,2,1,0:T(2,128)} %bitcast.15), custom_call_target="tpu_custom_call" | custom-call | flops 1000000 | bytes 1000000 | tf_op jit(solution)/shard_map/edges/pallas_call | solution.py:105
  2.4 0.5 %collective-permute-start = (f32[6,2,8,500]{3,2,1,0:T(8,128)S(1)}, f32[6,2,8,500]{3,2,1,0:T(8,128)S(1)}, u32[]{:S(2)}, u32[]{:S(2)}) collective-permute-start(f32[6,2,8,500]{3,2,1,0:T(8,128)S(1)} %get-tuple-element.18), channel_id=1, source_target_pairs={{0,1},{1,0},{2,3},{3,2},{4,5},{5,4},{6,7},{7,6},{8,9},{9,8},{10,11... | collective-permute-start | bytes 576008 | tf_op jit(solution)/shard_map/ppermute | solution.py:493
  2.9 2.6 %collective-permute-start.1 = (f32[6,2,8,500]{3,2,1,0:T(8,128)S(1)}, f32[6,2,8,500]{3,2,1,0:T(8,128)S(1)}, u32[]{:S(2)}, u32[]{:S(2)}) collective-permute-start(f32[6,2,8,500]{3,2,1,0:T(8,128)S(1)} %get-tuple-element.19), channel_id=1, source_target_pairs={{0,8},{1,2},{2,1},{3,4},{4,3},{5,6},{6,5},{7,15},{8,0},{9,10},{10,... | collective-permute-start | bytes 576008 | tf_op jit(solution)/shard_map/ppermute | solution.py:493
  5.5 6.1 %prepare.1 = (f32[52,2,8,500]{3,2,1,0:T(8,128)S(1)}, f32[52,2,8,500]{3,2,1,0:T(8,128)S(1)}, f32[52,2,8,500]{3,2,1,0:T(8,128)S(1)}, f32[52,2,8,500]{3,2,1,0:T(8,1...) custom-call(f32[8,50,2,500]{3,2,1,0:T(2,128)S(1)} %bitcast.8, ...), custom_call_target="tpu_custom_call" | custom-call | flops 10000000 | bytes 10000000 | tf_op jit(solution)/shard_map/prepare/pallas_call | solution.py:189
  11.5 0.0 collective-permute-done.near
  11.5 0.0 collective-permute-done.1.far
  11.6 2.6 %solve.1 = (f32[50,2,8,500]{3,2,1,0:T(8,128)S(1)}, f32[2,8,128]{2,1,0:T(8,128)S(1)}) custom-call(f32[6,2,8,500]{3,2,1,0:T(8,128)S(1)} %collective-permute-done.near, f32[6,2,8,500]{3,2,1,0:T(8,128)S(1)} %collective-permute-done.1.far, f32[52,2,8,500]{3,2,1,0:T(8,128)S(1)} %get-tuple-element.20.diag, f32[52,2,8,500]{3,2,1,0:T(8,128)S(1)} %get-tuple-element.21.off_one, ...), custom_call_target="tpu_custom_call" | custom-call | flops 10000000 | bytes 10000000 | tf_op jit(solution)/shard_map/solve/pallas_call | solution.py:342
  14.1 0.2 collective-permute-start.2
  14.3 1.0 %collective-permute-done.2 = f32[2,8,128]{2,1,0:T(8,128)S(1)} collective-permute-done((f32[2,8,128]{2,1,0:T(8,128)S(1)}, f32[2,8,128]{2,1,0:T(8,128)S(1)}, u32[]{:S(2)}, u32[]{:S(2)}) %collective-permute-start.2) | collective-permute-done | bytes 8224 | tf_op jit(solution)/shard_map/ppermute | solution.py:493
  15.3 0.2 collective-permute-start.3
  15.5 1.5 %collective-permute-start.4 = (f32[4,8,128]{2,1,0:T(8,128)S(1)}, f32[4,8,128]{2,1,0:T(8,128)S(1)}, u32[]{:S(2)}, u32[]{:S(2)}) collective-permute-start(f32[4,8,128]{2,1,0:T(8,128)S(1)} %constant_dynamic-update-slice_fusion), channel_id=1, source_target_pairs={{0,16},{1,9},{2,18},{3,11},{4,20},{5,13},{6,22},{7,15},{8,24},{9,1... | collective-permute-start | bytes 49160 | tf_op jit(solution)/shard_map/ppermute | solution.py:493
  17.0 2.2 %collective-permute-done.4 = f32[4,8,128]{2,1,0:T(8,128)S(1)} collective-permute-done((f32[4,8,128]{2,1,0:T(8,128)S(1)}, f32[4,8,128]{2,1,0:T(8,128)S(1)}, u32[]{:S(2)}, u32[]{:S(2)}) %collective-permute-start.4) | collective-permute-done | bytes 16416 | tf_op jit(solution)/shard_map/ppermute | solution.py:493
  19.3 2.4 %collective-permute-start.6 = (f32[4,8,128]{2,1,0:T(8,128)S(1)}, f32[4,8,128]{2,1,0:T(8,128)S(1)}, u32[]{:S(2)}, u32[]{:S(2)}) collective-permute-start(f32[4,8,128]{2,1,0:T(8,128)S(1)} %constant_dynamic-update-slice_fusion), channel_id=1, source_target_pairs={{0,24},{1,25},{2,26},{3,27},{4,28},{5,29},{6,30},{7,31},{8,16},{9,... | collective-permute-start | bytes 49160 | tf_op jit(solution)/shard_map/ppermute | solution.py:493
  21.7 0.0 collective-permute-done.5
  21.7 2.2 %collective-permute-done.6 = f32[4,8,128]{2,1,0:T(8,128)S(1)} collective-permute-done((f32[4,8,128]{2,1,0:T(8,128)S(1)}, f32[4,8,128]{2,1,0:T(8,128)S(1)}, u32[]{:S(2)}, u32[]{:S(2)}) %collective-permute-start.6) | collective-permute-done | bytes 16416 | tf_op jit(solution)/shard_map/ppermute | solution.py:493
  23.9 0.0 collective-permute-done.3.other
  23.9 0.9 %regress.1 = (f32[4,8,512]{2,1,0:T(8,128)S(1)}, f32[8,128]{1,0:T(8,128)S(1)}, f32[8,128]{1,0:T(8,128)}) custom-call(f32[50,2,8,500]{3,2,1,0:T(8,128)S(1)} %get-tuple-element.29.flux, f32[50,2,8,500]{3,2,1,0:T(8,128)S(1)} %collective-permute-done.3.other, f32[4,8,128]{2,1,0:T(8,128)S(1)} %add_add_fusion.sums), custom_call_target="tpu_custom_call" | custom-call | flops 1000000 | bytes 1000000 | tf_op jit(solution)/shard_map/regress/pallas_call | solution.py:403
  24.8 1.6 %collective-permute-start.7 = (f32[4,8,512]{2,1,0:T(8,128)S(1)}, f32[4,8,512]{2,1,0:T(8,128)S(1)}, u32[]{:S(2)}, u32[]{:S(2)}) collective-permute-start(f32[4,8,512]{2,1,0:T(8,128)S(1)} %get-tuple-element.32.refs_0_), channel_id=1, source_target_pairs={{0,2},{1,5},{2,0},{3,7},{4,6},{5,1},{6,4},{7,3},{8,10},{9,13},{10,... | collective-permute-start | bytes 196616 | tf_op jit(solution)/shard_map/ppermute | solution.py:493
  26.4 1.5 %collective-permute-start.8 = (f32[4,8,512]{2,1,0:T(8,128)S(1)}, f32[4,8,512]{2,1,0:T(8,128)S(1)}, u32[]{:S(2)}, u32[]{:S(2)}) collective-permute-start(f32[4,8,512]{2,1,0:T(8,128)S(1)} %get-tuple-element.32.refs_0_), channel_id=1, source_target_pairs={{0,8},{1,7},{2,10},{3,5},{4,12},{5,3},{6,14},{7,1},{8,0},{9,15},{1... | collective-permute-start | bytes 196616 | tf_op jit(solution)/shard_map/ppermute | solution.py:493
  27.9 1.2 %collective-permute-done.7 = f32[4,8,512]{2,1,0:T(8,128)S(1)} collective-permute-done((f32[4,8,512]{2,1,0:T(8,128)S(1)}, f32[4,8,512]{2,1,0:T(8,128)S(1)}, u32[]{:S(2)}, u32[]{:S(2)}) %collective-permute-start.7) | collective-permute-done | bytes 65568 | tf_op jit(solution)/shard_map/ppermute | solution.py:493
  29.1 1.6 %collective-permute-done.8 = f32[4,8,512]{2,1,0:T(8,128)S(1)} collective-permute-done((f32[4,8,512]{2,1,0:T(8,128)S(1)}, f32[4,8,512]{2,1,0:T(8,128)S(1)}, u32[]{:S(2)}, u32[]{:S(2)}) %collective-permute-start.8) | collective-permute-done | bytes 65568 | tf_op jit(solution)/shard_map/ppermute | solution.py:493
  30.7 1.0 %collective-permute-start.9 = (f32[4,8,512]{2,1,0:T(8,128)S(1)}, f32[4,8,512]{2,1,0:T(8,128)S(1)}, u32[]{:S(2)}, u32[]{:S(2)}) collective-permute-start(f32[4,8,512]{2,1,0:T(8,128)S(1)} %select_add_fusion.refs_1_), channel_id=1, source_target_pairs={{0,1},{1,0},{2,3},{3,2},{4,5},{5,4},{6,7},{7,6},{8,9},{9,8},{10,11... | collective-permute-start | bytes 196616 | tf_op jit(solution)/shard_map/ppermute | solution.py:493
  31.7 0.9 %collective-permute-done.9.refs_2_ = f32[4,8,512]{2,1,0:T(8,128)S(1)} collective-permute-done((f32[4,8,512]{2,1,0:T(8,128)S(1)}, f32[4,8,512]{2,1,0:T(8,128)S(1)}, u32[]{:S(2)}, u32[]{:S(2)}) %collective-permute-start.9) | collective-permute-done | bytes 65568 | tf_op jit(solution)/shard_map/ppermute | solution.py:493
  32.6 1.4 %clean.1 = f32[8,50,2,500]{3,2,1,0:T(2,128)} custom-call(f32[50,2,8,500]{3,2,1,0:T(8,128)S(1)} %get-tuple-element.29.flux, f32[8,128]{1,0:T(8,128)S(1)} %get-tuple-element.31.sky_ref, f32[4,8,512]{2,1,0:T(8,128)S(1)} %get-tuple-element.32.refs_0_, f32[4,8,512]{2,1,0:T(8,128)S(1)} %select_add_fusion.refs_1_, f32[4,8,512]{2,1,0:T(8,128)S(1)} %collective-permute-done.9.refs_2_), custom_call_target="tpu_custom_call" | custom-call | flops 1000000 | bytes 1000000 | tf_op jit(solution)/shard_map/clean/pallas_call | solution.py:460
  (14 shorter events, 0.0 us)
Async XLA Ops:
  0.6 4.8 %copy-start = (f32[8,2,50,500]{3,1,2,0:T(2,128)S(1)}, f32[8,2,50,500]{3,1,2,0:T(2,128)}, u32[]{:S(2)}) copy-start(f32[8,2,50,500]{3,1,2,0:T(2,128)} %param.6) | copy-start | bytes 4800004
  0.6 4.8 %copy-start.1 = (f32[8,2,50,500]{3,1,2,0:T(2,128)S(1)}, f32[8,2,50,500]{3,1,2,0:T(2,128)}, u32[]{:S(2)}) copy-start(f32[8,2,50,500]{3,1,2,0:T(2,128)} %param.7) | copy-start | bytes 4800004
  0.7 4.8 %copy-start.2 = (s32[8,2,50,500]{3,1,2,0:T(2,128)S(1)}, s32[8,2,50,500]{3,1,2,0:T(2,128)}, u32[]{:S(2)}) copy-start(s32[8,2,50,500]{3,1,2,0:T(2,128)} %param.8) | copy-start | bytes 4800004
  0.7 4.8 %copy-start.3 = (s32[2,40]{1,0:T(2,128)S(1)}, s32[2,40]{1,0:T(2,128)}, u32[]{:S(2)}) copy-start(s32[2,40]{1,0:T(2,128)} %sky_index.1) | copy-start | bytes 964
  2.4 9.2 %collective-permute-start = (f32[6,2,8,500]{3,2,1,0:T(8,128)S(1)}, f32[6,2,8,500]{3,2,1,0:T(8,128)S(1)}, u32[]{:S(2)}, u32[]{:S(2)}) collective-permute-start(f32[6,2,8,500]{3,2,1,0:T(8,128)S(1)} %get-tuple-element.18), channel_id=1, source_target_pairs={{0,1},{1,0},{2,3},{3,2},{4,5},{5,4},{6,7},{7,6},{8,9},{9,8},{10,11... | collective-permute-start | bytes 576008 | tf_op jit(solution)/shard_map/ppermute | solution.py:493
  2.9 8.7 %collective-permute-start.1 = (f32[6,2,8,500]{3,2,1,0:T(8,128)S(1)}, f32[6,2,8,500]{3,2,1,0:T(8,128)S(1)}, u32[]{:S(2)}, u32[]{:S(2)}) collective-permute-start(f32[6,2,8,500]{3,2,1,0:T(8,128)S(1)} %get-tuple-element.19), channel_id=1, source_target_pairs={{0,8},{1,2},{2,1},{3,4},{4,3},{5,6},{6,5},{7,15},{8,0},{9,10},{10,... | collective-permute-start | bytes 576008 | tf_op jit(solution)/shard_map/ppermute | solution.py:493
  14.1 1.2 %collective-permute-start.2 = (f32[2,8,128]{2,1,0:T(8,128)S(1)}, f32[2,8,128]{2,1,0:T(8,128)S(1)}, u32[]{:S(2)}, u32[]{:S(2)}) collective-permute-start(f32[2,8,128]{2,1,0:T(8,128)S(1)} %get-tuple-element.28), channel_id=1, source_target_pairs={{0,1},{1,0},{2,3},{3,2},{4,5},{5,4},{6,7},{7,6},{8,9},{9,8},{10,11... | collective-permute-start | bytes 24584 | tf_op jit(solution)/shard_map/ppermute | solution.py:493
  15.3 8.6 %collective-permute-start.3 = (f32[50,2,8,500]{3,2,1,0:T(8,128)S(1)}, f32[50,2,8,500]{3,2,1,0:T(8,128)S(1)}, u32[]{:S(2)}, u32[]{:S(2)}) collective-permute-start(f32[50,2,8,500]{3,2,1,0:T(8,128)S(1)} %get-tuple-element.29.flux), channel_id=1, source_target_pairs={{0,1},{1,0},{2,3},{3,2},{4,5},{5,4},{6,7},{7,6},{8,9},{9,8},{10,11... | collective-permute-start | bytes 4800008 | tf_op jit(solution)/shard_map/ppermute | solution.py:493
  15.5 3.7 %collective-permute-start.4 = (f32[4,8,128]{2,1,0:T(8,128)S(1)}, f32[4,8,128]{2,1,0:T(8,128)S(1)}, u32[]{:S(2)}, u32[]{:S(2)}) collective-permute-start(f32[4,8,128]{2,1,0:T(8,128)S(1)} %constant_dynamic-update-slice_fusion), channel_id=1, source_target_pairs={{0,16},{1,9},{2,18},{3,11},{4,20},{5,13},{6,22},{7,15},{8,24},{9,1... | collective-permute-start | bytes 49160 | tf_op jit(solution)/shard_map/ppermute | solution.py:493
  19.3 2.5 %collective-permute-start.5 = (f32[4,8,128]{2,1,0:T(8,128)S(1)}, f32[4,8,128]{2,1,0:T(8,128)S(1)}, u32[]{:S(2)}, u32[]{:S(2)}) collective-permute-start(f32[4,8,128]{2,1,0:T(8,128)S(1)} %collective-permute-done.4), channel_id=1, source_target_pairs={{0,1},{1,0},{2,3},{3,2},{4,5},{5,4},{6,7},{7,6},{8,9},{9,8},{10,11... | collective-permute-start | bytes 49160 | tf_op jit(solution)/shard_map/ppermute | solution.py:493
  19.3 4.6 %collective-permute-start.6 = (f32[4,8,128]{2,1,0:T(8,128)S(1)}, f32[4,8,128]{2,1,0:T(8,128)S(1)}, u32[]{:S(2)}, u32[]{:S(2)}) collective-permute-start(f32[4,8,128]{2,1,0:T(8,128)S(1)} %constant_dynamic-update-slice_fusion), channel_id=1, source_target_pairs={{0,24},{1,25},{2,26},{3,27},{4,28},{5,29},{6,30},{7,31},{8,16},{9,... | collective-permute-start | bytes 49160 | tf_op jit(solution)/shard_map/ppermute | solution.py:493
  24.8 4.3 %collective-permute-start.7 = (f32[4,8,512]{2,1,0:T(8,128)S(1)}, f32[4,8,512]{2,1,0:T(8,128)S(1)}, u32[]{:S(2)}, u32[]{:S(2)}) collective-permute-start(f32[4,8,512]{2,1,0:T(8,128)S(1)} %get-tuple-element.32.refs_0_), channel_id=1, source_target_pairs={{0,2},{1,5},{2,0},{3,7},{4,6},{5,1},{6,4},{7,3},{8,10},{9,13},{10,... | collective-permute-start | bytes 196616 | tf_op jit(solution)/shard_map/ppermute | solution.py:493
  26.4 4.3 %collective-permute-start.8 = (f32[4,8,512]{2,1,0:T(8,128)S(1)}, f32[4,8,512]{2,1,0:T(8,128)S(1)}, u32[]{:S(2)}, u32[]{:S(2)}) collective-permute-start(f32[4,8,512]{2,1,0:T(8,128)S(1)} %get-tuple-element.32.refs_0_), channel_id=1, source_target_pairs={{0,8},{1,7},{2,10},{3,5},{4,12},{5,3},{6,14},{7,1},{8,0},{9,15},{1... | collective-permute-start | bytes 196616 | tf_op jit(solution)/shard_map/ppermute | solution.py:493
  30.7 1.9 %collective-permute-start.9 = (f32[4,8,512]{2,1,0:T(8,128)S(1)}, f32[4,8,512]{2,1,0:T(8,128)S(1)}, u32[]{:S(2)}, u32[]{:S(2)}) collective-permute-start(f32[4,8,512]{2,1,0:T(8,128)S(1)} %select_add_fusion.refs_1_), channel_id=1, source_target_pairs={{0,1},{1,0},{2,3},{3,2},{4,5},{5,4},{6,7},{7,6},{8,9},{9,8},{10,11... | collective-permute-start | bytes 196616 | tf_op jit(solution)/shard_map/ppermute | solution.py:493

commit v5 on v4

--- a/solution.py
+++ b/solution.py
@@ -11,7 +11,6 @@
 RIDGE = 1.0
 HALO = 4
 PARTS = 6
-PREFETCH = 3
 LANES = 128
 
 F32 = jnp.float32
@@ -197,7 +196,7 @@
             in_vmem((specs, exposures, fibres)),
             in_vmem((exposures, LANES)),
         ),
-        in_specs=[pl.BlockSpec(memory_space=pl.ANY)] * 5 + [SM],
+        in_specs=[HB] * 5 + [SM],
         out_specs=(VM,) * 7,
         scratch_shapes=[
             pltpu.VMEM((4, rows, specs, exposures, fibres), F32),
@@ -359,15 +358,16 @@
     rows, specs, exposures, fibres = flux.shape
     lanes = regress.shape[2]
     device = lax.axis_index("wave")
-    partner = device + 1 - 2 * lax.rem(device, 2)
+    odd = lax.rem(device, 2)
     lane = lax.broadcasted_iota(jnp.int32, (exposures, LANES), 1)
     valid = lane < rows
     step = 2.0 / (total_rows - 1)
     plain = [0.0] * specs
     tilted = [0.0] * specs
     moments = [0.0] * 3
-    for which, (ref, owner) in enumerate(((flux, device), (other, partner))):
-        sky = jnp.where(valid, sums[2 * which] / jnp.where(valid, sums[2 * which + 1], 1.0), 0.0)
+    for which, (ref, core) in enumerate(((flux, odd), (other, 1 - odd))):
+        owner = device - odd + core
+        sky = jnp.where(valid, sums[2 * core] / jnp.where(valid, sums[2 * core + 1], 1.0), 0.0)
         position = position_of(owner * rows + lane, total_rows)
         slanted = sky * position
         moments[0] += jnp.sum(sky * sky, axis=1, keepdims=True)
@@ -507,17 +507,16 @@
     near, far = edge_call(hbm)
     far = swap(far, lambda s, i: (s, i + 1 if i % 2 else i - 1))
     near = swap(near, other_core)
-    bands = prepare_call(arrays[:PREFETCH] + hbm[PREFETCH:], sky_index)
+    bands = prepare_call(hbm, sky_index)
     flux, sums = solve_call(wave, near, far, bands)
     got = swap(sums, other_core)
     flux, got = lax.optimization_barrier((flux, got))
     other = swap(flux, other_core)
-    sums = jnp.concatenate([sums, got])
+    sums = jnp.where(odd, jnp.concatenate([got, sums]), jnp.concatenate([sums, got]))
     if spec == 4:
         first = swap(sums, lambda s, i: (s ^ (1 if i % 2 else 2), i))
         third = swap(sums, lambda s, i: (s ^ 3, i))
         second = swap(first, other_core)
-        second = jnp.concatenate([second[2:], second[:2]])
         sums = (sums + jnp.where(odd, first, second)) + (jnp.where(odd, second, first) + third)
     else:
         for k in powers(1, spec):

time: 34.2 us -> 30 us (0.88)
  Pallas kernels: 12.6 us -> 10.7 us
  waiting for transfers between devices: 9.06 us -> 7.85 us
  starting transfers between devices: 11.6 us -> 10.5 us
    pallas_call x1, Pallas kernels: 6.06 us -> 4.35 us  [prepare_call(): pl.pallas_call(functools.partial(prepare_kernel, chunks), out_shape=(grow...]
    ppermute x10, waiting for transfers between devices: 9.06 us -> 7.85 us  [swap(): return lax.ppermute(values, ('spec', 'wave'), pairs)]
    ppermute x10, starting transfers between devices: 11.6 us -> 10.5 us  [swap(): return lax.ppermute(values, ('spec', 'wave'), pairs)]
  transfers between devices with their start and end apart: 10 -> 10, of which waited for: 6 -> 6; matrix products, arithmetic and copies ran while one was open for 0% -> 0% of each run, Pallas kernels for 18% -> 15%
where the time goes in v5:
time: 30 us; the launch traced here: 29.8 us
  Pallas kernels  10.7 us (36%)
  starting transfers between devices  10.5 us (35%)
  waiting for transfers between devices  7.85 us (26%)
  between operations  0.69 us (2%)
    ppermute x10, starting transfers between devices, swap(): return lax.ppermute(values, ('spec', 'wave'), pairs)  10.5 us
    ppermute x10, waiting for transfers between devices, swap(): return lax.ppermute(values, ('spec', 'wave'), pairs)  7.85 us
    pallas_call x1, Pallas kernels, prepare_call(): pl.pallas_call(functools.partial(prepare_kernel, chunks), out_shape=(grow...  4.35 us
    pallas_call x1, Pallas kernels, solve_call(): pl.pallas_call(functools.partial(solve_kernel, wave), out_shape=(in_vmem(...  2.57 us
    pallas_call x1, Pallas kernels, edge_call(): pl.pallas_call(edge_kernel, out_shape=(message, message), in_specs=[HB] *...  1.48 us
    pallas_call x1, Pallas kernels, clean_call(): pl.pallas_call(functools.partial(clean_kernel, total_rows), out_shape=jax...  1.36 us
    pallas_call x1, Pallas kernels, regress_call(): pl.pallas_call(functools.partial(regress_kernel, total_rows), out_shape=(...  0.9 us
  transfers between devices with their start and end apart: 10, of which 6 were waited for; matrix products, arithmetic and copies ran while one was open for 0% of the time, Pallas kernels for 15%

profile of v5, /device:TPU:0, one launch (start us, length us, event | category | flops | bytes accessed | tf_op | source)
XLA Modules:
  0.0 29.8 jit_solution(12802900231568792107)
XLA Ops:
  0.6 1.5 %edges.1 = (f32[6,2,8,500]{3,2,1,0:T(8,128)S(1)}, f32[6,2,8,500]{3,2,1,0:T(8,128)S(1)}) custom-call(f32[8,50,2,500]{3,2,1,0:T(2,128)} %bitcast.7, f32[8,50,2,500]{3,2,1,0:T(2,128)} %bitcast.9, s32[8,50,2,500]{3,2,1,0:T(2,128)} %bitcast.11, f32[8,50,2,500]{3,2,1,0:T(2,128)} %bitcast.13, f32[8,50,2,500]{3,2,1,0:T(2,128)} %bitcast.15), custom_call_target="tpu_custom_call" | custom-call | flops 1000000 | bytes 1000000 | tf_op jit(solution)/shard_map/edges/pallas_call | solution.py:104
  2.1 0.5 %collective-permute-start = (f32[6,2,8,500]{3,2,1,0:T(8,128)S(1)}, f32[6,2,8,500]{3,2,1,0:T(8,128)S(1)}, u32[]{:S(2)}, u32[]{:S(2)}) collective-permute-start(f32[6,2,8,500]{3,2,1,0:T(8,128)S(1)} %get-tuple-element.18), channel_id=1, source_target_pairs={{0,1},{1,0},{2,3},{3,2},{4,5},{5,4},{6,7},{7,6},{8,9},{9,8},{10,11... | collective-permute-start | bytes 576008 | tf_op jit(solution)/shard_map/ppermute | solution.py:493
  2.6 2.6 %collective-permute-start.1 = (f32[6,2,8,500]{3,2,1,0:T(8,128)S(1)}, f32[6,2,8,500]{3,2,1,0:T(8,128)S(1)}, u32[]{:S(2)}, u32[]{:S(2)}) collective-permute-start(f32[6,2,8,500]{3,2,1,0:T(8,128)S(1)} %get-tuple-element.19), channel_id=1, source_target_pairs={{0,8},{1,2},{2,1},{3,4},{4,3},{5,6},{6,5},{7,15},{8,0},{9,10},{10,... | collective-permute-start | bytes 576008 | tf_op jit(solution)/shard_map/ppermute | solution.py:493
  5.2 4.3 %prepare.1 = (f32[52,2,8,500]{3,2,1,0:T(8,128)S(1)}, f32[52,2,8,500]{3,2,1,0:T(8,128)S(1)}, f32[52,2,8,500]{3,2,1,0:T(8,128)S(1)}, f32[52,2,8,500]{3,2,1,0:T(8,1...) custom-call(f32[8,50,2,500]{3,2,1,0:T(2,128)} %bitcast.8, ...), custom_call_target="tpu_custom_call" | custom-call | flops 10000000 | bytes 10000000 | tf_op jit(solution)/shard_map/prepare/pallas_call | solution.py:188
  9.6 0.0 collective-permute-done.near
  9.6 2.6 %solve.1 = (f32[50,2,8,500]{3,2,1,0:T(8,128)S(1)}, f32[2,8,128]{2,1,0:T(8,128)S(1)}) custom-call(f32[6,2,8,500]{3,2,1,0:T(8,128)S(1)} %collective-permute-done.near, f32[6,2,8,500]{3,2,1,0:T(8,128)S(1)} %collective-permute-done.1.far, f32[52,2,8,500]{3,2,1,0:T(8,128)S(1)} %get-tuple-element.20.diag, f32[52,2,8,500]{3,2,1,0:T(8,128)S(1)} %get-tuple-element.21.off_one, ...), custom_call_target="tpu_custom_call" | custom-call | flops 10000000 | bytes 10000000 | tf_op jit(solution)/shard_map/solve/pallas_call | solution.py:341
  12.2 0.2 collective-permute-start.2
  12.4 1.0 %collective-permute-done.2 = f32[2,8,128]{2,1,0:T(8,128)S(1)} collective-permute-done((f32[2,8,128]{2,1,0:T(8,128)S(1)}, f32[2,8,128]{2,1,0:T(8,128)S(1)}, u32[]{:S(2)}, u32[]{:S(2)}) %collective-permute-start.2) | collective-permute-done | bytes 8224 | tf_op jit(solution)/shard_map/ppermute | solution.py:493
  13.3 0.2 collective-permute-start.3
  13.5 1.5 %collective-permute-start.4 = (f32[4,8,128]{2,1,0:T(8,128)S(1)}, f32[4,8,128]{2,1,0:T(8,128)S(1)}, u32[]{:S(2)}, u32[]{:S(2)}) collective-permute-start(f32[4,8,128]{2,1,0:T(8,128)S(1)} %maximum_select_fusion), channel_id=1, source_target_pairs={{0,16},{1,9},{2,18},{3,11},{4,20},{5,13},{6,22},{7,15},{8,24},{9,1... | collective-permute-start | bytes 49160 | tf_op jit(solution)/shard_map/ppermute | solution.py:493
  15.1 1.4 %collective-permute-start.6 = (f32[4,8,128]{2,1,0:T(8,128)S(1)}, f32[4,8,128]{2,1,0:T(8,128)S(1)}, u32[]{:S(2)}, u32[]{:S(2)}) collective-permute-start(f32[4,8,128]{2,1,0:T(8,128)S(1)} %maximum_select_fusion), channel_id=1, source_target_pairs={{0,24},{1,25},{2,26},{3,27},{4,28},{5,29},{6,30},{7,31},{8,16},{9,... | collective-permute-start | bytes 49160 | tf_op jit(solution)/shard_map/ppermute | solution.py:493
  16.5 0.8 %collective-permute-done.4 = f32[4,8,128]{2,1,0:T(8,128)S(1)} collective-permute-done((f32[4,8,128]{2,1,0:T(8,128)S(1)}, f32[4,8,128]{2,1,0:T(8,128)S(1)}, u32[]{:S(2)}, u32[]{:S(2)}) %collective-permute-start.4) | collective-permute-done | bytes 16416 | tf_op jit(solution)/shard_map/ppermute | solution.py:493
  17.3 0.0 collective-permute-start.5
  17.3 2.4 %collective-permute-done.6 = f32[4,8,128]{2,1,0:T(8,128)S(1)} collective-permute-done((f32[4,8,128]{2,1,0:T(8,128)S(1)}, f32[4,8,128]{2,1,0:T(8,128)S(1)}, u32[]{:S(2)}, u32[]{:S(2)}) %collective-permute-start.6) | collective-permute-done | bytes 16416 | tf_op jit(solution)/shard_map/ppermute | solution.py:493
  19.7 0.0 collective-permute-done.5
  19.7 0.0 collective-permute-done.3.other
  19.7 0.9 %regress.1 = (f32[4,8,512]{2,1,0:T(8,128)S(1)}, f32[8,128]{1,0:T(8,128)S(1)}, f32[8,128]{1,0:T(8,128)}) custom-call(f32[50,2,8,500]{3,2,1,0:T(8,128)S(1)} %get-tuple-element.29.flux, f32[50,2,8,500]{3,2,1,0:T(8,128)S(1)} %collective-permute-done.3.other, f32[4,8,128]{2,1,0:T(8,128)S(1)} %add_add_fusion.sums), custom_call_target="tpu_custom_call" | custom-call | flops 1000000 | bytes 1000000 | tf_op jit(solution)/shard_map/regress/pallas_call | solution.py:403
  20.6 1.6 %collective-permute-start.7 = (f32[4,8,512]{2,1,0:T(8,128)S(1)}, f32[4,8,512]{2,1,0:T(8,128)S(1)}, u32[]{:S(2)}, u32[]{:S(2)}) collective-permute-start(f32[4,8,512]{2,1,0:T(8,128)S(1)} %get-tuple-element.32.refs_0_), channel_id=1, source_target_pairs={{0,2},{1,5},{2,0},{3,7},{4,6},{5,1},{6,4},{7,3},{8,10},{9,13},{10,... | collective-permute-start | bytes 196616 | tf_op jit(solution)/shard_map/ppermute | solution.py:493
  22.2 1.5 %collective-permute-start.8 = (f32[4,8,512]{2,1,0:T(8,128)S(1)}, f32[4,8,512]{2,1,0:T(8,128)S(1)}, u32[]{:S(2)}, u32[]{:S(2)}) collective-permute-start(f32[4,8,512]{2,1,0:T(8,128)S(1)} %get-tuple-element.32.refs_0_), channel_id=1, source_target_pairs={{0,8},{1,7},{2,10},{3,5},{4,12},{5,3},{6,14},{7,1},{8,0},{9,15},{1... | collective-permute-start | bytes 196616 | tf_op jit(solution)/shard_map/ppermute | solution.py:493
  23.7 1.2 %collective-permute-done.7 = f32[4,8,512]{2,1,0:T(8,128)S(1)} collective-permute-done((f32[4,8,512]{2,1,0:T(8,128)S(1)}, f32[4,8,512]{2,1,0:T(8,128)S(1)}, u32[]{:S(2)}, u32[]{:S(2)}) %collective-permute-start.7) | collective-permute-done | bytes 65568 | tf_op jit(solution)/shard_map/ppermute | solution.py:493
  24.9 1.6 %collective-permute-done.8 = f32[4,8,512]{2,1,0:T(8,128)S(1)} collective-permute-done((f32[4,8,512]{2,1,0:T(8,128)S(1)}, f32[4,8,512]{2,1,0:T(8,128)S(1)}, u32[]{:S(2)}, u32[]{:S(2)}) %collective-permute-start.8) | collective-permute-done | bytes 65568 | tf_op jit(solution)/shard_map/ppermute | solution.py:493
  26.5 1.0 %collective-permute-start.9 = (f32[4,8,512]{2,1,0:T(8,128)S(1)}, f32[4,8,512]{2,1,0:T(8,128)S(1)}, u32[]{:S(2)}, u32[]{:S(2)}) collective-permute-start(f32[4,8,512]{2,1,0:T(8,128)S(1)} %select_add_fusion.refs_1_), channel_id=1, source_target_pairs={{0,1},{1,0},{2,3},{3,2},{4,5},{5,4},{6,7},{7,6},{8,9},{9,8},{10,11... | collective-permute-start | bytes 196616 | tf_op jit(solution)/shard_map/ppermute | solution.py:493
  27.5 0.9 %collective-permute-done.9.refs_2_ = f32[4,8,512]{2,1,0:T(8,128)S(1)} collective-permute-done((f32[4,8,512]{2,1,0:T(8,128)S(1)}, f32[4,8,512]{2,1,0:T(8,128)S(1)}, u32[]{:S(2)}, u32[]{:S(2)}) %collective-permute-start.9) | collective-permute-done | bytes 65568 | tf_op jit(solution)/shard_map/ppermute | solution.py:493
  28.4 1.4 %clean.1 = f32[8,50,2,500]{3,2,1,0:T(2,128)} custom-call(f32[50,2,8,500]{3,2,1,0:T(8,128)S(1)} %get-tuple-element.29.flux, f32[8,128]{1,0:T(8,128)S(1)} %get-tuple-element.31.sky_ref, f32[4,8,512]{2,1,0:T(8,128)S(1)} %get-tuple-element.32.refs_0_, f32[4,8,512]{2,1,0:T(8,128)S(1)} %select_add_fusion.refs_1_, f32[4,8,512]{2,1,0:T(8,128)S(1)} %collective-permute-done.9.refs_2_), custom_call_target="tpu_custom_call" | custom-call | flops 1000000 | bytes 1000000 | tf_op jit(solution)/shard_map/clean/pallas_call | solution.py:460
  (6 shorter events, 0.0 us)
Async XLA Ops:
  0.6 4.6 %copy-start = (s32[2,40]{1,0:T(2,128)S(1)}, s32[2,40]{1,0:T(2,128)}, u32[]{:S(2)}) copy-start(s32[2,40]{1,0:T(2,128)} %sky_index.1) | copy-start | bytes 964
  2.1 7.4 %collective-permute-start = (f32[6,2,8,500]{3,2,1,0:T(8,128)S(1)}, f32[6,2,8,500]{3,2,1,0:T(8,128)S(1)}, u32[]{:S(2)}, u32[]{:S(2)}) collective-permute-start(f32[6,2,8,500]{3,2,1,0:T(8,128)S(1)} %get-tuple-element.18), channel_id=1, source_target_pairs={{0,1},{1,0},{2,3},{3,2},{4,5},{5,4},{6,7},{7,6},{8,9},{9,8},{10,11... | collective-permute-start | bytes 576008 | tf_op jit(solution)/shard_map/ppermute | solution.py:493
  2.6 6.9 %collective-permute-start.1 = (f32[6,2,8,500]{3,2,1,0:T(8,128)S(1)}, f32[6,2,8,500]{3,2,1,0:T(8,128)S(1)}, u32[]{:S(2)}, u32[]{:S(2)}) collective-permute-start(f32[6,2,8,500]{3,2,1,0:T(8,128)S(1)} %get-tuple-element.19), channel_id=1, source_target_pairs={{0,8},{1,2},{2,1},{3,4},{4,3},{5,6},{6,5},{7,15},{8,0},{9,10},{10,... | collective-permute-start | bytes 576008 | tf_op jit(solution)/shard_map/ppermute | solution.py:493
  12.2 1.2 %collective-permute-start.2 = (f32[2,8,128]{2,1,0:T(8,128)S(1)}, f32[2,8,128]{2,1,0:T(8,128)S(1)}, u32[]{:S(2)}, u32[]{:S(2)}) collective-permute-start(f32[2,8,128]{2,1,0:T(8,128)S(1)} %get-tuple-element.28), channel_id=1, source_target_pairs={{0,1},{1,0},{2,3},{3,2},{4,5},{5,4},{6,7},{7,6},{8,9},{9,8},{10,11... | collective-permute-start | bytes 24584 | tf_op jit(solution)/shard_map/ppermute | solution.py:493
  13.3 6.4 %collective-permute-start.3 = (f32[50,2,8,500]{3,2,1,0:T(8,128)S(1)}, f32[50,2,8,500]{3,2,1,0:T(8,128)S(1)}, u32[]{:S(2)}, u32[]{:S(2)}) collective-permute-start(f32[50,2,8,500]{3,2,1,0:T(8,128)S(1)} %get-tuple-element.29.flux), channel_id=1, source_target_pairs={{0,1},{1,0},{2,3},{3,2},{4,5},{5,4},{6,7},{7,6},{8,9},{9,8},{10,11... | collective-permute-start | bytes 4800008 | tf_op jit(solution)/shard_map/ppermute | solution.py:493
  13.5 3.7 %collective-permute-start.4 = (f32[4,8,128]{2,1,0:T(8,128)S(1)}, f32[4,8,128]{2,1,0:T(8,128)S(1)}, u32[]{:S(2)}, u32[]{:S(2)}) collective-permute-start(f32[4,8,128]{2,1,0:T(8,128)S(1)} %maximum_select_fusion), channel_id=1, source_target_pairs={{0,16},{1,9},{2,18},{3,11},{4,20},{5,13},{6,22},{7,15},{8,24},{9,1... | collective-permute-start | bytes 49160 | tf_op jit(solution)/shard_map/ppermute | solution.py:493
  15.1 4.6 %collective-permute-start.6 = (f32[4,8,128]{2,1,0:T(8,128)S(1)}, f32[4,8,128]{2,1,0:T(8,128)S(1)}, u32[]{:S(2)}, u32[]{:S(2)}) collective-permute-start(f32[4,8,128]{2,1,0:T(8,128)S(1)} %maximum_select_fusion), channel_id=1, source_target_pairs={{0,24},{1,25},{2,26},{3,27},{4,28},{5,29},{6,30},{7,31},{8,16},{9,... | collective-permute-start | bytes 49160 | tf_op jit(solution)/shard_map/ppermute | solution.py:493
  17.3 2.4 %collective-permute-start.5 = (f32[4,8,128]{2,1,0:T(8,128)S(1)}, f32[4,8,128]{2,1,0:T(8,128)S(1)}, u32[]{:S(2)}, u32[]{:S(2)}) collective-permute-start(f32[4,8,128]{2,1,0:T(8,128)S(1)} %collective-permute-done.4), channel_id=1, source_target_pairs={{0,1},{1,0},{2,3},{3,2},{4,5},{5,4},{6,7},{7,6},{8,9},{9,8},{10,11... | collective-permute-start | bytes 49160 | tf_op jit(solution)/shard_map/ppermute | solution.py:493
  20.6 4.3 %collective-permute-start.7 = (f32[4,8,512]{2,1,0:T(8,128)S(1)}, f32[4,8,512]{2,1,0:T(8,128)S(1)}, u32[]{:S(2)}, u32[]{:S(2)}) collective-permute-start(f32[4,8,512]{2,1,0:T(8,128)S(1)} %get-tuple-element.32.refs_0_), channel_id=1, source_target_pairs={{0,2},{1,5},{2,0},{3,7},{4,6},{5,1},{6,4},{7,3},{8,10},{9,13},{10,... | collective-permute-start | bytes 196616 | tf_op jit(solution)/shard_map/ppermute | solution.py:493
  22.2 4.3 %collective-permute-start.8 = (f32[4,8,512]{2,1,0:T(8,128)S(1)}, f32[4,8,512]{2,1,0:T(8,128)S(1)}, u32[]{:S(2)}, u32[]{:S(2)}) collective-permute-start(f32[4,8,512]{2,1,0:T(8,128)S(1)} %get-tuple-element.32.refs_0_), channel_id=1, source_target_pairs={{0,8},{1,7},{2,10},{3,5},{4,12},{5,3},{6,14},{7,1},{8,0},{9,15},{1... | collective-permute-start | bytes 196616 | tf_op jit(solution)/shard_map/ppermute | solution.py:493
  26.5 1.9 %collective-permute-start.9 = (f32[4,8,512]{2,1,0:T(8,128)S(1)}, f32[4,8,512]{2,1,0:T(8,128)S(1)}, u32[]{:S(2)}, u32[]{:S(2)}) collective-permute-start(f32[4,8,512]{2,1,0:T(8,128)S(1)} %select_add_fusion.refs_1_), channel_id=1, source_target_pairs={{0,1},{1,0},{2,3},{3,2},{4,5},{5,4},{6,7},{7,6},{8,9},{9,8},{10,11... | collective-permute-start | bytes 196616 | tf_op jit(solution)/shard_map/ppermute | solution.py:493

commit v6 on v5

--- a/solution.py
+++ b/solution.py
@@ -117,86 +117,125 @@
     )(*arrays)
 
 
-def prepare_kernel(
-    chunks, pix, iva, msk, lef, rig, sky_index, diag, off_one, off_two, rhs, shares, sky_mask, denom, bufs, mbuf, sems
+def forward_kernel(
+    chunks, near, pix, iva, msk, lef, rig, sky_index, lower, lower_far, half, shares, tail, sky_mask, denom, bufs, mbuf, sems
 ):
     exposures, rows, specs, fibres = pix.shape
+    odd = lax.rem(lax.axis_index("wave"), 2)
+    spans = range(specs)
     bounds = [rows * c // chunks for c in range(chunks + 1)]
+
+    def place(low, high):
+        return pl.ds(odd * low + (1 - odd) * (rows - high), high - low)
+
     for c in range(chunks):
-        low, high = bounds[c], bounds[c + 1]
+        here = place(bounds[c], bounds[c + 1])
         for e in range(exposures):
             for slot, ref in enumerate((pix, iva, lef, rig)):
                 pltpu.make_async_copy(
-                    ref.at[e, low:high], bufs.at[slot, low:high, :, e], sems.at[0, c]
+                    ref.at[e, here], bufs.at[slot, here, :, e], sems.at[0, c]
                 ).start()
-            pltpu.make_async_copy(
-                msk.at[e, low:high], mbuf.at[low:high, :, e], sems.at[1, c]
-            ).start()
+            pltpu.make_async_copy(msk.at[e, here], mbuf.at[here, :, e], sems.at[1, c]).start()
     lane = lax.broadcasted_iota(jnp.int32, (exposures, fibres), 1)
-    for s in range(specs):
+    for s in spans:
         found = lane == sky_index[s, 0]
         for k in range(1, sky_index.shape[1]):
             found = found | (lane == sky_index[s, k])
         sky_mask[s] = jnp.where(found, 1.0, 0.0)
 
     spot = lax.broadcasted_iota(jnp.int32, (exposures, LANES), 1)
-
-    def share(k, s, value, total):
-        part = sky_mask[s] * value
-        shares[k, s] = part
-        return jnp.where(spot == k, total + jnp.sum(part, axis=1, keepdims=True), total)
-
-    def row(k, s, carry, total):
-        w1, wp1, wr1, wrr2, wrp2, wrr1, wrp1 = carry
-        p, w, l, r = bufs[0, k, s], weight_of(bufs[1, k, s], mbuf[k, s]), bufs[2, k, s], bufs[3, k, s]
-        wl, wr, wp = w * l, w * r, w * p
-        here = w1 + wl * l + (wrr2 + REG)
-        diag[k, s] = here
-        if k > 0:
-            total = share(k - 1, s, here, total)
-        off_one[k, s] = wr1 + wl
-        off_two[k, s] = wl * r
-        rhs[k, s] = wp1 + wl * p + wrp2
-        return (w, wp, wr, wrr1, wrp1, wr * r, wr * p), total
-
-    carries = [(0.0,) * 7 for _ in range(specs)]
+    before, after = 3 - odd, 2 + odd
+
+    def share(k, parts, total):
+        parts = [sky_mask[s] * parts[s] for s in spans]
+        for s in spans:
+            shares[k, s] = parts[s]
+        row = odd * k + (1 - odd) * (rows - 1 - k)
+        return jnp.where(spot == row, jnp.sum(sum(parts), axis=1, keepdims=True), total)
+
+    made = [dict(d1=REG, b1=0.0, d2=REG, b2=0.0, r1=0.0) for _ in spans]
+    offs = [[] for _ in spans]
+    fars = [[] for _ in spans]
+    states = [None] * specs
     total = jnp.zeros((exposures, LANES), F32)
     for c in range(chunks):
-        low, high = bounds[c], bounds[c + 1]
-        part, mpart = bufs.at[:, low:high], mbuf.at[low:high]
+        here = place(bounds[c], bounds[c + 1])
+        part, mpart = bufs.at[:, here], mbuf.at[here]
         pltpu.make_async_copy(part, part, sems.at[0, c]).wait()
         pltpu.make_async_copy(mpart, mpart, sems.at[1, c]).wait()
-        for s in range(specs):
-            for k in range(low, high):
-                carries[s], total = row(k, s, carries[s], total)
-    for s in range(specs):
-        w1, wp1, wr1, wrr2, wrp2, wrr1, wrp1 = carries[s]
-        here = w1 + (wrr2 + REG)
-        diag[rows, s] = here
-        total = share(rows - 1, s, here, total)
-        off_one[rows, s] = wr1
-        rhs[rows, s] = wp1 + wrp2
-        diag[rows + 1, s] = wrr1 + REG
-        rhs[rows + 1, s] = wrp1
-    denom[...] = total
-
-
-def prepare_call(arrays, sky_index):
+        for k in range(bounds[c], bounds[c + 1]):
+            row = odd * k + (1 - odd) * (rows - 1 - k)
+            diags = []
+            for s in spans:
+                p, l, r = bufs[0, row, s], bufs[before, row, s], bufs[after, row, s]
+                w = weight_of(bufs[1, row, s], mbuf[row, s])
+                wl, wr, wp = w * l, w * r, w * p
+                m = made[s]
+                d, b = m["d1"] + wl * l, m["b1"] + wl * p
+                offs[s].append(m["r1"] + wl)
+                fars[s].append(wl * r)
+                made[s] = dict(
+                    d1=w + m["d2"], b1=wp + m["b2"], d2=wr * r + REG, b2=wr * p, r1=wr
+                )
+                if k == 0:
+                    d, b = d + near[0, s], b + near[3, s]
+                    offs[s][0] = offs[s][0] + near[1, s]
+                    inv = recip(d)
+                    states[s] = (inv, None, None, b, None)
+                elif k == 1:
+                    diags.append(d + near[5, s])
+                    d, b = d + near[2, s], b + near[4, s]
+                    inv1, _, _, y1, _ = states[s]
+                    upper = offs[s][0]
+                    g = upper * inv1
+                    inv, y = recip(d - g * upper), b - g * y1
+                    lower[1, s], half[1, s] = g, y * inv
+                    states[s] = (inv, inv1, g, y, y1)
+                else:
+                    diags.append(d)
+                    f, g, y, states[s] = eliminate(states[s], d, offs[s][k - 1], b, fars[s][k - 2])
+                    lower_far[k, s], lower[k, s], half[k, s] = f, g, y * states[s][0]
+            if k > 0:
+                total = share(k - 1, diags, total)
+    for s in spans:
+        m = made[s]
+        tail_parts = states[s] + (
+            m["d1"], offs[s][rows - 1], m["b1"], fars[s][rows - 2], m["d2"], m["r1"], m["b2"], fars[s][rows - 1]
+        )
+        for slot, value in enumerate(tail_parts):
+            tail[slot, s] = value
+    denom[...] = share(rows - 1, [made[s]["d1"] for s in spans], total)
+
+
+TAIL = 13
+
+
+def eliminate(state, d, a, b, far_a):
+    inv1, inv2, mult1, y1, y2 = state
+    f = far_a * inv2
+    upper = a - far_a * mult1
+    g = upper * inv1
+    pivot = d - f * far_a - g * upper
+    y = b - f * y2 - g * y1
+    return f, g, y, (recip(pivot), inv1, g, y, y1)
+
+
+def forward_call(near, arrays, sky_index):
     exposures, rows, specs, fibres = arrays[0].shape
     chunks = 5
-    grown = in_vmem((rows + 2, specs, exposures, fibres))
+    whole = in_vmem((rows, specs, exposures, fibres))
     return pl.pallas_call(
-        functools.partial(prepare_kernel, chunks),
+        functools.partial(forward_kernel, chunks),
         out_shape=(
-            grown,
-            grown,
-            grown,
-            grown,
-            in_vmem((rows, specs, exposures, fibres)),
+            whole,
+            whole,
+            whole,
+            whole,
+            in_vmem((TAIL, specs, exposures, fibres)),
             in_vmem((specs, exposures, fibres)),
             in_vmem((exposures, LANES)),
         ),
-        in_specs=[HB] * 5 + [SM],
+        in_specs=[VM] + [HB] * 5 + [SM],
         out_specs=(VM,) * 7,
         scratch_shapes=[
             pltpu.VMEM((4, rows, specs, exposures, fibres), F32),
@@ -205,149 +244,75 @@
         ],
         compiler_params=pltpu.CompilerParams(vmem_limit_bytes=24 * 2**20),
         cost_estimate=pl.CostEstimate(flops=10**7, bytes_accessed=10**7, transcendentals=0),
-        name="prepare",
-    )(*arrays, sky_index)
-
-
-def solve_kernel(
-    wave, near, far, diag, off_one, off_two, rhs, shares, sky_mask, denom, flux, sums, lower, lower_far, half
-):
-    count, specs, exposures, fibres = diag.shape
-    rows = count - 2
+        name="forward",
+    )(near, *arrays, sky_index)
+
+
+def backward_kernel(wave, far, lower, lower_far, half, shares, tail, sky_mask, denom, flux, sums):
+    rows, specs, exposures, fibres = lower.shape
     device = lax.axis_index("wave")
-    is_odd = lax.rem(device, 2) == 1
+    odd = lax.rem(device, 2)
     at_end = (device == 0) | (device == wave - 1)
-
-    def from_far(part, s):
+    lane = lax.broadcasted_iota(jnp.int32, (exposures, LANES), 1)
+    spans = range(specs)
+
+    def message(part, s):
         return jnp.where(at_end, 0.0, far[part, s])
 
-    def left(part, s):
-        return jnp.where(is_odd, near[part, s], from_far(part, s))
-
-    def right(part, s):
-        return jnp.where(is_odd, from_far(part, s), near[part, s])
-
-    lane = lax.broadcasted_iota(jnp.int32, (exposures, LANES), 1)
-    numer = jnp.zeros((exposures, LANES), F32)
-
-    zero = jnp.zeros((exposures, fibres), F32)
-    spans = range(specs)
-
-    def step(k, state, d, a, b, far_a):
-        inv1, inv2, mult1, y1, y2 = state
-        f = far_a * inv2
-        upper = a - far_a * mult1
-        g = upper * inv1
-        pivot = d - f * far_a - g * upper
-        y = b - f * y2 - g * y1
-        return f, g, y, (recip(pivot), inv1, g, y, y1)
-
-    def put(k, s, f, g, y, state):
-        lower_far[k, s] = f
-        lower[k, s] = g
-        half[k, s] = y * state[0]
-
-    states = []
-    for s in spans:
-        state = (zero,) * 5
-        f, g, y, state = step(0, state, diag[0, s] + left(0, s), zero, rhs[0, s] + left(3, s), zero)
-        put(0, s, f, g, y, state)
-        f, g, y, state = step(
-            1,
-            state,
-            diag[1, s] + left(2, s),
-            off_one[0, s] + left(1, s),
-            rhs[1, s] + left(4, s),
-            zero,
-        )
-        put(1, s, f, g, y, state)
-        states.append(state)
-
-    def forward(k, states):
-        results = []
-        for s in spans:
-            f, g, y, state = step(
-                k, states[s], diag[k, s], off_one[k - 1, s], rhs[k, s], off_two[k - 2, s]
-            )
-            put(k, s, f, g, y, state)
-            results.append(state)
-        return tuple(results)
-
-    states = lax.fori_loop(2, rows, forward, tuple(states), unroll=4)
-
-    after = [None] * specs
-    for s in spans:
-        f, g, y, state = step(
-            rows,
-            states[s],
-            diag[rows, s] + right(2, s),
-            off_one[rows - 1, s],
-            rhs[rows, s] + right(4, s),
-            off_two[rows - 2, s],
-        )
-        f1, g1, y1, state1 = step(
-            rows + 1,
-            state,
-            diag[rows + 1, s] + right(0, s),
-            off_one[rows, s] + right(1, s),
-            rhs[rows + 1, s] + right(3, s),
-            off_two[rows - 1, s],
-        )
-        last = y1 * state1[0]
-        here = y * state[0] - g1 * last
-        flux[rows - 1, s] = here
-        after[s] = (here, last, g, f1, f)
+    def place(k):
+        return odd * k + (1 - odd) * (rows - 1 - k)
 
     def total(parts):
         return jnp.sum(parts, axis=1, keepdims=True)
 
     def spread(k, numer, parts, values):
-        return jnp.where(lane == k, total(sum(parts[s] * values[s] for s in spans)), numer)
-
-    extra = [sky_mask[s] * right(5, s) for s in spans]
+        return jnp.where(lane == place(k), total(sum(parts[s] * values[s] for s in spans)), numer)
+
+    after, extra = [], []
+    for s in spans:
+        t = [tail[slot, s] for slot in range(TAIL)]
+        f, g, y, state = eliminate(t[:5], t[5] + message(2, s), t[6], t[7] + message(4, s), t[8])
+        f1, g1, y1, last = eliminate(
+            state, t[9] + message(0, s), t[10] + message(1, s), t[11] + message(3, s), t[12]
+        )
+        beyond = y1 * last[0]
+        value = y * state[0] - g1 * beyond
+        flux[place(rows - 1), s] = value
+        after.append((value, beyond, g, f1, f))
+        extra.append(sky_mask[s] * message(5, s))
     parts = [shares[rows - 1, s] + extra[s] for s in spans]
+    numer = jnp.zeros((exposures, LANES), F32)
     numer = spread(rows - 1, numer, parts, [after[s][0] for s in spans])
-    weights = denom[...] + jnp.where(lane == rows - 1, total(sum(extra)), 0.0)
-
-    def backward(step_row, carry):
-        k = rows - 1 - step_row
-        numer, after = carry
+    sums[1] = denom[...] + jnp.where(lane == place(rows - 1), total(sum(extra)), 0.0)
+
+    def step(k, numer, after, bottom=False):
         results = []
         for s in spans:
             x1, x2, g1, f2, f1 = after[s]
             value = half[k, s] - g1 * x1 - f2 * x2
-            flux[k - 1, s] = value
-            results.append((value, x1, lower[k, s], f1, lower_far[k, s]))
+            flux[place(k - 1), s] = value
+            results.append((value, x1) if bottom else (value, x1, lower[k, s], f1, lower_far[k, s]))
         parts = [shares[k - 1, s] for s in spans]
-        return (spread(k - 1, numer, parts, [r[0] for r in results]), tuple(results))
-
-    numer, after = lax.fori_loop(0, rows - 2, backward, (numer, tuple(after)), unroll=4)
-    values = []
-    for s in spans:
-        x1, x2, g1, f2, f1 = after[s]
-        value = half[1, s] - g1 * x1 - f2 * x2
-        flux[0, s] = value
-        values.append(value)
-    extra = [sky_mask[s] * left(5, s) for s in spans]
-    parts = [shares[0, s] + extra[s] for s in spans]
-    sums[0] = spread(0, numer, parts, values)
-    sums[1] = weights + jnp.where(lane == 0, total(sum(extra)), 0.0)
-
-
-def solve_call(wave, near, far, bands):
-    count, specs, exposures, fibres = bands[0].shape
-    rows = count - 2
-    scratch = pltpu.VMEM((count, specs, exposures, fibres), F32)
+        return spread(k - 1, numer, parts, [r[0] for r in results]), tuple(results)
+
+    numer, after = lax.fori_loop(
+        0, rows - 2, lambda i, carry: step(rows - 1 - i, *carry), (numer, tuple(after)), unroll=4
+    )
+    numer, after = step(1, numer, after, bottom=True)
+    sums[0] = numer
+
+
+def backward_call(wave, far, factors):
+    rows, specs, exposures, fibres = factors[0].shape
     return pl.pallas_call(
-        functools.partial(solve_kernel, wave),
+        functools.partial(backward_kernel, wave),
         out_shape=(in_vmem((rows, specs, exposures, fibres)), in_vmem((2, exposures, LANES))),
-        in_specs=[VM] * 9,
+        in_specs=[VM] * 8,
         out_specs=(VM, VM),
-        scratch_shapes=[scratch] * 3,
         compiler_params=pltpu.CompilerParams(vmem_limit_bytes=24 * 2**20),
         cost_estimate=pl.CostEstimate(flops=10**7, bytes_accessed=10**7, transcendentals=0),
-        name="solve",
-    )(near, far, *bands)
+        name="backward",
+    )(far, *factors)
 
 
 def position_of(index, total_rows):
@@ -507,15 +472,15 @@
     near, far = edge_call(hbm)
     far = swap(far, lambda s, i: (s, i + 1 if i % 2 else i - 1))
     near = swap(near, other_core)
-    bands = prepare_call(hbm, sky_index)
-    flux, sums = solve_call(wave, near, far, bands)
+    factors = forward_call(near, hbm, sky_index)
+    flux, sums = backward_call(wave, far, factors)
     got = swap(sums, other_core)
     flux, got = lax.optimization_barrier((flux, got))
     other = swap(flux, other_core)
     sums = jnp.where(odd, jnp.concatenate([got, sums]), jnp.concatenate([sums, got]))
     if spec == 4:
         first = swap(sums, lambda s, i: (s ^ (1 if i % 2 else 2), i))
-        third = swap(sums, lambda s, i: (s ^ 3, i))
+        third = swap(sums, lambda s, i: (s ^ 3, i ^ 1))
         second = swap(first, other_core)
         sums = (sums + jnp.where(odd, first, second)) + (jnp.where(odd, second, first) + third)
     else:

time: 30 us -> 29.3 us (0.977)
  Pallas kernels: 10.7 us -> 9.83 us
    pallas_call x2, Pallas kernels: 6.92 us -> 6.09 us  [the longest x1 4.48 us: forward_call(): pl.pallas_call(functools.partial(forward_kernel, chunks), out_shape=(whol...]
where the time goes in v6:
time: 29.3 us; the launch traced here: 29 us
  starting transfers between devices  10.6 us (36%)
  Pallas kernels  9.83 us (34%)
  waiting for transfers between devices  7.86 us (27%)
  between operations  0.69 us (2%)
    ppermute x10, starting transfers between devices, swap(): return lax.ppermute(values, ('spec', 'wave'), pairs)  10.6 us
    ppermute x10, waiting for transfers between devices, swap(): return lax.ppermute(values, ('spec', 'wave'), pairs)  7.86 us
    pallas_call x1, Pallas kernels, forward_call(): pl.pallas_call(functools.partial(forward_kernel, chunks), out_shape=(whol...  4.48 us
    pallas_call x1, Pallas kernels, backward_call(): pl.pallas_call(functools.partial(backward_kernel, wave), out_shape=(in_vm...  1.61 us
    pallas_call x1, Pallas kernels, edge_call(): pl.pallas_call(edge_kernel, out_shape=(message, message), in_specs=[HB] *...  1.48 us
    pallas_call x1, Pallas kernels, clean_call(): pl.pallas_call(functools.partial(clean_kernel, total_rows), out_shape=jax...  1.36 us
    pallas_call x1, Pallas kernels, regress_call(): pl.pallas_call(functools.partial(regress_kernel, total_rows), out_shape=(...  0.9 us
  transfers between devices with their start and end apart: 10, of which 6 were waited for; matrix products, arithmetic and copies ran while one was open for 0% of the time, Pallas kernels for 15%

profile of v6, /device:TPU:0, one launch (start us, length us, event | category | flops | bytes accessed | tf_op | source)
XLA Modules:
  0.0 29.0 jit_solution(4014781436606408376)
XLA Ops:
  0.6 1.5 %edges.1 = (f32[6,2,8,500]{3,2,1,0:T(8,128)S(1)}, f32[6,2,8,500]{3,2,1,0:T(8,128)S(1)}) custom-call(f32[8,50,2,500]{3,2,1,0:T(2,128)} %bitcast.7, f32[8,50,2,500]{3,2,1,0:T(2,128)} %bitcast.9, s32[8,50,2,500]{3,2,1,0:T(2,128)} %bitcast.11, f32[8,50,2,500]{3,2,1,0:T(2,128)} %bitcast.13, f32[8,50,2,500]{3,2,1,0:T(2,128)} %bitcast.15), custom_call_target="tpu_custom_call" | custom-call | flops 1000000 | bytes 1000000 | tf_op jit(solution)/shard_map/edges/pallas_call | solution.py:104
  2.1 0.5 %collective-permute-start.1 = (f32[6,2,8,500]{3,2,1,0:T(8,128)S(1)}, f32[6,2,8,500]{3,2,1,0:T(8,128)S(1)}, u32[]{:S(2)}, u32[]{:S(2)}) collective-permute-start(f32[6,2,8,500]{3,2,1,0:T(8,128)S(1)} %get-tuple-element.19), channel_id=1, source_target_pairs={{0,1},{1,0},{2,3},{3,2},{4,5},{5,4},{6,7},{7,6},{8,9},{9,8},{10,11... | collective-permute-start | bytes 576008 | tf_op jit(solution)/shard_map/ppermute | solution.py:458
  2.6 2.6 %collective-permute-start = (f32[6,2,8,500]{3,2,1,0:T(8,128)S(1)}, f32[6,2,8,500]{3,2,1,0:T(8,128)S(1)}, u32[]{:S(2)}, u32[]{:S(2)}) collective-permute-start(f32[6,2,8,500]{3,2,1,0:T(8,128)S(1)} %get-tuple-element.18), channel_id=1, source_target_pairs={{0,8},{1,2},{2,1},{3,4},{4,3},{5,6},{6,5},{7,15},{8,0},{9,10},{10,... | collective-permute-start | bytes 576008 | tf_op jit(solution)/shard_map/ppermute | solution.py:458
  5.2 0.0 collective-permute-done.1.near
  5.2 4.5 %forward.1 = (f32[50,2,8,500]{3,2,1,0:T(8,128)S(1)}, f32[50,2,8,500]{3,2,1,0:T(8,128)S(1)}, f32[50,2,8,500]{3,2,1,0:T(8,128)S(1)}, f32[50,2,8,500]{3,2,1,0:T(8,1...) custom-call(f32[6,2,8,500]{3,2,1,0:T(8,128)S(1)} %collective-permute-done.1.near, ...), custom_call_target="tpu_custom_call" | custom-call | flops 10000000 | bytes 10000000 | tf_op jit(solution)/shard_map/forward/pallas_call | solution.py:227
  9.7 1.6 %backward.1 = (f32[50,2,8,500]{3,2,1,0:T(8,128)S(1)}, f32[2,8,128]{2,1,0:T(8,128)S(1)}) custom-call(f32[6,2,8,500]{3,2,1,0:T(8,128)S(1)} %collective-permute-done.far, f32[50,2,8,500]{3,2,1,0:T(8,128)S(1)} %get-tuple-element.20.lower, f32[50,2,8,500]{3,2,1,0:T(8,128)S(1)} %get-tuple-element.21.lower_far, f32[50,2,8,500]{3,2,1,0:T(8,128)S(1)} %get-tuple-element.22.half, ...), custom_call_target="tpu_custom_call" | custom-call | flops 10000000 | bytes 10000000 | tf_op jit(solution)/shard_map/backward/pallas_call | solution.py:307
  11.3 0.2 collective-permute-start.2
  11.5 1.0 %collective-permute-done.2 = f32[2,8,128]{2,1,0:T(8,128)S(1)} collective-permute-done((f32[2,8,128]{2,1,0:T(8,128)S(1)}, f32[2,8,128]{2,1,0:T(8,128)S(1)}, u32[]{:S(2)}, u32[]{:S(2)}) %collective-permute-start.2) | collective-permute-done | bytes 8224 | tf_op jit(solution)/shard_map/ppermute | solution.py:458
  12.5 0.2 collective-permute-start.3
  12.7 1.5 %collective-permute-start.4 = (f32[4,8,128]{2,1,0:T(8,128)S(1)}, f32[4,8,128]{2,1,0:T(8,128)S(1)}, u32[]{:S(2)}, u32[]{:S(2)}) collective-permute-start(f32[4,8,128]{2,1,0:T(8,128)S(1)} %maximum_select_fusion), channel_id=1, source_target_pairs={{0,16},{1,9},{2,18},{3,11},{4,20},{5,13},{6,22},{7,15},{8,24},{9,1... | collective-permute-start | bytes 49160 | tf_op jit(solution)/shard_map/ppermute | solution.py:458
  14.2 1.1 %collective-permute-start.6 = (f32[4,8,128]{2,1,0:T(8,128)S(1)}, f32[4,8,128]{2,1,0:T(8,128)S(1)}, u32[]{:S(2)}, u32[]{:S(2)}) collective-permute-start(f32[4,8,128]{2,1,0:T(8,128)S(1)} %maximum_select_fusion), channel_id=1, source_target_pairs={{0,25},{1,24},{2,27},{3,26},{4,29},{5,28},{6,31},{7,30},{8,17},{9,... | collective-permute-start | bytes 49160 | tf_op jit(solution)/shard_map/ppermute | solution.py:458
  15.3 1.1 %collective-permute-done.4 = f32[4,8,128]{2,1,0:T(8,128)S(1)} collective-permute-done((f32[4,8,128]{2,1,0:T(8,128)S(1)}, f32[4,8,128]{2,1,0:T(8,128)S(1)}, u32[]{:S(2)}, u32[]{:S(2)}) %collective-permute-start.4) | collective-permute-done | bytes 16416 | tf_op jit(solution)/shard_map/ppermute | solution.py:458
  16.4 0.0 collective-permute-start.5
  16.4 2.0 %collective-permute-done.6 = f32[4,8,128]{2,1,0:T(8,128)S(1)} collective-permute-done((f32[4,8,128]{2,1,0:T(8,128)S(1)}, f32[4,8,128]{2,1,0:T(8,128)S(1)}, u32[]{:S(2)}, u32[]{:S(2)}) %collective-permute-start.6) | collective-permute-done | bytes 16416 | tf_op jit(solution)/shard_map/ppermute | solution.py:458
  18.4 0.0 collective-permute-done.5
  18.4 0.0 collective-permute-done.3.other
  18.4 0.9 %regress.1 = (f32[4,8,512]{2,1,0:T(8,128)S(1)}, f32[8,128]{1,0:T(8,128)S(1)}, f32[8,128]{1,0:T(8,128)}) custom-call(f32[50,2,8,500]{3,2,1,0:T(8,128)S(1)} %get-tuple-element.29.flux, f32[50,2,8,500]{3,2,1,0:T(8,128)S(1)} %collective-permute-done.3.other, f32[4,8,128]{2,1,0:T(8,128)S(1)} %add_add_fusion.sums), custom_call_target="tpu_custom_call" | custom-call | flops 1000000 | bytes 1000000 | tf_op jit(solution)/shard_map/regress/pallas_call | solution.py:368
  19.3 1.6 %collective-permute-start.7 = (f32[4,8,512]{2,1,0:T(8,128)S(1)}, f32[4,8,512]{2,1,0:T(8,128)S(1)}, u32[]{:S(2)}, u32[]{:S(2)}) collective-permute-start(f32[4,8,512]{2,1,0:T(8,128)S(1)} %get-tuple-element.32.refs_0_), channel_id=1, source_target_pairs={{0,2},{1,5},{2,0},{3,7},{4,6},{5,1},{6,4},{7,3},{8,10},{9,13},{10,... | collective-permute-start | bytes 196616 | tf_op jit(solution)/shard_map/ppermute | solution.py:458
  20.9 1.4 %collective-permute-start.8 = (f32[4,8,512]{2,1,0:T(8,128)S(1)}, f32[4,8,512]{2,1,0:T(8,128)S(1)}, u32[]{:S(2)}, u32[]{:S(2)}) collective-permute-start(f32[4,8,512]{2,1,0:T(8,128)S(1)} %get-tuple-element.32.refs_0_), channel_id=1, source_target_pairs={{0,8},{1,7},{2,10},{3,5},{4,12},{5,3},{6,14},{7,1},{8,0},{9,15},{1... | collective-permute-start | bytes 196616 | tf_op jit(solution)/shard_map/ppermute | solution.py:458
  22.3 2.0 %collective-permute-done.7 = f32[4,8,512]{2,1,0:T(8,128)S(1)} collective-permute-done((f32[4,8,512]{2,1,0:T(8,128)S(1)}, f32[4,8,512]{2,1,0:T(8,128)S(1)}, u32[]{:S(2)}, u32[]{:S(2)}) %collective-permute-start.7) | collective-permute-done | bytes 65568 | tf_op jit(solution)/shard_map/ppermute | solution.py:458
  24.3 0.9 %collective-permute-done.8 = f32[4,8,512]{2,1,0:T(8,128)S(1)} collective-permute-done((f32[4,8,512]{2,1,0:T(8,128)S(1)}, f32[4,8,512]{2,1,0:T(8,128)S(1)}, u32[]{:S(2)}, u32[]{:S(2)}) %collective-permute-start.8) | collective-permute-done | bytes 65568 | tf_op jit(solution)/shard_map/ppermute | solution.py:458
  25.2 1.6 %collective-permute-start.9 = (f32[4,8,512]{2,1,0:T(8,128)S(1)}, f32[4,8,512]{2,1,0:T(8,128)S(1)}, u32[]{:S(2)}, u32[]{:S(2)}) collective-permute-start(f32[4,8,512]{2,1,0:T(8,128)S(1)} %select_add_fusion.refs_1_), channel_id=1, source_target_pairs={{0,1},{1,0},{2,3},{3,2},{4,5},{5,4},{6,7},{7,6},{8,9},{9,8},{10,11... | collective-permute-start | bytes 196616 | tf_op jit(solution)/shard_map/ppermute | solution.py:458
  26.8 0.9 %collective-permute-done.9.refs_2_ = f32[4,8,512]{2,1,0:T(8,128)S(1)} collective-permute-done((f32[4,8,512]{2,1,0:T(8,128)S(1)}, f32[4,8,512]{2,1,0:T(8,128)S(1)}, u32[]{:S(2)}, u32[]{:S(2)}) %collective-permute-start.9) | collective-permute-done | bytes 65568 | tf_op jit(solution)/shard_map/ppermute | solution.py:458
  27.7 1.4 %clean.1 = f32[8,50,2,500]{3,2,1,0:T(2,128)} custom-call(f32[50,2,8,500]{3,2,1,0:T(8,128)S(1)} %get-tuple-element.29.flux, f32[8,128]{1,0:T(8,128)S(1)} %get-tuple-element.31.sky_ref, f32[4,8,512]{2,1,0:T(8,128)S(1)} %get-tuple-element.32.refs_0_, f32[4,8,512]{2,1,0:T(8,128)S(1)} %select_add_fusion.refs_1_, f32[4,8,512]{2,1,0:T(8,128)S(1)} %collective-permute-done.9.refs_2_), custom_call_target="tpu_custom_call" | custom-call | flops 1000000 | bytes 1000000 | tf_op jit(solution)/shard_map/clean/pallas_call | solution.py:425
  (6 shorter events, 0.0 us)
Async XLA Ops:
  0.6 4.6 %copy-start = (s32[2,40]{1,0:T(2,128)S(1)}, s32[2,40]{1,0:T(2,128)}, u32[]{:S(2)}) copy-start(s32[2,40]{1,0:T(2,128)} %sky_index.1) | copy-start | bytes 964
  2.1 3.1 %collective-permute-start.1 = (f32[6,2,8,500]{3,2,1,0:T(8,128)S(1)}, f32[6,2,8,500]{3,2,1,0:T(8,128)S(1)}, u32[]{:S(2)}, u32[]{:S(2)}) collective-permute-start(f32[6,2,8,500]{3,2,1,0:T(8,128)S(1)} %get-tuple-element.19), channel_id=1, source_target_pairs={{0,1},{1,0},{2,3},{3,2},{4,5},{5,4},{6,7},{7,6},{8,9},{9,8},{10,11... | collective-permute-start | bytes 576008 | tf_op jit(solution)/shard_map/ppermute | solution.py:458
  2.6 7.1 %collective-permute-start = (f32[6,2,8,500]{3,2,1,0:T(8,128)S(1)}, f32[6,2,8,500]{3,2,1,0:T(8,128)S(1)}, u32[]{:S(2)}, u32[]{:S(2)}) collective-permute-start(f32[6,2,8,500]{3,2,1,0:T(8,128)S(1)} %get-tuple-element.18), channel_id=1, source_target_pairs={{0,8},{1,2},{2,1},{3,4},{4,3},{5,6},{6,5},{7,15},{8,0},{9,10},{10,... | collective-permute-start | bytes 576008 | tf_op jit(solution)/shard_map/ppermute | solution.py:458
  11.3 1.2 %collective-permute-start.2 = (f32[2,8,128]{2,1,0:T(8,128)S(1)}, f32[2,8,128]{2,1,0:T(8,128)S(1)}, u32[]{:S(2)}, u32[]{:S(2)}) collective-permute-start(f32[2,8,128]{2,1,0:T(8,128)S(1)} %get-tuple-element.28), channel_id=1, source_target_pairs={{0,1},{1,0},{2,3},{3,2},{4,5},{5,4},{6,7},{7,6},{8,9},{9,8},{10,11... | collective-permute-start | bytes 24584 | tf_op jit(solution)/shard_map/ppermute | solution.py:458
  12.5 5.9 %collective-permute-start.3 = (f32[50,2,8,500]{3,2,1,0:T(8,128)S(1)}, f32[50,2,8,500]{3,2,1,0:T(8,128)S(1)}, u32[]{:S(2)}, u32[]{:S(2)}) collective-permute-start(f32[50,2,8,500]{3,2,1,0:T(8,128)S(1)} %get-tuple-element.29.flux), channel_id=1, source_target_pairs={{0,1},{1,0},{2,3},{3,2},{4,5},{5,4},{6,7},{7,6},{8,9},{9,8},{10,11... | collective-permute-start | bytes 4800008 | tf_op jit(solution)/shard_map/ppermute | solution.py:458
  12.7 3.7 %collective-permute-start.4 = (f32[4,8,128]{2,1,0:T(8,128)S(1)}, f32[4,8,128]{2,1,0:T(8,128)S(1)}, u32[]{:S(2)}, u32[]{:S(2)}) collective-permute-start(f32[4,8,128]{2,1,0:T(8,128)S(1)} %maximum_select_fusion), channel_id=1, source_target_pairs={{0,16},{1,9},{2,18},{3,11},{4,20},{5,13},{6,22},{7,15},{8,24},{9,1... | collective-permute-start | bytes 49160 | tf_op jit(solution)/shard_map/ppermute | solution.py:458
  14.2 4.2 %collective-permute-start.6 = (f32[4,8,128]{2,1,0:T(8,128)S(1)}, f32[4,8,128]{2,1,0:T(8,128)S(1)}, u32[]{:S(2)}, u32[]{:S(2)}) collective-permute-start(f32[4,8,128]{2,1,0:T(8,128)S(1)} %maximum_select_fusion), channel_id=1, source_target_pairs={{0,25},{1,24},{2,27},{3,26},{4,29},{5,28},{6,31},{7,30},{8,17},{9,... | collective-permute-start | bytes 49160 | tf_op jit(solution)/shard_map/ppermute | solution.py:458
  16.4 2.0 %collective-permute-start.5 = (f32[4,8,128]{2,1,0:T(8,128)S(1)}, f32[4,8,128]{2,1,0:T(8,128)S(1)}, u32[]{:S(2)}, u32[]{:S(2)}) collective-permute-start(f32[4,8,128]{2,1,0:T(8,128)S(1)} %collective-permute-done.4), channel_id=1, source_target_pairs={{0,1},{1,0},{2,3},{3,2},{4,5},{5,4},{6,7},{7,6},{8,9},{9,8},{10,11... | collective-permute-start | bytes 49160 | tf_op jit(solution)/shard_map/ppermute | solution.py:458
  19.3 5.0 %collective-permute-start.7 = (f32[4,8,512]{2,1,0:T(8,128)S(1)}, f32[4,8,512]{2,1,0:T(8,128)S(1)}, u32[]{:S(2)}, u32[]{:S(2)}) collective-permute-start(f32[4,8,512]{2,1,0:T(8,128)S(1)} %get-tuple-element.32.refs_0_), channel_id=1, source_target_pairs={{0,2},{1,5},{2,0},{3,7},{4,6},{5,1},{6,4},{7,3},{8,10},{9,13},{10,... | collective-permute-start | bytes 196616 | tf_op jit(solution)/shard_map/ppermute | solution.py:458
  20.9 4.3 %collective-permute-start.8 = (f32[4,8,512]{2,1,0:T(8,128)S(1)}, f32[4,8,512]{2,1,0:T(8,128)S(1)}, u32[]{:S(2)}, u32[]{:S(2)}) collective-permute-start(f32[4,8,512]{2,1,0:T(8,128)S(1)} %get-tuple-element.32.refs_0_), channel_id=1, source_target_pairs={{0,8},{1,7},{2,10},{3,5},{4,12},{5,3},{6,14},{7,1},{8,0},{9,15},{1... | collective-permute-start | bytes 196616 | tf_op jit(solution)/shard_map/ppermute | solution.py:458
  25.2 2.5 %collective-permute-start.9 = (f32[4,8,512]{2,1,0:T(8,128)S(1)}, f32[4,8,512]{2,1,0:T(8,128)S(1)}, u32[]{:S(2)}, u32[]{:S(2)}) collective-permute-start(f32[4,8,512]{2,1,0:T(8,128)S(1)} %select_add_fusion.refs_1_), channel_id=1, source_target_pairs={{0,1},{1,0},{2,3},{3,2},{4,5},{5,4},{6,7},{7,6},{8,9},{9,8},{10,11... | collective-permute-start | bytes 196616 | tf_op jit(solution)/shard_map/ppermute | solution.py:458

commit v7 on v6

--- a/solution.py
+++ b/solution.py
@@ -295,9 +295,8 @@
         parts = [shares[k - 1, s] for s in spans]
         return spread(k - 1, numer, parts, [r[0] for r in results]), tuple(results)
 
-    numer, after = lax.fori_loop(
-        0, rows - 2, lambda i, carry: step(rows - 1 - i, *carry), (numer, tuple(after)), unroll=4
-    )
+    for k in range(rows - 1, 1, -1):
+        numer, after = step(k, numer, after)
     numer, after = step(1, numer, after, bottom=True)
     sums[0] = numer
 
@@ -319,7 +318,7 @@
     return 2.0 * jnp.asarray(index).astype(F32) / (total_rows - 1) - 1.0
 
 
-def regress_kernel(total_rows, flux, other, sums, regress, sky_out, sky_copy):
+def regress_kernel(total_rows, flux, other, sums, regress, sky_out):
     rows, specs, exposures, fibres = flux.shape
     lanes = regress.shape[2]
     device = lax.axis_index("wave")
@@ -340,7 +339,6 @@
         moments[2] += jnp.sum(slanted * slanted, axis=1, keepdims=True)
         if which == 0:
             sky_out[...] = sky
-            sky_copy[...] = sky
         end = position_of(owner * rows + rows, total_rows)
         running = [None] * specs
         summed = [None] * specs
@@ -370,10 +368,9 @@
         out_shape=(
             in_vmem((2 * specs, exposures, lanes)),
             in_vmem((exposures, LANES)),
-            in_vmem((exposures, LANES)),
         ),
         in_specs=[VM] * 3,
-        out_specs=(VM, VM, VM),
+        out_specs=(VM, VM),
         compiler_params=pltpu.CompilerParams(vmem_limit_bytes=24 * 2**20),
         cost_estimate=pl.CostEstimate(flops=10**6, bytes_accessed=10**6, transcendentals=0),
         name="regress",
@@ -381,8 +378,10 @@
 
 
 def clean_kernel(total_rows, flux, sky_ref, *refs):
-    *terms, out, buf, sems = refs
+    *terms, out, sky_out, buf, sems, sky_sem = refs
     rows, specs, exposures, fibres = flux.shape
+    sky_copy = pltpu.make_async_copy(sky_ref, sky_out, sky_sem)
+    sky_copy.start()
     device = lax.axis_index("wave")
 
     def got(slot):
@@ -418,18 +417,23 @@
     for c in range(chunks):
         part = buf.at[bounds[c] : bounds[c + 1]]
         pltpu.make_async_copy(part, part, sems.at[c]).wait()
+    sky_copy.wait()
 
 
 def clean_call(total_rows, flux, sky, terms):
     rows, specs, exposures, fibres = flux.shape
     return pl.pallas_call(
         functools.partial(clean_kernel, total_rows),
-        out_shape=jax.ShapeDtypeStruct((exposures, rows, specs, fibres), F32),
+        out_shape=(
+            jax.ShapeDtypeStruct((exposures, rows, specs, fibres), F32),
+            jax.ShapeDtypeStruct((exposures, LANES), F32),
+        ),
         in_specs=[VM] * (2 + len(terms)),
-        out_specs=HB,
+        out_specs=(HB, HB),
         scratch_shapes=[
             pltpu.VMEM((rows, specs, exposures, fibres), F32),
-            pltpu.SemaphoreType.DMA((5,)),
+            pltpu.SemaphoreType.DMA((4,)),
+            pltpu.SemaphoreType.DMA,
         ],
         compiler_params=pltpu.CompilerParams(vmem_limit_bytes=24 * 2**20),
         cost_estimate=pl.CostEstimate(flops=10**6, bytes_accessed=10**6, transcendentals=0),
@@ -486,7 +490,7 @@
     else:
         for k in powers(1, spec):
             sums = sums + swap(sums, lambda s, i: (s ^ k, i))
-    regress, sky, sky_out = regress_call(total_rows, flux, other, sums)
+    regress, sky = regress_call(total_rows, flux, other, sums)
     if wave == 8:
         first = swap(regress, lambda s, i: (s, i ^ (4 if i % 2 else 2)))
         third = swap(regress, lambda s, i: (s, i ^ 6 if i % 2 else -1))
@@ -496,8 +500,8 @@
         for k in powers(2, wave):
             regress = regress + swap(regress, lambda s, i: (s, i ^ k if i % 2 else -1))
         terms = [jnp.where(odd, regress, swap(regress, other_core))]
-    cleaned = clean_call(total_rows, flux, sky, terms)
-    return (jnp.transpose(cleaned, (0, 2, 1, 3)), sky_out[:, :rows])
+    cleaned, sky = clean_call(total_rows, flux, sky, terms)
+    return (jnp.transpose(cleaned, (0, 2, 1, 3)), sky[:, :rows])
 
 
 def solution(mesh):

time: 29.3 us -> 28 us (0.956)
  Pallas kernels: 9.83 us -> 8.46 us
    pallas_call x1, Pallas kernels: 1.61 us -> 0.68 us  [backward_call(): pl.pallas_call(functools.partial(backward_kernel, wave), out_shape=(in_vm...]
    pallas_call x1, Pallas kernels: 0.9 us -> 0.44 us  [regress_call(): pl.pallas_call(functools.partial(regress_kernel, total_rows), out_shape=(...]
  transfers between devices with their start and end apart: 10 -> 10, of which waited for: 6 -> 6; matrix products, arithmetic and copies ran while one was open for 0% -> 0% of each run, Pallas kernels for 15% -> 16%
where the time goes in v7:
time: 28 us; the launch traced here: 27.7 us
  starting transfers between devices  10.7 us (38%)
  Pallas kernels  8.46 us (30%)
  waiting for transfers between devices  7.87 us (28%)
  between operations  0.69 us (2%)
    ppermute x10, starting transfers between devices, swap(): return lax.ppermute(values, ('spec', 'wave'), pairs)  10.7 us
    ppermute x10, waiting for transfers between devices, swap(): return lax.ppermute(values, ('spec', 'wave'), pairs)  7.87 us
    pallas_call x1, Pallas kernels, forward_call(): pl.pallas_call(functools.partial(forward_kernel, chunks), out_shape=(whol...  4.48 us
    pallas_call x1, Pallas kernels, edge_call(): pl.pallas_call(edge_kernel, out_shape=(message, message), in_specs=[HB] *...  1.48 us
    pallas_call x1, Pallas kernels, clean_call(): pl.pallas_call(functools.partial(clean_kernel, total_rows), out_shape=(ja...  1.38 us
    pallas_call x1, Pallas kernels, backward_call(): pl.pallas_call(functools.partial(backward_kernel, wave), out_shape=(in_vm...  0.68 us
  transfers between devices with their start and end apart: 10, of which 6 were waited for; matrix products, arithmetic and copies ran while one was open for 0% of the time, Pallas kernels for 16%

profile of v7, /device:TPU:0, one launch (start us, length us, event | category | flops | bytes accessed | tf_op | source)
XLA Modules:
  0.0 27.7 jit_solution(1614022777547312281)
XLA Ops:
  0.6 1.5 %edges.1 = (f32[6,2,8,500]{3,2,1,0:T(8,128)S(1)}, f32[6,2,8,500]{3,2,1,0:T(8,128)S(1)}) custom-call(f32[8,50,2,500]{3,2,1,0:T(2,128)} %bitcast.7, f32[8,50,2,500]{3,2,1,0:T(2,128)} %bitcast.9, s32[8,50,2,500]{3,2,1,0:T(2,128)} %bitcast.11, f32[8,50,2,500]{3,2,1,0:T(2,128)} %bitcast.13, f32[8,50,2,500]{3,2,1,0:T(2,128)} %bitcast.15), custom_call_target="tpu_custom_call" | custom-call | flops 1000000 | bytes 1000000 | tf_op jit(solution)/shard_map/edges/pallas_call | solution.py:104
  2.1 0.5 %collective-permute-start.1 = (f32[6,2,8,500]{3,2,1,0:T(8,128)S(1)}, f32[6,2,8,500]{3,2,1,0:T(8,128)S(1)}, u32[]{:S(2)}, u32[]{:S(2)}) collective-permute-start(f32[6,2,8,500]{3,2,1,0:T(8,128)S(1)} %get-tuple-element.20), channel_id=1, source_target_pairs={{0,1},{1,0},{2,3},{3,2},{4,5},{5,4},{6,7},{7,6},{8,9},{9,8},{10,11... | collective-permute-start | bytes 576008 | tf_op jit(solution)/shard_map/ppermute | solution.py:462
  2.6 2.6 %collective-permute-start = (f32[6,2,8,500]{3,2,1,0:T(8,128)S(1)}, f32[6,2,8,500]{3,2,1,0:T(8,128)S(1)}, u32[]{:S(2)}, u32[]{:S(2)}) collective-permute-start(f32[6,2,8,500]{3,2,1,0:T(8,128)S(1)} %get-tuple-element.19), channel_id=1, source_target_pairs={{0,8},{1,2},{2,1},{3,4},{4,3},{5,6},{6,5},{7,15},{8,0},{9,10},{10,... | collective-permute-start | bytes 576008 | tf_op jit(solution)/shard_map/ppermute | solution.py:462
  5.2 0.0 collective-permute-done.1.near
  5.2 4.5 %forward.1 = (f32[50,2,8,500]{3,2,1,0:T(8,128)S(1)}, f32[50,2,8,500]{3,2,1,0:T(8,128)S(1)}, f32[50,2,8,500]{3,2,1,0:T(8,128)S(1)}, f32[50,2,8,500]{3,2,1,0:T(8,1...) custom-call(f32[6,2,8,500]{3,2,1,0:T(8,128)S(1)} %collective-permute-done.1.near, ...), custom_call_target="tpu_custom_call" | custom-call | flops 10000000 | bytes 10000000 | tf_op jit(solution)/shard_map/forward/pallas_call | solution.py:227
  9.7 0.0 collective-permute-done.far
  9.7 0.7 %backward.1 = (f32[50,2,8,500]{3,2,1,0:T(8,128)S(1)}, f32[2,8,128]{2,1,0:T(8,128)S(1)}) custom-call(f32[6,2,8,500]{3,2,1,0:T(8,128)S(1)} %collective-permute-done.far, f32[50,2,8,500]{3,2,1,0:T(8,128)S(1)} %get-tuple-element.21.lower, f32[50,2,8,500]{3,2,1,0:T(8,128)S(1)} %get-tuple-element.22.lower_far, f32[50,2,8,500]{3,2,1,0:T(8,128)S(1)} %get-tuple-element.23.half, ...), custom_call_target="tpu_custom_call" | custom-call | flops 10000000 | bytes 10000000 | tf_op jit(solution)/shard_map/backward/pallas_call | solution.py:306
  10.4 0.2 collective-permute-start.2
  10.6 1.0 %collective-permute-done.2 = f32[2,8,128]{2,1,0:T(8,128)S(1)} collective-permute-done((f32[2,8,128]{2,1,0:T(8,128)S(1)}, f32[2,8,128]{2,1,0:T(8,128)S(1)}, u32[]{:S(2)}, u32[]{:S(2)}) %collective-permute-start.2) | collective-permute-done | bytes 8224 | tf_op jit(solution)/shard_map/ppermute | solution.py:462
  11.6 0.2 collective-permute-start.3
  11.8 1.5 %collective-permute-start.4 = (f32[4,8,128]{2,1,0:T(8,128)S(1)}, f32[4,8,128]{2,1,0:T(8,128)S(1)}, u32[]{:S(2)}, u32[]{:S(2)}) collective-permute-start(f32[4,8,128]{2,1,0:T(8,128)S(1)} %maximum_select_fusion), channel_id=1, source_target_pairs={{0,16},{1,9},{2,18},{3,11},{4,20},{5,13},{6,22},{7,15},{8,24},{9,1... | collective-permute-start | bytes 49160 | tf_op jit(solution)/shard_map/ppermute | solution.py:462
  13.3 1.1 %collective-permute-start.6 = (f32[4,8,128]{2,1,0:T(8,128)S(1)}, f32[4,8,128]{2,1,0:T(8,128)S(1)}, u32[]{:S(2)}, u32[]{:S(2)}) collective-permute-start(f32[4,8,128]{2,1,0:T(8,128)S(1)} %maximum_select_fusion), channel_id=1, source_target_pairs={{0,25},{1,24},{2,27},{3,26},{4,29},{5,28},{6,31},{7,30},{8,17},{9,... | collective-permute-start | bytes 49160 | tf_op jit(solution)/shard_map/ppermute | solution.py:462
  14.4 1.1 %collective-permute-done.4 = f32[4,8,128]{2,1,0:T(8,128)S(1)} collective-permute-done((f32[4,8,128]{2,1,0:T(8,128)S(1)}, f32[4,8,128]{2,1,0:T(8,128)S(1)}, u32[]{:S(2)}, u32[]{:S(2)}) %collective-permute-start.4) | collective-permute-done | bytes 16416 | tf_op jit(solution)/shard_map/ppermute | solution.py:462
  15.5 0.0 collective-permute-start.5
  15.5 2.0 %collective-permute-done.6 = f32[4,8,128]{2,1,0:T(8,128)S(1)} collective-permute-done((f32[4,8,128]{2,1,0:T(8,128)S(1)}, f32[4,8,128]{2,1,0:T(8,128)S(1)}, u32[]{:S(2)}, u32[]{:S(2)}) %collective-permute-start.6) | collective-permute-done | bytes 16416 | tf_op jit(solution)/shard_map/ppermute | solution.py:462
  17.5 0.0 collective-permute-done.5
  17.5 0.4 %regress.1 = (f32[4,8,512]{2,1,0:T(8,128)S(1)}, f32[8,128]{1,0:T(8,128)S(1)}) custom-call(f32[50,2,8,500]{3,2,1,0:T(8,128)S(1)} %get-tuple-element.30.flux, f32[50,2,8,500]{3,2,1,0:T(8,128)S(1)} %collective-permute-done.3.other, f32[4,8,128]{2,1,0:T(8,128)S(1)} %add_add_fusion.sums), custom_call_target="tpu_custom_call" | custom-call | flops 1000000 | bytes 1000000 | tf_op jit(solution)/shard_map/regress/pallas_call | solution.py:366
  18.0 1.6 %collective-permute-start.7 = (f32[4,8,512]{2,1,0:T(8,128)S(1)}, f32[4,8,512]{2,1,0:T(8,128)S(1)}, u32[]{:S(2)}, u32[]{:S(2)}) collective-permute-start(f32[4,8,512]{2,1,0:T(8,128)S(1)} %get-tuple-element.33.refs_0_), channel_id=1, source_target_pairs={{0,2},{1,5},{2,0},{3,7},{4,6},{5,1},{6,4},{7,3},{8,10},{9,13},{10,... | collective-permute-start | bytes 196616 | tf_op jit(solution)/shard_map/ppermute | solution.py:462
  19.6 1.4 %collective-permute-start.8 = (f32[4,8,512]{2,1,0:T(8,128)S(1)}, f32[4,8,512]{2,1,0:T(8,128)S(1)}, u32[]{:S(2)}, u32[]{:S(2)}) collective-permute-start(f32[4,8,512]{2,1,0:T(8,128)S(1)} %get-tuple-element.33.refs_0_), channel_id=1, source_target_pairs={{0,8},{1,7},{2,10},{3,5},{4,12},{5,3},{6,14},{7,1},{8,0},{9,15},{1... | collective-permute-start | bytes 196616 | tf_op jit(solution)/shard_map/ppermute | solution.py:462
  21.0 2.0 %collective-permute-done.7 = f32[4,8,512]{2,1,0:T(8,128)S(1)} collective-permute-done((f32[4,8,512]{2,1,0:T(8,128)S(1)}, f32[4,8,512]{2,1,0:T(8,128)S(1)}, u32[]{:S(2)}, u32[]{:S(2)}) %collective-permute-start.7) | collective-permute-done | bytes 65568 | tf_op jit(solution)/shard_map/ppermute | solution.py:462
  23.0 0.9 %collective-permute-done.8 = f32[4,8,512]{2,1,0:T(8,128)S(1)} collective-permute-done((f32[4,8,512]{2,1,0:T(8,128)S(1)}, f32[4,8,512]{2,1,0:T(8,128)S(1)}, u32[]{:S(2)}, u32[]{:S(2)}) %collective-permute-start.8) | collective-permute-done | bytes 65568 | tf_op jit(solution)/shard_map/ppermute | solution.py:462
  23.9 1.6 %collective-permute-start.9 = (f32[4,8,512]{2,1,0:T(8,128)S(1)}, f32[4,8,512]{2,1,0:T(8,128)S(1)}, u32[]{:S(2)}, u32[]{:S(2)}) collective-permute-start(f32[4,8,512]{2,1,0:T(8,128)S(1)} %select_add_fusion.refs_1_), channel_id=1, source_target_pairs={{0,1},{1,0},{2,3},{3,2},{4,5},{5,4},{6,7},{7,6},{8,9},{9,8},{10,11... | collective-permute-start | bytes 196616 | tf_op jit(solution)/shard_map/ppermute | solution.py:462
  25.5 0.9 %collective-permute-done.9.refs_2_ = f32[4,8,512]{2,1,0:T(8,128)S(1)} collective-permute-done((f32[4,8,512]{2,1,0:T(8,128)S(1)}, f32[4,8,512]{2,1,0:T(8,128)S(1)}, u32[]{:S(2)}, u32[]{:S(2)}) %collective-permute-start.9) | collective-permute-done | bytes 65568 | tf_op jit(solution)/shard_map/ppermute | solution.py:462
  26.4 1.4 %clean.1 = (f32[8,50,2,500]{3,2,1,0:T(2,128)}, f32[8,128]{1,0:T(8,128)}) custom-call(f32[50,2,8,500]{3,2,1,0:T(8,128)S(1)} %get-tuple-element.30.flux, f32[8,128]{1,0:T(8,128)S(1)} %get-tuple-element.32.sky_ref, f32[4,8,512]{2,1,0:T(8,128)S(1)} %get-tuple-element.33.refs_0_, f32[4,8,512]{2,1,0:T(8,128)S(1)} %select_add_fusion.refs_1_, ...), custom_call_target="tpu_custom_call" | custom-call | flops 1000000 | bytes 1000000 | tf_op jit(solution)/shard_map/clean/pallas_call | solution.py:425
  (6 shorter events, 0.0 us)
Async XLA Ops:
  0.6 4.6 %copy-start = (s32[2,40]{1,0:T(2,128)S(1)}, s32[2,40]{1,0:T(2,128)}, u32[]{:S(2)}) copy-start(s32[2,40]{1,0:T(2,128)} %sky_index.1) | copy-start | bytes 964
  2.1 3.1 %collective-permute-start.1 = (f32[6,2,8,500]{3,2,1,0:T(8,128)S(1)}, f32[6,2,8,500]{3,2,1,0:T(8,128)S(1)}, u32[]{:S(2)}, u32[]{:S(2)}) collective-permute-start(f32[6,2,8,500]{3,2,1,0:T(8,128)S(1)} %get-tuple-element.20), channel_id=1, source_target_pairs={{0,1},{1,0},{2,3},{3,2},{4,5},{5,4},{6,7},{7,6},{8,9},{9,8},{10,11... | collective-permute-start | bytes 576008 | tf_op jit(solution)/shard_map/ppermute | solution.py:462
  2.6 7.1 %collective-permute-start = (f32[6,2,8,500]{3,2,1,0:T(8,128)S(1)}, f32[6,2,8,500]{3,2,1,0:T(8,128)S(1)}, u32[]{:S(2)}, u32[]{:S(2)}) collective-permute-start(f32[6,2,8,500]{3,2,1,0:T(8,128)S(1)} %get-tuple-element.19), channel_id=1, source_target_pairs={{0,8},{1,2},{2,1},{3,4},{4,3},{5,6},{6,5},{7,15},{8,0},{9,10},{10,... | collective-permute-start | bytes 576008 | tf_op jit(solution)/shard_map/ppermute | solution.py:462
  10.4 1.2 %collective-permute-start.2 = (f32[2,8,128]{2,1,0:T(8,128)S(1)}, f32[2,8,128]{2,1,0:T(8,128)S(1)}, u32[]{:S(2)}, u32[]{:S(2)}) collective-permute-start(f32[2,8,128]{2,1,0:T(8,128)S(1)} %get-tuple-element.29), channel_id=1, source_target_pairs={{0,1},{1,0},{2,3},{3,2},{4,5},{5,4},{6,7},{7,6},{8,9},{9,8},{10,11... | collective-permute-start | bytes 24584 | tf_op jit(solution)/shard_map/ppermute | solution.py:462
  11.6 5.9 %collective-permute-start.3 = (f32[50,2,8,500]{3,2,1,0:T(8,128)S(1)}, f32[50,2,8,500]{3,2,1,0:T(8,128)S(1)}, u32[]{:S(2)}, u32[]{:S(2)}) collective-permute-start(f32[50,2,8,500]{3,2,1,0:T(8,128)S(1)} %get-tuple-element.30.flux), channel_id=1, source_target_pairs={{0,1},{1,0},{2,3},{3,2},{4,5},{5,4},{6,7},{7,6},{8,9},{9,8},{10,11... | collective-permute-start | bytes 4800008 | tf_op jit(solution)/shard_map/ppermute | solution.py:462
  11.8 3.7 %collective-permute-start.4 = (f32[4,8,128]{2,1,0:T(8,128)S(1)}, f32[4,8,128]{2,1,0:T(8,128)S(1)}, u32[]{:S(2)}, u32[]{:S(2)}) collective-permute-start(f32[4,8,128]{2,1,0:T(8,128)S(1)} %maximum_select_fusion), channel_id=1, source_target_pairs={{0,16},{1,9},{2,18},{3,11},{4,20},{5,13},{6,22},{7,15},{8,24},{9,1... | collective-permute-start | bytes 49160 | tf_op jit(solution)/shard_map/ppermute | solution.py:462
  13.3 4.2 %collective-permute-start.6 = (f32[4,8,128]{2,1,0:T(8,128)S(1)}, f32[4,8,128]{2,1,0:T(8,128)S(1)}, u32[]{:S(2)}, u32[]{:S(2)}) collective-permute-start(f32[4,8,128]{2,1,0:T(8,128)S(1)} %maximum_select_fusion), channel_id=1, source_target_pairs={{0,25},{1,24},{2,27},{3,26},{4,29},{5,28},{6,31},{7,30},{8,17},{9,... | collective-permute-start | bytes 49160 | tf_op jit(solution)/shard_map/ppermute | solution.py:462
  15.5 2.0 %collective-permute-start.5 = (f32[4,8,128]{2,1,0:T(8,128)S(1)}, f32[4,8,128]{2,1,0:T(8,128)S(1)}, u32[]{:S(2)}, u32[]{:S(2)}) collective-permute-start(f32[4,8,128]{2,1,0:T(8,128)S(1)} %collective-permute-done.4), channel_id=1, source_target_pairs={{0,1},{1,0},{2,3},{3,2},{4,5},{5,4},{6,7},{7,6},{8,9},{9,8},{10,11... | collective-permute-start | bytes 49160 | tf_op jit(solution)/shard_map/ppermute | solution.py:462
  18.0 5.0 %collective-permute-start.7 = (f32[4,8,512]{2,1,0:T(8,128)S(1)}, f32[4,8,512]{2,1,0:T(8,128)S(1)}, u32[]{:S(2)}, u32[]{:S(2)}) collective-permute-start(f32[4,8,512]{2,1,0:T(8,128)S(1)} %get-tuple-element.33.refs_0_), channel_id=1, source_target_pairs={{0,2},{1,5},{2,0},{3,7},{4,6},{5,1},{6,4},{7,3},{8,10},{9,13},{10,... | collective-permute-start | bytes 196616 | tf_op jit(solution)/shard_map/ppermute | solution.py:462
  19.6 4.3 %collective-permute-start.8 = (f32[4,8,512]{2,1,0:T(8,128)S(1)}, f32[4,8,512]{2,1,0:T(8,128)S(1)}, u32[]{:S(2)}, u32[]{:S(2)}) collective-permute-start(f32[4,8,512]{2,1,0:T(8,128)S(1)} %get-tuple-element.33.refs_0_), channel_id=1, source_target_pairs={{0,8},{1,7},{2,10},{3,5},{4,12},{5,3},{6,14},{7,1},{8,0},{9,15},{1... | collective-permute-start | bytes 196616 | tf_op jit(solution)/shard_map/ppermute | solution.py:462
  23.9 2.5 %collective-permute-start.9 = (f32[4,8,512]{2,1,0:T(8,128)S(1)}, f32[4,8,512]{2,1,0:T(8,128)S(1)}, u32[]{:S(2)}, u32[]{:S(2)}) collective-permute-start(f32[4,8,512]{2,1,0:T(8,128)S(1)} %select_add_fusion.refs_1_), channel_id=1, source_target_pairs={{0,1},{1,0},{2,3},{3,2},{4,5},{5,4},{6,7},{7,6},{8,9},{9,8},{10,11... | collective-permute-start | bytes 196616 | tf_op jit(solution)/shard_map/ppermute | solution.py:462

commit v8 on v7

--- a/solution.py
+++ b/solution.py
@@ -67,49 +67,58 @@
     return (d3, a34, d4, b3, b4, raw)
 
 
-def edge_kernel(pix, iva, msk, lef, rig, near_out, far_out, bufs, mbuf, sems):
+def edge_kernel(pix, iva, msk, lef, rig, near_out, far_out, head, bufs, mhead, mbuf, sems):
     exposures, rows, specs, fibres = pix.shape
-    odd = lax.rem(lax.axis_index("wave"), 2) == 1
-    for end, start in enumerate((0, rows - HALO)):
-        for e in range(exposures):
-            for slot, ref in enumerate((pix, iva, lef, rig)):
-                pltpu.make_async_copy(
-                    ref.at[e, start : start + HALO], bufs.at[end, slot, :, :, e], sems.at[0, end]
-                ).start()
+    size = head.shape[1]
+    odd = lax.rem(lax.axis_index("wave"), 2)
+    first, last = (1 - odd) * (rows - size), odd * (rows - HALO)
+    for e in range(exposures):
+        for slot, ref in enumerate((pix, iva, lef, rig)):
             pltpu.make_async_copy(
-                msk.at[e, start : start + HALO], mbuf.at[end, :, :, e], sems.at[1, end]
+                ref.at[e, pl.ds(first, size)], head.at[slot, :, :, e], sems.at[0]
             ).start()
-    for end in range(2):
-        pltpu.make_async_copy(bufs.at[end], bufs.at[end], sems.at[0, end]).wait()
-        pltpu.make_async_copy(mbuf.at[end], mbuf.at[end], sems.at[1, end]).wait()
-        order = range(HALO - 1, -1, -1) if end == 0 else range(HALO)
+        pltpu.make_async_copy(msk.at[e, pl.ds(first, size)], mhead.at[:, :, e], sems.at[1]).start()
+    for e in range(exposures):
+        for slot, ref in enumerate((pix, iva, lef, rig)):
+            pltpu.make_async_copy(
+                ref.at[e, pl.ds(last, HALO)], bufs.at[slot, :, :, e], sems.at[2]
+            ).start()
+        pltpu.make_async_copy(msk.at[e, pl.ds(last, HALO)], mbuf.at[:, :, e], sems.at[3]).start()
+    before, after = 3 - odd, 2 + odd
+    pltpu.make_async_copy(head, head, sems.at[0]).wait()
+    pltpu.make_async_copy(mhead, mhead, sems.at[1]).wait()
+    for k in range(size):
         for s in range(specs):
-            p = [bufs[end, 0, k, s] for k in order]
-            w = [weight_of(bufs[end, 1, k, s], mbuf[end, k, s]) for k in order]
-            l = [bufs[end, 2, k, s] for k in order]
-            r = [bufs[end, 3, k, s] for k in order]
-            if end == 0:
-                for slot, value in enumerate(edge_message(p, w, r, l)):
-                    near_out[slot, s] = value
-                continue
-            for slot, value in enumerate(edge_message(p, w, l, r)):
-                top = near_out[slot, s]
-                near_out[slot, s] = jnp.where(odd, top, value)
-                far_out[slot, s] = jnp.where(odd, value, top)
+            head[1, k, s] = weight_of(head[1, k, s], mhead[k, s])
+    order = [odd * k + (1 - odd) * (size - 1 - k) for k in range(HALO - 1, -1, -1)]
+    for s in range(specs):
+        p, w, l, r = [[head[slot, k, s] for k in order] for slot in (0, 1, before, after)]
+        for slot, value in enumerate(edge_message(p, w, r, l)):
+            near_out[slot, s] = value
+    pltpu.make_async_copy(bufs, bufs, sems.at[2]).wait()
+    pltpu.make_async_copy(mbuf, mbuf, sems.at[3]).wait()
+    order = [odd * k + (1 - odd) * (HALO - 1 - k) for k in range(HALO)]
+    for s in range(specs):
+        p, l, r = [[bufs[slot, k, s] for k in order] for slot in (0, before, after)]
+        w = [weight_of(bufs[1, k, s], mbuf[k, s]) for k in order]
+        for slot, value in enumerate(edge_message(p, w, l, r)):
+            far_out[slot, s] = value
 
 
 def edge_call(arrays):
     exposures, rows, specs, fibres = arrays[0].shape
+    size = max(HALO, rows // 5)
     message = in_vmem((PARTS, specs, exposures, fibres))
     return pl.pallas_call(
         edge_kernel,
-        out_shape=(message, message),
+        out_shape=(message, message, in_vmem((4, size, specs, exposures, fibres))),
         in_specs=[HB] * 5,
-        out_specs=(VM, VM),
+        out_specs=(VM, VM, VM),
         scratch_shapes=[
-            pltpu.VMEM((2, 4, HALO, specs, exposures, fibres), F32),
-            pltpu.VMEM((2, HALO, specs, exposures, fibres), jnp.int32),
-            pltpu.SemaphoreType.DMA((2, 2)),
+            pltpu.VMEM((4, HALO, specs, exposures, fibres), F32),
+            pltpu.VMEM((size, specs, exposures, fibres), jnp.int32),
+            pltpu.VMEM((HALO, specs, exposures, fibres), jnp.int32),
+            pltpu.SemaphoreType.DMA((4,)),
         ],
         compiler_params=pltpu.CompilerParams(vmem_limit_bytes=8 * 2**20),
         cost_estimate=pl.CostEstimate(flops=10**6, bytes_accessed=10**6, transcendentals=0),
@@ -118,24 +127,25 @@
 
 
 def forward_kernel(
-    chunks, near, pix, iva, msk, lef, rig, sky_index, lower, lower_far, half, shares, tail, sky_mask, denom, bufs, mbuf, sems
+    chunks, near, head, pix, iva, msk, lef, rig, sky_index, lower, lower_far, half, shares, tail, sky_mask, denom, bufs, mbuf, sems
 ):
     exposures, rows, specs, fibres = pix.shape
+    size = head.shape[1]
     odd = lax.rem(lax.axis_index("wave"), 2)
     spans = range(specs)
-    bounds = [rows * c // chunks for c in range(chunks + 1)]
+    bounds = [0] + [size + (rows - size) * c // chunks for c in range(chunks + 1)]
 
     def place(low, high):
         return pl.ds(odd * low + (1 - odd) * (rows - high), high - low)
 
-    for c in range(chunks):
+    for c in range(1, chunks + 1):
         here = place(bounds[c], bounds[c + 1])
         for e in range(exposures):
             for slot, ref in enumerate((pix, iva, lef, rig)):
                 pltpu.make_async_copy(
-                    ref.at[e, here], bufs.at[slot, here, :, e], sems.at[0, c]
+                    ref.at[e, here], bufs.at[slot, here, :, e], sems.at[0, c - 1]
                 ).start()
-            pltpu.make_async_copy(msk.at[e, here], mbuf.at[here, :, e], sems.at[1, c]).start()
+            pltpu.make_async_copy(msk.at[e, here], mbuf.at[here, :, e], sems.at[1, c - 1]).start()
     lane = lax.broadcasted_iota(jnp.int32, (exposures, fibres), 1)
     for s in spans:
         found = lane == sky_index[s, 0]
@@ -158,17 +168,22 @@
     fars = [[] for _ in spans]
     states = [None] * specs
     total = jnp.zeros((exposures, LANES), F32)
-    for c in range(chunks):
-        here = place(bounds[c], bounds[c + 1])
-        part, mpart = bufs.at[:, here], mbuf.at[here]
-        pltpu.make_async_copy(part, part, sems.at[0, c]).wait()
-        pltpu.make_async_copy(mpart, mpart, sems.at[1, c]).wait()
+    for c in range(chunks + 1):
+        if c > 0:
+            here = place(bounds[c], bounds[c + 1])
+            part, mpart = bufs.at[:, here], mbuf.at[here]
+            pltpu.make_async_copy(part, part, sems.at[0, c - 1]).wait()
+            pltpu.make_async_copy(mpart, mpart, sems.at[1, c - 1]).wait()
         for k in range(bounds[c], bounds[c + 1]):
             row = odd * k + (1 - odd) * (rows - 1 - k)
+            top = odd * k + (1 - odd) * (size - 1 - k)
             diags = []
             for s in spans:
-                p, l, r = bufs[0, row, s], bufs[before, row, s], bufs[after, row, s]
-                w = weight_of(bufs[1, row, s], mbuf[row, s])
+                if c == 0:
+                    p, w, l, r = [head[slot, top, s] for slot in (0, 1, before, after)]
+                else:
+                    p, l, r = bufs[0, row, s], bufs[before, row, s], bufs[after, row, s]
+                    w = weight_of(bufs[1, row, s], mbuf[row, s])
                 wl, wr, wp = w * l, w * r, w * p
                 m = made[s]
                 d, b = m["d1"] + wl * l, m["b1"] + wl * p
@@ -220,9 +235,9 @@
     return f, g, y, (recip(pivot), inv1, g, y, y1)
 
 
-def forward_call(near, arrays, sky_index):
+def forward_call(near, head, arrays, sky_index):
     exposures, rows, specs, fibres = arrays[0].shape
-    chunks = 5
+    chunks = 4
     whole = in_vmem((rows, specs, exposures, fibres))
     return pl.pallas_call(
         functools.partial(forward_kernel, chunks),
@@ -235,7 +250,7 @@
             in_vmem((specs, exposures, fibres)),
             in_vmem((exposures, LANES)),
         ),
-        in_specs=[VM] + [HB] * 5 + [SM],
+        in_specs=[VM] * 2 + [HB] * 5 + [SM],
         out_specs=(VM,) * 7,
         scratch_shapes=[
             pltpu.VMEM((4, rows, specs, exposures, fibres), F32),
@@ -245,7 +260,7 @@
         compiler_params=pltpu.CompilerParams(vmem_limit_bytes=24 * 2**20),
         cost_estimate=pl.CostEstimate(flops=10**7, bytes_accessed=10**7, transcendentals=0),
         name="forward",
-    )(near, *arrays, sky_index)
+    )(near, head, *arrays, sky_index)
 
 
 def backward_kernel(wave, far, lower, lower_far, half, shares, tail, sky_mask, denom, flux, sums):
@@ -473,10 +488,10 @@
     def other_core(s, i):
         return (s, i ^ 1)
 
-    near, far = edge_call(hbm)
+    near, far, head = edge_call(hbm)
     far = swap(far, lambda s, i: (s, i + 1 if i % 2 else i - 1))
     near = swap(near, other_core)
-    factors = forward_call(near, hbm, sky_index)
+    factors = forward_call(near, head, hbm, sky_index)
     flux, sums = backward_call(wave, far, factors)
     got = swap(sums, other_core)
     flux, got = lax.optimization_barrier((flux, got))
@@ -492,9 +507,9 @@
             sums = sums + swap(sums, lambda s, i: (s ^ k, i))
     regress, sky = regress_call(total_rows, flux, other, sums)
     if wave == 8:
+        third = swap(regress, lambda s, i: (s, i ^ 6 if i % 2 else -1))
         first = swap(regress, lambda s, i: (s, i ^ (4 if i % 2 else 2)))
-        third = swap(regress, lambda s, i: (s, i ^ 6 if i % 2 else -1))
-        fetched = first + jnp.where(odd, third, 0.0)
+        fetched = jnp.where(odd, third, 0.0) + first
         terms = [regress, fetched, swap(fetched, other_core)]
     else:
         for k in powers(2, wave):

time: 28 us -> 27.8 us (level)
    pallas_call x1, Pallas kernels: 4.48 us -> 4.01 us  [forward_call(): pl.pallas_call(functools.partial(forward_kernel, chunks), out_shape=(whol...]
    pallas_call x1, Pallas kernels: 1.48 us -> 1.76 us  [edge_call(): pl.pallas_call(edge_kernel, out_shape=(message, message, in_vmem((4, size...]
  transfers between devices with their start and end apart: 10 -> 10, of which waited for: 6 -> 6; matrix products, arithmetic and copies ran while one was open for 0% -> 0% of each run, Pallas kernels for 16% -> 15%
where the time goes in v8:
time: 27.8 us; the launch traced here: 27.6 us
  starting transfers between devices  10.8 us (39%)
  Pallas kernels  8.27 us (30%)
  waiting for transfers between devices  7.75 us (28%)
  between operations  0.69 us (2%)
    ppermute x10, starting transfers between devices, swap(): return lax.ppermute(values, ('spec', 'wave'), pairs)  10.8 us
    ppermute x10, waiting for transfers between devices, swap(): return lax.ppermute(values, ('spec', 'wave'), pairs)  7.75 us
    pallas_call x1, Pallas kernels, forward_call(): pl.pallas_call(functools.partial(forward_kernel, chunks), out_shape=(whol...  4.01 us
    pallas_call x1, Pallas kernels, edge_call(): pl.pallas_call(edge_kernel, out_shape=(message, message, in_vmem((4, size...  1.76 us
    pallas_call x1, Pallas kernels, clean_call(): pl.pallas_call(functools.partial(clean_kernel, total_rows), out_shape=(ja...  1.38 us
    pallas_call x1, Pallas kernels, backward_call(): pl.pallas_call(functools.partial(backward_kernel, wave), out_shape=(in_vm...  0.69 us
  transfers between devices with their start and end apart: 10, of which 6 were waited for; matrix products, arithmetic and copies ran while one was open for 0% of the time, Pallas kernels for 15%

profile of v8, /device:TPU:0, one launch (start us, length us, event | category | flops | bytes accessed | tf_op | source)
XLA Modules:
  0.0 27.6 jit_solution(734196982872986258)
XLA Ops:
  0.6 1.8 %edges.1 = (f32[6,2,8,500]{3,2,1,0:T(8,128)S(1)}, f32[6,2,8,500]{3,2,1,0:T(8,128)S(1)}, f32[4,10,2,8,500]{4,3,2,1,0:T(8,128)S(1)}) custom-call(f32[8,50,2,500]{3,2,1,0:T(2,128)} %bitcast.7, f32[8,50,2,500]{3,2,1,0:T(2,128)} %bitcast.9, s32[8,50,2,500]{3,2,1,0:T(2,128)} %bitcast.11, f32[8,50,2,500]{3,2,1,0:T(2,128)} %bitcast.13, f32[8,50,2,500]{3,2,1,0:T(2,128)} %bitcast.15), custom_call_target="tpu_custom_call" | custom-call | flops 1000000 | bytes 1000000 | tf_op jit(solution)/shard_map/edges/pallas_call | solution.py:112
  2.4 0.5 %collective-permute-start.1 = (f32[6,2,8,500]{3,2,1,0:T(8,128)S(1)}, f32[6,2,8,500]{3,2,1,0:T(8,128)S(1)}, u32[]{:S(2)}, u32[]{:S(2)}) collective-permute-start(f32[6,2,8,500]{3,2,1,0:T(8,128)S(1)} %get-tuple-element.21), channel_id=1, source_target_pairs={{0,1},{1,0},{2,3},{3,2},{4,5},{5,4},{6,7},{7,6},{8,9},{9,8},{10,11... | collective-permute-start | bytes 576008 | tf_op jit(solution)/shard_map/ppermute | solution.py:477
  2.9 2.6 %collective-permute-start = (f32[6,2,8,500]{3,2,1,0:T(8,128)S(1)}, f32[6,2,8,500]{3,2,1,0:T(8,128)S(1)}, u32[]{:S(2)}, u32[]{:S(2)}) collective-permute-start(f32[6,2,8,500]{3,2,1,0:T(8,128)S(1)} %get-tuple-element.20), channel_id=1, source_target_pairs={{0,8},{1,2},{2,1},{3,4},{4,3},{5,6},{6,5},{7,15},{8,0},{9,10},{10,... | collective-permute-start | bytes 576008 | tf_op jit(solution)/shard_map/ppermute | solution.py:477
  5.5 0.0 collective-permute-done.1.near
  5.5 4.0 %forward.1 = (f32[50,2,8,500]{3,2,1,0:T(8,128)S(1)}, f32[50,2,8,500]{3,2,1,0:T(8,128)S(1)}, f32[50,2,8,500]{3,2,1,0:T(8,128)S(1)}, f32[50,2,8,500]{3,2,1,0:T(8,1...) custom-call(f32[6,2,8,500]{3,2,1,0:T(8,128)S(1)} %collective-permute-done.1.near, ...), custom_call_target="tpu_custom_call" | custom-call | flops 10000000 | bytes 10000000 | tf_op jit(solution)/shard_map/forward/pallas_call | solution.py:242
  9.5 0.0 collective-permute-done.far
  9.5 0.7 %backward.1 = (f32[50,2,8,500]{3,2,1,0:T(8,128)S(1)}, f32[2,8,128]{2,1,0:T(8,128)S(1)}) custom-call(f32[6,2,8,500]{3,2,1,0:T(8,128)S(1)} %collective-permute-done.far, f32[50,2,8,500]{3,2,1,0:T(8,128)S(1)} %get-tuple-element.23.lower, f32[50,2,8,500]{3,2,1,0:T(8,128)S(1)} %get-tuple-element.24.lower_far, f32[50,2,8,500]{3,2,1,0:T(8,128)S(1)} %get-tuple-element.25.half, ...), custom_call_target="tpu_custom_call" | custom-call | flops 10000000 | bytes 10000000 | tf_op jit(solution)/shard_map/backward/pallas_call | solution.py:321
  10.2 0.2 collective-permute-start.2
  10.4 1.0 %collective-permute-done.2 = f32[2,8,128]{2,1,0:T(8,128)S(1)} collective-permute-done((f32[2,8,128]{2,1,0:T(8,128)S(1)}, f32[2,8,128]{2,1,0:T(8,128)S(1)}, u32[]{:S(2)}, u32[]{:S(2)}) %collective-permute-start.2) | collective-permute-done | bytes 8224 | tf_op jit(solution)/shard_map/ppermute | solution.py:477
  11.4 0.2 collective-permute-start.3
  11.6 1.6 %collective-permute-start.4 = (f32[4,8,128]{2,1,0:T(8,128)S(1)}, f32[4,8,128]{2,1,0:T(8,128)S(1)}, u32[]{:S(2)}, u32[]{:S(2)}) collective-permute-start(f32[4,8,128]{2,1,0:T(8,128)S(1)} %maximum_select_fusion), channel_id=1, source_target_pairs={{0,16},{1,9},{2,18},{3,11},{4,20},{5,13},{6,22},{7,15},{8,24},{9,1... | collective-permute-start | bytes 49160 | tf_op jit(solution)/shard_map/ppermute | solution.py:477
  13.2 1.1 %collective-permute-start.6 = (f32[4,8,128]{2,1,0:T(8,128)S(1)}, f32[4,8,128]{2,1,0:T(8,128)S(1)}, u32[]{:S(2)}, u32[]{:S(2)}) collective-permute-start(f32[4,8,128]{2,1,0:T(8,128)S(1)} %maximum_select_fusion), channel_id=1, source_target_pairs={{0,25},{1,24},{2,27},{3,26},{4,29},{5,28},{6,31},{7,30},{8,17},{9,... | collective-permute-start | bytes 49160 | tf_op jit(solution)/shard_map/ppermute | solution.py:477
  14.4 1.0 %collective-permute-done.4 = f32[4,8,128]{2,1,0:T(8,128)S(1)} collective-permute-done((f32[4,8,128]{2,1,0:T(8,128)S(1)}, f32[4,8,128]{2,1,0:T(8,128)S(1)}, u32[]{:S(2)}, u32[]{:S(2)}) %collective-permute-start.4) | collective-permute-done | bytes 16416 | tf_op jit(solution)/shard_map/ppermute | solution.py:477
  15.4 1.9 %collective-permute-done.6 = f32[4,8,128]{2,1,0:T(8,128)S(1)} collective-permute-done((f32[4,8,128]{2,1,0:T(8,128)S(1)}, f32[4,8,128]{2,1,0:T(8,128)S(1)}, u32[]{:S(2)}, u32[]{:S(2)}) %collective-permute-start.6) | collective-permute-done | bytes 16416 | tf_op jit(solution)/shard_map/ppermute | solution.py:477
  17.3 0.0 collective-permute-done.5
  17.3 0.0 collective-permute-done.3.other
  17.3 0.4 %regress.1 = (f32[4,8,512]{2,1,0:T(8,128)S(1)}, f32[8,128]{1,0:T(8,128)S(1)}) custom-call(f32[50,2,8,500]{3,2,1,0:T(8,128)S(1)} %get-tuple-element.32.flux, f32[50,2,8,500]{3,2,1,0:T(8,128)S(1)} %collective-permute-done.3.other, f32[4,8,128]{2,1,0:T(8,128)S(1)} %add_add_fusion.sums), custom_call_target="tpu_custom_call" | custom-call | flops 1000000 | bytes 1000000 | tf_op jit(solution)/shard_map/regress/pallas_call | solution.py:381
  17.8 1.6 %collective-permute-start.7 = (f32[4,8,512]{2,1,0:T(8,128)S(1)}, f32[4,8,512]{2,1,0:T(8,128)S(1)}, u32[]{:S(2)}, u32[]{:S(2)}) collective-permute-start(f32[4,8,512]{2,1,0:T(8,128)S(1)} %get-tuple-element.35.refs_0_), channel_id=1, source_target_pairs={{0,8},{1,7},{2,10},{3,5},{4,12},{5,3},{6,14},{7,1},{8,0},{9,15},{1... | collective-permute-start | bytes 196616 | tf_op jit(solution)/shard_map/ppermute | solution.py:477
  19.3 1.5 %collective-permute-start.8 = (f32[4,8,512]{2,1,0:T(8,128)S(1)}, f32[4,8,512]{2,1,0:T(8,128)S(1)}, u32[]{:S(2)}, u32[]{:S(2)}) collective-permute-start(f32[4,8,512]{2,1,0:T(8,128)S(1)} %get-tuple-element.35.refs_0_), channel_id=1, source_target_pairs={{0,2},{1,5},{2,0},{3,7},{4,6},{5,1},{6,4},{7,3},{8,10},{9,13},{10,... | collective-permute-start | bytes 196616 | tf_op jit(solution)/shard_map/ppermute | solution.py:477
  20.8 1.3 %collective-permute-done.7 = f32[4,8,512]{2,1,0:T(8,128)S(1)} collective-permute-done((f32[4,8,512]{2,1,0:T(8,128)S(1)}, f32[4,8,512]{2,1,0:T(8,128)S(1)}, u32[]{:S(2)}, u32[]{:S(2)}) %collective-permute-start.7) | collective-permute-done | bytes 65568 | tf_op jit(solution)/shard_map/ppermute | solution.py:477
  22.1 1.6 %collective-permute-done.8 = f32[4,8,512]{2,1,0:T(8,128)S(1)} collective-permute-done((f32[4,8,512]{2,1,0:T(8,128)S(1)}, f32[4,8,512]{2,1,0:T(8,128)S(1)}, u32[]{:S(2)}, u32[]{:S(2)}) %collective-permute-start.8) | collective-permute-done | bytes 65568 | tf_op jit(solution)/shard_map/ppermute | solution.py:477
  23.8 1.5 %collective-permute-start.9 = (f32[4,8,512]{2,1,0:T(8,128)S(1)}, f32[4,8,512]{2,1,0:T(8,128)S(1)}, u32[]{:S(2)}, u32[]{:S(2)}) collective-permute-start(f32[4,8,512]{2,1,0:T(8,128)S(1)} %select_add_fusion.refs_1_), channel_id=1, source_target_pairs={{0,1},{1,0},{2,3},{3,2},{4,5},{5,4},{6,7},{7,6},{8,9},{9,8},{10,11... | collective-permute-start | bytes 196616 | tf_op jit(solution)/shard_map/ppermute | solution.py:477
  25.3 0.9 %collective-permute-done.9.refs_2_ = f32[4,8,512]{2,1,0:T(8,128)S(1)} collective-permute-done((f32[4,8,512]{2,1,0:T(8,128)S(1)}, f32[4,8,512]{2,1,0:T(8,128)S(1)}, u32[]{:S(2)}, u32[]{:S(2)}) %collective-permute-start.9) | collective-permute-done | bytes 65568 | tf_op jit(solution)/shard_map/ppermute | solution.py:477
  26.2 1.4 %clean.1 = (f32[8,50,2,500]{3,2,1,0:T(2,128)}, f32[8,128]{1,0:T(8,128)}) custom-call(f32[50,2,8,500]{3,2,1,0:T(8,128)S(1)} %get-tuple-element.32.flux, f32[8,128]{1,0:T(8,128)S(1)} %get-tuple-element.34.sky_ref, f32[4,8,512]{2,1,0:T(8,128)S(1)} %get-tuple-element.35.refs_0_, f32[4,8,512]{2,1,0:T(8,128)S(1)} %select_add_fusion.refs_1_, ...), custom_call_target="tpu_custom_call" | custom-call | flops 1000000 | bytes 1000000 | tf_op jit(solution)/shard_map/clean/pallas_call | solution.py:440
  (6 shorter events, 0.0 us)
Async XLA Ops:
  0.6 4.9 %copy-start = (s32[2,40]{1,0:T(2,128)S(1)}, s32[2,40]{1,0:T(2,128)}, u32[]{:S(2)}) copy-start(s32[2,40]{1,0:T(2,128)} %sky_index.1) | copy-start | bytes 964
  2.4 3.1 %collective-permute-start.1 = (f32[6,2,8,500]{3,2,1,0:T(8,128)S(1)}, f32[6,2,8,500]{3,2,1,0:T(8,128)S(1)}, u32[]{:S(2)}, u32[]{:S(2)}) collective-permute-start(f32[6,2,8,500]{3,2,1,0:T(8,128)S(1)} %get-tuple-element.21), channel_id=1, source_target_pairs={{0,1},{1,0},{2,3},{3,2},{4,5},{5,4},{6,7},{7,6},{8,9},{9,8},{10,11... | collective-permute-start | bytes 576008 | tf_op jit(solution)/shard_map/ppermute | solution.py:477
  2.9 6.6 %collective-permute-start = (f32[6,2,8,500]{3,2,1,0:T(8,128)S(1)}, f32[6,2,8,500]{3,2,1,0:T(8,128)S(1)}, u32[]{:S(2)}, u32[]{:S(2)}) collective-permute-start(f32[6,2,8,500]{3,2,1,0:T(8,128)S(1)} %get-tuple-element.20), channel_id=1, source_target_pairs={{0,8},{1,2},{2,1},{3,4},{4,3},{5,6},{6,5},{7,15},{8,0},{9,10},{10,... | collective-permute-start | bytes 576008 | tf_op jit(solution)/shard_map/ppermute | solution.py:477
  10.2 1.2 %collective-permute-start.2 = (f32[2,8,128]{2,1,0:T(8,128)S(1)}, f32[2,8,128]{2,1,0:T(8,128)S(1)}, u32[]{:S(2)}, u32[]{:S(2)}) collective-permute-start(f32[2,8,128]{2,1,0:T(8,128)S(1)} %get-tuple-element.31), channel_id=1, source_target_pairs={{0,1},{1,0},{2,3},{3,2},{4,5},{5,4},{6,7},{7,6},{8,9},{9,8},{10,11... | collective-permute-start | bytes 24584 | tf_op jit(solution)/shard_map/ppermute | solution.py:477
  11.4 5.9 %collective-permute-start.3 = (f32[50,2,8,500]{3,2,1,0:T(8,128)S(1)}, f32[50,2,8,500]{3,2,1,0:T(8,128)S(1)}, u32[]{:S(2)}, u32[]{:S(2)}) collective-permute-start(f32[50,2,8,500]{3,2,1,0:T(8,128)S(1)} %get-tuple-element.32.flux), channel_id=1, source_target_pairs={{0,1},{1,0},{2,3},{3,2},{4,5},{5,4},{6,7},{7,6},{8,9},{9,8},{10,11... | collective-permute-start | bytes 4800008 | tf_op jit(solution)/shard_map/ppermute | solution.py:477
  11.6 3.7 %collective-permute-start.4 = (f32[4,8,128]{2,1,0:T(8,128)S(1)}, f32[4,8,128]{2,1,0:T(8,128)S(1)}, u32[]{:S(2)}, u32[]{:S(2)}) collective-permute-start(f32[4,8,128]{2,1,0:T(8,128)S(1)} %maximum_select_fusion), channel_id=1, source_target_pairs={{0,16},{1,9},{2,18},{3,11},{4,20},{5,13},{6,22},{7,15},{8,24},{9,1... | collective-permute-start | bytes 49160 | tf_op jit(solution)/shard_map/ppermute | solution.py:477
  13.2 4.1 %collective-permute-start.6 = (f32[4,8,128]{2,1,0:T(8,128)S(1)}, f32[4,8,128]{2,1,0:T(8,128)S(1)}, u32[]{:S(2)}, u32[]{:S(2)}) collective-permute-start(f32[4,8,128]{2,1,0:T(8,128)S(1)} %maximum_select_fusion), channel_id=1, source_target_pairs={{0,25},{1,24},{2,27},{3,26},{4,29},{5,28},{6,31},{7,30},{8,17},{9,... | collective-permute-start | bytes 49160 | tf_op jit(solution)/shard_map/ppermute | solution.py:477
  15.4 2.0 %collective-permute-start.5 = (f32[4,8,128]{2,1,0:T(8,128)S(1)}, f32[4,8,128]{2,1,0:T(8,128)S(1)}, u32[]{:S(2)}, u32[]{:S(2)}) collective-permute-start(f32[4,8,128]{2,1,0:T(8,128)S(1)} %collective-permute-done.4), channel_id=1, source_target_pairs={{0,1},{1,0},{2,3},{3,2},{4,5},{5,4},{6,7},{7,6},{8,9},{9,8},{10,11... | collective-permute-start | bytes 49160 | tf_op jit(solution)/shard_map/ppermute | solution.py:477
  17.8 4.3 %collective-permute-start.7 = (f32[4,8,512]{2,1,0:T(8,128)S(1)}, f32[4,8,512]{2,1,0:T(8,128)S(1)}, u32[]{:S(2)}, u32[]{:S(2)}) collective-permute-start(f32[4,8,512]{2,1,0:T(8,128)S(1)} %get-tuple-element.35.refs_0_), channel_id=1, source_target_pairs={{0,8},{1,7},{2,10},{3,5},{4,12},{5,3},{6,14},{7,1},{8,0},{9,15},{1... | collective-permute-start | bytes 196616 | tf_op jit(solution)/shard_map/ppermute | solution.py:477
  19.3 4.4 %collective-permute-start.8 = (f32[4,8,512]{2,1,0:T(8,128)S(1)}, f32[4,8,512]{2,1,0:T(8,128)S(1)}, u32[]{:S(2)}, u32[]{:S(2)}) collective-permute-start(f32[4,8,512]{2,1,0:T(8,128)S(1)} %get-tuple-element.35.refs_0_), channel_id=1, source_target_pairs={{0,2},{1,5},{2,0},{3,7},{4,6},{5,1},{6,4},{7,3},{8,10},{9,13},{10,... | collective-permute-start | bytes 196616 | tf_op jit(solution)/shard_map/ppermute | solution.py:477
  23.8 2.4 %collective-permute-start.9 = (f32[4,8,512]{2,1,0:T(8,128)S(1)}, f32[4,8,512]{2,1,0:T(8,128)S(1)}, u32[]{:S(2)}, u32[]{:S(2)}) collective-permute-start(f32[4,8,512]{2,1,0:T(8,128)S(1)} %select_add_fusion.refs_1_), channel_id=1, source_target_pairs={{0,1},{1,0},{2,3},{3,2},{4,5},{5,4},{6,7},{7,6},{8,9},{9,8},{10,11... | collective-permute-start | bytes 196616 | tf_op jit(solution)/shard_map/ppermute | solution.py:477

commit v9 on v8

--- a/solution.py
+++ b/solution.py
@@ -11,6 +11,8 @@
 RIDGE = 1.0
 HALO = 4
 PARTS = 6
+TAIL = 13
+CUTS = (0, 14, 26, 35, 40)
 LANES = 128
 
 F32 = jnp.float32
@@ -127,18 +129,18 @@
 
 
 def forward_kernel(
-    chunks, near, head, pix, iva, msk, lef, rig, sky_index, lower, lower_far, half, shares, tail, sky_mask, denom, bufs, mbuf, sems
+    near, head, pix, iva, msk, lef, rig, sky_index, lower, lower_far, half, shares, tail, sky_mask, denom, bufs, mbuf, sems
 ):
     exposures, rows, specs, fibres = pix.shape
     size = head.shape[1]
     odd = lax.rem(lax.axis_index("wave"), 2)
     spans = range(specs)
-    bounds = [0] + [size + (rows - size) * c // chunks for c in range(chunks + 1)]
+    bounds = [0] + [size + (rows - size) * part // 40 for part in CUTS]
 
     def place(low, high):
         return pl.ds(odd * low + (1 - odd) * (rows - high), high - low)
 
-    for c in range(1, chunks + 1):
+    for c in range(1, len(CUTS)):
         here = place(bounds[c], bounds[c + 1])
         for e in range(exposures):
             for slot, ref in enumerate((pix, iva, lef, rig)):
@@ -168,7 +170,7 @@
     fars = [[] for _ in spans]
     states = [None] * specs
     total = jnp.zeros((exposures, LANES), F32)
-    for c in range(chunks + 1):
+    for c in range(len(CUTS)):
         if c > 0:
             here = place(bounds[c], bounds[c + 1])
             part, mpart = bufs.at[:, here], mbuf.at[here]
@@ -222,9 +224,6 @@
     denom[...] = share(rows - 1, [made[s]["d1"] for s in spans], total)
 
 
-TAIL = 13
-
-
 def eliminate(state, d, a, b, far_a):
     inv1, inv2, mult1, y1, y2 = state
     f = far_a * inv2
@@ -237,10 +236,10 @@
 
 def forward_call(near, head, arrays, sky_index):
     exposures, rows, specs, fibres = arrays[0].shape
-    chunks = 4
+    chunks = len(CUTS) - 1
     whole = in_vmem((rows, specs, exposures, fibres))
     return pl.pallas_call(
-        functools.partial(forward_kernel, chunks),
+        forward_kernel,
         out_shape=(
             whole,
             whole,
@@ -507,9 +506,9 @@
             sums = sums + swap(sums, lambda s, i: (s ^ k, i))
     regress, sky = regress_call(total_rows, flux, other, sums)
     if wave == 8:
-        third = swap(regress, lambda s, i: (s, i ^ 6 if i % 2 else -1))
-        first = swap(regress, lambda s, i: (s, i ^ (4 if i % 2 else 2)))
-        fetched = jnp.where(odd, third, 0.0) + first
+        first = swap(regress, lambda s, i: (s, i ^ (6 if i % 2 else 2)))
+        third = swap(regress, lambda s, i: (s, i ^ 4 if i % 2 else -1))
+        fetched = first + jnp.where(odd, third, 0.0)
         terms = [regress, fetched, swap(fetched, other_core)]
     else:
         for k in powers(2, wave):

time: 27.8 us -> 28 us (level)
  transfers between devices with their start and end apart: 10 -> 10, of which waited for: 6 -> 6; matrix products, arithmetic and copies ran while one was open for 0% -> 0% of each run, Pallas kernels for 15% -> 14%
where the time goes in v9:
time: 28 us; the launch traced here: 27.7 us
  starting transfers between devices  11 us (39%)
  Pallas kernels  8.22 us (29%)
  waiting for transfers between devices  7.7 us (28%)
  between operations  0.69 us (2%)
    ppermute x10, starting transfers between devices, swap(): return lax.ppermute(values, ('spec', 'wave'), pairs)  11 us
    ppermute x10, waiting for transfers between devices, swap(): return lax.ppermute(values, ('spec', 'wave'), pairs)  7.7 us
    pallas_call x1, Pallas kernels, forward_call(): pl.pallas_call(forward_kernel, out_shape=(whole, whole, whole, whole, in_...  3.96 us
    pallas_call x1, Pallas kernels, edge_call(): pl.pallas_call(edge_kernel, out_shape=(message, message, in_vmem((4, size...  1.76 us
    pallas_call x1, Pallas kernels, clean_call(): pl.pallas_call(functools.partial(clean_kernel, total_rows), out_shape=(ja...  1.38 us
    pallas_call x1, Pallas kernels, backward_call(): pl.pallas_call(functools.partial(backward_kernel, wave), out_shape=(in_vm...  0.69 us
  transfers between devices with their start and end apart: 10, of which 6 were waited for; matrix products, arithmetic and copies ran while one was open for 0% of the time, Pallas kernels for 14%

profile of v9, /device:TPU:0, one launch (start us, length us, event | category | flops | bytes accessed | tf_op | source)
XLA Modules:
  0.0 27.7 jit_solution(4274534492980556828)
XLA Ops:
  0.6 1.8 %edges.1 = (f32[6,2,8,500]{3,2,1,0:T(8,128)S(1)}, f32[6,2,8,500]{3,2,1,0:T(8,128)S(1)}, f32[4,10,2,8,500]{4,3,2,1,0:T(8,128)S(1)}) custom-call(f32[8,50,2,500]{3,2,1,0:T(2,128)} %bitcast.7, f32[8,50,2,500]{3,2,1,0:T(2,128)} %bitcast.9, s32[8,50,2,500]{3,2,1,0:T(2,128)} %bitcast.11, f32[8,50,2,500]{3,2,1,0:T(2,128)} %bitcast.13, f32[8,50,2,500]{3,2,1,0:T(2,128)} %bitcast.15), custom_call_target="tpu_custom_call" | custom-call | flops 1000000 | bytes 1000000 | tf_op jit(solution)/shard_map/edges/pallas_call | solution.py:114
  2.4 0.5 %collective-permute-start.1 = (f32[6,2,8,500]{3,2,1,0:T(8,128)S(1)}, f32[6,2,8,500]{3,2,1,0:T(8,128)S(1)}, u32[]{:S(2)}, u32[]{:S(2)}) collective-permute-start(f32[6,2,8,500]{3,2,1,0:T(8,128)S(1)} %get-tuple-element.21), channel_id=1, source_target_pairs={{0,1},{1,0},{2,3},{3,2},{4,5},{5,4},{6,7},{7,6},{8,9},{9,8},{10,11... | collective-permute-start | bytes 576008 | tf_op jit(solution)/shard_map/ppermute | solution.py:476
  2.9 2.6 %collective-permute-start = (f32[6,2,8,500]{3,2,1,0:T(8,128)S(1)}, f32[6,2,8,500]{3,2,1,0:T(8,128)S(1)}, u32[]{:S(2)}, u32[]{:S(2)}) collective-permute-start(f32[6,2,8,500]{3,2,1,0:T(8,128)S(1)} %get-tuple-element.20), channel_id=1, source_target_pairs={{0,8},{1,2},{2,1},{3,4},{4,3},{5,6},{6,5},{7,15},{8,0},{9,10},{10,... | collective-permute-start | bytes 576008 | tf_op jit(solution)/shard_map/ppermute | solution.py:476
  5.5 0.0 collective-permute-done.1.near
  5.5 4.0 %forward.1 = (f32[50,2,8,500]{3,2,1,0:T(8,128)S(1)}, f32[50,2,8,500]{3,2,1,0:T(8,128)S(1)}, f32[50,2,8,500]{3,2,1,0:T(8,128)S(1)}, f32[50,2,8,500]{3,2,1,0:T(8,1...) custom-call(f32[6,2,8,500]{3,2,1,0:T(8,128)S(1)} %collective-permute-done.1.near, ...), custom_call_target="tpu_custom_call" | custom-call | flops 10000000 | bytes 10000000 | tf_op jit(solution)/shard_map/forward/pallas_call | solution.py:241
  9.5 0.0 collective-permute-done.far
  9.5 0.7 %backward.1 = (f32[50,2,8,500]{3,2,1,0:T(8,128)S(1)}, f32[2,8,128]{2,1,0:T(8,128)S(1)}) custom-call(f32[6,2,8,500]{3,2,1,0:T(8,128)S(1)} %collective-permute-done.far, f32[50,2,8,500]{3,2,1,0:T(8,128)S(1)} %get-tuple-element.23.lower, f32[50,2,8,500]{3,2,1,0:T(8,128)S(1)} %get-tuple-element.24.lower_far, f32[50,2,8,500]{3,2,1,0:T(8,128)S(1)} %get-tuple-element.25.half, ...), custom_call_target="tpu_custom_call" | custom-call | flops 10000000 | bytes 10000000 | tf_op jit(solution)/shard_map/backward/pallas_call | solution.py:320
  10.2 0.2 collective-permute-start.2
  10.4 1.0 %collective-permute-done.2 = f32[2,8,128]{2,1,0:T(8,128)S(1)} collective-permute-done((f32[2,8,128]{2,1,0:T(8,128)S(1)}, f32[2,8,128]{2,1,0:T(8,128)S(1)}, u32[]{:S(2)}, u32[]{:S(2)}) %collective-permute-start.2) | collective-permute-done | bytes 8224 | tf_op jit(solution)/shard_map/ppermute | solution.py:476
  11.4 0.2 collective-permute-start.3
  11.6 1.7 %collective-permute-start.4 = (f32[4,8,128]{2,1,0:T(8,128)S(1)}, f32[4,8,128]{2,1,0:T(8,128)S(1)}, u32[]{:S(2)}, u32[]{:S(2)}) collective-permute-start(f32[4,8,128]{2,1,0:T(8,128)S(1)} %maximum_select_fusion), channel_id=1, source_target_pairs={{0,16},{1,9},{2,18},{3,11},{4,20},{5,13},{6,22},{7,15},{8,24},{9,1... | collective-permute-start | bytes 49160 | tf_op jit(solution)/shard_map/ppermute | solution.py:476
  13.2 1.1 %collective-permute-start.6 = (f32[4,8,128]{2,1,0:T(8,128)S(1)}, f32[4,8,128]{2,1,0:T(8,128)S(1)}, u32[]{:S(2)}, u32[]{:S(2)}) collective-permute-start(f32[4,8,128]{2,1,0:T(8,128)S(1)} %maximum_select_fusion), channel_id=1, source_target_pairs={{0,25},{1,24},{2,27},{3,26},{4,29},{5,28},{6,31},{7,30},{8,17},{9,... | collective-permute-start | bytes 49160 | tf_op jit(solution)/shard_map/ppermute | solution.py:476
  14.4 0.9 %collective-permute-done.4 = f32[4,8,128]{2,1,0:T(8,128)S(1)} collective-permute-done((f32[4,8,128]{2,1,0:T(8,128)S(1)}, f32[4,8,128]{2,1,0:T(8,128)S(1)}, u32[]{:S(2)}, u32[]{:S(2)}) %collective-permute-start.4) | collective-permute-done | bytes 16416 | tf_op jit(solution)/shard_map/ppermute | solution.py:476
  15.3 0.0 collective-permute-start.5
  15.3 2.0 %collective-permute-done.6 = f32[4,8,128]{2,1,0:T(8,128)S(1)} collective-permute-done((f32[4,8,128]{2,1,0:T(8,128)S(1)}, f32[4,8,128]{2,1,0:T(8,128)S(1)}, u32[]{:S(2)}, u32[]{:S(2)}) %collective-permute-start.6) | collective-permute-done | bytes 16416 | tf_op jit(solution)/shard_map/ppermute | solution.py:476
  17.3 0.0 collective-permute-done.3.other
  17.3 0.4 %regress.1 = (f32[4,8,512]{2,1,0:T(8,128)S(1)}, f32[8,128]{1,0:T(8,128)S(1)}) custom-call(f32[50,2,8,500]{3,2,1,0:T(8,128)S(1)} %get-tuple-element.32.flux, f32[50,2,8,500]{3,2,1,0:T(8,128)S(1)} %collective-permute-done.3.other, f32[4,8,128]{2,1,0:T(8,128)S(1)} %add_add_fusion.sums), custom_call_target="tpu_custom_call" | custom-call | flops 1000000 | bytes 1000000 | tf_op jit(solution)/shard_map/regress/pallas_call | solution.py:380
  17.8 1.6 %collective-permute-start.7 = (f32[4,8,512]{2,1,0:T(8,128)S(1)}, f32[4,8,512]{2,1,0:T(8,128)S(1)}, u32[]{:S(2)}, u32[]{:S(2)}) collective-permute-start(f32[4,8,512]{2,1,0:T(8,128)S(1)} %get-tuple-element.35.refs_0_), channel_id=1, source_target_pairs={{0,2},{1,7},{2,0},{3,5},{4,6},{5,3},{6,4},{7,1},{8,10},{9,15},{10,... | collective-permute-start | bytes 196616 | tf_op jit(solution)/shard_map/ppermute | solution.py:476
  19.4 1.4 %collective-permute-start.8 = (f32[4,8,512]{2,1,0:T(8,128)S(1)}, f32[4,8,512]{2,1,0:T(8,128)S(1)}, u32[]{:S(2)}, u32[]{:S(2)}) collective-permute-start(f32[4,8,512]{2,1,0:T(8,128)S(1)} %get-tuple-element.35.refs_0_), channel_id=1, source_target_pairs={{0,8},{1,5},{2,10},{3,7},{4,12},{5,1},{6,14},{7,3},{8,0},{9,13},{1... | collective-permute-start | bytes 196616 | tf_op jit(solution)/shard_map/ppermute | solution.py:476
  20.8 1.3 %collective-permute-done.7 = f32[4,8,512]{2,1,0:T(8,128)S(1)} collective-permute-done((f32[4,8,512]{2,1,0:T(8,128)S(1)}, f32[4,8,512]{2,1,0:T(8,128)S(1)}, u32[]{:S(2)}, u32[]{:S(2)}) %collective-permute-start.7) | collective-permute-done | bytes 65568 | tf_op jit(solution)/shard_map/ppermute | solution.py:476
  22.1 1.5 %collective-permute-done.8 = f32[4,8,512]{2,1,0:T(8,128)S(1)} collective-permute-done((f32[4,8,512]{2,1,0:T(8,128)S(1)}, f32[4,8,512]{2,1,0:T(8,128)S(1)}, u32[]{:S(2)}, u32[]{:S(2)}) %collective-permute-start.8) | collective-permute-done | bytes 65568 | tf_op jit(solution)/shard_map/ppermute | solution.py:476
  23.7 1.7 %collective-permute-start.9 = (f32[4,8,512]{2,1,0:T(8,128)S(1)}, f32[4,8,512]{2,1,0:T(8,128)S(1)}, u32[]{:S(2)}, u32[]{:S(2)}) collective-permute-start(f32[4,8,512]{2,1,0:T(8,128)S(1)} %select_add_fusion.refs_1_), channel_id=1, source_target_pairs={{0,1},{1,0},{2,3},{3,2},{4,5},{5,4},{6,7},{7,6},{8,9},{9,8},{10,11... | collective-permute-start | bytes 196616 | tf_op jit(solution)/shard_map/ppermute | solution.py:476
  25.4 0.9 %collective-permute-done.9.refs_2_ = f32[4,8,512]{2,1,0:T(8,128)S(1)} collective-permute-done((f32[4,8,512]{2,1,0:T(8,128)S(1)}, f32[4,8,512]{2,1,0:T(8,128)S(1)}, u32[]{:S(2)}, u32[]{:S(2)}) %collective-permute-start.9) | collective-permute-done | bytes 65568 | tf_op jit(solution)/shard_map/ppermute | solution.py:476
  26.3 1.4 %clean.1 = (f32[8,50,2,500]{3,2,1,0:T(2,128)}, f32[8,128]{1,0:T(8,128)}) custom-call(f32[50,2,8,500]{3,2,1,0:T(8,128)S(1)} %get-tuple-element.32.flux, f32[8,128]{1,0:T(8,128)S(1)} %get-tuple-element.34.sky_ref, f32[4,8,512]{2,1,0:T(8,128)S(1)} %get-tuple-element.35.refs_0_, f32[4,8,512]{2,1,0:T(8,128)S(1)} %select_add_fusion.refs_1_, ...), custom_call_target="tpu_custom_call" | custom-call | flops 1000000 | bytes 1000000 | tf_op jit(solution)/shard_map/clean/pallas_call | solution.py:439
  (6 shorter events, 0.0 us)
Async XLA Ops:
  0.6 4.9 %copy-start = (s32[2,40]{1,0:T(2,128)S(1)}, s32[2,40]{1,0:T(2,128)}, u32[]{:S(2)}) copy-start(s32[2,40]{1,0:T(2,128)} %sky_index.1) | copy-start | bytes 964
  2.4 3.1 %collective-permute-start.1 = (f32[6,2,8,500]{3,2,1,0:T(8,128)S(1)}, f32[6,2,8,500]{3,2,1,0:T(8,128)S(1)}, u32[]{:S(2)}, u32[]{:S(2)}) collective-permute-start(f32[6,2,8,500]{3,2,1,0:T(8,128)S(1)} %get-tuple-element.21), channel_id=1, source_target_pairs={{0,1},{1,0},{2,3},{3,2},{4,5},{5,4},{6,7},{7,6},{8,9},{9,8},{10,11... | collective-permute-start | bytes 576008 | tf_op jit(solution)/shard_map/ppermute | solution.py:476
  2.9 6.5 %collective-permute-start = (f32[6,2,8,500]{3,2,1,0:T(8,128)S(1)}, f32[6,2,8,500]{3,2,1,0:T(8,128)S(1)}, u32[]{:S(2)}, u32[]{:S(2)}) collective-permute-start(f32[6,2,8,500]{3,2,1,0:T(8,128)S(1)} %get-tuple-element.20), channel_id=1, source_target_pairs={{0,8},{1,2},{2,1},{3,4},{4,3},{5,6},{6,5},{7,15},{8,0},{9,10},{10,... | collective-permute-start | bytes 576008 | tf_op jit(solution)/shard_map/ppermute | solution.py:476
  10.2 1.2 %collective-permute-start.2 = (f32[2,8,128]{2,1,0:T(8,128)S(1)}, f32[2,8,128]{2,1,0:T(8,128)S(1)}, u32[]{:S(2)}, u32[]{:S(2)}) collective-permute-start(f32[2,8,128]{2,1,0:T(8,128)S(1)} %get-tuple-element.31), channel_id=1, source_target_pairs={{0,1},{1,0},{2,3},{3,2},{4,5},{5,4},{6,7},{7,6},{8,9},{9,8},{10,11... | collective-permute-start | bytes 24584 | tf_op jit(solution)/shard_map/ppermute | solution.py:476
  11.4 6.0 %collective-permute-start.3 = (f32[50,2,8,500]{3,2,1,0:T(8,128)S(1)}, f32[50,2,8,500]{3,2,1,0:T(8,128)S(1)}, u32[]{:S(2)}, u32[]{:S(2)}) collective-permute-start(f32[50,2,8,500]{3,2,1,0:T(8,128)S(1)} %get-tuple-element.32.flux), channel_id=1, source_target_pairs={{0,1},{1,0},{2,3},{3,2},{4,5},{5,4},{6,7},{7,6},{8,9},{9,8},{10,11... | collective-permute-start | bytes 4800008 | tf_op jit(solution)/shard_map/ppermute | solution.py:476
  11.6 3.7 %collective-permute-start.4 = (f32[4,8,128]{2,1,0:T(8,128)S(1)}, f32[4,8,128]{2,1,0:T(8,128)S(1)}, u32[]{:S(2)}, u32[]{:S(2)}) collective-permute-start(f32[4,8,128]{2,1,0:T(8,128)S(1)} %maximum_select_fusion), channel_id=1, source_target_pairs={{0,16},{1,9},{2,18},{3,11},{4,20},{5,13},{6,22},{7,15},{8,24},{9,1... | collective-permute-start | bytes 49160 | tf_op jit(solution)/shard_map/ppermute | solution.py:476
  13.2 4.1 %collective-permute-start.6 = (f32[4,8,128]{2,1,0:T(8,128)S(1)}, f32[4,8,128]{2,1,0:T(8,128)S(1)}, u32[]{:S(2)}, u32[]{:S(2)}) collective-permute-start(f32[4,8,128]{2,1,0:T(8,128)S(1)} %maximum_select_fusion), channel_id=1, source_target_pairs={{0,25},{1,24},{2,27},{3,26},{4,29},{5,28},{6,31},{7,30},{8,17},{9,... | collective-permute-start | bytes 49160 | tf_op jit(solution)/shard_map/ppermute | solution.py:476
  15.3 2.0 %collective-permute-start.5 = (f32[4,8,128]{2,1,0:T(8,128)S(1)}, f32[4,8,128]{2,1,0:T(8,128)S(1)}, u32[]{:S(2)}, u32[]{:S(2)}) collective-permute-start(f32[4,8,128]{2,1,0:T(8,128)S(1)} %collective-permute-done.4), channel_id=1, source_target_pairs={{0,1},{1,0},{2,3},{3,2},{4,5},{5,4},{6,7},{7,6},{8,9},{9,8},{10,11... | collective-permute-start | bytes 49160 | tf_op jit(solution)/shard_map/ppermute | solution.py:476
  17.8 4.3 %collective-permute-start.7 = (f32[4,8,512]{2,1,0:T(8,128)S(1)}, f32[4,8,512]{2,1,0:T(8,128)S(1)}, u32[]{:S(2)}, u32[]{:S(2)}) collective-permute-start(f32[4,8,512]{2,1,0:T(8,128)S(1)} %get-tuple-element.35.refs_0_), channel_id=1, source_target_pairs={{0,2},{1,7},{2,0},{3,5},{4,6},{5,3},{6,4},{7,1},{8,10},{9,15},{10,... | collective-permute-start | bytes 196616 | tf_op jit(solution)/shard_map/ppermute | solution.py:476
  19.4 4.3 %collective-permute-start.8 = (f32[4,8,512]{2,1,0:T(8,128)S(1)}, f32[4,8,512]{2,1,0:T(8,128)S(1)}, u32[]{:S(2)}, u32[]{:S(2)}) collective-permute-start(f32[4,8,512]{2,1,0:T(8,128)S(1)} %get-tuple-element.35.refs_0_), channel_id=1, source_target_pairs={{0,8},{1,5},{2,10},{3,7},{4,12},{5,1},{6,14},{7,3},{8,0},{9,13},{1... | collective-permute-start | bytes 196616 | tf_op jit(solution)/shard_map/ppermute | solution.py:476
  23.7 2.6 %collective-permute-start.9 = (f32[4,8,512]{2,1,0:T(8,128)S(1)}, f32[4,8,512]{2,1,0:T(8,128)S(1)}, u32[]{:S(2)}, u32[]{:S(2)}) collective-permute-start(f32[4,8,512]{2,1,0:T(8,128)S(1)} %select_add_fusion.refs_1_), channel_id=1, source_target_pairs={{0,1},{1,0},{2,3},{3,2},{4,5},{5,4},{6,7},{7,6},{8,9},{9,8},{10,11... | collective-permute-start | bytes 196616 | tf_op jit(solution)/shard_map/ppermute | solution.py:476

commit v10 on v9

--- a/solution.py
+++ b/solution.py
@@ -507,8 +507,8 @@
     regress, sky = regress_call(total_rows, flux, other, sums)
     if wave == 8:
         first = swap(regress, lambda s, i: (s, i ^ (6 if i % 2 else 2)))
-        third = swap(regress, lambda s, i: (s, i ^ 4 if i % 2 else -1))
-        fetched = first + jnp.where(odd, third, 0.0)
+        third = swap(regress, lambda s, i: (s, i ^ (5 if i % 2 else 1)))
+        fetched = first + jnp.where(odd, 0.0, third)
         terms = [regress, fetched, swap(fetched, other_core)]
     else:
         for k in powers(2, wave):

time: 28 us -> 27.6 us (0.986)
  starting transfers between devices: 11 us -> 9.76 us
  waiting for transfers between devices: 7.7 us -> 8.6 us
    ppermute x10, starting transfers between devices: 11 us -> 9.76 us  [swap(): return lax.ppermute(values, ('spec', 'wave'), pairs)]
    ppermute x10, waiting for transfers between devices: 7.7 us -> 8.6 us  [swap(): return lax.ppermute(values, ('spec', 'wave'), pairs)]
  transfers between devices with their start and end apart: 10 -> 10, of which waited for: 6 -> 6; matrix products, arithmetic and copies ran while one was open for 0% -> 0% of each run, Pallas kernels for 14% -> 15%
where the time goes in v10:
time: 27.6 us; the launch traced here: 27.3 us
  starting transfers between devices  9.76 us (35%)
  waiting for transfers between devices  8.6 us (31%)
  Pallas kernels  8.23 us (30%)
  between operations  0.7 us (3%)
    ppermute x10, starting transfers between devices, swap(): return lax.ppermute(values, ('spec', 'wave'), pairs)  9.76 us
    ppermute x10, waiting for transfers between devices, swap(): return lax.ppermute(values, ('spec', 'wave'), pairs)  8.6 us
    pallas_call x1, Pallas kernels, forward_call(): pl.pallas_call(forward_kernel, out_shape=(whole, whole, whole, whole, in_...  3.96 us
    pallas_call x1, Pallas kernels, edge_call(): pl.pallas_call(edge_kernel, out_shape=(message, message, in_vmem((4, size...  1.76 us
    pallas_call x1, Pallas kernels, clean_call(): pl.pallas_call(functools.partial(clean_kernel, total_rows), out_shape=(ja...  1.38 us
    pallas_call x1, Pallas kernels, backward_call(): pl.pallas_call(functools.partial(backward_kernel, wave), out_shape=(in_vm...  0.69 us
  transfers between devices with their start and end apart: 10, of which 6 were waited for; matrix products, arithmetic and copies ran while one was open for 0% of the time, Pallas kernels for 15%

profile of v10, /device:TPU:0, one launch (start us, length us, event | category | flops | bytes accessed | tf_op | source)
XLA Modules:
  0.0 27.3 jit_solution(18270692676290512320)
XLA Ops:
  0.6 1.8 %edges.1 = (f32[6,2,8,500]{3,2,1,0:T(8,128)S(1)}, f32[6,2,8,500]{3,2,1,0:T(8,128)S(1)}, f32[4,10,2,8,500]{4,3,2,1,0:T(8,128)S(1)}) custom-call(f32[8,50,2,500]{3,2,1,0:T(2,128)} %bitcast.7, f32[8,50,2,500]{3,2,1,0:T(2,128)} %bitcast.9, s32[8,50,2,500]{3,2,1,0:T(2,128)} %bitcast.11, f32[8,50,2,500]{3,2,1,0:T(2,128)} %bitcast.13, f32[8,50,2,500]{3,2,1,0:T(2,128)} %bitcast.15), custom_call_target="tpu_custom_call" | custom-call | flops 1000000 | bytes 1000000 | tf_op jit(solution)/shard_map/edges/pallas_call | solution.py:114
  2.4 0.5 %collective-permute-start.1 = (f32[6,2,8,500]{3,2,1,0:T(8,128)S(1)}, f32[6,2,8,500]{3,2,1,0:T(8,128)S(1)}, u32[]{:S(2)}, u32[]{:S(2)}) collective-permute-start(f32[6,2,8,500]{3,2,1,0:T(8,128)S(1)} %get-tuple-element.21), channel_id=1, source_target_pairs={{0,1},{1,0},{2,3},{3,2},{4,5},{5,4},{6,7},{7,6},{8,9},{9,8},{10,11... | collective-permute-start | bytes 576008 | tf_op jit(solution)/shard_map/ppermute | solution.py:476
  2.9 2.6 %collective-permute-start = (f32[6,2,8,500]{3,2,1,0:T(8,128)S(1)}, f32[6,2,8,500]{3,2,1,0:T(8,128)S(1)}, u32[]{:S(2)}, u32[]{:S(2)}) collective-permute-start(f32[6,2,8,500]{3,2,1,0:T(8,128)S(1)} %get-tuple-element.20), channel_id=1, source_target_pairs={{0,8},{1,2},{2,1},{3,4},{4,3},{5,6},{6,5},{7,15},{8,0},{9,10},{10,... | collective-permute-start | bytes 576008 | tf_op jit(solution)/shard_map/ppermute | solution.py:476
  5.5 0.0 collective-permute-done.1.near
  5.5 4.0 %forward.1 = (f32[50,2,8,500]{3,2,1,0:T(8,128)S(1)}, f32[50,2,8,500]{3,2,1,0:T(8,128)S(1)}, f32[50,2,8,500]{3,2,1,0:T(8,128)S(1)}, f32[50,2,8,500]{3,2,1,0:T(8,1...) custom-call(f32[6,2,8,500]{3,2,1,0:T(8,128)S(1)} %collective-permute-done.1.near, ...), custom_call_target="tpu_custom_call" | custom-call | flops 10000000 | bytes 10000000 | tf_op jit(solution)/shard_map/forward/pallas_call | solution.py:241
  9.5 0.0 collective-permute-done.far
  9.5 0.7 %backward.1 = (f32[50,2,8,500]{3,2,1,0:T(8,128)S(1)}, f32[2,8,128]{2,1,0:T(8,128)S(1)}) custom-call(f32[6,2,8,500]{3,2,1,0:T(8,128)S(1)} %collective-permute-done.far, f32[50,2,8,500]{3,2,1,0:T(8,128)S(1)} %get-tuple-element.23.lower, f32[50,2,8,500]{3,2,1,0:T(8,128)S(1)} %get-tuple-element.24.lower_far, f32[50,2,8,500]{3,2,1,0:T(8,128)S(1)} %get-tuple-element.25.half, ...), custom_call_target="tpu_custom_call" | custom-call | flops 10000000 | bytes 10000000 | tf_op jit(solution)/shard_map/backward/pallas_call | solution.py:320
  10.2 0.2 collective-permute-start.2
  10.4 1.0 %collective-permute-done.2 = f32[2,8,128]{2,1,0:T(8,128)S(1)} collective-permute-done((f32[2,8,128]{2,1,0:T(8,128)S(1)}, f32[2,8,128]{2,1,0:T(8,128)S(1)}, u32[]{:S(2)}, u32[]{:S(2)}) %collective-permute-start.2) | collective-permute-done | bytes 8224 | tf_op jit(solution)/shard_map/ppermute | solution.py:476
  11.4 0.2 collective-permute-start.3
  11.6 1.7 %collective-permute-start.4 = (f32[4,8,128]{2,1,0:T(8,128)S(1)}, f32[4,8,128]{2,1,0:T(8,128)S(1)}, u32[]{:S(2)}, u32[]{:S(2)}) collective-permute-start(f32[4,8,128]{2,1,0:T(8,128)S(1)} %maximum_select_fusion), channel_id=1, source_target_pairs={{0,16},{1,9},{2,18},{3,11},{4,20},{5,13},{6,22},{7,15},{8,24},{9,1... | collective-permute-start | bytes 49160 | tf_op jit(solution)/shard_map/ppermute | solution.py:476
  13.2 1.1 %collective-permute-start.6 = (f32[4,8,128]{2,1,0:T(8,128)S(1)}, f32[4,8,128]{2,1,0:T(8,128)S(1)}, u32[]{:S(2)}, u32[]{:S(2)}) collective-permute-start(f32[4,8,128]{2,1,0:T(8,128)S(1)} %maximum_select_fusion), channel_id=1, source_target_pairs={{0,25},{1,24},{2,27},{3,26},{4,29},{5,28},{6,31},{7,30},{8,17},{9,... | collective-permute-start | bytes 49160 | tf_op jit(solution)/shard_map/ppermute | solution.py:476
  14.4 0.9 %collective-permute-done.4 = f32[4,8,128]{2,1,0:T(8,128)S(1)} collective-permute-done((f32[4,8,128]{2,1,0:T(8,128)S(1)}, f32[4,8,128]{2,1,0:T(8,128)S(1)}, u32[]{:S(2)}, u32[]{:S(2)}) %collective-permute-start.4) | collective-permute-done | bytes 16416 | tf_op jit(solution)/shard_map/ppermute | solution.py:476
  15.3 0.0 collective-permute-start.5
  15.3 2.0 %collective-permute-done.6 = f32[4,8,128]{2,1,0:T(8,128)S(1)} collective-permute-done((f32[4,8,128]{2,1,0:T(8,128)S(1)}, f32[4,8,128]{2,1,0:T(8,128)S(1)}, u32[]{:S(2)}, u32[]{:S(2)}) %collective-permute-start.6) | collective-permute-done | bytes 16416 | tf_op jit(solution)/shard_map/ppermute | solution.py:476
  17.3 0.0 collective-permute-done.5
  17.3 0.4 %regress.1 = (f32[4,8,512]{2,1,0:T(8,128)S(1)}, f32[8,128]{1,0:T(8,128)S(1)}) custom-call(f32[50,2,8,500]{3,2,1,0:T(8,128)S(1)} %get-tuple-element.32.flux, f32[50,2,8,500]{3,2,1,0:T(8,128)S(1)} %collective-permute-done.3.other, f32[4,8,128]{2,1,0:T(8,128)S(1)} %add_add_fusion.sums), custom_call_target="tpu_custom_call" | custom-call | flops 1000000 | bytes 1000000 | tf_op jit(solution)/shard_map/regress/pallas_call | solution.py:380
  17.8 1.6 %collective-permute-start.7 = (f32[4,8,512]{2,1,0:T(8,128)S(1)}, f32[4,8,512]{2,1,0:T(8,128)S(1)}, u32[]{:S(2)}, u32[]{:S(2)}) collective-permute-start(f32[4,8,512]{2,1,0:T(8,128)S(1)} %get-tuple-element.35.refs_0_), channel_id=1, source_target_pairs={{0,2},{1,7},{2,0},{3,5},{4,6},{5,3},{6,4},{7,1},{8,10},{9,15},{10,... | collective-permute-start | bytes 196616 | tf_op jit(solution)/shard_map/ppermute | solution.py:476
  19.4 1.7 %collective-permute-start.8 = (f32[4,8,512]{2,1,0:T(8,128)S(1)}, f32[4,8,512]{2,1,0:T(8,128)S(1)}, u32[]{:S(2)}, u32[]{:S(2)}) collective-permute-start(f32[4,8,512]{2,1,0:T(8,128)S(1)} %get-tuple-element.35.refs_0_), channel_id=1, source_target_pairs={{0,1},{1,4},{2,3},{3,6},{4,5},{5,0},{6,7},{7,2},{8,9},{9,12},{10,1... | collective-permute-start | bytes 196616 | tf_op jit(solution)/shard_map/ppermute | solution.py:476
  21.1 1.0 %collective-permute-done.7 = f32[4,8,512]{2,1,0:T(8,128)S(1)} collective-permute-done((f32[4,8,512]{2,1,0:T(8,128)S(1)}, f32[4,8,512]{2,1,0:T(8,128)S(1)}, u32[]{:S(2)}, u32[]{:S(2)}) %collective-permute-start.7) | collective-permute-done | bytes 65568 | tf_op jit(solution)/shard_map/ppermute | solution.py:476
  22.1 2.5 %collective-permute-done.8 = f32[4,8,512]{2,1,0:T(8,128)S(1)} collective-permute-done((f32[4,8,512]{2,1,0:T(8,128)S(1)}, f32[4,8,512]{2,1,0:T(8,128)S(1)}, u32[]{:S(2)}, u32[]{:S(2)}) %collective-permute-start.8) | collective-permute-done | bytes 65568 | tf_op jit(solution)/shard_map/ppermute | solution.py:476
  24.6 0.1 collective-permute-start.9
  24.7 1.2 %collective-permute-done.9.refs_2_ = f32[4,8,512]{2,1,0:T(8,128)S(1)} collective-permute-done((f32[4,8,512]{2,1,0:T(8,128)S(1)}, f32[4,8,512]{2,1,0:T(8,128)S(1)}, u32[]{:S(2)}, u32[]{:S(2)}) %collective-permute-start.9) | collective-permute-done | bytes 65568 | tf_op jit(solution)/shard_map/ppermute | solution.py:476
  25.9 1.4 %clean.1 = (f32[8,50,2,500]{3,2,1,0:T(2,128)}, f32[8,128]{1,0:T(8,128)}) custom-call(f32[50,2,8,500]{3,2,1,0:T(8,128)S(1)} %get-tuple-element.32.flux, f32[8,128]{1,0:T(8,128)S(1)} %get-tuple-element.34.sky_ref, f32[4,8,512]{2,1,0:T(8,128)S(1)} %get-tuple-element.35.refs_0_, f32[4,8,512]{2,1,0:T(8,128)S(1)} %select_add_fusion.refs_1_, ...), custom_call_target="tpu_custom_call" | custom-call | flops 1000000 | bytes 1000000 | tf_op jit(solution)/shard_map/clean/pallas_call | solution.py:439
  (6 shorter events, 0.0 us)
Async XLA Ops:
  0.6 4.9 %copy-start = (s32[2,40]{1,0:T(2,128)S(1)}, s32[2,40]{1,0:T(2,128)}, u32[]{:S(2)}) copy-start(s32[2,40]{1,0:T(2,128)} %sky_index.1) | copy-start | bytes 964
  2.4 3.1 %collective-permute-start.1 = (f32[6,2,8,500]{3,2,1,0:T(8,128)S(1)}, f32[6,2,8,500]{3,2,1,0:T(8,128)S(1)}, u32[]{:S(2)}, u32[]{:S(2)}) collective-permute-start(f32[6,2,8,500]{3,2,1,0:T(8,128)S(1)} %get-tuple-element.21), channel_id=1, source_target_pairs={{0,1},{1,0},{2,3},{3,2},{4,5},{5,4},{6,7},{7,6},{8,9},{9,8},{10,11... | collective-permute-start | bytes 576008 | tf_op jit(solution)/shard_map/ppermute | solution.py:476
  2.9 6.5 %collective-permute-start = (f32[6,2,8,500]{3,2,1,0:T(8,128)S(1)}, f32[6,2,8,500]{3,2,1,0:T(8,128)S(1)}, u32[]{:S(2)}, u32[]{:S(2)}) collective-permute-start(f32[6,2,8,500]{3,2,1,0:T(8,128)S(1)} %get-tuple-element.20), channel_id=1, source_target_pairs={{0,8},{1,2},{2,1},{3,4},{4,3},{5,6},{6,5},{7,15},{8,0},{9,10},{10,... | collective-permute-start | bytes 576008 | tf_op jit(solution)/shard_map/ppermute | solution.py:476
  10.2 1.2 %collective-permute-start.2 = (f32[2,8,128]{2,1,0:T(8,128)S(1)}, f32[2,8,128]{2,1,0:T(8,128)S(1)}, u32[]{:S(2)}, u32[]{:S(2)}) collective-permute-start(f32[2,8,128]{2,1,0:T(8,128)S(1)} %get-tuple-element.31), channel_id=1, source_target_pairs={{0,1},{1,0},{2,3},{3,2},{4,5},{5,4},{6,7},{7,6},{8,9},{9,8},{10,11... | collective-permute-start | bytes 24584 | tf_op jit(solution)/shard_map/ppermute | solution.py:476
  11.4 6.0 %collective-permute-start.3 = (f32[50,2,8,500]{3,2,1,0:T(8,128)S(1)}, f32[50,2,8,500]{3,2,1,0:T(8,128)S(1)}, u32[]{:S(2)}, u32[]{:S(2)}) collective-permute-start(f32[50,2,8,500]{3,2,1,0:T(8,128)S(1)} %get-tuple-element.32.flux), channel_id=1, source_target_pairs={{0,1},{1,0},{2,3},{3,2},{4,5},{5,4},{6,7},{7,6},{8,9},{9,8},{10,11... | collective-permute-start | bytes 4800008 | tf_op jit(solution)/shard_map/ppermute | solution.py:476
  11.6 3.7 %collective-permute-start.4 = (f32[4,8,128]{2,1,0:T(8,128)S(1)}, f32[4,8,128]{2,1,0:T(8,128)S(1)}, u32[]{:S(2)}, u32[]{:S(2)}) collective-permute-start(f32[4,8,128]{2,1,0:T(8,128)S(1)} %maximum_select_fusion), channel_id=1, source_target_pairs={{0,16},{1,9},{2,18},{3,11},{4,20},{5,13},{6,22},{7,15},{8,24},{9,1... | collective-permute-start | bytes 49160 | tf_op jit(solution)/shard_map/ppermute | solution.py:476
  13.2 4.1 %collective-permute-start.6 = (f32[4,8,128]{2,1,0:T(8,128)S(1)}, f32[4,8,128]{2,1,0:T(8,128)S(1)}, u32[]{:S(2)}, u32[]{:S(2)}) collective-permute-start(f32[4,8,128]{2,1,0:T(8,128)S(1)} %maximum_select_fusion), channel_id=1, source_target_pairs={{0,25},{1,24},{2,27},{3,26},{4,29},{5,28},{6,31},{7,30},{8,17},{9,... | collective-permute-start | bytes 49160 | tf_op jit(solution)/shard_map/ppermute | solution.py:476
  15.3 2.0 %collective-permute-start.5 = (f32[4,8,128]{2,1,0:T(8,128)S(1)}, f32[4,8,128]{2,1,0:T(8,128)S(1)}, u32[]{:S(2)}, u32[]{:S(2)}) collective-permute-start(f32[4,8,128]{2,1,0:T(8,128)S(1)} %collective-permute-done.4), channel_id=1, source_target_pairs={{0,1},{1,0},{2,3},{3,2},{4,5},{5,4},{6,7},{7,6},{8,9},{9,8},{10,11... | collective-permute-start | bytes 49160 | tf_op jit(solution)/shard_map/ppermute | solution.py:476
  17.8 4.3 %collective-permute-start.7 = (f32[4,8,512]{2,1,0:T(8,128)S(1)}, f32[4,8,512]{2,1,0:T(8,128)S(1)}, u32[]{:S(2)}, u32[]{:S(2)}) collective-permute-start(f32[4,8,512]{2,1,0:T(8,128)S(1)} %get-tuple-element.35.refs_0_), channel_id=1, source_target_pairs={{0,2},{1,7},{2,0},{3,5},{4,6},{5,3},{6,4},{7,1},{8,10},{9,15},{10,... | collective-permute-start | bytes 196616 | tf_op jit(solution)/shard_map/ppermute | solution.py:476
  19.4 5.2 %collective-permute-start.8 = (f32[4,8,512]{2,1,0:T(8,128)S(1)}, f32[4,8,512]{2,1,0:T(8,128)S(1)}, u32[]{:S(2)}, u32[]{:S(2)}) collective-permute-start(f32[4,8,512]{2,1,0:T(8,128)S(1)} %get-tuple-element.35.refs_0_), channel_id=1, source_target_pairs={{0,1},{1,4},{2,3},{3,6},{4,5},{5,0},{6,7},{7,2},{8,9},{9,12},{10,1... | collective-permute-start | bytes 196616 | tf_op jit(solution)/shard_map/ppermute | solution.py:476
  24.6 1.3 %collective-permute-start.9 = (f32[4,8,512]{2,1,0:T(8,128)S(1)}, f32[4,8,512]{2,1,0:T(8,128)S(1)}, u32[]{:S(2)}, u32[]{:S(2)}) collective-permute-start(f32[4,8,512]{2,1,0:T(8,128)S(1)} %select_add_fusion.refs_1_), channel_id=1, source_target_pairs={{0,1},{1,0},{2,3},{3,2},{4,5},{5,4},{6,7},{7,6},{8,9},{9,8},{10,11... | collective-permute-start | bytes 196616 | tf_op jit(solution)/shard_map/ppermute | solution.py:476

commit v11 on v10

--- a/solution.py
+++ b/solution.py
@@ -497,7 +497,7 @@
     other = swap(flux, other_core)
     sums = jnp.where(odd, jnp.concatenate([got, sums]), jnp.concatenate([sums, got]))
     if spec == 4:
-        first = swap(sums, lambda s, i: (s ^ (1 if i % 2 else 2), i))
+        first = swap(sums, lambda s, i: (s ^ (2 if i % 2 else 1), i ^ 1))
         third = swap(sums, lambda s, i: (s ^ 3, i ^ 1))
         second = swap(first, other_core)
         sums = (sums + jnp.where(odd, first, second)) + (jnp.where(odd, second, first) + third)
@@ -506,8 +506,8 @@
             sums = sums + swap(sums, lambda s, i: (s ^ k, i))
     regress, sky = regress_call(total_rows, flux, other, sums)
     if wave == 8:
-        first = swap(regress, lambda s, i: (s, i ^ (6 if i % 2 else 2)))
-        third = swap(regress, lambda s, i: (s, i ^ (5 if i % 2 else 1)))
+        first = swap(regress, lambda s, i: (s, i ^ (6 if i % 2 else 4)))
+        third = swap(regress, lambda s, i: (s, i ^ (3 if i % 2 else 1)))
         fetched = first + jnp.where(odd, 0.0, third)
         terms = [regress, fetched, swap(fetched, other_core)]
     else:

time: 27.6 us -> 27.3 us (0.989)
  waiting for transfers between devices: 8.6 us -> 8 us
  starting transfers between devices: 9.76 us -> 10.1 us
    ppermute x10, waiting for transfers between devices: 8.6 us -> 8 us  [swap(): return lax.ppermute(values, ('spec', 'wave'), pairs)]
    ppermute x10, starting transfers between devices: 9.76 us -> 10.1 us  [swap(): return lax.ppermute(values, ('spec', 'wave'), pairs)]
  transfers between devices with their start and end apart: 10 -> 10, of which waited for: 6 -> 5; matrix products, arithmetic and copies ran while one was open for 0% -> 0% of each run, Pallas kernels for 15% -> 15%
where the time goes in v11:
time: 27.3 us; the launch traced here: 27 us
  starting transfers between devices  10.1 us (37%)
  Pallas kernels  8.23 us (30%)
  waiting for transfers between devices  8 us (29%)
  between operations  0.7 us (3%)
    ppermute x10, starting transfers between devices, swap(): return lax.ppermute(values, ('spec', 'wave'), pairs)  10.1 us
    ppermute x10, waiting for transfers between devices, swap(): return lax.ppermute(values, ('spec', 'wave'), pairs)  8 us
    pallas_call x1, Pallas kernels, forward_call(): pl.pallas_call(forward_kernel, out_shape=(whole, whole, whole, whole, in_...  3.96 us
    pallas_call x1, Pallas kernels, edge_call(): pl.pallas_call(edge_kernel, out_shape=(message, message, in_vmem((4, size...  1.76 us
    pallas_call x1, Pallas kernels, clean_call(): pl.pallas_call(functools.partial(clean_kernel, total_rows), out_shape=(ja...  1.38 us
    pallas_call x1, Pallas kernels, backward_call(): pl.pallas_call(functools.partial(backward_kernel, wave), out_shape=(in_vm...  0.69 us
  transfers between devices with their start and end apart: 10, of which 5 were waited for; matrix products, arithmetic and copies ran while one was open for 0% of the time, Pallas kernels for 15%

profile of v11, /device:TPU:0, one launch (start us, length us, event | category | flops | bytes accessed | tf_op | source)
XLA Modules:
  0.0 27.0 jit_solution(3330365625998279022)
XLA Ops:
  0.6 1.8 %edges.1 = (f32[6,2,8,500]{3,2,1,0:T(8,128)S(1)}, f32[6,2,8,500]{3,2,1,0:T(8,128)S(1)}, f32[4,10,2,8,500]{4,3,2,1,0:T(8,128)S(1)}) custom-call(f32[8,50,2,500]{3,2,1,0:T(2,128)} %bitcast.7, f32[8,50,2,500]{3,2,1,0:T(2,128)} %bitcast.9, s32[8,50,2,500]{3,2,1,0:T(2,128)} %bitcast.11, f32[8,50,2,500]{3,2,1,0:T(2,128)} %bitcast.13, f32[8,50,2,500]{3,2,1,0:T(2,128)} %bitcast.15), custom_call_target="tpu_custom_call" | custom-call | flops 1000000 | bytes 1000000 | tf_op jit(solution)/shard_map/edges/pallas_call | solution.py:114
  2.4 0.5 %collective-permute-start.1 = (f32[6,2,8,500]{3,2,1,0:T(8,128)S(1)}, f32[6,2,8,500]{3,2,1,0:T(8,128)S(1)}, u32[]{:S(2)}, u32[]{:S(2)}) collective-permute-start(f32[6,2,8,500]{3,2,1,0:T(8,128)S(1)} %get-tuple-element.21), channel_id=1, source_target_pairs={{0,1},{1,0},{2,3},{3,2},{4,5},{5,4},{6,7},{7,6},{8,9},{9,8},{10,11... | collective-permute-start | bytes 576008 | tf_op jit(solution)/shard_map/ppermute | solution.py:476
  2.9 2.6 %collective-permute-start = (f32[6,2,8,500]{3,2,1,0:T(8,128)S(1)}, f32[6,2,8,500]{3,2,1,0:T(8,128)S(1)}, u32[]{:S(2)}, u32[]{:S(2)}) collective-permute-start(f32[6,2,8,500]{3,2,1,0:T(8,128)S(1)} %get-tuple-element.20), channel_id=1, source_target_pairs={{0,8},{1,2},{2,1},{3,4},{4,3},{5,6},{6,5},{7,15},{8,0},{9,10},{10,... | collective-permute-start | bytes 576008 | tf_op jit(solution)/shard_map/ppermute | solution.py:476
  5.5 0.0 collective-permute-done.1.near
  5.5 4.0 %forward.1 = (f32[50,2,8,500]{3,2,1,0:T(8,128)S(1)}, f32[50,2,8,500]{3,2,1,0:T(8,128)S(1)}, f32[50,2,8,500]{3,2,1,0:T(8,128)S(1)}, f32[50,2,8,500]{3,2,1,0:T(8,1...) custom-call(f32[6,2,8,500]{3,2,1,0:T(8,128)S(1)} %collective-permute-done.1.near, ...), custom_call_target="tpu_custom_call" | custom-call | flops 10000000 | bytes 10000000 | tf_op jit(solution)/shard_map/forward/pallas_call | solution.py:241
  9.5 0.0 collective-permute-done.far
  9.5 0.7 %backward.1 = (f32[50,2,8,500]{3,2,1,0:T(8,128)S(1)}, f32[2,8,128]{2,1,0:T(8,128)S(1)}) custom-call(f32[6,2,8,500]{3,2,1,0:T(8,128)S(1)} %collective-permute-done.far, f32[50,2,8,500]{3,2,1,0:T(8,128)S(1)} %get-tuple-element.23.lower, f32[50,2,8,500]{3,2,1,0:T(8,128)S(1)} %get-tuple-element.24.lower_far, f32[50,2,8,500]{3,2,1,0:T(8,128)S(1)} %get-tuple-element.25.half, ...), custom_call_target="tpu_custom_call" | custom-call | flops 10000000 | bytes 10000000 | tf_op jit(solution)/shard_map/backward/pallas_call | solution.py:320
  10.2 0.2 collective-permute-start.2
  10.4 1.0 %collective-permute-done.2 = f32[2,8,128]{2,1,0:T(8,128)S(1)} collective-permute-done((f32[2,8,128]{2,1,0:T(8,128)S(1)}, f32[2,8,128]{2,1,0:T(8,128)S(1)}, u32[]{:S(2)}, u32[]{:S(2)}) %collective-permute-start.2) | collective-permute-done | bytes 8224 | tf_op jit(solution)/shard_map/ppermute | solution.py:476
  11.4 0.2 collective-permute-start.3
  11.6 1.6 %collective-permute-start.4 = (f32[4,8,128]{2,1,0:T(8,128)S(1)}, f32[4,8,128]{2,1,0:T(8,128)S(1)}, u32[]{:S(2)}, u32[]{:S(2)}) collective-permute-start(f32[4,8,128]{2,1,0:T(8,128)S(1)} %maximum_select_fusion), channel_id=1, source_target_pairs={{0,9},{1,16},{2,11},{3,18},{4,13},{5,20},{6,15},{7,22},{8,1},{9,24... | collective-permute-start | bytes 49160 | tf_op jit(solution)/shard_map/ppermute | solution.py:476
  13.2 1.2 %collective-permute-start.6 = (f32[4,8,128]{2,1,0:T(8,128)S(1)}, f32[4,8,128]{2,1,0:T(8,128)S(1)}, u32[]{:S(2)}, u32[]{:S(2)}) collective-permute-start(f32[4,8,128]{2,1,0:T(8,128)S(1)} %maximum_select_fusion), channel_id=1, source_target_pairs={{0,25},{1,24},{2,27},{3,26},{4,29},{5,28},{6,31},{7,30},{8,17},{9,... | collective-permute-start | bytes 49160 | tf_op jit(solution)/shard_map/ppermute | solution.py:476
  14.4 0.3 %collective-permute-done.4 = f32[4,8,128]{2,1,0:T(8,128)S(1)} collective-permute-done((f32[4,8,128]{2,1,0:T(8,128)S(1)}, f32[4,8,128]{2,1,0:T(8,128)S(1)}, u32[]{:S(2)}, u32[]{:S(2)}) %collective-permute-start.4) | collective-permute-done | bytes 16416 | tf_op jit(solution)/shard_map/ppermute | solution.py:476
  14.7 0.3 %collective-permute-start.5 = (f32[4,8,128]{2,1,0:T(8,128)S(1)}, f32[4,8,128]{2,1,0:T(8,128)S(1)}, u32[]{:S(2)}, u32[]{:S(2)}) collective-permute-start(f32[4,8,128]{2,1,0:T(8,128)S(1)} %collective-permute-done.4), channel_id=1, source_target_pairs={{0,1},{1,0},{2,3},{3,2},{4,5},{5,4},{6,7},{7,6},{8,9},{9,8},{10,11... | collective-permute-start | bytes 49160 | tf_op jit(solution)/shard_map/ppermute | solution.py:476
  15.0 2.2 %collective-permute-done.6 = f32[4,8,128]{2,1,0:T(8,128)S(1)} collective-permute-done((f32[4,8,128]{2,1,0:T(8,128)S(1)}, f32[4,8,128]{2,1,0:T(8,128)S(1)}, u32[]{:S(2)}, u32[]{:S(2)}) %collective-permute-start.6) | collective-permute-done | bytes 16416 | tf_op jit(solution)/shard_map/ppermute | solution.py:476
  17.2 0.0 collective-permute-done.5
  17.2 0.4 %regress.1 = (f32[4,8,512]{2,1,0:T(8,128)S(1)}, f32[8,128]{1,0:T(8,128)S(1)}) custom-call(f32[50,2,8,500]{3,2,1,0:T(8,128)S(1)} %get-tuple-element.32.flux, f32[50,2,8,500]{3,2,1,0:T(8,128)S(1)} %collective-permute-done.3.other, f32[4,8,128]{2,1,0:T(8,128)S(1)} %add_add_fusion.sums), custom_call_target="tpu_custom_call" | custom-call | flops 1000000 | bytes 1000000 | tf_op jit(solution)/shard_map/regress/pallas_call | solution.py:380
  17.7 2.4 %collective-permute-start.7 = (f32[4,8,512]{2,1,0:T(8,128)S(1)}, f32[4,8,512]{2,1,0:T(8,128)S(1)}, u32[]{:S(2)}, u32[]{:S(2)}) collective-permute-start(f32[4,8,512]{2,1,0:T(8,128)S(1)} %get-tuple-element.35.refs_0_), channel_id=1, source_target_pairs={{0,4},{1,7},{2,6},{3,5},{4,0},{5,3},{6,2},{7,1},{8,12},{9,15},{10,... | collective-permute-start | bytes 196616 | tf_op jit(solution)/shard_map/ppermute | solution.py:476
  20.1 1.0 %collective-permute-start.8 = (f32[4,8,512]{2,1,0:T(8,128)S(1)}, f32[4,8,512]{2,1,0:T(8,128)S(1)}, u32[]{:S(2)}, u32[]{:S(2)}) collective-permute-start(f32[4,8,512]{2,1,0:T(8,128)S(1)} %get-tuple-element.35.refs_0_), channel_id=1, source_target_pairs={{0,1},{1,2},{2,3},{3,0},{4,5},{5,6},{6,7},{7,4},{8,9},{9,10},{10,1... | collective-permute-start | bytes 196616 | tf_op jit(solution)/shard_map/ppermute | solution.py:476
  21.1 3.3 %collective-permute-done.7 = f32[4,8,512]{2,1,0:T(8,128)S(1)} collective-permute-done((f32[4,8,512]{2,1,0:T(8,128)S(1)}, f32[4,8,512]{2,1,0:T(8,128)S(1)}, u32[]{:S(2)}, u32[]{:S(2)}) %collective-permute-start.7) | collective-permute-done | bytes 65568 | tf_op jit(solution)/shard_map/ppermute | solution.py:476
  24.3 0.0 collective-permute-done.8
  24.3 0.1 collective-permute-start.9
  24.4 1.2 %collective-permute-done.9.refs_2_ = f32[4,8,512]{2,1,0:T(8,128)S(1)} collective-permute-done((f32[4,8,512]{2,1,0:T(8,128)S(1)}, f32[4,8,512]{2,1,0:T(8,128)S(1)}, u32[]{:S(2)}, u32[]{:S(2)}) %collective-permute-start.9) | collective-permute-done | bytes 65568 | tf_op jit(solution)/shard_map/ppermute | solution.py:476
  25.7 1.4 %clean.1 = (f32[8,50,2,500]{3,2,1,0:T(2,128)}, f32[8,128]{1,0:T(8,128)}) custom-call(f32[50,2,8,500]{3,2,1,0:T(8,128)S(1)} %get-tuple-element.32.flux, f32[8,128]{1,0:T(8,128)S(1)} %get-tuple-element.34.sky_ref, f32[4,8,512]{2,1,0:T(8,128)S(1)} %get-tuple-element.35.refs_0_, f32[4,8,512]{2,1,0:T(8,128)S(1)} %select_add_fusion.refs_1_, ...), custom_call_target="tpu_custom_call" | custom-call | flops 1000000 | bytes 1000000 | tf_op jit(solution)/shard_map/clean/pallas_call | solution.py:439
  (6 shorter events, 0.0 us)
Async XLA Ops:
  0.6 4.9 %copy-start = (s32[2,40]{1,0:T(2,128)S(1)}, s32[2,40]{1,0:T(2,128)}, u32[]{:S(2)}) copy-start(s32[2,40]{1,0:T(2,128)} %sky_index.1) | copy-start | bytes 964
  2.4 3.1 %collective-permute-start.1 = (f32[6,2,8,500]{3,2,1,0:T(8,128)S(1)}, f32[6,2,8,500]{3,2,1,0:T(8,128)S(1)}, u32[]{:S(2)}, u32[]{:S(2)}) collective-permute-start(f32[6,2,8,500]{3,2,1,0:T(8,128)S(1)} %get-tuple-element.21), channel_id=1, source_target_pairs={{0,1},{1,0},{2,3},{3,2},{4,5},{5,4},{6,7},{7,6},{8,9},{9,8},{10,11... | collective-permute-start | bytes 576008 | tf_op jit(solution)/shard_map/ppermute | solution.py:476
  2.9 6.5 %collective-permute-start = (f32[6,2,8,500]{3,2,1,0:T(8,128)S(1)}, f32[6,2,8,500]{3,2,1,0:T(8,128)S(1)}, u32[]{:S(2)}, u32[]{:S(2)}) collective-permute-start(f32[6,2,8,500]{3,2,1,0:T(8,128)S(1)} %get-tuple-element.20), channel_id=1, source_target_pairs={{0,8},{1,2},{2,1},{3,4},{4,3},{5,6},{6,5},{7,15},{8,0},{9,10},{10,... | collective-permute-start | bytes 576008 | tf_op jit(solution)/shard_map/ppermute | solution.py:476
  10.2 1.2 %collective-permute-start.2 = (f32[2,8,128]{2,1,0:T(8,128)S(1)}, f32[2,8,128]{2,1,0:T(8,128)S(1)}, u32[]{:S(2)}, u32[]{:S(2)}) collective-permute-start(f32[2,8,128]{2,1,0:T(8,128)S(1)} %get-tuple-element.31), channel_id=1, source_target_pairs={{0,1},{1,0},{2,3},{3,2},{4,5},{5,4},{6,7},{7,6},{8,9},{9,8},{10,11... | collective-permute-start | bytes 24584 | tf_op jit(solution)/shard_map/ppermute | solution.py:476
  11.4 5.9 %collective-permute-start.3 = (f32[50,2,8,500]{3,2,1,0:T(8,128)S(1)}, f32[50,2,8,500]{3,2,1,0:T(8,128)S(1)}, u32[]{:S(2)}, u32[]{:S(2)}) collective-permute-start(f32[50,2,8,500]{3,2,1,0:T(8,128)S(1)} %get-tuple-element.32.flux), channel_id=1, source_target_pairs={{0,1},{1,0},{2,3},{3,2},{4,5},{5,4},{6,7},{7,6},{8,9},{9,8},{10,11... | collective-permute-start | bytes 4800008 | tf_op jit(solution)/shard_map/ppermute | solution.py:476
  11.6 3.2 %collective-permute-start.4 = (f32[4,8,128]{2,1,0:T(8,128)S(1)}, f32[4,8,128]{2,1,0:T(8,128)S(1)}, u32[]{:S(2)}, u32[]{:S(2)}) collective-permute-start(f32[4,8,128]{2,1,0:T(8,128)S(1)} %maximum_select_fusion), channel_id=1, source_target_pairs={{0,9},{1,16},{2,11},{3,18},{4,13},{5,20},{6,15},{7,22},{8,1},{9,24... | collective-permute-start | bytes 49160 | tf_op jit(solution)/shard_map/ppermute | solution.py:476
  13.2 4.1 %collective-permute-start.6 = (f32[4,8,128]{2,1,0:T(8,128)S(1)}, f32[4,8,128]{2,1,0:T(8,128)S(1)}, u32[]{:S(2)}, u32[]{:S(2)}) collective-permute-start(f32[4,8,128]{2,1,0:T(8,128)S(1)} %maximum_select_fusion), channel_id=1, source_target_pairs={{0,25},{1,24},{2,27},{3,26},{4,29},{5,28},{6,31},{7,30},{8,17},{9,... | collective-permute-start | bytes 49160 | tf_op jit(solution)/shard_map/ppermute | solution.py:476
  14.7 2.5 %collective-permute-start.5 = (f32[4,8,128]{2,1,0:T(8,128)S(1)}, f32[4,8,128]{2,1,0:T(8,128)S(1)}, u32[]{:S(2)}, u32[]{:S(2)}) collective-permute-start(f32[4,8,128]{2,1,0:T(8,128)S(1)} %collective-permute-done.4), channel_id=1, source_target_pairs={{0,1},{1,0},{2,3},{3,2},{4,5},{5,4},{6,7},{7,6},{8,9},{9,8},{10,11... | collective-permute-start | bytes 49160 | tf_op jit(solution)/shard_map/ppermute | solution.py:476
  17.7 6.6 %collective-permute-start.7 = (f32[4,8,512]{2,1,0:T(8,128)S(1)}, f32[4,8,512]{2,1,0:T(8,128)S(1)}, u32[]{:S(2)}, u32[]{:S(2)}) collective-permute-start(f32[4,8,512]{2,1,0:T(8,128)S(1)} %get-tuple-element.35.refs_0_), channel_id=1, source_target_pairs={{0,4},{1,7},{2,6},{3,5},{4,0},{5,3},{6,2},{7,1},{8,12},{9,15},{10,... | collective-permute-start | bytes 196616 | tf_op jit(solution)/shard_map/ppermute | solution.py:476
  20.1 4.3 %collective-permute-start.8 = (f32[4,8,512]{2,1,0:T(8,128)S(1)}, f32[4,8,512]{2,1,0:T(8,128)S(1)}, u32[]{:S(2)}, u32[]{:S(2)}) collective-permute-start(f32[4,8,512]{2,1,0:T(8,128)S(1)} %get-tuple-element.35.refs_0_), channel_id=1, source_target_pairs={{0,1},{1,2},{2,3},{3,0},{4,5},{5,6},{6,7},{7,4},{8,9},{9,10},{10,1... | collective-permute-start | bytes 196616 | tf_op jit(solution)/shard_map/ppermute | solution.py:476
  24.3 1.3 %collective-permute-start.9 = (f32[4,8,512]{2,1,0:T(8,128)S(1)}, f32[4,8,512]{2,1,0:T(8,128)S(1)}, u32[]{:S(2)}, u32[]{:S(2)}) collective-permute-start(f32[4,8,512]{2,1,0:T(8,128)S(1)} %select_add_fusion.refs_1_), channel_id=1, source_target_pairs={{0,1},{1,0},{2,3},{3,2},{4,5},{5,4},{6,7},{7,6},{8,9},{9,8},{10,11... | collective-permute-start | bytes 196616 | tf_op jit(solution)/shard_map/ppermute | solution.py:476

commit v12 on v11

--- a/solution.py
+++ b/solution.py
@@ -506,10 +506,11 @@
             sums = sums + swap(sums, lambda s, i: (s ^ k, i))
     regress, sky = regress_call(total_rows, flux, other, sums)
     if wave == 8:
-        first = swap(regress, lambda s, i: (s, i ^ (6 if i % 2 else 4)))
-        third = swap(regress, lambda s, i: (s, i ^ (3 if i % 2 else 1)))
-        fetched = first + jnp.where(odd, 0.0, third)
-        terms = [regress, fetched, swap(fetched, other_core)]
+        routes = ((1, 0, 3, 2), (2, 3, 1, 0))
+        third_route = (3, 2, 0, 1)
+        first = swap(regress, lambda s, i: (s, 2 * routes[i % 2][i // 2] + i % 2))
+        third = swap(regress, lambda s, i: (s, 2 * third_route[i // 2] + 1 - i % 2))
+        terms = [regress, first, swap(first, other_core), third]
     else:
         for k in powers(2, wave):
             regress = regress + swap(regress, lambda s, i: (s, i ^ k if i % 2 else -1))

time: 27.3 us -> 26.2 us (0.960)
  waiting for transfers between devices: 8 us -> 6.06 us
  starting transfers between devices: 10.1 us -> 10.9 us
    ppermute x10, waiting for transfers between devices: 8 us -> 6.06 us  [swap(): return lax.ppermute(values, ('spec', 'wave'), pairs)]
    ppermute x10, starting transfers between devices: 10.1 us -> 10.9 us  [swap(): return lax.ppermute(values, ('spec', 'wave'), pairs)]
where the time goes in v12:
time: 26.2 us; the launch traced here: 25.9 us
  starting transfers between devices  10.9 us (42%)
  Pallas kernels  8.23 us (31%)
  waiting for transfers between devices  6.06 us (23%)
  between operations  0.69 us (3%)
    ppermute x10, starting transfers between devices, swap(): return lax.ppermute(values, ('spec', 'wave'), pairs)  10.9 us
    ppermute x10, waiting for transfers between devices, swap(): return lax.ppermute(values, ('spec', 'wave'), pairs)  6.06 us
    pallas_call x1, Pallas kernels, forward_call(): pl.pallas_call(forward_kernel, out_shape=(whole, whole, whole, whole, in_...  3.96 us
    pallas_call x1, Pallas kernels, edge_call(): pl.pallas_call(edge_kernel, out_shape=(message, message, in_vmem((4, size...  1.76 us
    pallas_call x1, Pallas kernels, clean_call(): pl.pallas_call(functools.partial(clean_kernel, total_rows), out_shape=(ja...  1.38 us
    pallas_call x1, Pallas kernels, backward_call(): pl.pallas_call(functools.partial(backward_kernel, wave), out_shape=(in_vm...  0.69 us
  transfers between devices with their start and end apart: 10, of which 5 were waited for; matrix products, arithmetic and copies ran while one was open for 0% of the time, Pallas kernels for 15%

profile of v12, /device:TPU:0, one launch (start us, length us, event | category | flops | bytes accessed | tf_op | source)
XLA Modules:
  0.0 25.9 jit_solution(15292173688095343444)
XLA Ops:
  0.6 1.8 %edges.1 = (f32[6,2,8,500]{3,2,1,0:T(8,128)S(1)}, f32[6,2,8,500]{3,2,1,0:T(8,128)S(1)}, f32[4,10,2,8,500]{4,3,2,1,0:T(8,128)S(1)}) custom-call(f32[8,50,2,500]{3,2,1,0:T(2,128)} %bitcast.7, f32[8,50,2,500]{3,2,1,0:T(2,128)} %bitcast.9, s32[8,50,2,500]{3,2,1,0:T(2,128)} %bitcast.11, f32[8,50,2,500]{3,2,1,0:T(2,128)} %bitcast.13, f32[8,50,2,500]{3,2,1,0:T(2,128)} %bitcast.15), custom_call_target="tpu_custom_call" | custom-call | flops 1000000 | bytes 1000000 | tf_op jit(solution)/shard_map/edges/pallas_call | solution.py:114
  2.4 0.5 %collective-permute-start.1 = (f32[6,2,8,500]{3,2,1,0:T(8,128)S(1)}, f32[6,2,8,500]{3,2,1,0:T(8,128)S(1)}, u32[]{:S(2)}, u32[]{:S(2)}) collective-permute-start(f32[6,2,8,500]{3,2,1,0:T(8,128)S(1)} %get-tuple-element.21), channel_id=1, source_target_pairs={{0,1},{1,0},{2,3},{3,2},{4,5},{5,4},{6,7},{7,6},{8,9},{9,8},{10,11... | collective-permute-start | bytes 576008 | tf_op jit(solution)/shard_map/ppermute | solution.py:476
  2.9 2.6 %collective-permute-start = (f32[6,2,8,500]{3,2,1,0:T(8,128)S(1)}, f32[6,2,8,500]{3,2,1,0:T(8,128)S(1)}, u32[]{:S(2)}, u32[]{:S(2)}) collective-permute-start(f32[6,2,8,500]{3,2,1,0:T(8,128)S(1)} %get-tuple-element.20), channel_id=1, source_target_pairs={{0,8},{1,2},{2,1},{3,4},{4,3},{5,6},{6,5},{7,15},{8,0},{9,10},{10,... | collective-permute-start | bytes 576008 | tf_op jit(solution)/shard_map/ppermute | solution.py:476
  5.5 0.0 collective-permute-done.1.near
  5.5 4.0 %forward.1 = (f32[50,2,8,500]{3,2,1,0:T(8,128)S(1)}, f32[50,2,8,500]{3,2,1,0:T(8,128)S(1)}, f32[50,2,8,500]{3,2,1,0:T(8,128)S(1)}, f32[50,2,8,500]{3,2,1,0:T(8,1...) custom-call(f32[6,2,8,500]{3,2,1,0:T(8,128)S(1)} %collective-permute-done.1.near, ...), custom_call_target="tpu_custom_call" | custom-call | flops 10000000 | bytes 10000000 | tf_op jit(solution)/shard_map/forward/pallas_call | solution.py:241
  9.5 0.0 collective-permute-done.far
  9.5 0.7 %backward.1 = (f32[50,2,8,500]{3,2,1,0:T(8,128)S(1)}, f32[2,8,128]{2,1,0:T(8,128)S(1)}) custom-call(f32[6,2,8,500]{3,2,1,0:T(8,128)S(1)} %collective-permute-done.far, f32[50,2,8,500]{3,2,1,0:T(8,128)S(1)} %get-tuple-element.23.lower, f32[50,2,8,500]{3,2,1,0:T(8,128)S(1)} %get-tuple-element.24.lower_far, f32[50,2,8,500]{3,2,1,0:T(8,128)S(1)} %get-tuple-element.25.half, ...), custom_call_target="tpu_custom_call" | custom-call | flops 10000000 | bytes 10000000 | tf_op jit(solution)/shard_map/backward/pallas_call | solution.py:320
  10.2 0.2 collective-permute-start.2
  10.4 1.0 %collective-permute-done.2 = f32[2,8,128]{2,1,0:T(8,128)S(1)} collective-permute-done((f32[2,8,128]{2,1,0:T(8,128)S(1)}, f32[2,8,128]{2,1,0:T(8,128)S(1)}, u32[]{:S(2)}, u32[]{:S(2)}) %collective-permute-start.2) | collective-permute-done | bytes 8224 | tf_op jit(solution)/shard_map/ppermute | solution.py:476
  11.4 0.2 collective-permute-start.3
  11.6 1.6 %collective-permute-start.4 = (f32[4,8,128]{2,1,0:T(8,128)S(1)}, f32[4,8,128]{2,1,0:T(8,128)S(1)}, u32[]{:S(2)}, u32[]{:S(2)}) collective-permute-start(f32[4,8,128]{2,1,0:T(8,128)S(1)} %maximum_select_fusion), channel_id=1, source_target_pairs={{0,9},{1,16},{2,11},{3,18},{4,13},{5,20},{6,15},{7,22},{8,1},{9,24... | collective-permute-start | bytes 49160 | tf_op jit(solution)/shard_map/ppermute | solution.py:476
  13.2 1.2 %collective-permute-start.6 = (f32[4,8,128]{2,1,0:T(8,128)S(1)}, f32[4,8,128]{2,1,0:T(8,128)S(1)}, u32[]{:S(2)}, u32[]{:S(2)}) collective-permute-start(f32[4,8,128]{2,1,0:T(8,128)S(1)} %maximum_select_fusion), channel_id=1, source_target_pairs={{0,25},{1,24},{2,27},{3,26},{4,29},{5,28},{6,31},{7,30},{8,17},{9,... | collective-permute-start | bytes 49160 | tf_op jit(solution)/shard_map/ppermute | solution.py:476
  14.4 0.3 %collective-permute-done.4 = f32[4,8,128]{2,1,0:T(8,128)S(1)} collective-permute-done((f32[4,8,128]{2,1,0:T(8,128)S(1)}, f32[4,8,128]{2,1,0:T(8,128)S(1)}, u32[]{:S(2)}, u32[]{:S(2)}) %collective-permute-start.4) | collective-permute-done | bytes 16416 | tf_op jit(solution)/shard_map/ppermute | solution.py:476
  14.7 0.3 %collective-permute-start.5 = (f32[4,8,128]{2,1,0:T(8,128)S(1)}, f32[4,8,128]{2,1,0:T(8,128)S(1)}, u32[]{:S(2)}, u32[]{:S(2)}) collective-permute-start(f32[4,8,128]{2,1,0:T(8,128)S(1)} %collective-permute-done.4), channel_id=1, source_target_pairs={{0,1},{1,0},{2,3},{3,2},{4,5},{5,4},{6,7},{7,6},{8,9},{9,8},{10,11... | collective-permute-start | bytes 49160 | tf_op jit(solution)/shard_map/ppermute | solution.py:476
  15.0 2.2 %collective-permute-done.6 = f32[4,8,128]{2,1,0:T(8,128)S(1)} collective-permute-done((f32[4,8,128]{2,1,0:T(8,128)S(1)}, f32[4,8,128]{2,1,0:T(8,128)S(1)}, u32[]{:S(2)}, u32[]{:S(2)}) %collective-permute-start.6) | collective-permute-done | bytes 16416 | tf_op jit(solution)/shard_map/ppermute | solution.py:476
  17.2 0.0 collective-permute-done.3.other
  17.2 0.4 %regress.1 = (f32[4,8,512]{2,1,0:T(8,128)S(1)}, f32[8,128]{1,0:T(8,128)S(1)}) custom-call(f32[50,2,8,500]{3,2,1,0:T(8,128)S(1)} %get-tuple-element.32.flux, f32[50,2,8,500]{3,2,1,0:T(8,128)S(1)} %collective-permute-done.3.other, f32[4,8,128]{2,1,0:T(8,128)S(1)} %add_add_fusion.sums), custom_call_target="tpu_custom_call" | custom-call | flops 1000000 | bytes 1000000 | tf_op jit(solution)/shard_map/regress/pallas_call | solution.py:380
  17.7 1.3 %collective-permute-start.7 = (f32[4,8,512]{2,1,0:T(8,128)S(1)}, f32[4,8,512]{2,1,0:T(8,128)S(1)}, u32[]{:S(2)}, u32[]{:S(2)}) collective-permute-start(f32[4,8,512]{2,1,0:T(8,128)S(1)} %get-tuple-element.35.refs_0_), channel_id=1, source_target_pairs={{0,2},{1,5},{2,0},{3,7},{4,6},{5,3},{6,4},{7,1},{8,10},{9,13},{10,... | collective-permute-start | bytes 196616 | tf_op jit(solution)/shard_map/ppermute | solution.py:476
  19.0 2.1 %collective-permute-start.9 = (f32[4,8,512]{2,1,0:T(8,128)S(1)}, f32[4,8,512]{2,1,0:T(8,128)S(1)}, u32[]{:S(2)}, u32[]{:S(2)}) collective-permute-start(f32[4,8,512]{2,1,0:T(8,128)S(1)} %get-tuple-element.35.refs_0_), channel_id=1, source_target_pairs={{0,7},{1,6},{2,5},{3,4},{4,1},{5,0},{6,3},{7,2},{8,15},{9,14},{10,... | collective-permute-start | bytes 196616 | tf_op jit(solution)/shard_map/ppermute | solution.py:476
  21.1 0.9 %collective-permute-done.7.refs_1_ = f32[4,8,512]{2,1,0:T(8,128)S(1)} collective-permute-done((f32[4,8,512]{2,1,0:T(8,128)S(1)}, f32[4,8,512]{2,1,0:T(8,128)S(1)}, u32[]{:S(2)}, u32[]{:S(2)}) %collective-permute-start.7) | collective-permute-done | bytes 65568 | tf_op jit(solution)/shard_map/ppermute | solution.py:476
  22.0 0.9 %collective-permute-start.8 = (f32[4,8,512]{2,1,0:T(8,128)S(1)}, f32[4,8,512]{2,1,0:T(8,128)S(1)}, u32[]{:S(2)}, u32[]{:S(2)}) collective-permute-start(f32[4,8,512]{2,1,0:T(8,128)S(1)} %collective-permute-done.7.refs_1_), channel_id=1, source_target_pairs={{0,1},{1,0},{2,3},{3,2},{4,5},{5,4},{6,7},{7,6},{8,9},{9,8},{10,11... | collective-permute-start | bytes 196616 | tf_op jit(solution)/shard_map/ppermute | solution.py:476
  22.9 1.6 %collective-permute-done.9.refs_3_ = f32[4,8,512]{2,1,0:T(8,128)S(1)} collective-permute-done((f32[4,8,512]{2,1,0:T(8,128)S(1)}, f32[4,8,512]{2,1,0:T(8,128)S(1)}, u32[]{:S(2)}, u32[]{:S(2)}) %collective-permute-start.9) | collective-permute-done | bytes 65568 | tf_op jit(solution)/shard_map/ppermute | solution.py:476
  24.5 0.0 collective-permute-done.8.refs_2_
  24.5 1.4 %clean.1 = (f32[8,50,2,500]{3,2,1,0:T(2,128)}, f32[8,128]{1,0:T(8,128)}) custom-call(f32[50,2,8,500]{3,2,1,0:T(8,128)S(1)} %get-tuple-element.32.flux, f32[8,128]{1,0:T(8,128)S(1)} %get-tuple-element.34.sky_ref, f32[4,8,512]{2,1,0:T(8,128)S(1)} %get-tuple-element.35.refs_0_, f32[4,8,512]{2,1,0:T(8,128)S(1)} %collective-permute-done.7.refs_1_, ...), custom_call_target="tpu_custom_call" | custom-call | flops 1000000 | bytes 1000000 | tf_op jit(solution)/shard_map/clean/pallas_call | solution.py:439
  (5 shorter events, 0.0 us)
Async XLA Ops:
  0.6 4.9 %copy-start = (s32[2,40]{1,0:T(2,128)S(1)}, s32[2,40]{1,0:T(2,128)}, u32[]{:S(2)}) copy-start(s32[2,40]{1,0:T(2,128)} %sky_index.1) | copy-start | bytes 964
  2.4 3.1 %collective-permute-start.1 = (f32[6,2,8,500]{3,2,1,0:T(8,128)S(1)}, f32[6,2,8,500]{3,2,1,0:T(8,128)S(1)}, u32[]{:S(2)}, u32[]{:S(2)}) collective-permute-start(f32[6,2,8,500]{3,2,1,0:T(8,128)S(1)} %get-tuple-element.21), channel_id=1, source_target_pairs={{0,1},{1,0},{2,3},{3,2},{4,5},{5,4},{6,7},{7,6},{8,9},{9,8},{10,11... | collective-permute-start | bytes 576008 | tf_op jit(solution)/shard_map/ppermute | solution.py:476
  2.9 6.5 %collective-permute-start = (f32[6,2,8,500]{3,2,1,0:T(8,128)S(1)}, f32[6,2,8,500]{3,2,1,0:T(8,128)S(1)}, u32[]{:S(2)}, u32[]{:S(2)}) collective-permute-start(f32[6,2,8,500]{3,2,1,0:T(8,128)S(1)} %get-tuple-element.20), channel_id=1, source_target_pairs={{0,8},{1,2},{2,1},{3,4},{4,3},{5,6},{6,5},{7,15},{8,0},{9,10},{10,... | collective-permute-start | bytes 576008 | tf_op jit(solution)/shard_map/ppermute | solution.py:476
  10.2 1.2 %collective-permute-start.2 = (f32[2,8,128]{2,1,0:T(8,128)S(1)}, f32[2,8,128]{2,1,0:T(8,128)S(1)}, u32[]{:S(2)}, u32[]{:S(2)}) collective-permute-start(f32[2,8,128]{2,1,0:T(8,128)S(1)} %get-tuple-element.31), channel_id=1, source_target_pairs={{0,1},{1,0},{2,3},{3,2},{4,5},{5,4},{6,7},{7,6},{8,9},{9,8},{10,11... | collective-permute-start | bytes 24584 | tf_op jit(solution)/shard_map/ppermute | solution.py:476
  11.4 5.9 %collective-permute-start.3 = (f32[50,2,8,500]{3,2,1,0:T(8,128)S(1)}, f32[50,2,8,500]{3,2,1,0:T(8,128)S(1)}, u32[]{:S(2)}, u32[]{:S(2)}) collective-permute-start(f32[50,2,8,500]{3,2,1,0:T(8,128)S(1)} %get-tuple-element.32.flux), channel_id=1, source_target_pairs={{0,1},{1,0},{2,3},{3,2},{4,5},{5,4},{6,7},{7,6},{8,9},{9,8},{10,11... | collective-permute-start | bytes 4800008 | tf_op jit(solution)/shard_map/ppermute | solution.py:476
  11.6 3.2 %collective-permute-start.4 = (f32[4,8,128]{2,1,0:T(8,128)S(1)}, f32[4,8,128]{2,1,0:T(8,128)S(1)}, u32[]{:S(2)}, u32[]{:S(2)}) collective-permute-start(f32[4,8,128]{2,1,0:T(8,128)S(1)} %maximum_select_fusion), channel_id=1, source_target_pairs={{0,9},{1,16},{2,11},{3,18},{4,13},{5,20},{6,15},{7,22},{8,1},{9,24... | collective-permute-start | bytes 49160 | tf_op jit(solution)/shard_map/ppermute | solution.py:476
  13.2 4.1 %collective-permute-start.6 = (f32[4,8,128]{2,1,0:T(8,128)S(1)}, f32[4,8,128]{2,1,0:T(8,128)S(1)}, u32[]{:S(2)}, u32[]{:S(2)}) collective-permute-start(f32[4,8,128]{2,1,0:T(8,128)S(1)} %maximum_select_fusion), channel_id=1, source_target_pairs={{0,25},{1,24},{2,27},{3,26},{4,29},{5,28},{6,31},{7,30},{8,17},{9,... | collective-permute-start | bytes 49160 | tf_op jit(solution)/shard_map/ppermute | solution.py:476
  14.7 2.5 %collective-permute-start.5 = (f32[4,8,128]{2,1,0:T(8,128)S(1)}, f32[4,8,128]{2,1,0:T(8,128)S(1)}, u32[]{:S(2)}, u32[]{:S(2)}) collective-permute-start(f32[4,8,128]{2,1,0:T(8,128)S(1)} %collective-permute-done.4), channel_id=1, source_target_pairs={{0,1},{1,0},{2,3},{3,2},{4,5},{5,4},{6,7},{7,6},{8,9},{9,8},{10,11... | collective-permute-start | bytes 49160 | tf_op jit(solution)/shard_map/ppermute | solution.py:476
  17.7 4.3 %collective-permute-start.7 = (f32[4,8,512]{2,1,0:T(8,128)S(1)}, f32[4,8,512]{2,1,0:T(8,128)S(1)}, u32[]{:S(2)}, u32[]{:S(2)}) collective-permute-start(f32[4,8,512]{2,1,0:T(8,128)S(1)} %get-tuple-element.35.refs_0_), channel_id=1, source_target_pairs={{0,2},{1,5},{2,0},{3,7},{4,6},{5,3},{6,4},{7,1},{8,10},{9,13},{10,... | collective-permute-start | bytes 196616 | tf_op jit(solution)/shard_map/ppermute | solution.py:476
  19.0 5.5 %collective-permute-start.9 = (f32[4,8,512]{2,1,0:T(8,128)S(1)}, f32[4,8,512]{2,1,0:T(8,128)S(1)}, u32[]{:S(2)}, u32[]{:S(2)}) collective-permute-start(f32[4,8,512]{2,1,0:T(8,128)S(1)} %get-tuple-element.35.refs_0_), channel_id=1, source_target_pairs={{0,7},{1,6},{2,5},{3,4},{4,1},{5,0},{6,3},{7,2},{8,15},{9,14},{10,... | collective-permute-start | bytes 196616 | tf_op jit(solution)/shard_map/ppermute | solution.py:476
  22.0 2.5 %collective-permute-start.8 = (f32[4,8,512]{2,1,0:T(8,128)S(1)}, f32[4,8,512]{2,1,0:T(8,128)S(1)}, u32[]{:S(2)}, u32[]{:S(2)}) collective-permute-start(f32[4,8,512]{2,1,0:T(8,128)S(1)} %collective-permute-done.7.refs_1_), channel_id=1, source_target_pairs={{0,1},{1,0},{2,3},{3,2},{4,5},{5,4},{6,7},{7,6},{8,9},{9,8},{10,11... | collective-permute-start | bytes 196616 | tf_op jit(solution)/shard_map/ppermute | solution.py:476

commit v13 on v12

--- a/solution.py
+++ b/solution.py
@@ -109,7 +109,7 @@
 
 def edge_call(arrays):
     exposures, rows, specs, fibres = arrays[0].shape
-    size = max(HALO, rows // 5)
+    size = max(HALO, rows * 4 // 25)
     message = in_vmem((PARTS, specs, exposures, fibres))
     return pl.pallas_call(
         edge_kernel,

time: 26.2 us -> 26 us (level)
  transfers between devices with their start and end apart: 10 -> 10, of which waited for: 5 -> 5; matrix products, arithmetic and copies ran while one was open for 0% -> 0% of each run, Pallas kernels for 15% -> 16%
where the time goes in v13:
time: 26 us; the launch traced here: 25.8 us
  starting transfers between devices  10.8 us (42%)
  Pallas kernels  8.25 us (32%)
  waiting for transfers between devices  6 us (23%)
  between operations  0.69 us (3%)
    ppermute x10, starting transfers between devices, swap(): return lax.ppermute(values, ('spec', 'wave'), pairs)  10.8 us
    ppermute x10, waiting for transfers between devices, swap(): return lax.ppermute(values, ('spec', 'wave'), pairs)  6 us
    pallas_call x1, Pallas kernels, forward_call(): pl.pallas_call(forward_kernel, out_shape=(whole, whole, whole, whole, in_...  4.09 us
    pallas_call x1, Pallas kernels, edge_call(): pl.pallas_call(edge_kernel, out_shape=(message, message, in_vmem((4, size...  1.66 us
    pallas_call x1, Pallas kernels, clean_call(): pl.pallas_call(functools.partial(clean_kernel, total_rows), out_shape=(ja...  1.38 us
    pallas_call x1, Pallas kernels, backward_call(): pl.pallas_call(functools.partial(backward_kernel, wave), out_shape=(in_vm...  0.68 us
  transfers between devices with their start and end apart: 10, of which 5 were waited for; matrix products, arithmetic and copies ran while one was open for 0% of the time, Pallas kernels for 16%

profile of v13, /device:TPU:0, one launch (start us, length us, event | category | flops | bytes accessed | tf_op | source)
XLA Modules:
  0.0 25.8 jit_solution(17665776020385525950)
XLA Ops:
  0.6 1.7 %edges.1 = (f32[6,2,8,500]{3,2,1,0:T(8,128)S(1)}, f32[6,2,8,500]{3,2,1,0:T(8,128)S(1)}, f32[4,8,2,8,500]{4,3,2,1,0:T(8,128)S(1)}) custom-call(f32[8,50,2,500]{3,2,1,0:T(2,128)} %bitcast.7, f32[8,50,2,500]{3,2,1,0:T(2,128)} %bitcast.9, s32[8,50,2,500]{3,2,1,0:T(2,128)} %bitcast.11, f32[8,50,2,500]{3,2,1,0:T(2,128)} %bitcast.13, f32[8,50,2,500]{3,2,1,0:T(2,128)} %bitcast.15), custom_call_target="tpu_custom_call" | custom-call | flops 1000000 | bytes 1000000 | tf_op jit(solution)/shard_map/edges/pallas_call | solution.py:114
  2.3 0.5 %collective-permute-start.1 = (f32[6,2,8,500]{3,2,1,0:T(8,128)S(1)}, f32[6,2,8,500]{3,2,1,0:T(8,128)S(1)}, u32[]{:S(2)}, u32[]{:S(2)}) collective-permute-start(f32[6,2,8,500]{3,2,1,0:T(8,128)S(1)} %get-tuple-element.21), channel_id=1, source_target_pairs={{0,1},{1,0},{2,3},{3,2},{4,5},{5,4},{6,7},{7,6},{8,9},{9,8},{10,11... | collective-permute-start | bytes 576008 | tf_op jit(solution)/shard_map/ppermute | solution.py:476
  2.8 2.6 %collective-permute-start = (f32[6,2,8,500]{3,2,1,0:T(8,128)S(1)}, f32[6,2,8,500]{3,2,1,0:T(8,128)S(1)}, u32[]{:S(2)}, u32[]{:S(2)}) collective-permute-start(f32[6,2,8,500]{3,2,1,0:T(8,128)S(1)} %get-tuple-element.20), channel_id=1, source_target_pairs={{0,8},{1,2},{2,1},{3,4},{4,3},{5,6},{6,5},{7,15},{8,0},{9,10},{10,... | collective-permute-start | bytes 576008 | tf_op jit(solution)/shard_map/ppermute | solution.py:476
  5.4 0.0 collective-permute-done.1.near
  5.4 4.1 %forward.1 = (f32[50,2,8,500]{3,2,1,0:T(8,128)S(1)}, f32[50,2,8,500]{3,2,1,0:T(8,128)S(1)}, f32[50,2,8,500]{3,2,1,0:T(8,128)S(1)}, f32[50,2,8,500]{3,2,1,0:T(8,1...) custom-call(f32[6,2,8,500]{3,2,1,0:T(8,128)S(1)} %collective-permute-done.1.near, ...), custom_call_target="tpu_custom_call" | custom-call | flops 10000000 | bytes 10000000 | tf_op jit(solution)/shard_map/forward/pallas_call | solution.py:241
  9.5 0.7 %backward.1 = (f32[50,2,8,500]{3,2,1,0:T(8,128)S(1)}, f32[2,8,128]{2,1,0:T(8,128)S(1)}) custom-call(f32[6,2,8,500]{3,2,1,0:T(8,128)S(1)} %collective-permute-done.far, f32[50,2,8,500]{3,2,1,0:T(8,128)S(1)} %get-tuple-element.23.lower, f32[50,2,8,500]{3,2,1,0:T(8,128)S(1)} %get-tuple-element.24.lower_far, f32[50,2,8,500]{3,2,1,0:T(8,128)S(1)} %get-tuple-element.25.half, ...), custom_call_target="tpu_custom_call" | custom-call | flops 10000000 | bytes 10000000 | tf_op jit(solution)/shard_map/backward/pallas_call | solution.py:320
  10.2 0.2 collective-permute-start.2
  10.4 1.0 %collective-permute-done.2 = f32[2,8,128]{2,1,0:T(8,128)S(1)} collective-permute-done((f32[2,8,128]{2,1,0:T(8,128)S(1)}, f32[2,8,128]{2,1,0:T(8,128)S(1)}, u32[]{:S(2)}, u32[]{:S(2)}) %collective-permute-start.2) | collective-permute-done | bytes 8224 | tf_op jit(solution)/shard_map/ppermute | solution.py:476
  11.4 0.2 collective-permute-start.3
  11.6 1.5 %collective-permute-start.4 = (f32[4,8,128]{2,1,0:T(8,128)S(1)}, f32[4,8,128]{2,1,0:T(8,128)S(1)}, u32[]{:S(2)}, u32[]{:S(2)}) collective-permute-start(f32[4,8,128]{2,1,0:T(8,128)S(1)} %maximum_select_fusion), channel_id=1, source_target_pairs={{0,9},{1,16},{2,11},{3,18},{4,13},{5,20},{6,15},{7,22},{8,1},{9,24... | collective-permute-start | bytes 49160 | tf_op jit(solution)/shard_map/ppermute | solution.py:476
  13.1 1.2 %collective-permute-start.6 = (f32[4,8,128]{2,1,0:T(8,128)S(1)}, f32[4,8,128]{2,1,0:T(8,128)S(1)}, u32[]{:S(2)}, u32[]{:S(2)}) collective-permute-start(f32[4,8,128]{2,1,0:T(8,128)S(1)} %maximum_select_fusion), channel_id=1, source_target_pairs={{0,25},{1,24},{2,27},{3,26},{4,29},{5,28},{6,31},{7,30},{8,17},{9,... | collective-permute-start | bytes 49160 | tf_op jit(solution)/shard_map/ppermute | solution.py:476
  14.3 0.5 %collective-permute-done.4 = f32[4,8,128]{2,1,0:T(8,128)S(1)} collective-permute-done((f32[4,8,128]{2,1,0:T(8,128)S(1)}, f32[4,8,128]{2,1,0:T(8,128)S(1)}, u32[]{:S(2)}, u32[]{:S(2)}) %collective-permute-start.4) | collective-permute-done | bytes 16416 | tf_op jit(solution)/shard_map/ppermute | solution.py:476
  14.8 0.3 %collective-permute-start.5 = (f32[4,8,128]{2,1,0:T(8,128)S(1)}, f32[4,8,128]{2,1,0:T(8,128)S(1)}, u32[]{:S(2)}, u32[]{:S(2)}) collective-permute-start(f32[4,8,128]{2,1,0:T(8,128)S(1)} %collective-permute-done.4), channel_id=1, source_target_pairs={{0,1},{1,0},{2,3},{3,2},{4,5},{5,4},{6,7},{7,6},{8,9},{9,8},{10,11... | collective-permute-start | bytes 49160 | tf_op jit(solution)/shard_map/ppermute | solution.py:476
  15.1 2.1 %collective-permute-done.6 = f32[4,8,128]{2,1,0:T(8,128)S(1)} collective-permute-done((f32[4,8,128]{2,1,0:T(8,128)S(1)}, f32[4,8,128]{2,1,0:T(8,128)S(1)}, u32[]{:S(2)}, u32[]{:S(2)}) %collective-permute-start.6) | collective-permute-done | bytes 16416 | tf_op jit(solution)/shard_map/ppermute | solution.py:476
  17.1 0.0 collective-permute-done.5
  17.1 0.0 collective-permute-done.3.other
  17.1 0.4 %regress.1 = (f32[4,8,512]{2,1,0:T(8,128)S(1)}, f32[8,128]{1,0:T(8,128)S(1)}) custom-call(f32[50,2,8,500]{3,2,1,0:T(8,128)S(1)} %get-tuple-element.32.flux, f32[50,2,8,500]{3,2,1,0:T(8,128)S(1)} %collective-permute-done.3.other, f32[4,8,128]{2,1,0:T(8,128)S(1)} %add_add_fusion.sums), custom_call_target="tpu_custom_call" | custom-call | flops 1000000 | bytes 1000000 | tf_op jit(solution)/shard_map/regress/pallas_call | solution.py:380
  17.6 1.5 %collective-permute-start.7 = (f32[4,8,512]{2,1,0:T(8,128)S(1)}, f32[4,8,512]{2,1,0:T(8,128)S(1)}, u32[]{:S(2)}, u32[]{:S(2)}) collective-permute-start(f32[4,8,512]{2,1,0:T(8,128)S(1)} %get-tuple-element.35.refs_0_), channel_id=1, source_target_pairs={{0,2},{1,5},{2,0},{3,7},{4,6},{5,3},{6,4},{7,1},{8,10},{9,13},{10,... | collective-permute-start | bytes 196616 | tf_op jit(solution)/shard_map/ppermute | solution.py:476
  19.0 2.0 %collective-permute-start.9 = (f32[4,8,512]{2,1,0:T(8,128)S(1)}, f32[4,8,512]{2,1,0:T(8,128)S(1)}, u32[]{:S(2)}, u32[]{:S(2)}) collective-permute-start(f32[4,8,512]{2,1,0:T(8,128)S(1)} %get-tuple-element.35.refs_0_), channel_id=1, source_target_pairs={{0,7},{1,6},{2,5},{3,4},{4,1},{5,0},{6,3},{7,2},{8,15},{9,14},{10,... | collective-permute-start | bytes 196616 | tf_op jit(solution)/shard_map/ppermute | solution.py:476
  21.0 0.9 %collective-permute-done.7.refs_1_ = f32[4,8,512]{2,1,0:T(8,128)S(1)} collective-permute-done((f32[4,8,512]{2,1,0:T(8,128)S(1)}, f32[4,8,512]{2,1,0:T(8,128)S(1)}, u32[]{:S(2)}, u32[]{:S(2)}) %collective-permute-start.7) | collective-permute-done | bytes 65568 | tf_op jit(solution)/shard_map/ppermute | solution.py:476
  21.9 0.8 %collective-permute-start.8 = (f32[4,8,512]{2,1,0:T(8,128)S(1)}, f32[4,8,512]{2,1,0:T(8,128)S(1)}, u32[]{:S(2)}, u32[]{:S(2)}) collective-permute-start(f32[4,8,512]{2,1,0:T(8,128)S(1)} %collective-permute-done.7.refs_1_), channel_id=1, source_target_pairs={{0,1},{1,0},{2,3},{3,2},{4,5},{5,4},{6,7},{7,6},{8,9},{9,8},{10,11... | collective-permute-start | bytes 196616 | tf_op jit(solution)/shard_map/ppermute | solution.py:476
  22.8 1.6 %collective-permute-done.9.refs_3_ = f32[4,8,512]{2,1,0:T(8,128)S(1)} collective-permute-done((f32[4,8,512]{2,1,0:T(8,128)S(1)}, f32[4,8,512]{2,1,0:T(8,128)S(1)}, u32[]{:S(2)}, u32[]{:S(2)}) %collective-permute-start.9) | collective-permute-done | bytes 65568 | tf_op jit(solution)/shard_map/ppermute | solution.py:476
  24.4 0.0 collective-permute-done.8.refs_2_
  24.4 1.4 %clean.1 = (f32[8,50,2,500]{3,2,1,0:T(2,128)}, f32[8,128]{1,0:T(8,128)}) custom-call(f32[50,2,8,500]{3,2,1,0:T(8,128)S(1)} %get-tuple-element.32.flux, f32[8,128]{1,0:T(8,128)S(1)} %get-tuple-element.34.sky_ref, f32[4,8,512]{2,1,0:T(8,128)S(1)} %get-tuple-element.35.refs_0_, f32[4,8,512]{2,1,0:T(8,128)S(1)} %collective-permute-done.7.refs_1_, ...), custom_call_target="tpu_custom_call" | custom-call | flops 1000000 | bytes 1000000 | tf_op jit(solution)/shard_map/clean/pallas_call | solution.py:439
  (5 shorter events, 0.0 us)
Async XLA Ops:
  0.6 4.8 %copy-start = (s32[2,40]{1,0:T(2,128)S(1)}, s32[2,40]{1,0:T(2,128)}, u32[]{:S(2)}) copy-start(s32[2,40]{1,0:T(2,128)} %sky_index.1) | copy-start | bytes 964
  2.3 3.1 %collective-permute-start.1 = (f32[6,2,8,500]{3,2,1,0:T(8,128)S(1)}, f32[6,2,8,500]{3,2,1,0:T(8,128)S(1)}, u32[]{:S(2)}, u32[]{:S(2)}) collective-permute-start(f32[6,2,8,500]{3,2,1,0:T(8,128)S(1)} %get-tuple-element.21), channel_id=1, source_target_pairs={{0,1},{1,0},{2,3},{3,2},{4,5},{5,4},{6,7},{7,6},{8,9},{9,8},{10,11... | collective-permute-start | bytes 576008 | tf_op jit(solution)/shard_map/ppermute | solution.py:476
  2.8 6.7 %collective-permute-start = (f32[6,2,8,500]{3,2,1,0:T(8,128)S(1)}, f32[6,2,8,500]{3,2,1,0:T(8,128)S(1)}, u32[]{:S(2)}, u32[]{:S(2)}) collective-permute-start(f32[6,2,8,500]{3,2,1,0:T(8,128)S(1)} %get-tuple-element.20), channel_id=1, source_target_pairs={{0,8},{1,2},{2,1},{3,4},{4,3},{5,6},{6,5},{7,15},{8,0},{9,10},{10,... | collective-permute-start | bytes 576008 | tf_op jit(solution)/shard_map/ppermute | solution.py:476
  10.2 1.2 %collective-permute-start.2 = (f32[2,8,128]{2,1,0:T(8,128)S(1)}, f32[2,8,128]{2,1,0:T(8,128)S(1)}, u32[]{:S(2)}, u32[]{:S(2)}) collective-permute-start(f32[2,8,128]{2,1,0:T(8,128)S(1)} %get-tuple-element.31), channel_id=1, source_target_pairs={{0,1},{1,0},{2,3},{3,2},{4,5},{5,4},{6,7},{7,6},{8,9},{9,8},{10,11... | collective-permute-start | bytes 24584 | tf_op jit(solution)/shard_map/ppermute | solution.py:476
  11.4 5.8 %collective-permute-start.3 = (f32[50,2,8,500]{3,2,1,0:T(8,128)S(1)}, f32[50,2,8,500]{3,2,1,0:T(8,128)S(1)}, u32[]{:S(2)}, u32[]{:S(2)}) collective-permute-start(f32[50,2,8,500]{3,2,1,0:T(8,128)S(1)} %get-tuple-element.32.flux), channel_id=1, source_target_pairs={{0,1},{1,0},{2,3},{3,2},{4,5},{5,4},{6,7},{7,6},{8,9},{9,8},{10,11... | collective-permute-start | bytes 4800008 | tf_op jit(solution)/shard_map/ppermute | solution.py:476
  11.6 3.2 %collective-permute-start.4 = (f32[4,8,128]{2,1,0:T(8,128)S(1)}, f32[4,8,128]{2,1,0:T(8,128)S(1)}, u32[]{:S(2)}, u32[]{:S(2)}) collective-permute-start(f32[4,8,128]{2,1,0:T(8,128)S(1)} %maximum_select_fusion), channel_id=1, source_target_pairs={{0,9},{1,16},{2,11},{3,18},{4,13},{5,20},{6,15},{7,22},{8,1},{9,24... | collective-permute-start | bytes 49160 | tf_op jit(solution)/shard_map/ppermute | solution.py:476
  13.1 4.1 %collective-permute-start.6 = (f32[4,8,128]{2,1,0:T(8,128)S(1)}, f32[4,8,128]{2,1,0:T(8,128)S(1)}, u32[]{:S(2)}, u32[]{:S(2)}) collective-permute-start(f32[4,8,128]{2,1,0:T(8,128)S(1)} %maximum_select_fusion), channel_id=1, source_target_pairs={{0,25},{1,24},{2,27},{3,26},{4,29},{5,28},{6,31},{7,30},{8,17},{9,... | collective-permute-start | bytes 49160 | tf_op jit(solution)/shard_map/ppermute | solution.py:476
  14.8 2.4 %collective-permute-start.5 = (f32[4,8,128]{2,1,0:T(8,128)S(1)}, f32[4,8,128]{2,1,0:T(8,128)S(1)}, u32[]{:S(2)}, u32[]{:S(2)}) collective-permute-start(f32[4,8,128]{2,1,0:T(8,128)S(1)} %collective-permute-done.4), channel_id=1, source_target_pairs={{0,1},{1,0},{2,3},{3,2},{4,5},{5,4},{6,7},{7,6},{8,9},{9,8},{10,11... | collective-permute-start | bytes 49160 | tf_op jit(solution)/shard_map/ppermute | solution.py:476
  17.6 4.3 %collective-permute-start.7 = (f32[4,8,512]{2,1,0:T(8,128)S(1)}, f32[4,8,512]{2,1,0:T(8,128)S(1)}, u32[]{:S(2)}, u32[]{:S(2)}) collective-permute-start(f32[4,8,512]{2,1,0:T(8,128)S(1)} %get-tuple-element.35.refs_0_), channel_id=1, source_target_pairs={{0,2},{1,5},{2,0},{3,7},{4,6},{5,3},{6,4},{7,1},{8,10},{9,13},{10,... | collective-permute-start | bytes 196616 | tf_op jit(solution)/shard_map/ppermute | solution.py:476
  19.0 5.3 %collective-permute-start.9 = (f32[4,8,512]{2,1,0:T(8,128)S(1)}, f32[4,8,512]{2,1,0:T(8,128)S(1)}, u32[]{:S(2)}, u32[]{:S(2)}) collective-permute-start(f32[4,8,512]{2,1,0:T(8,128)S(1)} %get-tuple-element.35.refs_0_), channel_id=1, source_target_pairs={{0,7},{1,6},{2,5},{3,4},{4,1},{5,0},{6,3},{7,2},{8,15},{9,14},{10,... | collective-permute-start | bytes 196616 | tf_op jit(solution)/shard_map/ppermute | solution.py:476
  21.9 2.5 %collective-permute-start.8 = (f32[4,8,512]{2,1,0:T(8,128)S(1)}, f32[4,8,512]{2,1,0:T(8,128)S(1)}, u32[]{:S(2)}, u32[]{:S(2)}) collective-permute-start(f32[4,8,512]{2,1,0:T(8,128)S(1)} %collective-permute-done.7.refs_1_), channel_id=1, source_target_pairs={{0,1},{1,0},{2,3},{3,2},{4,5},{5,4},{6,7},{7,6},{8,9},{9,8},{10,11... | collective-permute-start | bytes 196616 | tf_op jit(solution)/shard_map/ppermute | solution.py:476
